TPU v7x, 32 devices: a whole 2x2x4 slice. The times are simulated.
32 devices in a mesh: cluster: 4 (over z), sub: 8 (over y, x, core).
Axes of the slice: x: 2, y: 2, z: 4, core: 2. Of those that a mesh axis runs over, the one named last changes fastest.
Arguments:
- features: bfloat16 [12288, 256], P(('cluster', 'sub')), may hold values from -6 to 6
- grad_out: bfloat16 [12288, 256], P(('cluster', 'sub')), may hold values from -6 to 6
- w_self: bfloat16 [256, 256], replicated, may hold values from -0.375 to 0.375
- w_neigh: bfloat16 [256, 256], replicated, may hold values from -0.375 to 0.375
- bias: float32 [256], replicated, may hold values from -3 to 3
- tile_dst: int32 [768], P(('cluster', 'sub')), may hold values from 0 to 2
- tile_src: int32 [768], P(('cluster', 'sub')), may hold values from 0 to 14, as said below
- tile_weight: bfloat16 [768, 128, 128], P(('cluster', 'sub')), may hold values from 0 to 4
- recv_sub: int32 [32, 8], P(('cluster', 'sub')), may hold values from 0 to 1
- recv_cluster: int32 [32, 4], P(('cluster', 'sub')), may hold values from 0 to 1
Outputs:
- grad_features: bfloat16 [12288, 256], P(('cluster', 'sub'))
Inputs may be any that keep to these rules, and one draw needn't show every extreme that they name: `tile_src`: within one partition's 24 tiles, each of the source-table entries 3 to 14 is named by exactly one tile; the other tiles name own blocks.
All inputs are finite; a program needn't handle non-finite values.
Results may differ from a plain program's by a relative error of at most 0.005.
Values may be sent and summed in bfloat16 or wider, within the bound.
No kernel may reach another device: no remote copies, remote signals or barrier semaphores. Data moves between devices by JAX's collectives and lax.ppermute only.
A program may use at most 64 MiB of HBM per device.

v0:
```python
import jax
import jax.numpy as jnp
from jax import lax
from jax.sharding import PartitionSpec as P


def gelu_tanh(values):
    return (
        0.5
        * values
        * (1.0 + jnp.tanh(0.7978845608028654 * (values + 0.044715 * values * values * values)))
    )


def shards(
    features,
    grad_out,
    w_self,
    w_neigh,
    bias,
    tile_dst,
    tile_src,
    tile_weight,
    recv_sub,
    recv_cluster,
):
    sub_count = lax.axis_size("sub")
    cluster_count = lax.axis_size("cluster")
    tile_rows = tile_weight.shape[1]
    feature_dim = features.shape[1]
    own_count = features.shape[0] // tile_rows
    source_count = own_count + sub_count + cluster_count
    blocks = features.reshape(own_count, tile_rows, feature_dim)
    sent_sub = lax.all_to_all(
        recv_sub.reshape(sub_count, 1), "sub", split_axis=0, concat_axis=0, tiled=True
    )[:, 0]
    sent_cluster = lax.all_to_all(
        recv_cluster.reshape(cluster_count, 1), "cluster", split_axis=0, concat_axis=0, tiled=True
    )[:, 0]
    halo_sub = lax.all_to_all(blocks[sent_sub], "sub", split_axis=0, concat_axis=0, tiled=True)
    halo_cluster = lax.all_to_all(
        blocks[sent_cluster], "cluster", split_axis=0, concat_axis=0, tiled=True
    )
    source = jnp.concatenate([blocks, halo_sub, halo_cluster], axis=0)
    picked = source[tile_src]
    products = jnp.einsum("tij,tjd->tid", tile_weight, picked, preferred_element_type=jnp.float32)
    own_ids = jnp.arange(own_count, dtype=jnp.int32)
    dst_onehot = (tile_dst[None, :] == own_ids[:, None]).astype(jnp.float32)
    aggregate = jnp.einsum("bt,tid->bid", dst_onehot, products, precision=lax.Precision.HIGHEST)
    row_sums = jnp.sum(tile_weight.astype(jnp.float32), axis=2)
    degree = jnp.dot(dst_onehot, row_sums, precision=lax.Precision.HIGHEST)
    inverse = 1.0 / (degree + 1.0)
    neighbour_mean = (
        (aggregate * inverse[:, :, None])
        .astype(jnp.bfloat16)
        .reshape(own_count * tile_rows, feature_dim)
    )
    pre = jnp.dot(features, w_self, preferred_element_type=jnp.float32)
    pre = pre + jnp.dot(neighbour_mean, w_neigh, preferred_element_type=jnp.float32) + bias
    _, pullback = jax.vjp(gelu_tanh, pre)
    grad_pre = pullback(grad_out.astype(jnp.float32))[0].astype(jnp.bfloat16)
    grad_self = jnp.dot(grad_pre, w_self.T, preferred_element_type=jnp.float32)
    spread = jnp.dot(grad_pre, w_neigh.T, preferred_element_type=jnp.float32).reshape(
        own_count, tile_rows, feature_dim
    )
    spread = (spread * inverse[:, :, None]).astype(jnp.bfloat16)
    returned = jnp.einsum(
        "tij,tid->tjd", tile_weight, spread[tile_dst], preferred_element_type=jnp.float32
    )
    source_ids = jnp.arange(source_count, dtype=jnp.int32)
    src_onehot = (tile_src[None, :] == source_ids[:, None]).astype(jnp.float32)
    partial_value = jnp.einsum("st,tid->sid", src_onehot, returned, precision=lax.Precision.HIGHEST)
    sub_part = partial_value[own_count : own_count + sub_count].astype(jnp.bfloat16)
    cluster_part = partial_value[own_count + sub_count :].astype(jnp.bfloat16)
    back_sub = lax.all_to_all(sub_part, "sub", split_axis=0, concat_axis=0, tiled=True)
    back_cluster = lax.all_to_all(cluster_part, "cluster", split_axis=0, concat_axis=0, tiled=True)
    owner_sub = (sent_sub[None, :] == own_ids[:, None]).astype(jnp.float32)
    owner_cluster = (sent_cluster[None, :] == own_ids[:, None]).astype(jnp.float32)
    back = partial_value[:own_count]
    back = back + jnp.einsum(
        "bp,pid->bid", owner_sub, back_sub.astype(jnp.float32), precision=lax.Precision.HIGHEST
    )
    back = back + jnp.einsum(
        "bp,pid->bid",
        owner_cluster,
        back_cluster.astype(jnp.float32),
        precision=lax.Precision.HIGHEST,
    )
    total = grad_self + back.reshape(own_count * tile_rows, feature_dim)
    return total.astype(jnp.bfloat16)


def solution(mesh):
    placed = (
        P(("cluster", "sub"), None),
        P(("cluster", "sub"), None),
        P(),
        P(),
        P(),
        P(("cluster", "sub")),
        P(("cluster", "sub")),
        P(("cluster", "sub"), None, None),
        P(("cluster", "sub"), None),
        P(("cluster", "sub"), None),
    )
    return jax.shard_map(
        shards, mesh=mesh, in_specs=placed, out_specs=P(("cluster", "sub"), None), check_vma=False
    )
```

profile of v0, /device:TPU:0, one launch (start us, length us, event | category | flops | bytes accessed | tf_op | source)
XLA Modules:
  0.0 94.8 jit_solution(5474712879438760907)
XLA Ops:
  0.0 0.0 copy-start
  0.0 0.0 copy-start.11
  0.0 0.0 copy-start.1
  0.0 1.4 %copy.48 = s32[4,1,1]{2,1,0:T(1,128)} copy(s32[4,1,1]{0,2,1:T(1,128)} %bitcast.53) | data formatting | bytes 32 | tf_op jit(solution)/shard_map/all_to_all | solution.py:37
  1.4 6.4 %all-to-all-start.2 = ((s32[4,1,1]{2,1,0:T(1,128)}), s32[4,1,1]{2,1,0:T(1,128)S(1)}, u32[]{:S(2)}, u32[]{:S(2)}) async-start(s32[4,1,1]{2,1,0:T(1,128)} %copy.48), calls=%async_computation.2 | async-start | bytes 4096 | tf_op jit(solution)/shard_map/all_to_all | solution.py:37
  7.8 1.3 %copy.47 = s32[8,1,1]{2,1,0:T(1,128)} copy(s32[8,1,1]{0,2,1:T(1,128)} %bitcast.54) | data formatting | bytes 64 | tf_op jit(solution)/shard_map/all_to_all | solution.py:34
  9.1 0.7 compare_select_fusion.1
  9.7 1.4 %convert_reduce_fusion = f32[24,128]{1,0:T(8,128)S(1)} fusion(bf16[24,128,128]{2,1,0:T(8,128)(2,1)} %param.17), kind=kLoop, calls=%fused_computation.6 | loop fusion | flops 783360 | bytes 798720 | tf_op jit(solution)/shard_map/reduce_sum | solution.py:50
  11.2 0.7 compare_select_fusion
  11.8 1.3 %all-to-all-done.2 = s32[4,1,1]{2,1,0:T(1,128)S(1)} async-done(((s32[4,1,1]{2,1,0:T(1,128)}), s32[4,1,1]{2,1,0:T(1,128)S(1)}, u32[]{:S(2)}, u32[]{:S(2)}) %all-to-all-start.2) | async-done | bytes 48 | tf_op jit(solution)/shard_map/all_to_all | solution.py:37
  13.2 3.7 %all-to-all-start = ((s32[8,1,1]{2,1,0:T(1,128)}), s32[8,1,1]{2,1,0:T(1,128)S(1)}, u32[]{:S(2)}, u32[]{:S(2)}) async-start(s32[8,1,1]{2,1,0:T(1,128)} %copy.47), calls=%async_computation | async-start | bytes 8192 | tf_op jit(solution)/shard_map/all_to_all | solution.py:34
  16.9 0.2 reduce.1
  17.1 2.2 %gather_fusion.1 = bf16[4,128,256]{2,1,0:T(8,128)(2,1)} fusion(bf16[3,128,256]{2,1,0:T(8,128)(2,1)} %bitcast.47, s32[1024]{0:T(1024)S(1)} %pad_clamp_fusion.2), kind=kCustom, calls=%fused_computation.1 | custom fusion | bytes 524304 | tf_op jit(solution)/shard_map/gather | solution.py:42
  19.2 2.2 %all-to-all-done = s32[8,1,1]{2,1,0:T(1,128)S(1)} async-done(((s32[8,1,1]{2,1,0:T(1,128)}), s32[8,1,1]{2,1,0:T(1,128)S(1)}, u32[]{:S(2)}, u32[]{:S(2)}) %all-to-all-start) | async-done | bytes 64 | tf_op jit(solution)/shard_map/all_to_all | solution.py:34
  21.5 3.8 %all-to-all-start.3 = ((bf16[4,128,256]{2,1,0:T(8,128)(2,1)}), bf16[4,128,256]{2,1,0:T(8,128)(2,1)S(1)}, u32[]{:S(2)}, u32[]{:S(2)}) async-start(bf16[4,128,256]{2,1,0:T(8,128)(2,1)} %gather_fusion.1), calls=%async_computation.3 | async-start | bytes 524288 | tf_op jit(solution)/shard_map/all_to_all | solution.py:41
  25.2 0.2 reduce
  25.5 0.0 copy-done.1
  25.5 1.4 %gather_fusion = bf16[8,128,256]{2,1,0:T(8,128)(2,1)} fusion(bf16[3,128,256]{2,1,0:T(8,128)(2,1)S(1)} %bitcast.48, s32[1024]{0:T(1024)S(1)} %pad_clamp_fusion.3), kind=kCustom, calls=%fused_computation | custom fusion | bytes 1048608 | tf_op jit(solution)/shard_map/gather | solution.py:40
  26.9 7.2 %all-to-all-done.3 = bf16[4,128,256]{2,1,0:T(8,128)(2,1)S(1)} async-done(((bf16[4,128,256]{2,1,0:T(8,128)(2,1)}), bf16[4,128,256]{2,1,0:T(8,128)(2,1)S(1)}, u32[]{:S(2)}, u32[]{:S(2)}) %all-to-all-start.3) | async-done | bytes 262176 | tf_op jit(solution)/shard_map/all_to_all | solution.py:41
  34.1 3.5 %all-to-all-start.1 = ((bf16[8,128,256]{2,1,0:T(8,128)(2,1)}), bf16[8,128,256]{2,1,0:T(8,128)(2,1)S(1)}, u32[]{:S(2)}, u32[]{:S(2)}) async-start(bf16[8,128,256]{2,1,0:T(8,128)(2,1)} %gather_fusion), calls=%async_computation.1 | async-start | bytes 1048576 | tf_op jit(solution)/shard_map/all_to_all | solution.py:40
  37.6 0.0 copy-done.11
  37.6 0.1 fusion.3
  37.7 0.0 copy-done.7
  37.8 1.0 %fusion.35 = f32[384,256]{1,0:T(8,128)} fusion(bf16[384,256]{1,0:T(8,128)(2,1)S(1)} %copy-done.1, bf16[256,256]{1,0:T(8,128)(2,1)S(1)} %copy-done.7), kind=kOutput, calls=%fused_computation.63 | convolution fusion | flops 50331648 | bytes 720896 | tf_op jit(solution)/shard_map/dot_general | solution.py:58
  38.8 8.5 %all-to-all-done.1 = bf16[8,128,256]{2,1,0:T(8,128)(2,1)S(1)} async-done(((bf16[8,128,256]{2,1,0:T(8,128)(2,1)}), bf16[8,128,256]{2,1,0:T(8,128)(2,1)S(1)}, u32[]{:S(2)}, u32[]{:S(2)}) %all-to-all-start.1) | async-done | bytes 524320 | tf_op jit(solution)/shard_map/all_to_all | solution.py:40
  47.3 0.1 pad_maximum_fusion
  47.4 1.9 %gather_fusion.2 = bf16[24,128,256]{2,1,0:T(8,128)(2,1)} fusion(bf16[15,128,256]{2,1,0:T(8,128)(2,1)S(1)} %pad_maximum_fusion, s32[1024]{0:T(1024)S(1)} %pad_clamp_fusion.1), kind=kCustom, calls=%fused_computation.2 | custom fusion | bytes 3145824 | tf_op jit(solution)/shard_map/gather | solution.py:45
  49.3 2.2 %convolution_bitcast_fusion.1 = f32[24,128,256]{1,2,0:T(8,128)S(1)} fusion(bf16[24,128,256]{2,1,0:T(8,128)(2,1)} %gather_fusion.2, bf16[24,128,128]{2,1,0:T(8,128)(2,1)} %param.17), kind=kOutput, calls=%fused_computation.5 | convolution fusion | flops 201326592 | bytes 5505024 | tf_op jit(solution)/shard_map/tij,tjd->tid/dot_general | solution.py:46
  51.5 2.4 %copy.50 = f32[24,128,256]{2,0,1:T(8,128)} copy(f32[24,128,256]{1,2,0:T(8,128)S(1)} %convolution_bitcast_fusion.1) | data formatting | bytes 6291456 | tf_op jit(solution)/shard_map/tij,tjd->tid/dot_general | solution.py:46
  53.9 3.2 %fusion.22 = f32[3,128,256]{2,0,1:T(4,128)S(1)} fusion(f32[24,128,256]{2,0,1:T(8,128)} %copy.50, s32[24]{0:T(128)S(1)} %copy-done.11), kind=kOutput, calls=%fused_computation.53 | convolution fusion | flops 28311624 | bytes 3539040 | tf_op jit(solution)/shard_map/bt,tid->bid/dot_general | solution.py:49
  57.0 0.1 fusion.14
  57.2 0.0 copy-done
  57.2 0.0 copy-done.9
  57.2 0.0 copy-done.12
  57.2 0.0 copy-done.13
  57.2 0.5 fusion.9
  57.7 0.0 copy-start.5
  57.8 0.0 copy-start.2
  57.8 0.2 fusion.36
  58.0 0.4 copy-done.5
  58.4 0.1 multiply_convert_fusion
  58.5 0.6 gather_fusion.3
  59.2 0.0 copy-done.2
  59.2 2.3 %convolution_bitcast_fusion = f32[24,128,256]{1,2,0:T(8,128)} fusion(bf16[24,128,256]{2,1,0:T(8,128)(2,1)S(1)} %gather_fusion.3, bf16[24,128,128]{2,1,0:T(8,128)(2,1)S(1)} %copy-done.2), kind=kOutput, calls=%fused_computation.4 | convolution fusion | flops 201326592 | bytes 5505024 | tf_op jit(solution)/shard_map/tij,tid->tjd/dot_general | solution.py:67
  61.5 2.6 %copy.53 = f32[24,128,256]{2,0,1:T(8,128)S(1)} copy(f32[24,128,256]{1,2,0:T(8,128)} %convolution_bitcast_fusion) | data formatting | bytes 6291456 | tf_op jit(solution)/shard_map/tij,tid->tjd/dot_general | solution.py:67
  64.1 0.0 copy-done.10
  64.1 2.7 %fusion.34 = (bf16[15,128,256]{2,0,1:T(8,128)(2,1)S(1)}, f32[15,128,256]{2,0,1:T(8,128)}) fusion(f32[24,128,256]{2,0,1:T(8,128)S(1)} %copy.53, s32[24]{0:T(128)S(1)} %copy-done.10), kind=kOutput, calls=%fused_computation.62 | convolution fusion | flops 142049632 | bytes 6094944 | tf_op jit(solution)/shard_map/st,tid->sid/dot_general | solution.py:72
  66.8 1.0 %copy-done.4 = bf16[15,128,256]{2,0,1:T(8,128)(2,1)} copy-done((bf16[15,128,256]{2,0,1:T(8,128)(2,1)}, bf16[15,128,256]{2,0,1:T(8,128)(2,1)S(1)}, u32[]{:S(2)}) %copy-start.4) | copy-done | bytes 983064
  67.7 0.1 slice.24
  67.9 0.7 copy.56
  68.6 3.4 %all-to-all-start.5 = ((bf16[4,128,256]{2,1,0:T(8,128)(2,1)}), bf16[4,128,256]{2,1,0:T(8,128)(2,1)S(1)}, u32[]{:S(2)}, u32[]{:S(2)}) async-start(bf16[4,128,256]{2,1,0:T(8,128)(2,1)} %copy.56), calls=%async_computation.5 | async-start | bytes 524288 | tf_op jit(solution)/shard_map/all_to_all | solution.py:76
  72.0 0.0 copy-start.3
  72.1 1.5 %slice.23 = bf16[8,128,256]{2,0,1:T(8,128)(2,1)S(1)} slice(bf16[15,128,256]{2,0,1:T(8,128)(2,1)} %copy-done.4), slice={[3:11], [0:128], [0:256]} | slice | bytes 1048576 | tf_op jit(solution)/shard_map/slice | solution.py:73
  73.6 0.9 copy.54
  74.5 4.3 %all-to-all-done.5 = bf16[4,128,256]{2,1,0:T(8,128)(2,1)S(1)} async-done(((bf16[4,128,256]{2,1,0:T(8,128)(2,1)}), bf16[4,128,256]{2,1,0:T(8,128)(2,1)S(1)}, u32[]{:S(2)}, u32[]{:S(2)}) %all-to-all-start.5) | async-done | bytes 262176 | tf_op jit(solution)/shard_map/all_to_all | solution.py:76
  78.8 4.4 %all-to-all-start.4 = ((bf16[8,128,256]{2,1,0:T(8,128)(2,1)}), bf16[8,128,256]{2,1,0:T(8,128)(2,1)S(1)}, u32[]{:S(2)}, u32[]{:S(2)}) async-start(bf16[8,128,256]{2,1,0:T(8,128)(2,1)} %copy.54), calls=%async_computation.4 | async-start | bytes 1048576 | tf_op jit(solution)/shard_map/all_to_all | solution.py:75
  83.2 0.3 fusion.15
  83.5 9.4 %all-to-all-done.4 = bf16[8,128,256]{2,1,0:T(8,128)(2,1)S(1)} async-done(((bf16[8,128,256]{2,1,0:T(8,128)(2,1)}), bf16[8,128,256]{2,1,0:T(8,128)(2,1)S(1)}, u32[]{:S(2)}, u32[]{:S(2)}) %all-to-all-start.4) | async-done | bytes 524320 | tf_op jit(solution)/shard_map/all_to_all | solution.py:75
  93.0 0.0 copy-done.3
  93.0 0.4 fusion
  93.4 0.1 copy.58
  93.5 0.0 copy-done.6
  93.5 0.4 copy-done.8
  93.9 0.9 fusion.2
  (14 shorter events, 0.1 us)
Async XLA Ops:
  0.0 57.2 %copy-start = (bf16[256,256]{1,0:T(8,128)(2,1)S(1)}, bf16[256,256]{1,0:T(8,128)(2,1)}, u32[]{:S(2)}) copy-start(bf16[256,256]{1,0:T(8,128)(2,1)} %param.13) | copy-start | bytes 393220
  0.0 37.6 %copy-start.11 = (s32[24]{0:T(128)S(1)}, s32[24]{0:T(128)}, u32[]{:S(2)}) copy-start(s32[24]{0:T(128)} %param.15) | copy-start | bytes 292
  0.0 25.5 %copy-start.1 = (bf16[384,256]{1,0:T(8,128)(2,1)S(1)}, bf16[384,256]{1,0:T(8,128)(2,1)}, u32[]{:S(2)}) copy-start(bf16[384,256]{1,0:T(8,128)(2,1)} %param.10) | copy-start | bytes 589828
  0.0 37.7 %copy-start.7 = (bf16[256,256]{1,0:T(8,128)(2,1)S(1)}, bf16[256,256]{1,0:T(8,128)(2,1)}, u32[]{:S(2)}) copy-start(bf16[256,256]{1,0:T(8,128)(2,1)} %param.12) | copy-start | bytes 393220
  1.4 11.7 %all-to-all-start.2 = ((s32[4,1,1]{2,1,0:T(1,128)}), s32[4,1,1]{2,1,0:T(1,128)S(1)}, u32[]{:S(2)}, u32[]{:S(2)}) async-start(s32[4,1,1]{2,1,0:T(1,128)} %copy.48), calls=%async_computation.2 | async-start | bytes 4096 | tf_op jit(solution)/shard_map/all_to_all | solution.py:37
  13.2 8.3 %all-to-all-start = ((s32[8,1,1]{2,1,0:T(1,128)}), s32[8,1,1]{2,1,0:T(1,128)S(1)}, u32[]{:S(2)}, u32[]{:S(2)}) async-start(s32[8,1,1]{2,1,0:T(1,128)} %copy.47), calls=%async_computation | async-start | bytes 8192 | tf_op jit(solution)/shard_map/all_to_all | solution.py:34
  21.5 12.7 %all-to-all-start.3 = ((bf16[4,128,256]{2,1,0:T(8,128)(2,1)}), bf16[4,128,256]{2,1,0:T(8,128)(2,1)S(1)}, u32[]{:S(2)}, u32[]{:S(2)}) async-start(bf16[4,128,256]{2,1,0:T(8,128)(2,1)} %gather_fusion.1), calls=%async_computation.3 | async-start | bytes 524288 | tf_op jit(solution)/shard_map/all_to_all | solution.py:41
  34.1 13.2 %all-to-all-start.1 = ((bf16[8,128,256]{2,1,0:T(8,128)(2,1)}), bf16[8,128,256]{2,1,0:T(8,128)(2,1)S(1)}, u32[]{:S(2)}, u32[]{:S(2)}) async-start(bf16[8,128,256]{2,1,0:T(8,128)(2,1)} %gather_fusion), calls=%async_computation.1 | async-start | bytes 1048576 | tf_op jit(solution)/shard_map/all_to_all | solution.py:40
  53.9 3.3 %copy-start.9 = (f32[384,256]{1,0:T(8,128)S(1)}, f32[384,256]{1,0:T(8,128)}, u32[]{:S(2)}) copy-start(f32[384,256]{1,0:T(8,128)} %fusion.35) | copy-start | bytes 1179652
  53.9 3.3 %copy-start.12 = (bf16[384,256]{1,0:T(8,128)(2,1)S(1)}, bf16[384,256]{1,0:T(8,128)(2,1)}, u32[]{:S(2)}) copy-start(bf16[384,256]{1,0:T(8,128)(2,1)} %param.11) | copy-start | bytes 589828
  53.9 3.3 %copy-start.13 = (f32[256]{0:T(256)S(1)}, f32[256]{0:T(256)}, u32[]{:S(2)}) copy-start(f32[256]{0:T(256)} %param.14) | copy-start | bytes 3076
  57.7 0.7 copy-start.5
  57.8 1.4 %copy-start.2 = (bf16[24,128,128]{2,1,0:T(8,128)(2,1)S(1)}, bf16[24,128,128]{2,1,0:T(8,128)(2,1)}, u32[]{:S(2)}) copy-start(bf16[24,128,128]{2,1,0:T(8,128)(2,1)} %param.17) | copy-start | bytes 2359300
  61.5 2.6 %copy-start.10 = (s32[24]{0:T(128)S(1)}, s32[24]{0:T(128)}, u32[]{:S(2)}) copy-start(s32[24]{0:T(128)} %param.16) | copy-start | bytes 292
  66.8 1.0 %copy-start.4 = (bf16[15,128,256]{2,0,1:T(8,128)(2,1)}, bf16[15,128,256]{2,0,1:T(8,128)(2,1)S(1)}, u32[]{:S(2)}) copy-start(bf16[15,128,256]{2,0,1:T(8,128)(2,1)S(1)} %get-tuple-element.5) | copy-start | bytes 2949124
  68.6 10.2 %all-to-all-start.5 = ((bf16[4,128,256]{2,1,0:T(8,128)(2,1)}), bf16[4,128,256]{2,1,0:T(8,128)(2,1)S(1)}, u32[]{:S(2)}, u32[]{:S(2)}) async-start(bf16[4,128,256]{2,1,0:T(8,128)(2,1)} %copy.56), calls=%async_computation.5 | async-start | bytes 524288 | tf_op jit(solution)/shard_map/all_to_all | solution.py:76
  72.0 20.9 %copy-start.3 = (f32[15,128,256]{2,0,1:T(8,128)S(1)}, f32[15,128,256]{2,0,1:T(8,128)}, u32[]{:S(2)}) copy-start(f32[15,128,256]{2,0,1:T(8,128)} %get-tuple-element.6) | copy-start | bytes 5898244
  78.8 14.2 %all-to-all-start.4 = ((bf16[8,128,256]{2,1,0:T(8,128)(2,1)}), bf16[8,128,256]{2,1,0:T(8,128)(2,1)S(1)}, u32[]{:S(2)}, u32[]{:S(2)}) async-start(bf16[8,128,256]{2,1,0:T(8,128)(2,1)} %copy.54), calls=%async_computation.4 | async-start | bytes 1048576 | tf_op jit(solution)/shard_map/all_to_all | solution.py:75
  83.5 10.0 %copy-start.6 = (bf16[384,256]{1,0:T(8,128)(2,1)S(1)}, bf16[384,256]{1,0:T(8,128)(2,1)}, u32[]{:S(2)}) copy-start(bf16[384,256]{1,0:T(8,128)(2,1)} %copy-done.5) | copy-start | bytes 589828
  93.0 0.9 copy-start.8
where the time goes:
time: 95.5 us; the launch traced here: 94.8 us
  waiting for transfers between devices  33 us (35%)
  starting transfers between devices  25.2 us (26%)
  local copies, waits for them, and re-layouts  19 us (20%)
  matrix products  13.8 us (14%)
  other arithmetic  3.51 us (4%)
    all_to_all x1, waiting for transfers between devices, shards(): lax.all_to_all(sub_part, 'sub', split_axis=0, concat_axis=0, tiled=True)  9.44 us
    all_to_all x1, waiting for transfers between devices, shards(): lax.all_to_all(blocks[sent_sub], 'sub', split_axis=0, concat_axis=0, tile...  8.54 us
    all_to_all x1, waiting for transfers between devices, shards(): lax.all_to_all(blocks[sent_cluster], 'cluster', split_axis=0, concat_axis...  7.23 us
    all_to_all x1, starting transfers between devices, shards(): lax.all_to_all(recv_cluster.reshape(cluster_count, 1), 'cluster', split_a...  6.36 us
    all_to_all x1, starting transfers between devices, shards(): lax.all_to_all(sub_part, 'sub', split_axis=0, concat_axis=0, tiled=True)  4.44 us
    all_to_all x1, waiting for transfers between devices, shards(): lax.all_to_all(cluster_part, 'cluster', split_axis=0, concat_axis=0, tile...  4.29 us
    all_to_all x1, starting transfers between devices, shards(): lax.all_to_all(blocks[sent_cluster], 'cluster', split_axis=0, concat_axis...  3.76 us
    all_to_all x1, starting transfers between devices, shards(): lax.all_to_all(recv_sub.reshape(sub_count, 1), 'sub', split_axis=0, conca...  3.72 us
  transfers between devices with their start and end apart: 6, of which 6 were waited for; matrix products, arithmetic and copies ran while one was open for 13% of the time, Pallas kernels for 0%

commit v1 on v0

v1 whole, which is shorter than its diff:
```python
import functools

import jax
import jax.numpy as jnp
from jax import lax
from jax.experimental import pallas as pl
from jax.experimental.pallas import tpu as pltpu
from jax.sharding import PartitionSpec as P

BF = jnp.bfloat16
F32 = jnp.float32
BOUNDARY = 2
VMEM = pl.BlockSpec(memory_space=pltpu.VMEM)
SMEM = pl.BlockSpec(memory_space=pltpu.SMEM)
PARAMS = pltpu.CompilerParams(vmem_limit_bytes=24 * 1024 * 1024)


def dot(left, right):
    return jnp.dot(left, right, preferred_element_type=F32)


def dot_right_transposed(left, right):
    return lax.dot_general(left, right, (((1,), (1,)), ((), ())), preferred_element_type=F32)


def gelu_slope(v):
    scale = 0.7978845608028654
    t = jnp.tanh(scale * (v + 0.044715 * v * v * v))
    return 0.5 * (1.0 + t) + (0.5 * scale) * v * (1.0 - t * t) * (1.0 + 3.0 * 0.044715 * v * v)


def prepare_kernel(
    own, sub_count, cluster_count,
    tile_dst, tile_src, features, w_self, bias, tile_weight,
    dense, dense_t, own_sum, own_pre, inverse,
):
    size = tile_weight.shape[1]
    sub_id = lax.axis_index("sub")
    cluster_id = lax.axis_index("cluster")
    dense[...] = jnp.zeros_like(dense)
    dense_t[...] = jnp.zeros_like(dense_t)

    def place(t, carry):
        src = tile_src[t]
        from_sub = own + ((src - own) ^ sub_id)
        from_cluster = own + sub_count + ((src - own - sub_count) ^ cluster_id)
        slot = jnp.where(src < own, src, jnp.where(src < own + sub_count, from_sub, from_cluster))
        dst = pl.ds(pl.multiple_of(tile_dst[t] * size, size), size)
        col = pl.ds(pl.multiple_of(slot * size, size), size)
        tile = tile_weight[t]
        dense[dst, col] = dense[dst, col] + tile
        dense_t[col, dst] = dense_t[col, dst] + tile.T
        return carry

    lax.fori_loop(0, tile_weight.shape[0], place, 0, unroll=4)
    slots = own + sub_count + cluster_count
    total = dense[:, 0:size].astype(F32)
    for slot in range(1, slots):
        total = total + dense[:, slot * size : (slot + 1) * size].astype(F32)
    degree = jnp.sum(total, axis=1, keepdims=True)
    inverse[...] = jnp.broadcast_to(1.0 / (degree + 1.0), inverse.shape)
    own_sum[...] = dot(dense[:, 0 : own * size], features[...])
    own_pre[...] = dot(features[...], w_self[...]) + bias[...]


def middle_kernel(
    own, sub_count, cluster_count,
    recv_sub, recv_cluster, features, grad_out, w_neigh, dense, dense_t, own_sum, own_pre, inverse,
    *rest,
):
    peers = sub_count + cluster_count - 2
    received = rest[:peers]
    sent = rest[peers : 2 * peers]
    kept, spread, grad_pre, halo = rest[2 * peers :]
    size = halo.shape[0] // (sub_count + cluster_count)
    sub_id = lax.axis_index("sub")
    cluster_id = lax.axis_index("cluster")

    def pick(slot, source, index):
        halo[slot * size : (slot + 1) * size, :] = source[
            pl.ds(pl.multiple_of(index * size, size), size), :
        ]

    for d in range(sub_count):
        pick(d, received[d - 1] if d else features, recv_sub[0, sub_id ^ d])
    for d in range(cluster_count):
        source = received[sub_count - 1 + d - 1] if d else features
        pick(sub_count + d, source, recv_cluster[0, cluster_id ^ d])
    inv = jnp.concatenate([inverse[...]] * (features.shape[1] // size), axis=1)
    aggregate = own_sum[...] + dot(dense[:, own * size :], halo[...])
    mean = (aggregate * inv).astype(BF)
    pre = own_pre[...] + dot(mean, w_neigh[...])
    grad = (grad_out[...].astype(F32) * gelu_slope(pre)).astype(BF)
    grad_pre[...] = grad
    spread[...] = (dot_right_transposed(grad, w_neigh[...]) * inv).astype(BF)

    def partial(slot):
        rows = slice((own + slot) * size, (own + slot + 1) * size)
        return dot(dense_t[rows, :], spread[...]).astype(BF)

    for d in range(sub_count):
        if d:
            sent[d - 1][...] = partial(d)
        else:
            kept[0] = partial(0)
    for d in range(cluster_count):
        if d:
            sent[sub_count - 1 + d - 1][...] = partial(sub_count + d)
        else:
            kept[1] = partial(sub_count)


def own_kernel(own, recv_sub, recv_cluster, w_self, dense_t, kept, spread, grad_pre, total):
    size = kept.shape[1]
    total[...] = dot_right_transposed(grad_pre[...], w_self[...]) + dot(
        dense_t[0 : own * size, :], spread[...]
    )
    for i, index in enumerate(
        (recv_sub[0, lax.axis_index("sub")], recv_cluster[0, lax.axis_index("cluster")])
    ):
        rows = pl.ds(pl.multiple_of(index * size, size), size)
        total[rows, :] = total[rows, :] + kept[i].astype(F32)


def final_kernel(sub_count, cluster_count, asked, total, *rest):
    peers = sub_count + cluster_count - 2
    received = rest[:peers]
    out, work = rest[peers:]
    size = received[0].shape[0]
    sub_id = lax.axis_index("sub")
    cluster_id = lax.axis_index("cluster")
    work[...] = total[...]

    def add(part, index):
        rows = pl.ds(pl.multiple_of(index * size, size), size)
        work[rows, :] = work[rows, :] + part[...].astype(F32)

    for d in range(1, sub_count):
        add(received[d - 1], asked[cluster_id * sub_count + (sub_id ^ d), sub_id])
    for d in range(1, cluster_count):
        add(
            received[sub_count - 1 + d - 1],
            asked[(cluster_id ^ d) * sub_count + sub_id, sub_count + cluster_id],
        )
    out[...] = work[...].astype(BF)


def swap(value, axis, count, d):
    return lax.ppermute(value, axis, [(i, i ^ d) for i in range(count)])


def exchange(values, sub_count, cluster_count):
    got = [swap(values[d - 1], "sub", sub_count, d) for d in range(1, sub_count)]
    rest = values[sub_count - 1 :]
    got += [swap(rest[d - 1], "cluster", cluster_count, d) for d in range(1, cluster_count)]
    return got


def cost(flops, moved):
    return pl.CostEstimate(flops=flops, bytes_accessed=moved, transcendentals=0)


def shards(
    features, grad_out, w_self, w_neigh, bias, tile_dst, tile_src, tile_weight, recv_sub, recv_cluster
):
    sub_count = lax.axis_size("sub")
    cluster_count = lax.axis_size("cluster")
    peers = sub_count + cluster_count - 2
    size = tile_weight.shape[1]
    rows, width = features.shape
    own = rows // size
    slots = own + sub_count + cluster_count
    counts = (own, sub_count, cluster_count)

    asked = lax.all_gather(
        jnp.concatenate([recv_sub, recv_cluster], axis=1), ("cluster", "sub"), axis=0, tiled=True
    )
    edge = features[: BOUNDARY * size]
    halos = exchange([edge] * peers, sub_count, cluster_count)

    wide = jax.ShapeDtypeStruct((rows, width), F32)
    narrow = jax.ShapeDtypeStruct((rows, width), BF)
    block = jax.ShapeDtypeStruct((size, width), BF)
    dense, dense_t, own_sum, own_pre, inverse = pl.pallas_call(
        functools.partial(prepare_kernel, *counts),
        out_shape=[
            jax.ShapeDtypeStruct((rows, slots * size), BF),
            jax.ShapeDtypeStruct((slots * size, rows), BF),
            wide,
            wide,
            jax.ShapeDtypeStruct((rows, size), F32),
        ],
        in_specs=[SMEM, SMEM, VMEM, VMEM, VMEM, VMEM],
        out_specs=[VMEM] * 5,
        compiler_params=PARAMS,
        cost_estimate=cost(2 * rows * rows * width * 2, 6 * 1024 * 1024),
        name="prepare",
    )(tile_dst, tile_src, features, w_self, bias.reshape(1, width), tile_weight)

    outs = pl.pallas_call(
        functools.partial(middle_kernel, *counts),
        out_shape=[block] * peers + [jax.ShapeDtypeStruct((2, size, width), BF), narrow, narrow],
        in_specs=[SMEM, SMEM] + [VMEM] * (8 + peers),
        out_specs=[VMEM] * (peers + 3),
        scratch_shapes=[pltpu.VMEM(((sub_count + cluster_count) * size, width), BF)],
        compiler_params=PARAMS,
        cost_estimate=cost(4 * rows * slots * size * width, 6 * 1024 * 1024),
        name="middle",
    )(
        recv_sub, recv_cluster, features, grad_out, w_neigh,
        dense, dense_t, own_sum, own_pre, inverse, *halos,
    )
    sent, (kept, spread, grad_pre) = outs[:peers], outs[peers:]
    returned = exchange(sent, sub_count, cluster_count)

    total = pl.pallas_call(
        functools.partial(own_kernel, own),
        out_shape=wide,
        in_specs=[SMEM, SMEM] + [VMEM] * 5,
        out_specs=VMEM,
        compiler_params=PARAMS,
        cost_estimate=cost(4 * rows * rows * width, 2 * 1024 * 1024),
        name="own",
    )(recv_sub, recv_cluster, w_self, dense_t, kept, spread, grad_pre)

    return pl.pallas_call(
        functools.partial(final_kernel, sub_count, cluster_count),
        out_shape=narrow,
        in_specs=[SMEM, VMEM] + [VMEM] * peers,
        out_specs=VMEM,
        scratch_shapes=[pltpu.VMEM((rows, width), F32)],
        compiler_params=PARAMS,
        cost_estimate=cost(rows * width * 4, 2 * 1024 * 1024),
        name="final",
    )(asked, total, *returned)


def solution(mesh):
    placed = (
        P(("cluster", "sub"), None),
        P(("cluster", "sub"), None),
        P(),
        P(),
        P(),
        P(("cluster", "sub")),
        P(("cluster", "sub")),
        P(("cluster", "sub"), None, None),
        P(("cluster", "sub"), None),
        P(("cluster", "sub"), None),
    )
    return jax.shard_map(
        shards, mesh=mesh, in_specs=placed, out_specs=P(("cluster", "sub"), None), check_vma=False
    )
```

time: 95.5 us -> 86.2 us (0.903)
  blocking collectives: 0 us -> 39.3 us
  waiting for transfers between devices: 33 us -> 3.83 us
  matrix products: 13.8 us -> 0 us
  local copies, waits for them, and re-layouts: 19 us -> 8.12 us
  Pallas kernels: 0 us -> 6.73 us
  other arithmetic: 3.51 us -> 0.07 us
  starting transfers between devices: 25.2 us -> 27.7 us
    all_gather x0 -> x1, blocking collectives: none -> 39.3 us  [shards(): lax.all_gather(jnp.concatenate([recv_sub, recv_cluster], axis=1), ('clust...]
    all_to_all x6 -> x0, waiting for transfers between devices: 33 us -> none  [the longest x1 9.44 us: shards(): lax.all_to_all(sub_part, 'sub', split_axis=0, concat_axis=0, tiled=True)]
    ppermute x0 -> x20, starting transfers between devices: none -> 27.7 us  [swap(): return lax.ppermute(value, axis, [(i, i ^ d) for i in range(count)])]
    all_to_all x6 -> x0, starting transfers between devices: 25.2 us -> none  [the longest x1 6.36 us: shards(): lax.all_to_all(recv_cluster.reshape(cluster_count, 1), 'cluster', split_a...]
    dot_general x11 -> x0, matrix products: 13.8 us -> none  [the longest x1 3.16 us: shards(): jnp.einsum('bt,tid->bid', dst_onehot, products, precision=lax.Precision.H...]
    pallas_call x0 -> x4, Pallas kernels: none -> 6.73 us  [the longest x1 2.44 us: shards(): pl.pallas_call(functools.partial(middle_kernel, *counts), out_shape=[bloc...]
    gather x4 -> x0, local copies, waits for them, and re-layouts: 6.1 us -> none  [the longest x1 2.19 us: shards(): blocks[sent_cluster]]
    unnamed x28 -> x20, local copies, waits for them, and re-layouts: 1.82 us -> 7.16 us
  transfers between devices with their start and end apart: 6 -> 20, of which waited for: 6 -> 4; matrix products, arithmetic and copies ran while one was open for 13% -> 0% of each run, Pallas kernels for 0% -> 3%
where the time goes in v1:
time: 86.2 us; the launch traced here: 85.9 us
  blocking collectives  39.3 us (46%)
  starting transfers between devices  27.7 us (32%)
  local copies, waits for them, and re-layouts  8.12 us (9%)
  Pallas kernels  6.73 us (8%)
  waiting for transfers between devices  3.83 us (4%)
    all_gather x1, blocking collectives, shards(): lax.all_gather(jnp.concatenate([recv_sub, recv_cluster], axis=1), ('clust...  39.3 us
    ppermute x20, starting transfers between devices, swap(): return lax.ppermute(value, axis, [(i, i ^ d) for i in range(count)])  27.7 us
    unnamed x20, local copies, waits for them, and re-layouts  7.16 us
    ppermute x20, waiting for transfers between devices, swap(): return lax.ppermute(value, axis, [(i, i ^ d) for i in range(count)])  3.83 us
    pallas_call x1, Pallas kernels, shards(): pl.pallas_call(functools.partial(middle_kernel, *counts), out_shape=[bloc...  2.44 us
    pallas_call x1, Pallas kernels, shards(): pl.pallas_call(functools.partial(prepare_kernel, *counts), out_shape=[jax...  1.76 us
  transfers between devices with their start and end apart: 20, of which 4 were waited for; matrix products, arithmetic and copies ran while one was open for 0% of the time, Pallas kernels for 3%

profile of v1, /device:TPU:0, one launch (start us, length us, event | category | flops | bytes accessed | tf_op | source)
XLA Modules:
  0.0 85.9 jit_solution(17756703452144656526)
XLA Ops:
  0.0 0.0 copy-start.3
  0.0 1.0 %slice.3 = bf16[256,256]{1,0:T(8,128)(2,1)S(1)} slice(bf16[384,256]{1,0:T(8,128)(2,1)} %features.3), slice={[0:256], [0:256]} | slice | bytes 262144 | tf_op jit(solution)/shard_map/slice | solution.py:178
  1.0 0.5 collective-permute-start
  1.5 2.6 %collective-permute-start.1 = (bf16[256,256]{1,0:T(8,128)(2,1)S(1)}, bf16[256,256]{1,0:T(8,128)(2,1)S(1)}, u32[]{:S(2)}, u32[]{:S(2)}) collective-permute-start(bf16[256,256]{1,0:T(8,128)(2,1)S(1)} %slice.3), channel_id=1, source_target_pairs={{0,2},{1,3},{2,0},{3,1},{4,6},{5,7},{6,4},{7,5},{8,10},{9,11},{10,... | collective-permute-start | bytes 393224 | tf_op jit(solution)/shard_map/ppermute | solution.py:149
  4.0 0.1 collective-permute-start.2
  4.1 1.8 %collective-permute-start.3 = (bf16[256,256]{1,0:T(8,128)(2,1)S(1)}, bf16[256,256]{1,0:T(8,128)(2,1)S(1)}, u32[]{:S(2)}, u32[]{:S(2)}) collective-permute-start(bf16[256,256]{1,0:T(8,128)(2,1)S(1)} %slice.3), channel_id=1, source_target_pairs={{0,4},{1,5},{2,6},{3,7},{4,0},{5,1},{6,2},{7,3},{8,12},{9,13},{10,... | collective-permute-start | bytes 393224 | tf_op jit(solution)/shard_map/ppermute | solution.py:149
  5.9 0.0 collective-permute-start.4
  5.9 0.0 collective-permute-done.rest_0_
  5.9 2.6 %collective-permute-start.5 = (bf16[256,256]{1,0:T(8,128)(2,1)S(1)}, bf16[256,256]{1,0:T(8,128)(2,1)S(1)}, u32[]{:S(2)}, u32[]{:S(2)}) collective-permute-start(bf16[256,256]{1,0:T(8,128)(2,1)S(1)} %slice.3), channel_id=1, source_target_pairs={{0,6},{1,7},{2,4},{3,5},{4,2},{5,3},{6,0},{7,1},{8,14},{9,15},{10,... | collective-permute-start | bytes 393224 | tf_op jit(solution)/shard_map/ppermute | solution.py:149
  8.5 0.0 collective-permute-done.1.rest_1_
  8.5 1.6 %collective-permute-start.6 = (bf16[256,256]{1,0:T(8,128)(2,1)S(1)}, bf16[256,256]{1,0:T(8,128)(2,1)S(1)}, u32[]{:S(2)}, u32[]{:S(2)}) collective-permute-start(bf16[256,256]{1,0:T(8,128)(2,1)S(1)} %slice.3), channel_id=1, source_target_pairs={{0,7},{1,6},{2,5},{3,4},{4,3},{5,2},{6,1},{7,0},{8,15},{9,14},{10,... | collective-permute-start | bytes 393224 | tf_op jit(solution)/shard_map/ppermute | solution.py:149
  10.1 0.6 collective-permute-done.2.rest_2_
  10.7 1.7 %collective-permute-start.7 = (bf16[256,256]{1,0:T(8,128)(2,1)S(1)}, bf16[256,256]{1,0:T(8,128)(2,1)S(1)}, u32[]{:S(2)}, u32[]{:S(2)}) collective-permute-start(bf16[256,256]{1,0:T(8,128)(2,1)S(1)} %slice.3), channel_id=1, source_target_pairs={{0,8},{8,0},{16,24},{24,16},{1,9},{9,1},{17,25},{25,17},{2,10},{10... | collective-permute-start | bytes 393224 | tf_op jit(solution)/shard_map/ppermute | solution.py:149
  12.3 0.0 collective-permute-done.3.rest_3_
  12.3 2.6 %collective-permute-start.8 = (bf16[256,256]{1,0:T(8,128)(2,1)S(1)}, bf16[256,256]{1,0:T(8,128)(2,1)S(1)}, u32[]{:S(2)}, u32[]{:S(2)}) collective-permute-start(bf16[256,256]{1,0:T(8,128)(2,1)S(1)} %slice.3), channel_id=1, source_target_pairs={{0,16},{8,24},{16,0},{24,8},{1,17},{9,25},{17,1},{25,9},{2,18},{10... | collective-permute-start | bytes 393224 | tf_op jit(solution)/shard_map/ppermute | solution.py:149
  14.9 2.6 %collective-permute-done.4.rest_4_ = bf16[256,256]{1,0:T(8,128)(2,1)S(1)} collective-permute-done((bf16[256,256]{1,0:T(8,128)(2,1)S(1)}, bf16[256,256]{1,0:T(8,128)(2,1)S(1)}, u32[]{:S(2)}, u32[]{:S(2)}) %collective-permute-start.4) | collective-permute-done | bytes 131104 | tf_op jit(solution)/shard_map/ppermute | solution.py:149
  17.6 4.0 %collective-permute-start.9 = (bf16[256,256]{1,0:T(8,128)(2,1)S(1)}, bf16[256,256]{1,0:T(8,128)(2,1)S(1)}, u32[]{:S(2)}, u32[]{:S(2)}) collective-permute-start(bf16[256,256]{1,0:T(8,128)(2,1)S(1)} %slice.3), channel_id=1, source_target_pairs={{0,24},{8,16},{16,8},{24,0},{1,25},{9,17},{17,9},{25,1},{2,26},{10... | collective-permute-start | bytes 393224 | tf_op jit(solution)/shard_map/ppermute | solution.py:149
  21.6 0.0 copy-start
  21.6 0.9 %copy-done = bf16[384,256]{1,0:T(8,128)(2,1)S(1)} copy-done((bf16[384,256]{1,0:T(8,128)(2,1)S(1)}, bf16[384,256]{1,0:T(8,128)(2,1)}, u32[]{:S(2)}) %copy-start) | copy-done | bytes 196632
  22.5 0.0 copy-start.1
  22.5 1.1 %copy-done.1 = bf16[24,128,128]{2,1,0:T(8,128)(2,1)S(1)} copy-done((bf16[24,128,128]{2,1,0:T(8,128)(2,1)S(1)}, bf16[24,128,128]{2,1,0:T(8,128)(2,1)}, u32[]{:S(2)}) %copy-start.1) | copy-done | bytes 786456
  23.6 0.0 copy-start.2
  23.6 0.9 %copy-done.2 = bf16[256,256]{1,0:T(8,128)(2,1)S(1)} copy-done((bf16[256,256]{1,0:T(8,128)(2,1)S(1)}, bf16[256,256]{1,0:T(8,128)(2,1)}, u32[]{:S(2)}) %copy-start.2) | copy-done | bytes 131096
  24.5 0.0 copy-start.7
  24.5 0.7 copy-done.7
  25.2 0.0 copy-start.8
  25.2 0.7 copy-done.8
  25.9 0.7 copy-done.9
  26.5 1.8 %prepare.1 = (bf16[384,1920]{1,0:T(8,128)(2,1)S(1)}, bf16[1920,384]{1,0:T(8,128)(2,1)S(1)}, f32[384,256]{1,0:T(8,128)S(1)}, f32[384,256]{1,0:T(8,128)S(1)}, f32[384,128]{1,0:T(8,128)S(1)}) custom-call(s32[24]{0:T(128)S(1)} %copy-done.8, s32[24]{0:T(128)S(1)} %copy-done.9, bf16[384,256]{1,0:T(8,128)(2,1)S(1)} %copy-done, bf16[256,256]{1,0:T(8,128)(2,1)S(1)} %copy-done.2, ...), custom_call_target="tpu_custom_call" | custom-call | flops 150994944 | bytes 6291456 | tf_op jit(solution)/shard_map/prepare/pallas_call | solution.py:184
  28.3 0.0 collective-permute-done.5.rest_5_
  28.3 0.0 collective-permute-done.6.rest_6_
  28.3 0.0 collective-permute-done.7.rest_7_
  28.3 0.0 collective-permute-done.8.rest_8_
  28.3 0.0 collective-permute-done.9.rest_9_
  28.3 0.0 copy-done.3
  28.3 0.0 copy-start.4
  28.4 0.9 %copy-done.4 = bf16[256,256]{1,0:T(8,128)(2,1)S(1)} copy-done((bf16[256,256]{1,0:T(8,128)(2,1)S(1)}, bf16[256,256]{1,0:T(8,128)(2,1)}, u32[]{:S(2)}) %copy-start.4) | copy-done | bytes 131096
  29.2 0.7 copy-done.5
  29.9 0.7 copy-done.6
  30.6 2.4 %middle.1 = (bf16[128,256]{1,0:T(8,128)(2,1)S(1)}, bf16[128,256]{1,0:T(8,128)(2,1)S(1)}, bf16[128,256]{1,0:T(8,128)(2,1)S(1)}, bf16[128,256]{1,0:T(8,128)(2,1)S(...) custom-call(s32[1,8]{1,0:T(1,128)S(1)} %copy-done.6, ...), custom_call_target="tpu_custom_call" | custom-call | flops 754974720 | bytes 6291456 | tf_op jit(solution)/shard_map/middle/pallas_call | solution.py:200
  33.0 0.5 collective-permute-start.10
  33.5 1.5 %collective-permute-start.11 = (bf16[128,256]{1,0:T(8,128)(2,1)S(1)}, bf16[128,256]{1,0:T(8,128)(2,1)S(1)}, u32[]{:S(2)}, u32[]{:S(2)}) collective-permute-start(bf16[128,256]{1,0:T(8,128)(2,1)S(1)} %get-tuple-element.32), channel_id=1, source_target_pairs={{0,2},{1,3},{2,0},{3,1},{4,6},{5,7},{6,4},{7,5},{8,10},{9,11},{10,... | collective-permute-start | bytes 196616 | tf_op jit(solution)/shard_map/ppermute | solution.py:149
  35.0 0.0 collective-permute-start.12
  35.0 1.5 %collective-permute-start.13 = (bf16[128,256]{1,0:T(8,128)(2,1)S(1)}, bf16[128,256]{1,0:T(8,128)(2,1)S(1)}, u32[]{:S(2)}, u32[]{:S(2)}) collective-permute-start(bf16[128,256]{1,0:T(8,128)(2,1)S(1)} %get-tuple-element.34), channel_id=1, source_target_pairs={{0,4},{1,5},{2,6},{3,7},{4,0},{5,1},{6,2},{7,3},{8,12},{9,13},{10,... | collective-permute-start | bytes 196616 | tf_op jit(solution)/shard_map/ppermute | solution.py:149
  36.5 0.5 collective-permute-start.14
  37.0 0.0 collective-permute-done.10.rest_0_
  37.0 2.5 %collective-permute-start.15 = (bf16[128,256]{1,0:T(8,128)(2,1)S(1)}, bf16[128,256]{1,0:T(8,128)(2,1)S(1)}, u32[]{:S(2)}, u32[]{:S(2)}) collective-permute-start(bf16[128,256]{1,0:T(8,128)(2,1)S(1)} %get-tuple-element.36), channel_id=1, source_target_pairs={{0,6},{1,7},{2,4},{3,5},{4,2},{5,3},{6,0},{7,1},{8,14},{9,15},{10,... | collective-permute-start | bytes 196616 | tf_op jit(solution)/shard_map/ppermute | solution.py:149
  39.5 0.0 collective-permute-done.11.rest_1_
  39.5 0.0 collective-permute-start.16
  39.5 0.0 collective-permute-done.12.rest_2_
  39.5 0.1 collective-permute-start.17
  39.5 0.2 collective-permute-done.13.rest_3_
  39.8 1.4 %collective-permute-start.18 = (bf16[128,256]{1,0:T(8,128)(2,1)S(1)}, bf16[128,256]{1,0:T(8,128)(2,1)S(1)}, u32[]{:S(2)}, u32[]{:S(2)}) collective-permute-start(bf16[128,256]{1,0:T(8,128)(2,1)S(1)} %get-tuple-element.39), channel_id=1, source_target_pairs={{0,16},{8,24},{16,0},{24,8},{1,17},{9,25},{17,1},{25,9},{2,18},{10... | collective-permute-start | bytes 196616 | tf_op jit(solution)/shard_map/ppermute | solution.py:149
  41.1 0.4 collective-permute-done.14.rest_4_
  41.5 2.4 %collective-permute-start.19 = (bf16[128,256]{1,0:T(8,128)(2,1)S(1)}, bf16[128,256]{1,0:T(8,128)(2,1)S(1)}, u32[]{:S(2)}, u32[]{:S(2)}) collective-permute-start(bf16[128,256]{1,0:T(8,128)(2,1)S(1)} %get-tuple-element.40), channel_id=1, source_target_pairs={{0,24},{8,16},{16,8},{24,0},{1,25},{9,17},{17,9},{25,1},{2,26},{10... | collective-permute-start | bytes 196616 | tf_op jit(solution)/shard_map/ppermute | solution.py:149
  43.9 0.1 add_bitcast_fusion
  44.0 39.3 %all-gather = s32[32,1,12]{2,1,0:T(1,128)S(1)} all-gather(s32[1,1,12]{2,1,0:T(1,128)S(1)} %add_bitcast_fusion), channel_id=1, replica_groups=mesh['cluster'=4,'sub'=8] {'cluster','sub'}, dimensions={0}, use_global_device_ids=true | all-gather | bytes 1584 | tf_op jit(solution)/shard_map/all_gather | solution.py:175
  83.3 0.9 %own.1.total = f32[384,256]{1,0:T(8,128)S(1)} custom-call(s32[1,8]{1,0:T(1,128)S(1)} %copy-done.6, s32[1,4]{1,0:T(1,128)S(1)} %copy-done.5, bf16[256,256]{1,0:T(8,128)(2,1)S(1)} %copy-done.2, bf16[1920,384]{1,0:T(8,128)(2,1)S(1)} %get-tuple-element.23.dense_t, bf16[2,128,256]{2,1,0:T(8,128)(2,1)S(1)} %get-tuple-element.28.kept, ...), custom_call_target="tpu_custom_call" | custom-call | flops 150994944 | bytes 2097152 | tf_op jit(solution)/shard_map/own/pallas_call | solution.py:216
  84.2 0.0 collective-permute-done.15.rest_5_
  84.2 0.0 collective-permute-done.16.rest_6_
  84.2 0.0 collective-permute-done.17.rest_7_
  84.2 0.0 collective-permute-done.18.rest_8_
  84.2 0.0 collective-permute-done.19.rest_9_
  84.3 1.7 %final.1 = bf16[384,256]{1,0:T(8,128)(2,1)} custom-call(s32[32,12]{1,0:T(8,128)S(1)} %bitcast.4, f32[384,256]{1,0:T(8,128)S(1)} %own.1.total, bf16[128,256]{1,0:T(8,128)(2,1)S(1)} %collective-permute-done.10.rest_0_, bf16[128,256]{1,0:T(8,128)(2,1)S(1)} %collective-permute-done.11.rest_1_, bf16[128,256]{1,0:T(8,128)(2,1)S(1)} %collective-permute-done.12.rest_2_, ...), custom_call_target="tpu_custom_call" | custom-call | flops 393216 | bytes 2097152 | tf_op jit(solution)/shard_map/final/pallas_call | solution.py:226
  (3 shorter events, 0.0 us)
Async XLA Ops:
  0.0 28.3 %copy-start.3 = (bf16[384,256]{1,0:T(8,128)(2,1)S(1)}, bf16[384,256]{1,0:T(8,128)(2,1)}, u32[]{:S(2)}) copy-start(bf16[384,256]{1,0:T(8,128)(2,1)} %grad_out.1) | copy-start | bytes 589828
  1.0 4.9 %collective-permute-start = (bf16[256,256]{1,0:T(8,128)(2,1)S(1)}, bf16[256,256]{1,0:T(8,128)(2,1)S(1)}, u32[]{:S(2)}, u32[]{:S(2)}) collective-permute-start(bf16[256,256]{1,0:T(8,128)(2,1)S(1)} %slice.3), channel_id=1, source_target_pairs={{0,1},{1,0},{2,3},{3,2},{4,5},{5,4},{6,7},{7,6},{8,9},{9,8},{10,11... | collective-permute-start | bytes 393224 | tf_op jit(solution)/shard_map/ppermute | solution.py:149
  1.5 7.0 %collective-permute-start.1 = (bf16[256,256]{1,0:T(8,128)(2,1)S(1)}, bf16[256,256]{1,0:T(8,128)(2,1)S(1)}, u32[]{:S(2)}, u32[]{:S(2)}) collective-permute-start(bf16[256,256]{1,0:T(8,128)(2,1)S(1)} %slice.3), channel_id=1, source_target_pairs={{0,2},{1,3},{2,0},{3,1},{4,6},{5,7},{6,4},{7,5},{8,10},{9,11},{10,... | collective-permute-start | bytes 393224 | tf_op jit(solution)/shard_map/ppermute | solution.py:149
  4.0 6.6 %collective-permute-start.2 = (bf16[256,256]{1,0:T(8,128)(2,1)S(1)}, bf16[256,256]{1,0:T(8,128)(2,1)S(1)}, u32[]{:S(2)}, u32[]{:S(2)}) collective-permute-start(bf16[256,256]{1,0:T(8,128)(2,1)S(1)} %slice.3), channel_id=1, source_target_pairs={{0,3},{1,2},{2,1},{3,0},{4,7},{5,6},{6,5},{7,4},{8,11},{9,10},{10,... | collective-permute-start | bytes 393224 | tf_op jit(solution)/shard_map/ppermute | solution.py:149
  4.1 8.2 %collective-permute-start.3 = (bf16[256,256]{1,0:T(8,128)(2,1)S(1)}, bf16[256,256]{1,0:T(8,128)(2,1)S(1)}, u32[]{:S(2)}, u32[]{:S(2)}) collective-permute-start(bf16[256,256]{1,0:T(8,128)(2,1)S(1)} %slice.3), channel_id=1, source_target_pairs={{0,4},{1,5},{2,6},{3,7},{4,0},{5,1},{6,2},{7,3},{8,12},{9,13},{10,... | collective-permute-start | bytes 393224 | tf_op jit(solution)/shard_map/ppermute | solution.py:149
  5.9 11.7 %collective-permute-start.4 = (bf16[256,256]{1,0:T(8,128)(2,1)S(1)}, bf16[256,256]{1,0:T(8,128)(2,1)S(1)}, u32[]{:S(2)}, u32[]{:S(2)}) collective-permute-start(bf16[256,256]{1,0:T(8,128)(2,1)S(1)} %slice.3), channel_id=1, source_target_pairs={{0,5},{1,4},{2,7},{3,6},{4,1},{5,0},{6,3},{7,2},{8,13},{9,12},{10,... | collective-permute-start | bytes 393224 | tf_op jit(solution)/shard_map/ppermute | solution.py:149
  5.9 22.4 %collective-permute-start.5 = (bf16[256,256]{1,0:T(8,128)(2,1)S(1)}, bf16[256,256]{1,0:T(8,128)(2,1)S(1)}, u32[]{:S(2)}, u32[]{:S(2)}) collective-permute-start(bf16[256,256]{1,0:T(8,128)(2,1)S(1)} %slice.3), channel_id=1, source_target_pairs={{0,6},{1,7},{2,4},{3,5},{4,2},{5,3},{6,0},{7,1},{8,14},{9,15},{10,... | collective-permute-start | bytes 393224 | tf_op jit(solution)/shard_map/ppermute | solution.py:149
  8.5 19.8 %collective-permute-start.6 = (bf16[256,256]{1,0:T(8,128)(2,1)S(1)}, bf16[256,256]{1,0:T(8,128)(2,1)S(1)}, u32[]{:S(2)}, u32[]{:S(2)}) collective-permute-start(bf16[256,256]{1,0:T(8,128)(2,1)S(1)} %slice.3), channel_id=1, source_target_pairs={{0,7},{1,6},{2,5},{3,4},{4,3},{5,2},{6,1},{7,0},{8,15},{9,14},{10,... | collective-permute-start | bytes 393224 | tf_op jit(solution)/shard_map/ppermute | solution.py:149
  10.7 17.6 %collective-permute-start.7 = (bf16[256,256]{1,0:T(8,128)(2,1)S(1)}, bf16[256,256]{1,0:T(8,128)(2,1)S(1)}, u32[]{:S(2)}, u32[]{:S(2)}) collective-permute-start(bf16[256,256]{1,0:T(8,128)(2,1)S(1)} %slice.3), channel_id=1, source_target_pairs={{0,8},{8,0},{16,24},{24,16},{1,9},{9,1},{17,25},{25,17},{2,10},{10... | collective-permute-start | bytes 393224 | tf_op jit(solution)/shard_map/ppermute | solution.py:149
  12.3 16.0 %collective-permute-start.8 = (bf16[256,256]{1,0:T(8,128)(2,1)S(1)}, bf16[256,256]{1,0:T(8,128)(2,1)S(1)}, u32[]{:S(2)}, u32[]{:S(2)}) collective-permute-start(bf16[256,256]{1,0:T(8,128)(2,1)S(1)} %slice.3), channel_id=1, source_target_pairs={{0,16},{8,24},{16,0},{24,8},{1,17},{9,25},{17,1},{25,9},{2,18},{10... | collective-permute-start | bytes 393224 | tf_op jit(solution)/shard_map/ppermute | solution.py:149
  17.6 10.8 %collective-permute-start.9 = (bf16[256,256]{1,0:T(8,128)(2,1)S(1)}, bf16[256,256]{1,0:T(8,128)(2,1)S(1)}, u32[]{:S(2)}, u32[]{:S(2)}) collective-permute-start(bf16[256,256]{1,0:T(8,128)(2,1)S(1)} %slice.3), channel_id=1, source_target_pairs={{0,24},{8,16},{16,8},{24,0},{1,25},{9,17},{17,9},{25,1},{2,26},{10... | collective-permute-start | bytes 393224 | tf_op jit(solution)/shard_map/ppermute | solution.py:149
  21.6 0.9 %copy-start = (bf16[384,256]{1,0:T(8,128)(2,1)S(1)}, bf16[384,256]{1,0:T(8,128)(2,1)}, u32[]{:S(2)}) copy-start(bf16[384,256]{1,0:T(8,128)(2,1)} %features.3) | copy-start | bytes 589828
  22.5 1.1 %copy-start.1 = (bf16[24,128,128]{2,1,0:T(8,128)(2,1)S(1)}, bf16[24,128,128]{2,1,0:T(8,128)(2,1)}, u32[]{:S(2)}) copy-start(bf16[24,128,128]{2,1,0:T(8,128)(2,1)} %tile_weight.1) | copy-start | bytes 2359300
  23.6 0.9 %copy-start.2 = (bf16[256,256]{1,0:T(8,128)(2,1)S(1)}, bf16[256,256]{1,0:T(8,128)(2,1)}, u32[]{:S(2)}) copy-start(bf16[256,256]{1,0:T(8,128)(2,1)} %w_self.3) | copy-start | bytes 393220
  24.5 0.7 copy-start.7
  25.2 0.7 copy-start.8
  25.9 0.7 copy-start.9
  28.3 0.9 %copy-start.4 = (bf16[256,256]{1,0:T(8,128)(2,1)S(1)}, bf16[256,256]{1,0:T(8,128)(2,1)}, u32[]{:S(2)}) copy-start(bf16[256,256]{1,0:T(8,128)(2,1)} %w_neigh.1) | copy-start | bytes 393220
  29.2 0.7 copy-start.5
  29.9 0.7 copy-start.6
  33.0 4.0 %collective-permute-start.10 = (bf16[128,256]{1,0:T(8,128)(2,1)S(1)}, bf16[128,256]{1,0:T(8,128)(2,1)S(1)}, u32[]{:S(2)}, u32[]{:S(2)}) collective-permute-start(bf16[128,256]{1,0:T(8,128)(2,1)S(1)} %get-tuple-element.31), channel_id=1, source_target_pairs={{0,1},{1,0},{2,3},{3,2},{4,5},{5,4},{6,7},{7,6},{8,9},{9,8},{10,11... | collective-permute-start | bytes 196616 | tf_op jit(solution)/shard_map/ppermute | solution.py:149
  33.5 6.0 %collective-permute-start.11 = (bf16[128,256]{1,0:T(8,128)(2,1)S(1)}, bf16[128,256]{1,0:T(8,128)(2,1)S(1)}, u32[]{:S(2)}, u32[]{:S(2)}) collective-permute-start(bf16[128,256]{1,0:T(8,128)(2,1)S(1)} %get-tuple-element.32), channel_id=1, source_target_pairs={{0,2},{1,3},{2,0},{3,1},{4,6},{5,7},{6,4},{7,5},{8,10},{9,11},{10,... | collective-permute-start | bytes 196616 | tf_op jit(solution)/shard_map/ppermute | solution.py:149
  35.0 4.5 %collective-permute-start.12 = (bf16[128,256]{1,0:T(8,128)(2,1)S(1)}, bf16[128,256]{1,0:T(8,128)(2,1)S(1)}, u32[]{:S(2)}, u32[]{:S(2)}) collective-permute-start(bf16[128,256]{1,0:T(8,128)(2,1)S(1)} %get-tuple-element.33), channel_id=1, source_target_pairs={{0,3},{1,2},{2,1},{3,0},{4,7},{5,6},{6,5},{7,4},{8,11},{9,10},{10,... | collective-permute-start | bytes 196616 | tf_op jit(solution)/shard_map/ppermute | solution.py:149
  35.0 4.8 %collective-permute-start.13 = (bf16[128,256]{1,0:T(8,128)(2,1)S(1)}, bf16[128,256]{1,0:T(8,128)(2,1)S(1)}, u32[]{:S(2)}, u32[]{:S(2)}) collective-permute-start(bf16[128,256]{1,0:T(8,128)(2,1)S(1)} %get-tuple-element.34), channel_id=1, source_target_pairs={{0,4},{1,5},{2,6},{3,7},{4,0},{5,1},{6,2},{7,3},{8,12},{9,13},{10,... | collective-permute-start | bytes 196616 | tf_op jit(solution)/shard_map/ppermute | solution.py:149
  36.5 5.0 %collective-permute-start.14 = (bf16[128,256]{1,0:T(8,128)(2,1)S(1)}, bf16[128,256]{1,0:T(8,128)(2,1)S(1)}, u32[]{:S(2)}, u32[]{:S(2)}) collective-permute-start(bf16[128,256]{1,0:T(8,128)(2,1)S(1)} %get-tuple-element.35), channel_id=1, source_target_pairs={{0,5},{1,4},{2,7},{3,6},{4,1},{5,0},{6,3},{7,2},{8,13},{9,12},{10,... | collective-permute-start | bytes 196616 | tf_op jit(solution)/shard_map/ppermute | solution.py:149
  37.0 47.2 %collective-permute-start.15 = (bf16[128,256]{1,0:T(8,128)(2,1)S(1)}, bf16[128,256]{1,0:T(8,128)(2,1)S(1)}, u32[]{:S(2)}, u32[]{:S(2)}) collective-permute-start(bf16[128,256]{1,0:T(8,128)(2,1)S(1)} %get-tuple-element.36), channel_id=1, source_target_pairs={{0,6},{1,7},{2,4},{3,5},{4,2},{5,3},{6,0},{7,1},{8,14},{9,15},{10,... | collective-permute-start | bytes 196616 | tf_op jit(solution)/shard_map/ppermute | solution.py:149
  39.5 44.8 %collective-permute-start.16 = (bf16[128,256]{1,0:T(8,128)(2,1)S(1)}, bf16[128,256]{1,0:T(8,128)(2,1)S(1)}, u32[]{:S(2)}, u32[]{:S(2)}) collective-permute-start(bf16[128,256]{1,0:T(8,128)(2,1)S(1)} %get-tuple-element.37), channel_id=1, source_target_pairs={{0,7},{1,6},{2,5},{3,4},{4,3},{5,2},{6,1},{7,0},{8,15},{9,14},{10,... | collective-permute-start | bytes 196616 | tf_op jit(solution)/shard_map/ppermute | solution.py:149
  39.5 44.8 %collective-permute-start.17 = (bf16[128,256]{1,0:T(8,128)(2,1)S(1)}, bf16[128,256]{1,0:T(8,128)(2,1)S(1)}, u32[]{:S(2)}, u32[]{:S(2)}) collective-permute-start(bf16[128,256]{1,0:T(8,128)(2,1)S(1)} %get-tuple-element.38), channel_id=1, source_target_pairs={{0,8},{8,0},{16,24},{24,16},{1,9},{9,1},{17,25},{25,17},{2,10},{10... | collective-permute-start | bytes 196616 | tf_op jit(solution)/shard_map/ppermute | solution.py:149
  39.8 44.5 %collective-permute-start.18 = (bf16[128,256]{1,0:T(8,128)(2,1)S(1)}, bf16[128,256]{1,0:T(8,128)(2,1)S(1)}, u32[]{:S(2)}, u32[]{:S(2)}) collective-permute-start(bf16[128,256]{1,0:T(8,128)(2,1)S(1)} %get-tuple-element.39), channel_id=1, source_target_pairs={{0,16},{8,24},{16,0},{24,8},{1,17},{9,25},{17,1},{25,9},{2,18},{10... | collective-permute-start | bytes 196616 | tf_op jit(solution)/shard_map/ppermute | solution.py:149
  41.5 42.7 %collective-permute-start.19 = (bf16[128,256]{1,0:T(8,128)(2,1)S(1)}, bf16[128,256]{1,0:T(8,128)(2,1)S(1)}, u32[]{:S(2)}, u32[]{:S(2)}) collective-permute-start(bf16[128,256]{1,0:T(8,128)(2,1)S(1)} %get-tuple-element.40), channel_id=1, source_target_pairs={{0,24},{8,16},{16,8},{24,0},{1,25},{9,17},{17,9},{25,1},{2,26},{10... | collective-permute-start | bytes 196616 | tf_op jit(solution)/shard_map/ppermute | solution.py:149

commit v2 on v1

v2 whole, which is shorter than its diff:
```python
import functools

import jax
import jax.numpy as jnp
from jax import lax
from jax.experimental import pallas as pl
from jax.experimental.pallas import tpu as pltpu
from jax.sharding import PartitionSpec as P

BF = jnp.bfloat16
F32 = jnp.float32
BOUNDARY = 2
EXTRA = 16
VMEM = pl.BlockSpec(memory_space=pltpu.VMEM)
HBM = pl.BlockSpec(memory_space=pltpu.HBM)
PARAMS = pltpu.CompilerParams(vmem_limit_bytes=24 * 1024 * 1024)


def dot(left, right):
    return jnp.dot(left, right, preferred_element_type=F32)


def dot_right_transposed(left, right):
    return lax.dot_general(left, right, (((1,), (1,)), ((), ())), preferred_element_type=F32)


def gelu_slope(v):
    scale = 0.7978845608028654
    t = jnp.tanh(scale * (v + 0.044715 * v * v * v))
    return 0.5 * (1.0 + t) + (0.5 * scale) * v * (1.0 - t * t) * (1.0 + 3.0 * 0.044715 * v * v)


def edge_kernel(recv_sub, recv_cluster, features, edge, rows, sub_row, cluster_row, sems):
    count = rows.shape[0]
    copies = [
        pltpu.make_async_copy(recv_sub, sub_row, sems.at[0]),
        pltpu.make_async_copy(recv_cluster, cluster_row, sems.at[1]),
        pltpu.make_async_copy(features.at[0:count, :], rows, sems.at[2]),
    ]
    for copy in copies:
        copy.start()
    for copy in copies:
        copy.wait()
    edge[0:count, :] = rows[...]
    sub_count, cluster_count = sub_row.shape[1], cluster_row.shape[1]
    pad = jnp.zeros((1, edge.shape[1] - sub_count - cluster_count), F32)
    row = jnp.concatenate([sub_row[...].astype(F32), cluster_row[...].astype(F32), pad], axis=1)
    edge[count:, :] = jnp.broadcast_to(row, (EXTRA, edge.shape[1])).astype(BF)


def prepare_kernel(
    own, sub_count, cluster_count,
    tile_dst_hbm, tile_src_hbm, recv_sub_hbm, recv_cluster_hbm, features_hbm, w_self_hbm, bias,
    tile_weight_hbm, grad_out_hbm, w_neigh_hbm,
    dense, dense_t, own_sum, own_pre, inverse, choice, w_self, w_neigh, grad_out,
    tile_dst, tile_src, recv_sub, recv_cluster, features, tile_weight, sems,
):
    size = tile_weight.shape[1]
    pairs = (
        (tile_dst_hbm, tile_dst), (tile_src_hbm, tile_src), (recv_sub_hbm, recv_sub),
        (recv_cluster_hbm, recv_cluster), (tile_weight_hbm, tile_weight),
        (features_hbm, features), (w_self_hbm, w_self), (w_neigh_hbm, w_neigh),
        (grad_out_hbm, grad_out),
    )
    copies = [pltpu.make_async_copy(a, b, sems.at[i]) for i, (a, b) in enumerate(pairs)]
    for copy in copies:
        copy.start()
    sub_id = lax.axis_index("sub")
    cluster_id = lax.axis_index("cluster")
    dense[...] = jnp.zeros_like(dense)
    dense_t[...] = jnp.zeros_like(dense_t)
    for copy in copies[:5]:
        copy.wait()

    def place(t, carry):
        src = tile_src[t]
        from_sub = own + ((src - own) ^ sub_id)
        from_cluster = own + sub_count + ((src - own - sub_count) ^ cluster_id)
        slot = jnp.where(src < own, src, jnp.where(src < own + sub_count, from_sub, from_cluster))
        dst = pl.ds(pl.multiple_of(tile_dst[t] * size, size), size)
        col = pl.ds(pl.multiple_of(slot * size, size), size)
        tile = tile_weight[t]
        dense[dst, col] = dense[dst, col] + tile
        dense_t[col, dst] = dense_t[col, dst] + tile.T
        return carry

    lax.fori_loop(0, tile_weight.shape[0], place, 0, unroll=4)
    for d in range(sub_count):
        index = recv_sub[0, sub_id ^ d].astype(F32)
        choice[d : d + 1, :] = jnp.full((1, choice.shape[1]), index, F32)
    for d in range(cluster_count):
        index = recv_cluster[0, cluster_id ^ d].astype(F32)
        choice[sub_count + d : sub_count + d + 1, :] = jnp.full((1, choice.shape[1]), index, F32)
    slots = own + sub_count + cluster_count
    total = dense[:, 0:size].astype(F32)
    for slot in range(1, slots):
        total = total + dense[:, slot * size : (slot + 1) * size].astype(F32)
    degree = jnp.sum(total, axis=1, keepdims=True)
    inverse[...] = jnp.broadcast_to(1.0 / (degree + 1.0), inverse.shape)
    for copy in copies[5:]:
        copy.wait()
    own_sum[...] = dot(dense[:, 0 : own * size], features[...])
    own_pre[...] = dot(features[...], w_self[...]) + bias[...]


def middle_kernel(
    own, sub_count, cluster_count,
    choice, edge, grad_out, w_neigh, dense, dense_t, own_sum, own_pre, inverse,
    *rest,
):
    peers = sub_count + cluster_count - 2
    received = rest[:peers]
    sent = rest[peers : 2 * peers]
    kept, spread, grad_pre, halo = rest[2 * peers :]
    size = halo.shape[0] // (sub_count + cluster_count)

    def pick(slot, source):
        second = choice[slot : slot + 1, :] > 0.5
        halo[slot * size : (slot + 1) * size, :] = jnp.where(
            second, source[size : 2 * size, :].astype(F32), source[0:size, :].astype(F32)
        ).astype(BF)

    for d in range(sub_count):
        pick(d, received[d - 1] if d else edge)
    for d in range(cluster_count):
        pick(sub_count + d, received[sub_count - 1 + d - 1] if d else edge)
    inv = jnp.concatenate([inverse[...]] * (edge.shape[1] // size), axis=1)
    aggregate = own_sum[...] + dot(dense[:, own * size :], halo[...])
    mean = (aggregate * inv).astype(BF)
    pre = own_pre[...] + dot(mean, w_neigh[...])
    grad = (grad_out[...].astype(F32) * gelu_slope(pre)).astype(BF)
    grad_pre[...] = grad
    spread[...] = (dot_right_transposed(grad, w_neigh[...]) * inv).astype(BF)

    def partial(slot):
        rows = slice((own + slot) * size, (own + slot + 1) * size)
        return dot(dense_t[rows, :], spread[...]).astype(BF)

    for d in range(sub_count):
        if d:
            sent[d - 1][...] = partial(d)
        else:
            kept[0] = partial(0)
    for d in range(cluster_count):
        if d:
            sent[sub_count - 1 + d - 1][...] = partial(sub_count + d)
        else:
            kept[1] = partial(sub_count)


def split(total, value, second, size):
    zero = jnp.zeros_like(value)
    total[0:size, :] = total[0:size, :] + jnp.where(second, zero, value)
    total[size : 2 * size, :] = total[size : 2 * size, :] + jnp.where(second, value, zero)


def own_kernel(
    own, sub_count, cluster_count, choice, w_self, dense_t, kept, spread, grad_pre, *rest
):
    received, (total, owner) = rest[:-2], rest[-2:]
    size = kept.shape[1]
    width = total.shape[1]
    total[...] = dot_right_transposed(grad_pre[...], w_self[...]) + dot(
        dense_t[0 : own * size, :], spread[...]
    )
    for i, slot in enumerate((0, sub_count)):
        split(total, kept[i].astype(F32), choice[slot : slot + 1, :] > 0.5, size)
    lanes = lax.broadcasted_iota(jnp.int32, (1, width), 1)
    for i, message in enumerate(received):
        row = message[BOUNDARY * size : BOUNDARY * size + EXTRA, :].astype(F32)[0:1, :]
        if i < sub_count - 1:
            lane = lax.axis_index("sub")
        else:
            lane = sub_count + lax.axis_index("cluster")
        index = jnp.sum(jnp.where(lanes == lane, row, 0.0), axis=1, keepdims=True)
        owner[i : i + 1, :] = jnp.broadcast_to(index, (1, width))


def final_kernel(owner, total, *rest):
    received, out = rest[:-1], rest[-1]
    size = received[0].shape[0]
    first = total[0:size, :]
    second = total[size : 2 * size, :]
    for i, message in enumerate(received):
        value = message[...].astype(F32)
        to_second = owner[i : i + 1, :] > 0.5
        first = first + jnp.where(to_second, 0.0, value)
        second = second + jnp.where(to_second, value, 0.0)
    out[0:size, :] = first.astype(BF)
    out[size : 2 * size, :] = second.astype(BF)
    out[2 * size :, :] = total[2 * size :, :].astype(BF)


def swap(value, axis, count, d):
    return lax.ppermute(value, axis, [(i, i ^ d) for i in range(count)])


def gather_edges(edge, sub_count, cluster_count):
    by_cluster = [edge]
    for d in range(1, cluster_count):
        low = d & -d
        by_cluster.append(swap(by_cluster[d - low], "cluster", cluster_count, low))
    by_sub = [edge]
    for d in range(1, sub_count):
        if d % 2:
            by_sub.append(swap(by_sub[d - 1], "sub", sub_count, 1))
        else:
            by_sub.append(swap(edge, "sub", sub_count, d))
    return by_sub[1:] + by_cluster[1:]


def send_back(values, sub_count, cluster_count):
    got = [swap(values[d - 1], "sub", sub_count, d) for d in range(1, sub_count)]
    rest = values[sub_count - 1 :]
    got += [swap(rest[d - 1], "cluster", cluster_count, d) for d in range(1, cluster_count)]
    return got


def cost(flops, moved):
    return pl.CostEstimate(flops=flops, bytes_accessed=moved, transcendentals=0)


def shards(
    features, grad_out, w_self, w_neigh, bias, tile_dst, tile_src, tile_weight, recv_sub, recv_cluster
):
    sub_count = lax.axis_size("sub")
    cluster_count = lax.axis_size("cluster")
    peers = sub_count + cluster_count - 2
    size = tile_weight.shape[1]
    rows, width = features.shape
    own = rows // size
    slots = own + sub_count + cluster_count
    counts = (own, sub_count, cluster_count)

    wide = jax.ShapeDtypeStruct((rows, width), F32)
    narrow = jax.ShapeDtypeStruct((rows, width), BF)
    square = jax.ShapeDtypeStruct((width, width), BF)
    block = jax.ShapeDtypeStruct((size, width), BF)
    marks = jax.ShapeDtypeStruct((sub_count + cluster_count, width), F32)

    edge = pl.pallas_call(
        edge_kernel,
        out_shape=jax.ShapeDtypeStruct((BOUNDARY * size + EXTRA, width), BF),
        in_specs=[HBM] * 3,
        out_specs=VMEM,
        scratch_shapes=[
            pltpu.VMEM((BOUNDARY * size, width), BF),
            pltpu.VMEM(recv_sub.shape, jnp.int32),
            pltpu.VMEM(recv_cluster.shape, jnp.int32),
            pltpu.SemaphoreType.DMA((3,)),
        ],
        compiler_params=PARAMS,
        cost_estimate=cost(1024, 256 * 1024),
        name="edge",
    )(recv_sub, recv_cluster, features)
    halos = gather_edges(edge, sub_count, cluster_count)

    dense, dense_t, own_sum, own_pre, inverse, choice, w_self, w_neigh, grad_out = pl.pallas_call(
        functools.partial(prepare_kernel, *counts),
        out_shape=[
            jax.ShapeDtypeStruct((rows, slots * size), BF),
            jax.ShapeDtypeStruct((slots * size, rows), BF),
            wide,
            wide,
            jax.ShapeDtypeStruct((rows, size), F32),
            marks,
            square,
            square,
            narrow,
        ],
        in_specs=[HBM] * 6 + [VMEM] + [HBM] * 3,
        out_specs=[VMEM] * 9,
        scratch_shapes=[
            pltpu.SMEM(tile_dst.shape, jnp.int32),
            pltpu.SMEM(tile_src.shape, jnp.int32),
            pltpu.SMEM(recv_sub.shape, jnp.int32),
            pltpu.SMEM(recv_cluster.shape, jnp.int32),
            pltpu.VMEM(features.shape, BF),
            pltpu.VMEM(tile_weight.shape, BF),
            pltpu.SemaphoreType.DMA((9,)),
        ],
        compiler_params=PARAMS,
        cost_estimate=cost(2 * rows * rows * width * 2, 6 * 1024 * 1024),
        name="prepare",
    )(
        tile_dst, tile_src, recv_sub, recv_cluster, features, w_self, bias.reshape(1, width),
        tile_weight, grad_out, w_neigh,
    )

    outs = pl.pallas_call(
        functools.partial(middle_kernel, *counts),
        out_shape=[block] * peers + [jax.ShapeDtypeStruct((2, size, width), BF), narrow, narrow],
        in_specs=[VMEM] * (9 + peers),
        out_specs=[VMEM] * (peers + 3),
        scratch_shapes=[pltpu.VMEM(((sub_count + cluster_count) * size, width), BF)],
        compiler_params=PARAMS,
        cost_estimate=cost(4 * rows * slots * size * width, 6 * 1024 * 1024),
        name="middle",
    )(choice, edge, grad_out, w_neigh, dense, dense_t, own_sum, own_pre, inverse, *halos)
    sent, (kept, spread, grad_pre) = outs[:peers], outs[peers:]
    returned = send_back(sent, sub_count, cluster_count)

    total, owner = pl.pallas_call(
        functools.partial(own_kernel, *counts),
        out_shape=[wide, marks],
        in_specs=[VMEM] * (6 + peers),
        out_specs=[VMEM] * 2,
        compiler_params=PARAMS,
        cost_estimate=cost(4 * rows * rows * width, 2 * 1024 * 1024),
        name="own",
    )(choice, w_self, dense_t, kept, spread, grad_pre, *halos)

    return pl.pallas_call(
        final_kernel,
        out_shape=narrow,
        in_specs=[VMEM] * (2 + peers),
        out_specs=VMEM,
        compiler_params=PARAMS,
        cost_estimate=cost(rows * width * 4, 2 * 1024 * 1024),
        name="final",
    )(owner, total, *returned)


def solution(mesh):
    placed = (
        P(("cluster", "sub"), None),
        P(("cluster", "sub"), None),
        P(),
        P(),
        P(),
        P(("cluster", "sub")),
        P(("cluster", "sub")),
        P(("cluster", "sub"), None, None),
        P(("cluster", "sub"), None),
        P(("cluster", "sub"), None),
    )
    return jax.shard_map(
        shards, mesh=mesh, in_specs=placed, out_specs=P(("cluster", "sub"), None), check_vma=False
    )
```

time: 86.2 us -> 46.6 us (0.54)
  blocking collectives: 39.3 us -> 0 us
  starting transfers between devices: 27.7 us -> 21.6 us
  waiting for transfers between devices: 3.83 us -> 8.19 us
  local copies, waits for them, and re-layouts: 8.12 us -> 10.3 us
    all_gather x1 -> x0, blocking collectives: 39.3 us -> none  [shards(): lax.all_gather(jnp.concatenate([recv_sub, recv_cluster], axis=1), ('clust...]
    ppermute x20, starting transfers between devices: 27.7 us -> 21.6 us  [swap(): return lax.ppermute(value, axis, [(i, i ^ d) for i in range(count)])]
    ppermute x20, waiting for transfers between devices: 3.83 us -> 8.19 us  [swap(): return lax.ppermute(value, axis, [(i, i ^ d) for i in range(count)])]
    unnamed x20 -> x26, local copies, waits for them, and re-layouts: 7.16 us -> 10.3 us
    pallas_call x2 -> x3, Pallas kernels: 2.53 us -> 1.55 us  [the longest x1 0.97 us: shards(): pl.pallas_call(final_kernel, out_shape=narrow, in_specs=[VMEM] * (2 + pee...]
    slice x1 -> x0, local copies, waits for them, and re-layouts: 0.95 us -> none  [shards(): edge = features[:BOUNDARY * size]]
  transfers between devices with their start and end apart: 20 -> 20, of which waited for: 4 -> 7; matrix products, arithmetic and copies ran while one was open for 0% -> 0% of each run, Pallas kernels for 3% -> 6%
where the time goes in v2:
time: 46.6 us; the launch traced here: 46.2 us
  starting transfers between devices  21.6 us (46%)
  local copies, waits for them, and re-layouts  10.3 us (22%)
  waiting for transfers between devices  8.19 us (18%)
  Pallas kernels  6 us (13%)
    ppermute x20, starting transfers between devices, swap(): return lax.ppermute(value, axis, [(i, i ^ d) for i in range(count)])  21.6 us
    unnamed x26, local copies, waits for them, and re-layouts  10.3 us
    ppermute x20, waiting for transfers between devices, swap(): return lax.ppermute(value, axis, [(i, i ^ d) for i in range(count)])  8.19 us
    pallas_call x1, Pallas kernels, shards(): pl.pallas_call(functools.partial(prepare_kernel, *counts), out_shape=[jax...  2.52 us
    pallas_call x1, Pallas kernels, shards(): pl.pallas_call(functools.partial(middle_kernel, *counts), out_shape=[bloc...  1.94 us
    pallas_call x1, Pallas kernels, shards(): pl.pallas_call(final_kernel, out_shape=narrow, in_specs=[VMEM] * (2 + pee...  0.97 us
  transfers between devices with their start and end apart: 20, of which 7 were waited for; matrix products, arithmetic and copies ran while one was open for 0% of the time, Pallas kernels for 6%

profile of v2, /device:TPU:0, one launch (start us, length us, event | category | flops | bytes accessed | tf_op | source)
XLA Modules:
  0.0 46.2 jit_solution(10456946217098954583)
XLA Ops:
  0.0 0.0 copy-start.1
  0.0 0.9 %copy-done.1 = bf16[384,256]{1,0:T(8,128)(2,1)S(1)} copy-done((bf16[384,256]{1,0:T(8,128)(2,1)S(1)}, bf16[384,256]{1,0:T(8,128)(2,1)}, u32[]{:S(2)}) %copy-start.1) | copy-done | bytes 196632
  0.9 0.0 copy-start.6
  0.9 0.7 %copy-done.6 = s32[1,8]{1,0:T(1,128)S(1)} copy-done((s32[1,8]{1,0:T(1,128)S(1)}, s32[1,8]{1,0:T(1,128)}, u32[]{:S(2)}) %copy-start.6) | copy-done | bytes 56
  1.6 0.0 copy-start.8
  1.6 0.7 %copy-done.8 = s32[1,4]{1,0:T(1,128)S(1)} copy-done((s32[1,4]{1,0:T(1,128)S(1)}, s32[1,4]{1,0:T(1,128)}, u32[]{:S(2)}) %copy-start.8) | copy-done | bytes 40
  2.2 0.3 edge.1
  2.5 4.1 %collective-permute-start.8 = (bf16[272,256]{1,0:T(8,128)(2,1)S(1)}, bf16[272,256]{1,0:T(8,128)(2,1)S(1)}, u32[]{:S(2)}, u32[]{:S(2)}) collective-permute-start(bf16[272,256]{1,0:T(8,128)(2,1)S(1)} %edge.1), channel_id=1, source_target_pairs={{0,16},{8,24},{16,0},{24,8},{1,17},{9,25},{17,1},{25,9},{2,18},{10... | collective-permute-start | bytes 417800 | tf_op jit(solution)/shard_map/ppermute | solution.py:195
  6.6 1.6 %collective-permute-start.7 = (bf16[272,256]{1,0:T(8,128)(2,1)S(1)}, bf16[272,256]{1,0:T(8,128)(2,1)S(1)}, u32[]{:S(2)}, u32[]{:S(2)}) collective-permute-start(bf16[272,256]{1,0:T(8,128)(2,1)S(1)} %edge.1), channel_id=1, source_target_pairs={{0,8},{8,0},{16,24},{24,16},{1,9},{9,1},{17,25},{25,17},{2,10},{10... | collective-permute-start | bytes 417800 | tf_op jit(solution)/shard_map/ppermute | solution.py:195
  8.2 2.4 %collective-permute-start.5 = (bf16[272,256]{1,0:T(8,128)(2,1)S(1)}, bf16[272,256]{1,0:T(8,128)(2,1)S(1)}, u32[]{:S(2)}, u32[]{:S(2)}) collective-permute-start(bf16[272,256]{1,0:T(8,128)(2,1)S(1)} %edge.1), channel_id=1, source_target_pairs={{0,6},{1,7},{2,4},{3,5},{4,2},{5,3},{6,0},{7,1},{8,14},{9,15},{10,... | collective-permute-start | bytes 417800 | tf_op jit(solution)/shard_map/ppermute | solution.py:195
  10.6 0.5 %collective-permute-start.3 = (bf16[272,256]{1,0:T(8,128)(2,1)S(1)}, bf16[272,256]{1,0:T(8,128)(2,1)S(1)}, u32[]{:S(2)}, u32[]{:S(2)}) collective-permute-start(bf16[272,256]{1,0:T(8,128)(2,1)S(1)} %edge.1), channel_id=1, source_target_pairs={{0,4},{1,5},{2,6},{3,7},{4,0},{5,1},{6,2},{7,3},{8,12},{9,13},{10,... | collective-permute-start | bytes 417800 | tf_op jit(solution)/shard_map/ppermute | solution.py:195
  11.1 0.5 %collective-permute-start.1 = (bf16[272,256]{1,0:T(8,128)(2,1)S(1)}, bf16[272,256]{1,0:T(8,128)(2,1)S(1)}, u32[]{:S(2)}, u32[]{:S(2)}) collective-permute-start(bf16[272,256]{1,0:T(8,128)(2,1)S(1)} %edge.1), channel_id=1, source_target_pairs={{0,2},{1,3},{2,0},{3,1},{4,6},{5,7},{6,4},{7,5},{8,10},{9,11},{10,... | collective-permute-start | bytes 417800 | tf_op jit(solution)/shard_map/ppermute | solution.py:195
  11.7 1.7 %collective-permute-done.8.rest_8_ = bf16[272,256]{1,0:T(8,128)(2,1)S(1)} collective-permute-done((bf16[272,256]{1,0:T(8,128)(2,1)S(1)}, bf16[272,256]{1,0:T(8,128)(2,1)S(1)}, u32[]{:S(2)}, u32[]{:S(2)}) %collective-permute-start.8) | collective-permute-done | bytes 139296 | tf_op jit(solution)/shard_map/ppermute | solution.py:195
  13.4 0.0 collective-permute-start
  13.4 0.2 collective-permute-done.7.rest_7_
  13.6 1.5 %collective-permute-start.9 = (bf16[272,256]{1,0:T(8,128)(2,1)S(1)}, bf16[272,256]{1,0:T(8,128)(2,1)S(1)}, u32[]{:S(2)}, u32[]{:S(2)}) collective-permute-start(bf16[272,256]{1,0:T(8,128)(2,1)S(1)} %collective-permute-done.8.rest_8_), channel_id=1, source_target_pairs={{0,8},{8,0},{16,24},{24,16},{1,9},{9,1},{17,25},{25,17},{2,10},{10... | collective-permute-start | bytes 417800 | tf_op jit(solution)/shard_map/ppermute | solution.py:195
  15.0 0.0 collective-permute-done.5.rest_5_
  15.0 0.0 collective-permute-start.6
  15.0 1.9 %collective-permute-done.3.rest_3_ = bf16[272,256]{1,0:T(8,128)(2,1)S(1)} collective-permute-done((bf16[272,256]{1,0:T(8,128)(2,1)S(1)}, bf16[272,256]{1,0:T(8,128)(2,1)S(1)}, u32[]{:S(2)}, u32[]{:S(2)}) %collective-permute-start.3) | collective-permute-done | bytes 139296 | tf_op jit(solution)/shard_map/ppermute | solution.py:195
  16.9 0.0 collective-permute-start.4
  16.9 0.1 collective-permute-done.1.rest_1_
  17.0 0.5 collective-permute-start.2
  17.4 0.0 copy-start
  17.4 1.1 %copy-done = bf16[24,128,128]{2,1,0:T(8,128)(2,1)S(1)} copy-done((bf16[24,128,128]{2,1,0:T(8,128)(2,1)S(1)}, bf16[24,128,128]{2,1,0:T(8,128)(2,1)}, u32[]{:S(2)}) %copy-start) | copy-done | bytes 786456
  18.6 0.0 copy-start.2
  18.6 0.9 %copy-done.2 = bf16[384,256]{1,0:T(8,128)(2,1)S(1)} copy-done((bf16[384,256]{1,0:T(8,128)(2,1)S(1)}, bf16[384,256]{1,0:T(8,128)(2,1)}, u32[]{:S(2)}) %copy-start.2) | copy-done | bytes 196632
  19.5 0.0 copy-start.3
  19.5 0.9 %copy-done.3 = bf16[384,256]{1,0:T(8,128)(2,1)S(1)} copy-done((bf16[384,256]{1,0:T(8,128)(2,1)S(1)}, bf16[384,256]{1,0:T(8,128)(2,1)}, u32[]{:S(2)}) %copy-start.3) | copy-done | bytes 196632
  20.4 0.9 %copy-done.4 = bf16[256,256]{1,0:T(8,128)(2,1)S(1)} copy-done((bf16[256,256]{1,0:T(8,128)(2,1)S(1)}, bf16[256,256]{1,0:T(8,128)(2,1)}, u32[]{:S(2)}) %copy-start.4) | copy-done | bytes 131096
  21.3 0.9 %copy-done.5 = bf16[256,256]{1,0:T(8,128)(2,1)S(1)} copy-done((bf16[256,256]{1,0:T(8,128)(2,1)S(1)}, bf16[256,256]{1,0:T(8,128)(2,1)}, u32[]{:S(2)}) %copy-start.5) | copy-done | bytes 131096
  22.2 0.7 %copy-done.7 = s32[1,8]{1,0:T(1,128)S(1)} copy-done((s32[1,8]{1,0:T(1,128)S(1)}, s32[1,8]{1,0:T(1,128)}, u32[]{:S(2)}) %copy-start.7) | copy-done | bytes 56
  22.9 0.7 %copy-done.9 = s32[1,4]{1,0:T(1,128)S(1)} copy-done((s32[1,4]{1,0:T(1,128)S(1)}, s32[1,4]{1,0:T(1,128)}, u32[]{:S(2)}) %copy-start.9) | copy-done | bytes 40
  23.6 0.7 %copy-done.10 = f32[256]{0:T(256)S(1)} copy-done((f32[256]{0:T(256)S(1)}, f32[256]{0:T(256)}, u32[]{:S(2)}) %copy-start.10) | copy-done | bytes 1048
  24.2 0.7 %copy-done.11 = s32[24]{0:T(128)S(1)} copy-done((s32[24]{0:T(128)S(1)}, s32[24]{0:T(128)}, u32[]{:S(2)}) %copy-start.11) | copy-done | bytes 120
  24.9 0.7 %copy-done.12 = s32[24]{0:T(128)S(1)} copy-done((s32[24]{0:T(128)S(1)}, s32[24]{0:T(128)}, u32[]{:S(2)}) %copy-start.12) | copy-done | bytes 120
  25.5 2.5 %prepare.1 = (bf16[384,1920]{1,0:T(8,128)(2,1)S(1)}, bf16[1920,384]{1,0:T(8,128)(2,1)S(1)}, f32[384,256]{1,0:T(8,128)S(1)}, f32[384,256]{1,0:T(8,128)S(1)}, f32[...) custom-call(s32[24]{0:T(128)S(1)} %copy-done.11, ...), custom_call_target="tpu_custom_call" | custom-call | flops 150994944 | bytes 6291456 | tf_op jit(solution)/shard_map/prepare/pallas_call | solution.py:258
  28.1 0.0 collective-permute-done.rest_0_
  28.1 0.0 collective-permute-done.9.rest_9_
  28.1 0.0 collective-permute-done.6.rest_6_
  28.1 0.0 collective-permute-done.4.rest_4_
  28.1 0.0 collective-permute-done.2.rest_2_
  28.1 1.9 %middle.1 = (bf16[128,256]{1,0:T(8,128)(2,1)S(1)}, bf16[128,256]{1,0:T(8,128)(2,1)S(1)}, bf16[128,256]{1,0:T(8,128)(2,1)S(1)}, bf16[128,256]{1,0:T(8,128)(2,1)S(...) custom-call(f32[12,256]{1,0:T(8,128)S(1)} %get-tuple-element.29.choi, ...), custom_call_target="tpu_custom_call" | custom-call | flops 754974720 | bytes 6291456 | tf_op jit(solution)/shard_map/middle/pallas_call | solution.py:290
  30.1 0.1 collective-permute-start.10
  30.2 1.5 %collective-permute-start.11 = (bf16[128,256]{1,0:T(8,128)(2,1)S(1)}, bf16[128,256]{1,0:T(8,128)(2,1)S(1)}, u32[]{:S(2)}, u32[]{:S(2)}) collective-permute-start(bf16[128,256]{1,0:T(8,128)(2,1)S(1)} %get-tuple-element.44), channel_id=1, source_target_pairs={{0,2},{1,3},{2,0},{3,1},{4,6},{5,7},{6,4},{7,5},{8,10},{9,11},{10,... | collective-permute-start | bytes 196616 | tf_op jit(solution)/shard_map/ppermute | solution.py:195
  31.7 0.3 collective-permute-start.12
  32.0 1.5 %collective-permute-start.13 = (bf16[128,256]{1,0:T(8,128)(2,1)S(1)}, bf16[128,256]{1,0:T(8,128)(2,1)S(1)}, u32[]{:S(2)}, u32[]{:S(2)}) collective-permute-start(bf16[128,256]{1,0:T(8,128)(2,1)S(1)} %get-tuple-element.46), channel_id=1, source_target_pairs={{0,4},{1,5},{2,6},{3,7},{4,0},{5,1},{6,2},{7,3},{8,12},{9,13},{10,... | collective-permute-start | bytes 196616 | tf_op jit(solution)/shard_map/ppermute | solution.py:195
  33.5 0.2 collective-permute-start.14
  33.7 0.0 collective-permute-done.10.rest_0_
  33.7 1.7 %collective-permute-start.15 = (bf16[128,256]{1,0:T(8,128)(2,1)S(1)}, bf16[128,256]{1,0:T(8,128)(2,1)S(1)}, u32[]{:S(2)}, u32[]{:S(2)}) collective-permute-start(bf16[128,256]{1,0:T(8,128)(2,1)S(1)} %get-tuple-element.48), channel_id=1, source_target_pairs={{0,6},{1,7},{2,4},{3,5},{4,2},{5,3},{6,0},{7,1},{8,14},{9,15},{10,... | collective-permute-start | bytes 196616 | tf_op jit(solution)/shard_map/ppermute | solution.py:195
  35.5 0.0 collective-permute-done.11.rest_1_
  35.5 1.0 %collective-permute-start.16 = (bf16[128,256]{1,0:T(8,128)(2,1)S(1)}, bf16[128,256]{1,0:T(8,128)(2,1)S(1)}, u32[]{:S(2)}, u32[]{:S(2)}) collective-permute-start(bf16[128,256]{1,0:T(8,128)(2,1)S(1)} %get-tuple-element.49), channel_id=1, source_target_pairs={{0,7},{1,6},{2,5},{3,4},{4,3},{5,2},{6,1},{7,0},{8,15},{9,14},{10,... | collective-permute-start | bytes 196616 | tf_op jit(solution)/shard_map/ppermute | solution.py:195
  36.4 0.0 collective-permute-done.12.rest_2_
  36.4 0.5 %collective-permute-start.17 = (bf16[128,256]{1,0:T(8,128)(2,1)S(1)}, bf16[128,256]{1,0:T(8,128)(2,1)S(1)}, u32[]{:S(2)}, u32[]{:S(2)}) collective-permute-start(bf16[128,256]{1,0:T(8,128)(2,1)S(1)} %get-tuple-element.50), channel_id=1, source_target_pairs={{0,8},{8,0},{16,24},{24,16},{1,9},{9,1},{17,25},{25,17},{2,10},{10... | collective-permute-start | bytes 196616 | tf_op jit(solution)/shard_map/ppermute | solution.py:195
  36.9 0.0 collective-permute-done.13.rest_3_
  36.9 0.6 %collective-permute-start.18 = (bf16[128,256]{1,0:T(8,128)(2,1)S(1)}, bf16[128,256]{1,0:T(8,128)(2,1)S(1)}, u32[]{:S(2)}, u32[]{:S(2)}) collective-permute-start(bf16[128,256]{1,0:T(8,128)(2,1)S(1)} %get-tuple-element.51), channel_id=1, source_target_pairs={{0,16},{8,24},{16,0},{24,8},{1,17},{9,25},{17,1},{25,9},{2,18},{10... | collective-permute-start | bytes 196616 | tf_op jit(solution)/shard_map/ppermute | solution.py:195
  37.4 0.2 collective-permute-done.14.rest_4_
  37.7 3.1 %collective-permute-start.19 = (bf16[128,256]{1,0:T(8,128)(2,1)S(1)}, bf16[128,256]{1,0:T(8,128)(2,1)S(1)}, u32[]{:S(2)}, u32[]{:S(2)}) collective-permute-start(bf16[128,256]{1,0:T(8,128)(2,1)S(1)} %get-tuple-element.52), channel_id=1, source_target_pairs={{0,24},{8,16},{16,8},{24,0},{1,25},{9,17},{17,9},{25,1},{2,26},{10... | collective-permute-start | bytes 196616 | tf_op jit(solution)/shard_map/ppermute | solution.py:195
  40.8 0.3 own.1
  41.1 0.0 collective-permute-done.15.rest_5_
  41.1 0.0 collective-permute-done.16.rest_6_
  41.2 0.6 %collective-permute-done.17.rest_7_ = bf16[128,256]{1,0:T(8,128)(2,1)S(1)} collective-permute-done((bf16[128,256]{1,0:T(8,128)(2,1)S(1)}, bf16[128,256]{1,0:T(8,128)(2,1)S(1)}, u32[]{:S(2)}, u32[]{:S(2)}) %collective-permute-start.17) | collective-permute-done | bytes 65568 | tf_op jit(solution)/shard_map/ppermute | solution.py:195
  41.8 3.5 %collective-permute-done.18.rest_8_ = bf16[128,256]{1,0:T(8,128)(2,1)S(1)} collective-permute-done((bf16[128,256]{1,0:T(8,128)(2,1)S(1)}, bf16[128,256]{1,0:T(8,128)(2,1)S(1)}, u32[]{:S(2)}, u32[]{:S(2)}) %collective-permute-start.18) | collective-permute-done | bytes 65568 | tf_op jit(solution)/shard_map/ppermute | solution.py:195
  45.3 0.0 collective-permute-done.19.rest_9_
  45.3 1.0 %final.1 = bf16[384,256]{1,0:T(8,128)(2,1)} custom-call(f32[12,256]{1,0:T(8,128)S(1)} %get-tuple-element.41.owner, f32[384,256]{1,0:T(8,128)S(1)} %get-tuple-element.42.total, bf16[128,256]{1,0:T(8,128)(2,1)S(1)} %collective-permute-done.10.rest_0_, bf16[128,256]{1,0:T(8,128)(2,1)S(1)} %collective-permute-done.11.rest_1_, ...), custom_call_target="tpu_custom_call" | custom-call | flops 393216 | bytes 2097152 | tf_op jit(solution)/shard_map/final/pallas_call | solution.py:313
  (7 shorter events, 0.0 us)
Async XLA Ops:
  0.0 0.9 %copy-start.1 = (bf16[384,256]{1,0:T(8,128)(2,1)S(1)}, bf16[384,256]{1,0:T(8,128)(2,1)}, u32[]{:S(2)}) copy-start(bf16[384,256]{1,0:T(8,128)(2,1)} %features.1) | copy-start | bytes 589828
  0.9 0.7 %copy-start.6 = (s32[1,8]{1,0:T(1,128)S(1)}, s32[1,8]{1,0:T(1,128)}, u32[]{:S(2)}) copy-start(s32[1,8]{1,0:T(1,128)} %recv_sub.1) | copy-start | bytes 100
  1.6 0.7 %copy-start.8 = (s32[1,4]{1,0:T(1,128)S(1)}, s32[1,4]{1,0:T(1,128)}, u32[]{:S(2)}) copy-start(s32[1,4]{1,0:T(1,128)} %recv_cluster.1) | copy-start | bytes 52
  2.5 10.9 %collective-permute-start.8 = (bf16[272,256]{1,0:T(8,128)(2,1)S(1)}, bf16[272,256]{1,0:T(8,128)(2,1)S(1)}, u32[]{:S(2)}, u32[]{:S(2)}) collective-permute-start(bf16[272,256]{1,0:T(8,128)(2,1)S(1)} %edge.1), channel_id=1, source_target_pairs={{0,16},{8,24},{16,0},{24,8},{1,17},{9,25},{17,1},{25,9},{2,18},{10... | collective-permute-start | bytes 417800 | tf_op jit(solution)/shard_map/ppermute | solution.py:195
  6.6 7.0 %collective-permute-start.7 = (bf16[272,256]{1,0:T(8,128)(2,1)S(1)}, bf16[272,256]{1,0:T(8,128)(2,1)S(1)}, u32[]{:S(2)}, u32[]{:S(2)}) collective-permute-start(bf16[272,256]{1,0:T(8,128)(2,1)S(1)} %edge.1), channel_id=1, source_target_pairs={{0,8},{8,0},{16,24},{24,16},{1,9},{9,1},{17,25},{25,17},{2,10},{10... | collective-permute-start | bytes 417800 | tf_op jit(solution)/shard_map/ppermute | solution.py:195
  8.2 6.8 %collective-permute-start.5 = (bf16[272,256]{1,0:T(8,128)(2,1)S(1)}, bf16[272,256]{1,0:T(8,128)(2,1)S(1)}, u32[]{:S(2)}, u32[]{:S(2)}) collective-permute-start(bf16[272,256]{1,0:T(8,128)(2,1)S(1)} %edge.1), channel_id=1, source_target_pairs={{0,6},{1,7},{2,4},{3,5},{4,2},{5,3},{6,0},{7,1},{8,14},{9,15},{10,... | collective-permute-start | bytes 417800 | tf_op jit(solution)/shard_map/ppermute | solution.py:195
  10.6 6.3 %collective-permute-start.3 = (bf16[272,256]{1,0:T(8,128)(2,1)S(1)}, bf16[272,256]{1,0:T(8,128)(2,1)S(1)}, u32[]{:S(2)}, u32[]{:S(2)}) collective-permute-start(bf16[272,256]{1,0:T(8,128)(2,1)S(1)} %edge.1), channel_id=1, source_target_pairs={{0,4},{1,5},{2,6},{3,7},{4,0},{5,1},{6,2},{7,3},{8,12},{9,13},{10,... | collective-permute-start | bytes 417800 | tf_op jit(solution)/shard_map/ppermute | solution.py:195
  11.1 5.8 %collective-permute-start.1 = (bf16[272,256]{1,0:T(8,128)(2,1)S(1)}, bf16[272,256]{1,0:T(8,128)(2,1)S(1)}, u32[]{:S(2)}, u32[]{:S(2)}) collective-permute-start(bf16[272,256]{1,0:T(8,128)(2,1)S(1)} %edge.1), channel_id=1, source_target_pairs={{0,2},{1,3},{2,0},{3,1},{4,6},{5,7},{6,4},{7,5},{8,10},{9,11},{10,... | collective-permute-start | bytes 417800 | tf_op jit(solution)/shard_map/ppermute | solution.py:195
  13.4 14.7 %collective-permute-start = (bf16[272,256]{1,0:T(8,128)(2,1)S(1)}, bf16[272,256]{1,0:T(8,128)(2,1)S(1)}, u32[]{:S(2)}, u32[]{:S(2)}) collective-permute-start(bf16[272,256]{1,0:T(8,128)(2,1)S(1)} %edge.1), channel_id=1, source_target_pairs={{0,1},{1,0},{2,3},{3,2},{4,5},{5,4},{6,7},{7,6},{8,9},{9,8},{10,11... | collective-permute-start | bytes 417800 | tf_op jit(solution)/shard_map/ppermute | solution.py:195
  13.6 14.5 %collective-permute-start.9 = (bf16[272,256]{1,0:T(8,128)(2,1)S(1)}, bf16[272,256]{1,0:T(8,128)(2,1)S(1)}, u32[]{:S(2)}, u32[]{:S(2)}) collective-permute-start(bf16[272,256]{1,0:T(8,128)(2,1)S(1)} %collective-permute-done.8.rest_8_), channel_id=1, source_target_pairs={{0,8},{8,0},{16,24},{24,16},{1,9},{9,1},{17,25},{25,17},{2,10},{10... | collective-permute-start | bytes 417800 | tf_op jit(solution)/shard_map/ppermute | solution.py:195
  15.0 13.1 %collective-permute-start.6 = (bf16[272,256]{1,0:T(8,128)(2,1)S(1)}, bf16[272,256]{1,0:T(8,128)(2,1)S(1)}, u32[]{:S(2)}, u32[]{:S(2)}) collective-permute-start(bf16[272,256]{1,0:T(8,128)(2,1)S(1)} %collective-permute-done.5.rest_5_), channel_id=1, source_target_pairs={{0,1},{1,0},{2,3},{3,2},{4,5},{5,4},{6,7},{7,6},{8,9},{9,8},{10,11... | collective-permute-start | bytes 417800 | tf_op jit(solution)/shard_map/ppermute | solution.py:195
  16.9 11.2 %collective-permute-start.4 = (bf16[272,256]{1,0:T(8,128)(2,1)S(1)}, bf16[272,256]{1,0:T(8,128)(2,1)S(1)}, u32[]{:S(2)}, u32[]{:S(2)}) collective-permute-start(bf16[272,256]{1,0:T(8,128)(2,1)S(1)} %collective-permute-done.3.rest_3_), channel_id=1, source_target_pairs={{0,1},{1,0},{2,3},{3,2},{4,5},{5,4},{6,7},{7,6},{8,9},{9,8},{10,11... | collective-permute-start | bytes 417800 | tf_op jit(solution)/shard_map/ppermute | solution.py:195
  17.0 11.1 %collective-permute-start.2 = (bf16[272,256]{1,0:T(8,128)(2,1)S(1)}, bf16[272,256]{1,0:T(8,128)(2,1)S(1)}, u32[]{:S(2)}, u32[]{:S(2)}) collective-permute-start(bf16[272,256]{1,0:T(8,128)(2,1)S(1)} %collective-permute-done.1.rest_1_), channel_id=1, source_target_pairs={{0,1},{1,0},{2,3},{3,2},{4,5},{5,4},{6,7},{7,6},{8,9},{9,8},{10,11... | collective-permute-start | bytes 417800 | tf_op jit(solution)/shard_map/ppermute | solution.py:195
  17.4 1.1 %copy-start = (bf16[24,128,128]{2,1,0:T(8,128)(2,1)S(1)}, bf16[24,128,128]{2,1,0:T(8,128)(2,1)}, u32[]{:S(2)}) copy-start(bf16[24,128,128]{2,1,0:T(8,128)(2,1)} %tile_weight_hbm.1) | copy-start | bytes 2359300
  18.6 0.9 %copy-start.2 = (bf16[384,256]{1,0:T(8,128)(2,1)S(1)}, bf16[384,256]{1,0:T(8,128)(2,1)}, u32[]{:S(2)}) copy-start(bf16[384,256]{1,0:T(8,128)(2,1)} %features.1) | copy-start | bytes 589828
  19.5 0.9 %copy-start.3 = (bf16[384,256]{1,0:T(8,128)(2,1)S(1)}, bf16[384,256]{1,0:T(8,128)(2,1)}, u32[]{:S(2)}) copy-start(bf16[384,256]{1,0:T(8,128)(2,1)} %grad_out_hbm.1) | copy-start | bytes 589828
  20.4 0.9 %copy-start.4 = (bf16[256,256]{1,0:T(8,128)(2,1)S(1)}, bf16[256,256]{1,0:T(8,128)(2,1)}, u32[]{:S(2)}) copy-start(bf16[256,256]{1,0:T(8,128)(2,1)} %w_self_hbm.1) | copy-start | bytes 393220
  21.3 0.9 %copy-start.5 = (bf16[256,256]{1,0:T(8,128)(2,1)S(1)}, bf16[256,256]{1,0:T(8,128)(2,1)}, u32[]{:S(2)}) copy-start(bf16[256,256]{1,0:T(8,128)(2,1)} %w_neigh_hbm.1) | copy-start | bytes 393220
  22.2 0.7 %copy-start.7 = (s32[1,8]{1,0:T(1,128)S(1)}, s32[1,8]{1,0:T(1,128)}, u32[]{:S(2)}) copy-start(s32[1,8]{1,0:T(1,128)} %recv_sub.1) | copy-start | bytes 100
  22.9 0.7 %copy-start.9 = (s32[1,4]{1,0:T(1,128)S(1)}, s32[1,4]{1,0:T(1,128)}, u32[]{:S(2)}) copy-start(s32[1,4]{1,0:T(1,128)} %recv_cluster.1) | copy-start | bytes 52
  23.5 0.7 %copy-start.10 = (f32[256]{0:T(256)S(1)}, f32[256]{0:T(256)}, u32[]{:S(2)}) copy-start(f32[256]{0:T(256)} %param.14) | copy-start | bytes 3076
  24.2 0.7 %copy-start.11 = (s32[24]{0:T(128)S(1)}, s32[24]{0:T(128)}, u32[]{:S(2)}) copy-start(s32[24]{0:T(128)} %tile_dst_hbm.1) | copy-start | bytes 292
  24.9 0.7 %copy-start.12 = (s32[24]{0:T(128)S(1)}, s32[24]{0:T(128)}, u32[]{:S(2)}) copy-start(s32[24]{0:T(128)} %tile_src_hbm.1) | copy-start | bytes 292
  30.1 3.6 %collective-permute-start.10 = (bf16[128,256]{1,0:T(8,128)(2,1)S(1)}, bf16[128,256]{1,0:T(8,128)(2,1)S(1)}, u32[]{:S(2)}, u32[]{:S(2)}) collective-permute-start(bf16[128,256]{1,0:T(8,128)(2,1)S(1)} %get-tuple-element.43), channel_id=1, source_target_pairs={{0,1},{1,0},{2,3},{3,2},{4,5},{5,4},{6,7},{7,6},{8,9},{9,8},{10,11... | collective-permute-start | bytes 196616 | tf_op jit(solution)/shard_map/ppermute | solution.py:195
  30.2 5.3 %collective-permute-start.11 = (bf16[128,256]{1,0:T(8,128)(2,1)S(1)}, bf16[128,256]{1,0:T(8,128)(2,1)S(1)}, u32[]{:S(2)}, u32[]{:S(2)}) collective-permute-start(bf16[128,256]{1,0:T(8,128)(2,1)S(1)} %get-tuple-element.44), channel_id=1, source_target_pairs={{0,2},{1,3},{2,0},{3,1},{4,6},{5,7},{6,4},{7,5},{8,10},{9,11},{10,... | collective-permute-start | bytes 196616 | tf_op jit(solution)/shard_map/ppermute | solution.py:195
  31.7 4.7 %collective-permute-start.12 = (bf16[128,256]{1,0:T(8,128)(2,1)S(1)}, bf16[128,256]{1,0:T(8,128)(2,1)S(1)}, u32[]{:S(2)}, u32[]{:S(2)}) collective-permute-start(bf16[128,256]{1,0:T(8,128)(2,1)S(1)} %get-tuple-element.45), channel_id=1, source_target_pairs={{0,3},{1,2},{2,1},{3,0},{4,7},{5,6},{6,5},{7,4},{8,11},{9,10},{10,... | collective-permute-start | bytes 196616 | tf_op jit(solution)/shard_map/ppermute | solution.py:195
  32.0 4.9 %collective-permute-start.13 = (bf16[128,256]{1,0:T(8,128)(2,1)S(1)}, bf16[128,256]{1,0:T(8,128)(2,1)S(1)}, u32[]{:S(2)}, u32[]{:S(2)}) collective-permute-start(bf16[128,256]{1,0:T(8,128)(2,1)S(1)} %get-tuple-element.46), channel_id=1, source_target_pairs={{0,4},{1,5},{2,6},{3,7},{4,0},{5,1},{6,2},{7,3},{8,12},{9,13},{10,... | collective-permute-start | bytes 196616 | tf_op jit(solution)/shard_map/ppermute | solution.py:195
  33.5 4.2 %collective-permute-start.14 = (bf16[128,256]{1,0:T(8,128)(2,1)S(1)}, bf16[128,256]{1,0:T(8,128)(2,1)S(1)}, u32[]{:S(2)}, u32[]{:S(2)}) collective-permute-start(bf16[128,256]{1,0:T(8,128)(2,1)S(1)} %get-tuple-element.47), channel_id=1, source_target_pairs={{0,5},{1,4},{2,7},{3,6},{4,1},{5,0},{6,3},{7,2},{8,13},{9,12},{10,... | collective-permute-start | bytes 196616 | tf_op jit(solution)/shard_map/ppermute | solution.py:195
  33.7 7.4 %collective-permute-start.15 = (bf16[128,256]{1,0:T(8,128)(2,1)S(1)}, bf16[128,256]{1,0:T(8,128)(2,1)S(1)}, u32[]{:S(2)}, u32[]{:S(2)}) collective-permute-start(bf16[128,256]{1,0:T(8,128)(2,1)S(1)} %get-tuple-element.48), channel_id=1, source_target_pairs={{0,6},{1,7},{2,4},{3,5},{4,2},{5,3},{6,0},{7,1},{8,14},{9,15},{10,... | collective-permute-start | bytes 196616 | tf_op jit(solution)/shard_map/ppermute | solution.py:195
  35.5 5.7 %collective-permute-start.16 = (bf16[128,256]{1,0:T(8,128)(2,1)S(1)}, bf16[128,256]{1,0:T(8,128)(2,1)S(1)}, u32[]{:S(2)}, u32[]{:S(2)}) collective-permute-start(bf16[128,256]{1,0:T(8,128)(2,1)S(1)} %get-tuple-element.49), channel_id=1, source_target_pairs={{0,7},{1,6},{2,5},{3,4},{4,3},{5,2},{6,1},{7,0},{8,15},{9,14},{10,... | collective-permute-start | bytes 196616 | tf_op jit(solution)/shard_map/ppermute | solution.py:195
  36.4 5.4 %collective-permute-start.17 = (bf16[128,256]{1,0:T(8,128)(2,1)S(1)}, bf16[128,256]{1,0:T(8,128)(2,1)S(1)}, u32[]{:S(2)}, u32[]{:S(2)}) collective-permute-start(bf16[128,256]{1,0:T(8,128)(2,1)S(1)} %get-tuple-element.50), channel_id=1, source_target_pairs={{0,8},{8,0},{16,24},{24,16},{1,9},{9,1},{17,25},{25,17},{2,10},{10... | collective-permute-start | bytes 196616 | tf_op jit(solution)/shard_map/ppermute | solution.py:195
  36.9 8.4 %collective-permute-start.18 = (bf16[128,256]{1,0:T(8,128)(2,1)S(1)}, bf16[128,256]{1,0:T(8,128)(2,1)S(1)}, u32[]{:S(2)}, u32[]{:S(2)}) collective-permute-start(bf16[128,256]{1,0:T(8,128)(2,1)S(1)} %get-tuple-element.51), channel_id=1, source_target_pairs={{0,16},{8,24},{16,0},{24,8},{1,17},{9,25},{17,1},{25,9},{2,18},{10... | collective-permute-start | bytes 196616 | tf_op jit(solution)/shard_map/ppermute | solution.py:195
  37.7 7.6 %collective-permute-start.19 = (bf16[128,256]{1,0:T(8,128)(2,1)S(1)}, bf16[128,256]{1,0:T(8,128)(2,1)S(1)}, u32[]{:S(2)}, u32[]{:S(2)}) collective-permute-start(bf16[128,256]{1,0:T(8,128)(2,1)S(1)} %get-tuple-element.52), channel_id=1, source_target_pairs={{0,24},{8,16},{16,8},{24,0},{1,25},{9,17},{17,9},{25,1},{2,26},{10... | collective-permute-start | bytes 196616 | tf_op jit(solution)/shard_map/ppermute | solution.py:195

commit v3 on v2

--- a/solution.py
+++ b/solution.py
@@ -30,18 +30,17 @@
     return 0.5 * (1.0 + t) + (0.5 * scale) * v * (1.0 - t * t) * (1.0 + 3.0 * 0.044715 * v * v)
 
 
-def edge_kernel(recv_sub, recv_cluster, features, edge, rows, sub_row, cluster_row, sems):
-    count = rows.shape[0]
+def edge_kernel(recv_sub, recv_cluster, features, edge, sub_row, cluster_row, sems):
+    count = edge.shape[0] - EXTRA
     copies = [
-        pltpu.make_async_copy(recv_sub, sub_row, sems.at[0]),
-        pltpu.make_async_copy(recv_cluster, cluster_row, sems.at[1]),
-        pltpu.make_async_copy(features.at[0:count, :], rows, sems.at[2]),
+        pltpu.make_async_copy(features.at[0:count, :], edge.at[0:count, :], sems.at[0]),
+        pltpu.make_async_copy(recv_sub, sub_row, sems.at[1]),
+        pltpu.make_async_copy(recv_cluster, cluster_row, sems.at[2]),
     ]
     for copy in copies:
         copy.start()
     for copy in copies:
         copy.wait()
-    edge[0:count, :] = rows[...]
     sub_count, cluster_count = sub_row.shape[1], cluster_row.shape[1]
     pad = jnp.zeros((1, edge.shape[1] - sub_count - cluster_count), F32)
     row = jnp.concatenate([sub_row[...].astype(F32), cluster_row[...].astype(F32), pad], axis=1)
@@ -50,17 +49,17 @@
 
 def prepare_kernel(
     own, sub_count, cluster_count,
-    tile_dst_hbm, tile_src_hbm, recv_sub_hbm, recv_cluster_hbm, features_hbm, w_self_hbm, bias,
+    tile_dst_hbm, tile_src_hbm, recv_sub_hbm, recv_cluster_hbm, features_hbm, w_self_hbm, bias_hbm,
     tile_weight_hbm, grad_out_hbm, w_neigh_hbm,
     dense, dense_t, own_sum, own_pre, inverse, choice, w_self, w_neigh, grad_out,
-    tile_dst, tile_src, recv_sub, recv_cluster, features, tile_weight, sems,
+    tile_dst, tile_src, recv_sub, recv_cluster, features, tile_weight, bias, sems,
 ):
     size = tile_weight.shape[1]
     pairs = (
         (tile_dst_hbm, tile_dst), (tile_src_hbm, tile_src), (recv_sub_hbm, recv_sub),
         (recv_cluster_hbm, recv_cluster), (tile_weight_hbm, tile_weight),
         (features_hbm, features), (w_self_hbm, w_self), (w_neigh_hbm, w_neigh),
-        (grad_out_hbm, grad_out),
+        (grad_out_hbm, grad_out), (bias_hbm, bias),
     )
     copies = [pltpu.make_async_copy(a, b, sems.at[i]) for i, (a, b) in enumerate(pairs)]
     for copy in copies:
@@ -100,19 +99,19 @@
     for copy in copies[5:]:
         copy.wait()
     own_sum[...] = dot(dense[:, 0 : own * size], features[...])
-    own_pre[...] = dot(features[...], w_self[...]) + bias[...]
+    own_pre[...] = dot(features[...], w_self[...]) + bias[...].reshape(1, -1)
 
 
 def middle_kernel(
-    own, sub_count, cluster_count,
+    own, order, sent_order, sub_count,
     choice, edge, grad_out, w_neigh, dense, dense_t, own_sum, own_pre, inverse,
     *rest,
 ):
-    peers = sub_count + cluster_count - 2
+    peers = len(order)
     received = rest[:peers]
     sent = rest[peers : 2 * peers]
     kept, spread, grad_pre, halo = rest[2 * peers :]
-    size = halo.shape[0] // (sub_count + cluster_count)
+    size = halo.shape[0] // (peers + 2)
 
     def pick(slot, source):
         second = choice[slot : slot + 1, :] > 0.5
@@ -120,10 +119,10 @@
             second, source[size : 2 * size, :].astype(F32), source[0:size, :].astype(F32)
         ).astype(BF)
 
-    for d in range(sub_count):
-        pick(d, received[d - 1] if d else edge)
-    for d in range(cluster_count):
-        pick(sub_count + d, received[sub_count - 1 + d - 1] if d else edge)
+    pick(0, edge)
+    pick(sub_count, edge)
+    for source, slot in zip(received, order):
+        pick(slot, source)
     inv = jnp.concatenate([inverse[...]] * (edge.shape[1] // size), axis=1)
     aggregate = own_sum[...] + dot(dense[:, own * size :], halo[...])
     mean = (aggregate * inv).astype(BF)
@@ -136,16 +135,10 @@
         rows = slice((own + slot) * size, (own + slot + 1) * size)
         return dot(dense_t[rows, :], spread[...]).astype(BF)
 
-    for d in range(sub_count):
-        if d:
-            sent[d - 1][...] = partial(d)
-        else:
-            kept[0] = partial(0)
-    for d in range(cluster_count):
-        if d:
-            sent[sub_count - 1 + d - 1][...] = partial(sub_count + d)
-        else:
-            kept[1] = partial(sub_count)
+    for target, slot in zip(sent, sent_order):
+        target[...] = partial(slot)
+    kept[0] = partial(0)
+    kept[1] = partial(sub_count)
 
 
 def split(total, value, second, size):
@@ -155,7 +148,7 @@
 
 
 def own_kernel(
-    own, sub_count, cluster_count, choice, w_self, dense_t, kept, spread, grad_pre, *rest
+    own, order, sub_count, choice, w_self, dense_t, kept, spread, grad_pre, *rest
 ):
     received, (total, owner) = rest[:-2], rest[-2:]
     size = kept.shape[1]
@@ -166,24 +159,24 @@
     for i, slot in enumerate((0, sub_count)):
         split(total, kept[i].astype(F32), choice[slot : slot + 1, :] > 0.5, size)
     lanes = lax.broadcasted_iota(jnp.int32, (1, width), 1)
-    for i, message in enumerate(received):
+    for message, slot in zip(received, order):
         row = message[BOUNDARY * size : BOUNDARY * size + EXTRA, :].astype(F32)[0:1, :]
-        if i < sub_count - 1:
+        if slot < sub_count:
             lane = lax.axis_index("sub")
         else:
             lane = sub_count + lax.axis_index("cluster")
         index = jnp.sum(jnp.where(lanes == lane, row, 0.0), axis=1, keepdims=True)
-        owner[i : i + 1, :] = jnp.broadcast_to(index, (1, width))
-
-
-def final_kernel(owner, total, *rest):
+        owner[slot : slot + 1, :] = jnp.broadcast_to(index, (1, width))
+
+
+def final_kernel(order, owner, total, *rest):
     received, out = rest[:-1], rest[-1]
     size = received[0].shape[0]
     first = total[0:size, :]
     second = total[size : 2 * size, :]
-    for i, message in enumerate(received):
+    for message, slot in zip(received, order):
         value = message[...].astype(F32)
-        to_second = owner[i : i + 1, :] > 0.5
+        to_second = owner[slot : slot + 1, :] > 0.5
         first = first + jnp.where(to_second, 0.0, value)
         second = second + jnp.where(to_second, value, 0.0)
     out[0:size, :] = first.astype(BF)
@@ -195,25 +188,40 @@
     return lax.ppermute(value, axis, [(i, i ^ d) for i in range(count)])
 
 
-def gather_edges(edge, sub_count, cluster_count):
-    by_cluster = [edge]
+def gather_edges(edge, prepared, sub_count, cluster_count):
+    def relay(value):
+        return lax.optimization_barrier((value, prepared))[0]
+
+    got = {0: edge, sub_count: edge}
     for d in range(1, cluster_count):
         low = d & -d
-        by_cluster.append(swap(by_cluster[d - low], "cluster", cluster_count, low))
-    by_sub = [edge]
+        value = edge if d == low else relay(got[sub_count + d - low])
+        got[sub_count + d] = swap(value, "cluster", cluster_count, low)
     for d in range(1, sub_count):
         if d % 2:
-            by_sub.append(swap(by_sub[d - 1], "sub", sub_count, 1))
+            got[d] = swap(relay(got[d - 1]), "sub", sub_count, 1)
         else:
-            by_sub.append(swap(edge, "sub", sub_count, d))
-    return by_sub[1:] + by_cluster[1:]
-
-
-def send_back(values, sub_count, cluster_count):
-    got = [swap(values[d - 1], "sub", sub_count, d) for d in range(1, sub_count)]
-    rest = values[sub_count - 1 :]
-    got += [swap(rest[d - 1], "cluster", cluster_count, d) for d in range(1, cluster_count)]
+            got[d] = swap(edge, "sub", sub_count, d)
     return got
+
+
+def peer_orders(sub_count, cluster_count):
+    along = [sub_count + d for d in range(1, cluster_count)]
+    direct = [sub_count + d for d in range(1, cluster_count) if not d & (d - 1)]
+    relayed = [sub_count + d for d in range(1, cluster_count) if d & (d - 1)]
+    even = list(range(2, sub_count, 2))
+    odd = list(range(3, sub_count, 2))
+    return [1] + odd + even + relayed + direct, along[::-1] + even[::-1] + odd[::-1] + [1]
+
+
+def send_back(value, slot, sub_count, cluster_count):
+    if slot < sub_count:
+        return swap(value, "sub", sub_count, slot)
+    return swap(value, "cluster", cluster_count, slot - sub_count)
+
+
+def in_hbm(value):
+    return pltpu.with_memory_space_constraint(value, pltpu.HBM)
 
 
 def cost(flops, moved):
@@ -231,6 +239,7 @@
     own = rows // size
     slots = own + sub_count + cluster_count
     counts = (own, sub_count, cluster_count)
+    order, sent_order = peer_orders(sub_count, cluster_count)
 
     wide = jax.ShapeDtypeStruct((rows, width), F32)
     narrow = jax.ShapeDtypeStruct((rows, width), BF)
@@ -244,7 +253,6 @@
         in_specs=[HBM] * 3,
         out_specs=VMEM,
         scratch_shapes=[
-            pltpu.VMEM((BOUNDARY * size, width), BF),
             pltpu.VMEM(recv_sub.shape, jnp.int32),
             pltpu.VMEM(recv_cluster.shape, jnp.int32),
             pltpu.SemaphoreType.DMA((3,)),
@@ -252,8 +260,7 @@
         compiler_params=PARAMS,
         cost_estimate=cost(1024, 256 * 1024),
         name="edge",
-    )(recv_sub, recv_cluster, features)
-    halos = gather_edges(edge, sub_count, cluster_count)
+    )(in_hbm(recv_sub), in_hbm(recv_cluster), in_hbm(features))
 
     dense, dense_t, own_sum, own_pre, inverse, choice, w_self, w_neigh, grad_out = pl.pallas_call(
         functools.partial(prepare_kernel, *counts),
@@ -268,7 +275,7 @@
             square,
             narrow,
         ],
-        in_specs=[HBM] * 6 + [VMEM] + [HBM] * 3,
+        in_specs=[HBM] * 10,
         out_specs=[VMEM] * 9,
         scratch_shapes=[
             pltpu.SMEM(tile_dst.shape, jnp.int32),
@@ -277,18 +284,21 @@
             pltpu.SMEM(recv_cluster.shape, jnp.int32),
             pltpu.VMEM(features.shape, BF),
             pltpu.VMEM(tile_weight.shape, BF),
-            pltpu.SemaphoreType.DMA((9,)),
+            pltpu.VMEM(bias.shape, F32),
+            pltpu.SemaphoreType.DMA((10,)),
         ],
         compiler_params=PARAMS,
         cost_estimate=cost(2 * rows * rows * width * 2, 6 * 1024 * 1024),
         name="prepare",
     )(
-        tile_dst, tile_src, recv_sub, recv_cluster, features, w_self, bias.reshape(1, width),
-        tile_weight, grad_out, w_neigh,
-    )
+        *map(in_hbm, (tile_dst, tile_src, recv_sub, recv_cluster, features, w_self, bias)),
+        *map(in_hbm, (tile_weight, grad_out, w_neigh)),
+    )
+    got = gather_edges(edge, choice, sub_count, cluster_count)
+    halos = [got[slot] for slot in order]
 
     outs = pl.pallas_call(
-        functools.partial(middle_kernel, *counts),
+        functools.partial(middle_kernel, own, order, sent_order, sub_count),
         out_shape=[block] * peers + [jax.ShapeDtypeStruct((2, size, width), BF), narrow, narrow],
         in_specs=[VMEM] * (9 + peers),
         out_specs=[VMEM] * (peers + 3),
@@ -298,10 +308,12 @@
         name="middle",
     )(choice, edge, grad_out, w_neigh, dense, dense_t, own_sum, own_pre, inverse, *halos)
     sent, (kept, spread, grad_pre) = outs[:peers], outs[peers:]
-    returned = send_back(sent, sub_count, cluster_count)
+    returned = [
+        send_back(value, slot, sub_count, cluster_count) for value, slot in zip(sent, sent_order)
+    ]
 
     total, owner = pl.pallas_call(
-        functools.partial(own_kernel, *counts),
+        functools.partial(own_kernel, own, order, sub_count),
         out_shape=[wide, marks],
         in_specs=[VMEM] * (6 + peers),
         out_specs=[VMEM] * 2,
@@ -311,7 +323,7 @@
     )(choice, w_self, dense_t, kept, spread, grad_pre, *halos)
 
     return pl.pallas_call(
-        final_kernel,
+        functools.partial(final_kernel, sent_order),
         out_shape=narrow,
         in_specs=[VMEM] * (2 + peers),
         out_specs=VMEM,

time: 46.6 us -> 39.3 us (0.84)
  local copies, waits for them, and re-layouts: 10.3 us -> 0 us
  starting transfers between devices: 21.6 us -> 23.1 us
  waiting for transfers between devices: 8.19 us -> 9.31 us
  Pallas kernels: 6 us -> 6.62 us
    unnamed x26 -> x0, local copies, waits for them, and re-layouts: 10.3 us -> none
    ppermute x20, starting transfers between devices: 21.6 us -> 23.1 us  [swap(): return lax.ppermute(value, axis, [(i, i ^ d) for i in range(count)])]
    ppermute x20, waiting for transfers between devices: 8.19 us -> 9.31 us  [swap(): return lax.ppermute(value, axis, [(i, i ^ d) for i in range(count)])]
    pallas_call x1, Pallas kernels: 0.26 us -> 1.01 us  [shards(): pl.pallas_call(edge_kernel, out_shape=jax.ShapeDtypeStruct((BOUNDARY * si...]
  transfers between devices with their start and end apart: 20 -> 20, of which waited for: 7 -> 7; matrix products, arithmetic and copies ran while one was open for 0% -> 0% of each run, Pallas kernels for 6% -> 7%
where the time goes in v3:
time: 39.3 us; the launch traced here: 39.1 us
  starting transfers between devices  23.1 us (59%)
  waiting for transfers between devices  9.31 us (24%)
  Pallas kernels  6.62 us (17%)
    ppermute x20, starting transfers between devices, swap(): return lax.ppermute(value, axis, [(i, i ^ d) for i in range(count)])  23.1 us
    ppermute x20, waiting for transfers between devices, swap(): return lax.ppermute(value, axis, [(i, i ^ d) for i in range(count)])  9.31 us
    pallas_call x1, Pallas kernels, shards(): pl.pallas_call(functools.partial(prepare_kernel, *counts), out_shape=[jax...  2.42 us
    pallas_call x1, Pallas kernels, shards(): pl.pallas_call(functools.partial(middle_kernel, own, order, sent_order, s...  1.91 us
    pallas_call x1, Pallas kernels, shards(): pl.pallas_call(edge_kernel, out_shape=jax.ShapeDtypeStruct((BOUNDARY * si...  1.01 us
    pallas_call x1, Pallas kernels, shards(): pl.pallas_call(functools.partial(final_kernel, sent_order), out_shape=nar...  0.97 us
  transfers between devices with their start and end apart: 20, of which 7 were waited for; matrix products, arithmetic and copies ran while one was open for 0% of the time, Pallas kernels for 7%

profile of v3, /device:TPU:0, one launch (start us, length us, event | category | flops | bytes accessed | tf_op | source)
XLA Modules:
  0.0 39.1 jit_solution(18170845802190938112)
XLA Ops:
  0.0 1.0 %edge.1 = bf16[272,256]{1,0:T(8,128)(2,1)S(1)} custom-call(s32[1,8]{1,0:T(1,128)} %recv_sub.1, s32[1,4]{1,0:T(1,128)} %recv_cluster.1, bf16[384,256]{1,0:T(8,128)(2,1)} %features.1), custom_call_target="tpu_custom_call" | custom-call | flops 1024 | bytes 262144 | tf_op jit(solution)/shard_map/edge/pallas_call | solution.py:250
  1.0 4.1 %collective-permute-start.7 = (bf16[272,256]{1,0:T(8,128)(2,1)S(1)}, bf16[272,256]{1,0:T(8,128)(2,1)S(1)}, u32[]{:S(2)}, u32[]{:S(2)}) collective-permute-start(bf16[272,256]{1,0:T(8,128)(2,1)S(1)} %edge.1), channel_id=1, source_target_pairs={{0,16},{8,24},{16,0},{24,8},{1,17},{9,25},{17,1},{25,9},{2,18},{10... | collective-permute-start | bytes 417800 | tf_op jit(solution)/shard_map/ppermute | solution.py:188
  5.1 2.4 %collective-permute-start.5 = (bf16[272,256]{1,0:T(8,128)(2,1)S(1)}, bf16[272,256]{1,0:T(8,128)(2,1)S(1)}, u32[]{:S(2)}, u32[]{:S(2)}) collective-permute-start(bf16[272,256]{1,0:T(8,128)(2,1)S(1)} %edge.1), channel_id=1, source_target_pairs={{0,6},{1,7},{2,4},{3,5},{4,2},{5,3},{6,0},{7,1},{8,14},{9,15},{10,... | collective-permute-start | bytes 417800 | tf_op jit(solution)/shard_map/ppermute | solution.py:188
  7.6 0.5 %collective-permute-start.3 = (bf16[272,256]{1,0:T(8,128)(2,1)S(1)}, bf16[272,256]{1,0:T(8,128)(2,1)S(1)}, u32[]{:S(2)}, u32[]{:S(2)}) collective-permute-start(bf16[272,256]{1,0:T(8,128)(2,1)S(1)} %edge.1), channel_id=1, source_target_pairs={{0,4},{1,5},{2,6},{3,7},{4,0},{5,1},{6,2},{7,3},{8,12},{9,13},{10,... | collective-permute-start | bytes 417800 | tf_op jit(solution)/shard_map/ppermute | solution.py:188
  8.1 0.5 %collective-permute-start.1 = (bf16[272,256]{1,0:T(8,128)(2,1)S(1)}, bf16[272,256]{1,0:T(8,128)(2,1)S(1)}, u32[]{:S(2)}, u32[]{:S(2)}) collective-permute-start(bf16[272,256]{1,0:T(8,128)(2,1)S(1)} %edge.1), channel_id=1, source_target_pairs={{0,2},{1,3},{2,0},{3,1},{4,6},{5,7},{6,4},{7,5},{8,10},{9,11},{10,... | collective-permute-start | bytes 417800 | tf_op jit(solution)/shard_map/ppermute | solution.py:188
  8.6 1.6 %collective-permute-start.9 = (bf16[272,256]{1,0:T(8,128)(2,1)S(1)}, bf16[272,256]{1,0:T(8,128)(2,1)S(1)}, u32[]{:S(2)}, u32[]{:S(2)}) collective-permute-start(bf16[272,256]{1,0:T(8,128)(2,1)S(1)} %edge.1), channel_id=1, source_target_pairs={{0,8},{8,0},{16,24},{24,16},{1,9},{9,1},{17,25},{25,17},{2,10},{10... | collective-permute-start | bytes 417800 | tf_op jit(solution)/shard_map/ppermute | solution.py:188
  10.2 2.4 %prepare.1 = (bf16[384,1920]{1,0:T(8,128)(2,1)S(1)}, bf16[1920,384]{1,0:T(8,128)(2,1)S(1)}, f32[384,256]{1,0:T(8,128)S(1)}, f32[384,256]{1,0:T(8,128)S(1)}, f32[...) custom-call(s32[24]{0:T(128)} %tile_dst_hbm.1, ...), custom_call_target="tpu_custom_call" | custom-call | flops 150994944 | bytes 6291456 | tf_op jit(solution)/shard_map/prepare/pallas_call | solution.py:265
  12.6 0.0 collective-permute-done.7.rest_9_
  12.6 0.1 collective-permute-start
  12.7 0.0 collective-permute-done.5.rest_6_
  12.7 1.4 %collective-permute-done.3.rest_5_ = bf16[272,256]{1,0:T(8,128)(2,1)S(1)} collective-permute-done((bf16[272,256]{1,0:T(8,128)(2,1)S(1)}, bf16[272,256]{1,0:T(8,128)(2,1)S(1)}, u32[]{:S(2)}, u32[]{:S(2)}) %collective-permute-start.3) | collective-permute-done | bytes 139296 | tf_op jit(solution)/shard_map/ppermute | solution.py:188
  14.1 0.1 collective-permute-done.1.rest_4_
  14.2 0.0 collective-permute-start.2
  14.2 0.5 %collective-permute-start.4 = (bf16[272,256]{1,0:T(8,128)(2,1)S(1)}, bf16[272,256]{1,0:T(8,128)(2,1)S(1)}, u32[]{:S(2)}, u32[]{:S(2)}) collective-permute-start(bf16[272,256]{1,0:T(8,128)(2,1)S(1)} %collective-permute-done.3.rest_5_), channel_id=1, source_target_pairs={{0,1},{1,0},{2,3},{3,2},{4,5},{5,4},{6,7},{7,6},{8,9},{9,8},{10,11... | collective-permute-start | bytes 417800 | tf_op jit(solution)/shard_map/ppermute | solution.py:188
  14.7 0.0 collective-permute-start.6
  14.7 0.0 collective-permute-done.9.rest_8_
  14.7 1.6 %collective-permute-start.8 = (bf16[272,256]{1,0:T(8,128)(2,1)S(1)}, bf16[272,256]{1,0:T(8,128)(2,1)S(1)}, u32[]{:S(2)}, u32[]{:S(2)}) collective-permute-start(bf16[272,256]{1,0:T(8,128)(2,1)S(1)} %collective-permute-done.7.rest_9_), channel_id=1, source_target_pairs={{0,8},{8,0},{16,24},{24,16},{1,9},{9,1},{17,25},{25,17},{2,10},{10... | collective-permute-start | bytes 417800 | tf_op jit(solution)/shard_map/ppermute | solution.py:188
  16.3 0.0 collective-permute-done.rest_0_
  16.3 0.0 collective-permute-done.2.rest_1_
  16.3 0.0 collective-permute-done.4.rest_2_
  16.3 0.0 collective-permute-done.6.rest_3_
  16.3 4.5 %collective-permute-done.8.rest_7_ = bf16[272,256]{1,0:T(8,128)(2,1)S(1)} collective-permute-done((bf16[272,256]{1,0:T(8,128)(2,1)S(1)}, bf16[272,256]{1,0:T(8,128)(2,1)S(1)}, u32[]{:S(2)}, u32[]{:S(2)}) %collective-permute-start.8) | collective-permute-done | bytes 139296 | tf_op jit(solution)/shard_map/ppermute | solution.py:188
  20.8 1.9 %middle.1 = (bf16[128,256]{1,0:T(8,128)(2,1)S(1)}, bf16[128,256]{1,0:T(8,128)(2,1)S(1)}, bf16[128,256]{1,0:T(8,128)(2,1)S(1)}, bf16[128,256]{1,0:T(8,128)(2,1)S(...) custom-call(f32[12,256]{1,0:T(8,128)S(1)} %get-tuple-element.34.choi, ...), custom_call_target="tpu_custom_call" | custom-call | flops 754974720 | bytes 6291456 | tf_op jit(solution)/shard_map/middle/pallas_call | solution.py:300
  22.7 1.5 %collective-permute-start.10 = (bf16[128,256]{1,0:T(8,128)(2,1)S(1)}, bf16[128,256]{1,0:T(8,128)(2,1)S(1)}, u32[]{:S(2)}, u32[]{:S(2)}) collective-permute-start(bf16[128,256]{1,0:T(8,128)(2,1)S(1)} %get-tuple-element.53), channel_id=1, source_target_pairs={{0,24},{8,16},{16,8},{24,0},{1,25},{9,17},{17,9},{25,1},{2,26},{10... | collective-permute-start | bytes 196616 | tf_op jit(solution)/shard_map/ppermute | solution.py:188
  24.2 1.6 %collective-permute-start.11 = (bf16[128,256]{1,0:T(8,128)(2,1)S(1)}, bf16[128,256]{1,0:T(8,128)(2,1)S(1)}, u32[]{:S(2)}, u32[]{:S(2)}) collective-permute-start(bf16[128,256]{1,0:T(8,128)(2,1)S(1)} %get-tuple-element.54), channel_id=1, source_target_pairs={{0,16},{8,24},{16,0},{24,8},{1,17},{9,25},{17,1},{25,9},{2,18},{10... | collective-permute-start | bytes 196616 | tf_op jit(solution)/shard_map/ppermute | solution.py:188
  25.8 1.3 %collective-permute-start.12 = (bf16[128,256]{1,0:T(8,128)(2,1)S(1)}, bf16[128,256]{1,0:T(8,128)(2,1)S(1)}, u32[]{:S(2)}, u32[]{:S(2)}) collective-permute-start(bf16[128,256]{1,0:T(8,128)(2,1)S(1)} %get-tuple-element.55), channel_id=1, source_target_pairs={{0,8},{8,0},{16,24},{24,16},{1,9},{9,1},{17,25},{25,17},{2,10},{10... | collective-permute-start | bytes 196616 | tf_op jit(solution)/shard_map/ppermute | solution.py:188
  27.2 1.7 %collective-permute-start.13 = (bf16[128,256]{1,0:T(8,128)(2,1)S(1)}, bf16[128,256]{1,0:T(8,128)(2,1)S(1)}, u32[]{:S(2)}, u32[]{:S(2)}) collective-permute-start(bf16[128,256]{1,0:T(8,128)(2,1)S(1)} %get-tuple-element.56), channel_id=1, source_target_pairs={{0,6},{1,7},{2,4},{3,5},{4,2},{5,3},{6,0},{7,1},{8,14},{9,15},{10,... | collective-permute-start | bytes 196616 | tf_op jit(solution)/shard_map/ppermute | solution.py:188
  28.9 1.3 %collective-permute-start.14 = (bf16[128,256]{1,0:T(8,128)(2,1)S(1)}, bf16[128,256]{1,0:T(8,128)(2,1)S(1)}, u32[]{:S(2)}, u32[]{:S(2)}) collective-permute-start(bf16[128,256]{1,0:T(8,128)(2,1)S(1)} %get-tuple-element.57), channel_id=1, source_target_pairs={{0,4},{1,5},{2,6},{3,7},{4,0},{5,1},{6,2},{7,3},{8,12},{9,13},{10,... | collective-permute-start | bytes 196616 | tf_op jit(solution)/shard_map/ppermute | solution.py:188
  30.2 0.0 collective-permute-done.10.rest_0_
  30.2 1.0 %collective-permute-start.15 = (bf16[128,256]{1,0:T(8,128)(2,1)S(1)}, bf16[128,256]{1,0:T(8,128)(2,1)S(1)}, u32[]{:S(2)}, u32[]{:S(2)}) collective-permute-start(bf16[128,256]{1,0:T(8,128)(2,1)S(1)} %get-tuple-element.58), channel_id=1, source_target_pairs={{0,2},{1,3},{2,0},{3,1},{4,6},{5,7},{6,4},{7,5},{8,10},{9,11},{10,... | collective-permute-start | bytes 196616 | tf_op jit(solution)/shard_map/ppermute | solution.py:188
  31.2 0.6 %collective-permute-done.11.rest_1_ = bf16[128,256]{1,0:T(8,128)(2,1)S(1)} collective-permute-done((bf16[128,256]{1,0:T(8,128)(2,1)S(1)}, bf16[128,256]{1,0:T(8,128)(2,1)S(1)}, u32[]{:S(2)}, u32[]{:S(2)}) %collective-permute-start.11) | collective-permute-done | bytes 65568 | tf_op jit(solution)/shard_map/ppermute | solution.py:188
  31.7 0.8 %collective-permute-start.16 = (bf16[128,256]{1,0:T(8,128)(2,1)S(1)}, bf16[128,256]{1,0:T(8,128)(2,1)S(1)}, u32[]{:S(2)}, u32[]{:S(2)}) collective-permute-start(bf16[128,256]{1,0:T(8,128)(2,1)S(1)} %get-tuple-element.59), channel_id=1, source_target_pairs={{0,7},{1,6},{2,5},{3,4},{4,3},{5,2},{6,1},{7,0},{8,15},{9,14},{10,... | collective-permute-start | bytes 196616 | tf_op jit(solution)/shard_map/ppermute | solution.py:188
  32.6 0.0 collective-permute-done.12.rest_2_
  32.6 1.9 %collective-permute-start.17 = (bf16[128,256]{1,0:T(8,128)(2,1)S(1)}, bf16[128,256]{1,0:T(8,128)(2,1)S(1)}, u32[]{:S(2)}, u32[]{:S(2)}) collective-permute-start(bf16[128,256]{1,0:T(8,128)(2,1)S(1)} %get-tuple-element.60), channel_id=1, source_target_pairs={{0,5},{1,4},{2,7},{3,6},{4,1},{5,0},{6,3},{7,2},{8,13},{9,12},{10,... | collective-permute-start | bytes 196616 | tf_op jit(solution)/shard_map/ppermute | solution.py:188
  34.4 0.0 collective-permute-done.13.rest_3_
  34.4 0.0 collective-permute-start.18
  34.5 0.0 collective-permute-done.14.rest_4_
  34.5 0.6 %collective-permute-start.19 = (bf16[128,256]{1,0:T(8,128)(2,1)S(1)}, bf16[128,256]{1,0:T(8,128)(2,1)S(1)}, u32[]{:S(2)}, u32[]{:S(2)}) collective-permute-start(bf16[128,256]{1,0:T(8,128)(2,1)S(1)} %get-tuple-element.62), channel_id=1, source_target_pairs={{0,1},{1,0},{2,3},{3,2},{4,5},{5,4},{6,7},{7,6},{8,9},{9,8},{10,11... | collective-permute-start | bytes 196616 | tf_op jit(solution)/shard_map/ppermute | solution.py:188
  35.1 0.3 own.1
  35.4 0.0 collective-permute-done.15.rest_5_
  35.4 1.0 %collective-permute-done.16.rest_6_ = bf16[128,256]{1,0:T(8,128)(2,1)S(1)} collective-permute-done((bf16[128,256]{1,0:T(8,128)(2,1)S(1)}, bf16[128,256]{1,0:T(8,128)(2,1)S(1)}, u32[]{:S(2)}, u32[]{:S(2)}) %collective-permute-start.16) | collective-permute-done | bytes 65568 | tf_op jit(solution)/shard_map/ppermute | solution.py:188
  36.4 1.1 %collective-permute-done.17.rest_7_ = bf16[128,256]{1,0:T(8,128)(2,1)S(1)} collective-permute-done((bf16[128,256]{1,0:T(8,128)(2,1)S(1)}, bf16[128,256]{1,0:T(8,128)(2,1)S(1)}, u32[]{:S(2)}, u32[]{:S(2)}) %collective-permute-start.17) | collective-permute-done | bytes 65568 | tf_op jit(solution)/shard_map/ppermute | solution.py:188
  37.4 0.7 %collective-permute-done.18.rest_8_ = bf16[128,256]{1,0:T(8,128)(2,1)S(1)} collective-permute-done((bf16[128,256]{1,0:T(8,128)(2,1)S(1)}, bf16[128,256]{1,0:T(8,128)(2,1)S(1)}, u32[]{:S(2)}, u32[]{:S(2)}) %collective-permute-start.18) | collective-permute-done | bytes 65568 | tf_op jit(solution)/shard_map/ppermute | solution.py:188
  38.1 0.0 collective-permute-done.19.rest_9_
  38.1 1.0 %final.1 = bf16[384,256]{1,0:T(8,128)(2,1)} custom-call(f32[12,256]{1,0:T(8,128)S(1)} %get-tuple-element.51.owner, f32[384,256]{1,0:T(8,128)S(1)} %get-tuple-element.52.total, bf16[128,256]{1,0:T(8,128)(2,1)S(1)} %collective-permute-done.10.rest_0_, bf16[128,256]{1,0:T(8,128)(2,1)S(1)} %collective-permute-done.11.rest_1_, ...), custom_call_target="tpu_custom_call" | custom-call | flops 393216 | bytes 2097152 | tf_op jit(solution)/shard_map/final/pallas_call | solution.py:325
Async XLA Ops:
  1.0 11.6 %collective-permute-start.7 = (bf16[272,256]{1,0:T(8,128)(2,1)S(1)}, bf16[272,256]{1,0:T(8,128)(2,1)S(1)}, u32[]{:S(2)}, u32[]{:S(2)}) collective-permute-start(bf16[272,256]{1,0:T(8,128)(2,1)S(1)} %edge.1), channel_id=1, source_target_pairs={{0,16},{8,24},{16,0},{24,8},{1,17},{9,25},{17,1},{25,9},{2,18},{10... | collective-permute-start | bytes 417800 | tf_op jit(solution)/shard_map/ppermute | solution.py:188
  5.1 7.6 %collective-permute-start.5 = (bf16[272,256]{1,0:T(8,128)(2,1)S(1)}, bf16[272,256]{1,0:T(8,128)(2,1)S(1)}, u32[]{:S(2)}, u32[]{:S(2)}) collective-permute-start(bf16[272,256]{1,0:T(8,128)(2,1)S(1)} %edge.1), channel_id=1, source_target_pairs={{0,6},{1,7},{2,4},{3,5},{4,2},{5,3},{6,0},{7,1},{8,14},{9,15},{10,... | collective-permute-start | bytes 417800 | tf_op jit(solution)/shard_map/ppermute | solution.py:188
  7.6 6.6 %collective-permute-start.3 = (bf16[272,256]{1,0:T(8,128)(2,1)S(1)}, bf16[272,256]{1,0:T(8,128)(2,1)S(1)}, u32[]{:S(2)}, u32[]{:S(2)}) collective-permute-start(bf16[272,256]{1,0:T(8,128)(2,1)S(1)} %edge.1), channel_id=1, source_target_pairs={{0,4},{1,5},{2,6},{3,7},{4,0},{5,1},{6,2},{7,3},{8,12},{9,13},{10,... | collective-permute-start | bytes 417800 | tf_op jit(solution)/shard_map/ppermute | solution.py:188
  8.1 6.1 %collective-permute-start.1 = (bf16[272,256]{1,0:T(8,128)(2,1)S(1)}, bf16[272,256]{1,0:T(8,128)(2,1)S(1)}, u32[]{:S(2)}, u32[]{:S(2)}) collective-permute-start(bf16[272,256]{1,0:T(8,128)(2,1)S(1)} %edge.1), channel_id=1, source_target_pairs={{0,2},{1,3},{2,0},{3,1},{4,6},{5,7},{6,4},{7,5},{8,10},{9,11},{10,... | collective-permute-start | bytes 417800 | tf_op jit(solution)/shard_map/ppermute | solution.py:188
  8.6 6.1 %collective-permute-start.9 = (bf16[272,256]{1,0:T(8,128)(2,1)S(1)}, bf16[272,256]{1,0:T(8,128)(2,1)S(1)}, u32[]{:S(2)}, u32[]{:S(2)}) collective-permute-start(bf16[272,256]{1,0:T(8,128)(2,1)S(1)} %edge.1), channel_id=1, source_target_pairs={{0,8},{8,0},{16,24},{24,16},{1,9},{9,1},{17,25},{25,17},{2,10},{10... | collective-permute-start | bytes 417800 | tf_op jit(solution)/shard_map/ppermute | solution.py:188
  12.6 3.7 %collective-permute-start = (bf16[272,256]{1,0:T(8,128)(2,1)S(1)}, bf16[272,256]{1,0:T(8,128)(2,1)S(1)}, u32[]{:S(2)}, u32[]{:S(2)}) collective-permute-start(bf16[272,256]{1,0:T(8,128)(2,1)S(1)} %edge.1), channel_id=1, source_target_pairs={{0,1},{1,0},{2,3},{3,2},{4,5},{5,4},{6,7},{7,6},{8,9},{9,8},{10,11... | collective-permute-start | bytes 417800 | tf_op jit(solution)/shard_map/ppermute | solution.py:188
  14.2 2.1 %collective-permute-start.2 = (bf16[272,256]{1,0:T(8,128)(2,1)S(1)}, bf16[272,256]{1,0:T(8,128)(2,1)S(1)}, u32[]{:S(2)}, u32[]{:S(2)}) collective-permute-start(bf16[272,256]{1,0:T(8,128)(2,1)S(1)} %collective-permute-done.1.rest_4_), channel_id=1, source_target_pairs={{0,1},{1,0},{2,3},{3,2},{4,5},{5,4},{6,7},{7,6},{8,9},{9,8},{10,11... | collective-permute-start | bytes 417800 | tf_op jit(solution)/shard_map/ppermute | solution.py:188
  14.2 2.1 %collective-permute-start.4 = (bf16[272,256]{1,0:T(8,128)(2,1)S(1)}, bf16[272,256]{1,0:T(8,128)(2,1)S(1)}, u32[]{:S(2)}, u32[]{:S(2)}) collective-permute-start(bf16[272,256]{1,0:T(8,128)(2,1)S(1)} %collective-permute-done.3.rest_5_), channel_id=1, source_target_pairs={{0,1},{1,0},{2,3},{3,2},{4,5},{5,4},{6,7},{7,6},{8,9},{9,8},{10,11... | collective-permute-start | bytes 417800 | tf_op jit(solution)/shard_map/ppermute | solution.py:188
  14.7 1.6 %collective-permute-start.6 = (bf16[272,256]{1,0:T(8,128)(2,1)S(1)}, bf16[272,256]{1,0:T(8,128)(2,1)S(1)}, u32[]{:S(2)}, u32[]{:S(2)}) collective-permute-start(bf16[272,256]{1,0:T(8,128)(2,1)S(1)} %collective-permute-done.5.rest_6_), channel_id=1, source_target_pairs={{0,1},{1,0},{2,3},{3,2},{4,5},{5,4},{6,7},{7,6},{8,9},{9,8},{10,11... | collective-permute-start | bytes 417800 | tf_op jit(solution)/shard_map/ppermute | solution.py:188
  14.7 6.1 %collective-permute-start.8 = (bf16[272,256]{1,0:T(8,128)(2,1)S(1)}, bf16[272,256]{1,0:T(8,128)(2,1)S(1)}, u32[]{:S(2)}, u32[]{:S(2)}) collective-permute-start(bf16[272,256]{1,0:T(8,128)(2,1)S(1)} %collective-permute-done.7.rest_9_), channel_id=1, source_target_pairs={{0,8},{8,0},{16,24},{24,16},{1,9},{9,1},{17,25},{25,17},{2,10},{10... | collective-permute-start | bytes 417800 | tf_op jit(solution)/shard_map/ppermute | solution.py:188
  22.7 7.5 %collective-permute-start.10 = (bf16[128,256]{1,0:T(8,128)(2,1)S(1)}, bf16[128,256]{1,0:T(8,128)(2,1)S(1)}, u32[]{:S(2)}, u32[]{:S(2)}) collective-permute-start(bf16[128,256]{1,0:T(8,128)(2,1)S(1)} %get-tuple-element.53), channel_id=1, source_target_pairs={{0,24},{8,16},{16,8},{24,0},{1,25},{9,17},{17,9},{25,1},{2,26},{10... | collective-permute-start | bytes 196616 | tf_op jit(solution)/shard_map/ppermute | solution.py:188
  24.2 7.5 %collective-permute-start.11 = (bf16[128,256]{1,0:T(8,128)(2,1)S(1)}, bf16[128,256]{1,0:T(8,128)(2,1)S(1)}, u32[]{:S(2)}, u32[]{:S(2)}) collective-permute-start(bf16[128,256]{1,0:T(8,128)(2,1)S(1)} %get-tuple-element.54), channel_id=1, source_target_pairs={{0,16},{8,24},{16,0},{24,8},{1,17},{9,25},{17,1},{25,9},{2,18},{10... | collective-permute-start | bytes 196616 | tf_op jit(solution)/shard_map/ppermute | solution.py:188
  25.8 6.8 %collective-permute-start.12 = (bf16[128,256]{1,0:T(8,128)(2,1)S(1)}, bf16[128,256]{1,0:T(8,128)(2,1)S(1)}, u32[]{:S(2)}, u32[]{:S(2)}) collective-permute-start(bf16[128,256]{1,0:T(8,128)(2,1)S(1)} %get-tuple-element.55), channel_id=1, source_target_pairs={{0,8},{8,0},{16,24},{24,16},{1,9},{9,1},{17,25},{25,17},{2,10},{10... | collective-permute-start | bytes 196616 | tf_op jit(solution)/shard_map/ppermute | solution.py:188
  27.2 7.3 %collective-permute-start.13 = (bf16[128,256]{1,0:T(8,128)(2,1)S(1)}, bf16[128,256]{1,0:T(8,128)(2,1)S(1)}, u32[]{:S(2)}, u32[]{:S(2)}) collective-permute-start(bf16[128,256]{1,0:T(8,128)(2,1)S(1)} %get-tuple-element.56), channel_id=1, source_target_pairs={{0,6},{1,7},{2,4},{3,5},{4,2},{5,3},{6,0},{7,1},{8,14},{9,15},{10,... | collective-permute-start | bytes 196616 | tf_op jit(solution)/shard_map/ppermute | solution.py:188
  28.9 5.6 %collective-permute-start.14 = (bf16[128,256]{1,0:T(8,128)(2,1)S(1)}, bf16[128,256]{1,0:T(8,128)(2,1)S(1)}, u32[]{:S(2)}, u32[]{:S(2)}) collective-permute-start(bf16[128,256]{1,0:T(8,128)(2,1)S(1)} %get-tuple-element.57), channel_id=1, source_target_pairs={{0,4},{1,5},{2,6},{3,7},{4,0},{5,1},{6,2},{7,3},{8,12},{9,13},{10,... | collective-permute-start | bytes 196616 | tf_op jit(solution)/shard_map/ppermute | solution.py:188
  30.2 5.2 %collective-permute-start.15 = (bf16[128,256]{1,0:T(8,128)(2,1)S(1)}, bf16[128,256]{1,0:T(8,128)(2,1)S(1)}, u32[]{:S(2)}, u32[]{:S(2)}) collective-permute-start(bf16[128,256]{1,0:T(8,128)(2,1)S(1)} %get-tuple-element.58), channel_id=1, source_target_pairs={{0,2},{1,3},{2,0},{3,1},{4,6},{5,7},{6,4},{7,5},{8,10},{9,11},{10,... | collective-permute-start | bytes 196616 | tf_op jit(solution)/shard_map/ppermute | solution.py:188
  31.7 4.7 %collective-permute-start.16 = (bf16[128,256]{1,0:T(8,128)(2,1)S(1)}, bf16[128,256]{1,0:T(8,128)(2,1)S(1)}, u32[]{:S(2)}, u32[]{:S(2)}) collective-permute-start(bf16[128,256]{1,0:T(8,128)(2,1)S(1)} %get-tuple-element.59), channel_id=1, source_target_pairs={{0,7},{1,6},{2,5},{3,4},{4,3},{5,2},{6,1},{7,0},{8,15},{9,14},{10,... | collective-permute-start | bytes 196616 | tf_op jit(solution)/shard_map/ppermute | solution.py:188
  32.6 4.9 %collective-permute-start.17 = (bf16[128,256]{1,0:T(8,128)(2,1)S(1)}, bf16[128,256]{1,0:T(8,128)(2,1)S(1)}, u32[]{:S(2)}, u32[]{:S(2)}) collective-permute-start(bf16[128,256]{1,0:T(8,128)(2,1)S(1)} %get-tuple-element.60), channel_id=1, source_target_pairs={{0,5},{1,4},{2,7},{3,6},{4,1},{5,0},{6,3},{7,2},{8,13},{9,12},{10,... | collective-permute-start | bytes 196616 | tf_op jit(solution)/shard_map/ppermute | solution.py:188
  34.4 3.7 %collective-permute-start.18 = (bf16[128,256]{1,0:T(8,128)(2,1)S(1)}, bf16[128,256]{1,0:T(8,128)(2,1)S(1)}, u32[]{:S(2)}, u32[]{:S(2)}) collective-permute-start(bf16[128,256]{1,0:T(8,128)(2,1)S(1)} %get-tuple-element.61), channel_id=1, source_target_pairs={{0,3},{1,2},{2,1},{3,0},{4,7},{5,6},{6,5},{7,4},{8,11},{9,10},{10,... | collective-permute-start | bytes 196616 | tf_op jit(solution)/shard_map/ppermute | solution.py:188
  34.5 3.7 %collective-permute-start.19 = (bf16[128,256]{1,0:T(8,128)(2,1)S(1)}, bf16[128,256]{1,0:T(8,128)(2,1)S(1)}, u32[]{:S(2)}, u32[]{:S(2)}) collective-permute-start(bf16[128,256]{1,0:T(8,128)(2,1)S(1)} %get-tuple-element.62), channel_id=1, source_target_pairs={{0,1},{1,0},{2,3},{3,2},{4,5},{5,4},{6,7},{7,6},{8,9},{9,8},{10,11... | collective-permute-start | bytes 196616 | tf_op jit(solution)/shard_map/ppermute | solution.py:188

commit v4 on v3

--- a/solution.py
+++ b/solution.py
@@ -102,29 +102,37 @@
     own_pre[...] = dot(features[...], w_self[...]) + bias[...].reshape(1, -1)
 
 
+def halo_sum(choice, dense, slots, own, messages, halo):
+    size = dense.shape[0] // own
+    for i, slot in enumerate(slots):
+        message = messages[slot]
+        halo[i * size : (i + 1) * size, :] = jnp.where(
+            choice[slot : slot + 1, :] > 0.5,
+            message[size : 2 * size, :].astype(F32),
+            message[0:size, :].astype(F32),
+        ).astype(BF)
+    columns = slice((own + slots[0]) * size, (own + slots[-1] + 1) * size)
+    return dot(dense[:, columns], halo[...])
+
+
+def near_kernel(own, sub_count, choice, dense, own_sum, edge, *rest):
+    received, (out, halo) = rest[:-2], rest[-2:]
+    messages = dict(enumerate((edge, *received, edge)))
+    out[...] = own_sum[...] + halo_sum(choice, dense, range(sub_count + 1), own, messages, halo)
+
+
 def middle_kernel(
-    own, order, sent_order, sub_count,
-    choice, edge, grad_out, w_neigh, dense, dense_t, own_sum, own_pre, inverse,
+    own, sent_order, sub_count, cluster_count,
+    choice, grad_out, w_neigh, dense, dense_t, near_sum, own_pre, inverse, gathered,
     *rest,
 ):
-    peers = len(order)
-    received = rest[:peers]
-    sent = rest[peers : 2 * peers]
-    kept, spread, grad_pre, halo = rest[2 * peers :]
-    size = halo.shape[0] // (peers + 2)
-
-    def pick(slot, source):
-        second = choice[slot : slot + 1, :] > 0.5
-        halo[slot * size : (slot + 1) * size, :] = jnp.where(
-            second, source[size : 2 * size, :].astype(F32), source[0:size, :].astype(F32)
-        ).astype(BF)
-
-    pick(0, edge)
-    pick(sub_count, edge)
-    for source, slot in zip(received, order):
-        pick(slot, source)
-    inv = jnp.concatenate([inverse[...]] * (edge.shape[1] // size), axis=1)
-    aggregate = own_sum[...] + dot(dense[:, own * size :], halo[...])
+    sent, (kept, spread, grad_pre, halo) = rest[: len(sent_order)], rest[len(sent_order) :]
+    size = dense.shape[0] // own
+    cluster_id = lax.axis_index("cluster")
+    messages = {sub_count + d: gathered.at[cluster_id ^ d] for d in range(1, cluster_count)}
+    late = range(sub_count + 1, sub_count + cluster_count)
+    aggregate = near_sum[...] + halo_sum(choice, dense, late, own, messages, halo)
+    inv = jnp.concatenate([inverse[...]] * (grad_out.shape[1] // size), axis=1)
     mean = (aggregate * inv).astype(BF)
     pre = own_pre[...] + dot(mean, w_neigh[...])
     grad = (grad_out[...].astype(F32) * gelu_slope(pre)).astype(BF)
@@ -150,7 +158,7 @@
 def own_kernel(
     own, order, sub_count, choice, w_self, dense_t, kept, spread, grad_pre, *rest
 ):
-    received, (total, owner) = rest[:-2], rest[-2:]
+    (gathered, *received), (total, owner) = rest[:-2], rest[-2:]
     size = kept.shape[1]
     width = total.shape[1]
     total[...] = dot_right_transposed(grad_pre[...], w_self[...]) + dot(
@@ -159,12 +167,14 @@
     for i, slot in enumerate((0, sub_count)):
         split(total, kept[i].astype(F32), choice[slot : slot + 1, :] > 0.5, size)
     lanes = lax.broadcasted_iota(jnp.int32, (1, width), 1)
-    for message, slot in zip(received, order):
-        row = message[BOUNDARY * size : BOUNDARY * size + EXTRA, :].astype(F32)[0:1, :]
+    for slot in order:
         if slot < sub_count:
-            lane = lax.axis_index("sub")
+            message, lane = received[slot - 1], lax.axis_index("sub")
         else:
-            lane = sub_count + lax.axis_index("cluster")
+            cluster_id = lax.axis_index("cluster")
+            message, lane = gathered.at[cluster_id ^ (slot - sub_count)], sub_count + cluster_id
+        last = message.shape[0] - EXTRA
+        row = message[last : last + EXTRA, :].astype(F32)[0:1, :]
         index = jnp.sum(jnp.where(lanes == lane, row, 0.0), axis=1, keepdims=True)
         owner[slot : slot + 1, :] = jnp.broadcast_to(index, (1, width))
 
@@ -188,30 +198,21 @@
     return lax.ppermute(value, axis, [(i, i ^ d) for i in range(count)])
 
 
-def gather_edges(edge, prepared, sub_count, cluster_count):
-    def relay(value):
-        return lax.optimization_barrier((value, prepared))[0]
-
-    got = {0: edge, sub_count: edge}
-    for d in range(1, cluster_count):
-        low = d & -d
-        value = edge if d == low else relay(got[sub_count + d - low])
-        got[sub_count + d] = swap(value, "cluster", cluster_count, low)
-    for d in range(1, sub_count):
-        if d % 2:
-            got[d] = swap(relay(got[d - 1]), "sub", sub_count, 1)
-        else:
-            got[d] = swap(edge, "sub", sub_count, d)
-    return got
-
-
-def peer_orders(sub_count, cluster_count):
-    along = [sub_count + d for d in range(1, cluster_count)]
-    direct = [sub_count + d for d in range(1, cluster_count) if not d & (d - 1)]
-    relayed = [sub_count + d for d in range(1, cluster_count) if d & (d - 1)]
-    even = list(range(2, sub_count, 2))
-    odd = list(range(3, sub_count, 2))
-    return [1] + odd + even + relayed + direct, along[::-1] + even[::-1] + odd[::-1] + [1]
+def gather_edges(edge, prepared, sub_count):
+    got = {}
+    for d in range(2, sub_count, 2):
+        got[d] = swap(edge, "sub", sub_count, d)
+    for d in range(1, sub_count, 2):
+        value = edge if d == 1 else lax.optimization_barrier((got[d - 1], prepared))[0]
+        got[d] = swap(value, "sub", sub_count, 1)
+    return [got[d] for d in range(1, sub_count)]
+
+
+def sending_order(sub_count, cluster_count):
+    along = [sub_count + d for d in range(cluster_count - 1, 0, -1)]
+    across = list(range(sub_count - 1, 1, -1))
+    across = sorted(across, key=lambda d: (-(d // 2), d % 2))
+    return along[:1] + across[:4] + along[1:] + across[4:] + [1]
 
 
 def send_back(value, slot, sub_count, cluster_count):
@@ -239,7 +240,7 @@
     own = rows // size
     slots = own + sub_count + cluster_count
     counts = (own, sub_count, cluster_count)
-    order, sent_order = peer_orders(sub_count, cluster_count)
+    sent_order = sending_order(sub_count, cluster_count)
 
     wide = jax.ShapeDtypeStruct((rows, width), F32)
     narrow = jax.ShapeDtypeStruct((rows, width), BF)
@@ -261,6 +262,7 @@
         cost_estimate=cost(1024, 256 * 1024),
         name="edge",
     )(in_hbm(recv_sub), in_hbm(recv_cluster), in_hbm(features))
+    gathered = lax.all_gather(edge, "cluster", axis=0)
 
     dense, dense_t, own_sum, own_pre, inverse, choice, w_self, w_neigh, grad_out = pl.pallas_call(
         functools.partial(prepare_kernel, *counts),
@@ -294,33 +296,42 @@
         *map(in_hbm, (tile_dst, tile_src, recv_sub, recv_cluster, features, w_self, bias)),
         *map(in_hbm, (tile_weight, grad_out, w_neigh)),
     )
-    got = gather_edges(edge, choice, sub_count, cluster_count)
-    halos = [got[slot] for slot in order]
+    halos = gather_edges(edge, choice, sub_count)
+    near_sum = pl.pallas_call(
+        functools.partial(near_kernel, own, sub_count),
+        out_shape=wide,
+        in_specs=[VMEM] * (3 + sub_count),
+        out_specs=VMEM,
+        scratch_shapes=[pltpu.VMEM(((sub_count + 1) * size, width), BF)],
+        compiler_params=PARAMS,
+        cost_estimate=cost(2 * rows * (sub_count + 1) * size * width, 3 * 1024 * 1024),
+        name="near",
+    )(choice, dense, own_sum, edge, *halos)
 
     outs = pl.pallas_call(
-        functools.partial(middle_kernel, own, order, sent_order, sub_count),
+        functools.partial(middle_kernel, own, sent_order, sub_count, cluster_count),
         out_shape=[block] * peers + [jax.ShapeDtypeStruct((2, size, width), BF), narrow, narrow],
-        in_specs=[VMEM] * (9 + peers),
+        in_specs=[VMEM] * 9,
         out_specs=[VMEM] * (peers + 3),
-        scratch_shapes=[pltpu.VMEM(((sub_count + cluster_count) * size, width), BF)],
-        compiler_params=PARAMS,
-        cost_estimate=cost(4 * rows * slots * size * width, 6 * 1024 * 1024),
+        scratch_shapes=[pltpu.VMEM(((cluster_count - 1) * size, width), BF)],
+        compiler_params=PARAMS,
+        cost_estimate=cost(2 * rows * slots * size * width, 6 * 1024 * 1024),
         name="middle",
-    )(choice, edge, grad_out, w_neigh, dense, dense_t, own_sum, own_pre, inverse, *halos)
+    )(choice, grad_out, w_neigh, dense, dense_t, near_sum, own_pre, inverse, gathered)
     sent, (kept, spread, grad_pre) = outs[:peers], outs[peers:]
     returned = [
         send_back(value, slot, sub_count, cluster_count) for value, slot in zip(sent, sent_order)
     ]
 
     total, owner = pl.pallas_call(
-        functools.partial(own_kernel, own, order, sub_count),
+        functools.partial(own_kernel, own, sent_order, sub_count),
         out_shape=[wide, marks],
-        in_specs=[VMEM] * (6 + peers),
+        in_specs=[VMEM] * (6 + sub_count),
         out_specs=[VMEM] * 2,
         compiler_params=PARAMS,
         cost_estimate=cost(4 * rows * rows * width, 2 * 1024 * 1024),
         name="own",
-    )(choice, w_self, dense_t, kept, spread, grad_pre, *halos)
+    )(choice, w_self, dense_t, kept, spread, grad_pre, gathered, *halos)
 
     return pl.pallas_call(
         functools.partial(final_kernel, sent_order),

time: 39.3 us -> 48.2 us (1.23)
  blocking collectives: 0 us -> 17 us
  starting transfers between devices: 23.1 us -> 16.9 us
  waiting for transfers between devices: 9.31 us -> 7.56 us
    all_gather x0 -> x1, blocking collectives: none -> 17 us  [shards(): gathered = lax.all_gather(edge, 'cluster', axis=0)]
    ppermute x20 -> x17, starting transfers between devices: 23.1 us -> 16.9 us  [swap(): return lax.ppermute(value, axis, [(i, i ^ d) for i in range(count)])]
    ppermute x20 -> x17, waiting for transfers between devices: 9.31 us -> 7.56 us  [swap(): return lax.ppermute(value, axis, [(i, i ^ d) for i in range(count)])]
    pallas_call x2 -> x3, Pallas kernels: 2.22 us -> 2.09 us  [the longest x1 1.3 us: shards(): pl.pallas_call(functools.partial(middle_kernel, own, sent_order, sub_coun...]
  transfers between devices with their start and end apart: 20 -> 17, of which waited for: 7 -> 8; matrix products, arithmetic and copies ran while one was open for 0% -> 0% of each run, Pallas kernels for 7% -> 6%
where the time goes in v4:
time: 48.2 us; the launch traced here: 48 us
  blocking collectives  17 us (35%)
  starting transfers between devices  16.9 us (35%)
  waiting for transfers between devices  7.56 us (16%)
  Pallas kernels  6.5 us (13%)
    all_gather x1, blocking collectives, shards(): gathered = lax.all_gather(edge, 'cluster', axis=0)  17 us
    ppermute x17, starting transfers between devices, swap(): return lax.ppermute(value, axis, [(i, i ^ d) for i in range(count)])  16.9 us
    ppermute x17, waiting for transfers between devices, swap(): return lax.ppermute(value, axis, [(i, i ^ d) for i in range(count)])  7.56 us
    pallas_call x1, Pallas kernels, shards(): pl.pallas_call(functools.partial(prepare_kernel, *counts), out_shape=[jax...  2.42 us
    pallas_call x1, Pallas kernels, shards(): pl.pallas_call(functools.partial(middle_kernel, own, sent_order, sub_coun...  1.3 us
    pallas_call x1, Pallas kernels, shards(): pl.pallas_call(edge_kernel, out_shape=jax.ShapeDtypeStruct((BOUNDARY * si...  1.01 us
    pallas_call x1, Pallas kernels, shards(): pl.pallas_call(functools.partial(final_kernel, sent_order), out_shape=nar...  0.98 us
  transfers between devices with their start and end apart: 17, of which 8 were waited for; matrix products, arithmetic and copies ran while one was open for 0% of the time, Pallas kernels for 6%

profile of v4, /device:TPU:0, one launch (start us, length us, event | category | flops | bytes accessed | tf_op | source)
XLA Modules:
  0.0 48.0 jit_solution(6091542792214858559)
XLA Ops:
  0.0 1.0 %edge.1 = bf16[272,256]{1,0:T(8,128)(2,1)S(1)} custom-call(s32[1,8]{1,0:T(1,128)} %recv_sub.1, s32[1,4]{1,0:T(1,128)} %recv_cluster.1, bf16[384,256]{1,0:T(8,128)(2,1)} %features.1), custom_call_target="tpu_custom_call" | custom-call | flops 1024 | bytes 262144 | tf_op jit(solution)/shard_map/edge/pallas_call | solution.py:251
  1.0 4.0 %collective-permute-start.5 = (bf16[272,256]{1,0:T(8,128)(2,1)S(1)}, bf16[272,256]{1,0:T(8,128)(2,1)S(1)}, u32[]{:S(2)}, u32[]{:S(2)}) collective-permute-start(bf16[272,256]{1,0:T(8,128)(2,1)S(1)} %edge.1), channel_id=1, source_target_pairs={{0,6},{1,7},{2,4},{3,5},{4,2},{5,3},{6,0},{7,1},{8,14},{9,15},{10,... | collective-permute-start | bytes 417800 | tf_op jit(solution)/shard_map/ppermute | solution.py:198
  5.0 0.5 %collective-permute-start.3 = (bf16[272,256]{1,0:T(8,128)(2,1)S(1)}, bf16[272,256]{1,0:T(8,128)(2,1)S(1)}, u32[]{:S(2)}, u32[]{:S(2)}) collective-permute-start(bf16[272,256]{1,0:T(8,128)(2,1)S(1)} %edge.1), channel_id=1, source_target_pairs={{0,4},{1,5},{2,6},{3,7},{4,0},{5,1},{6,2},{7,3},{8,12},{9,13},{10,... | collective-permute-start | bytes 417800 | tf_op jit(solution)/shard_map/ppermute | solution.py:198
  5.5 0.1 collective-permute-start.1
  5.6 0.0 collective-permute-start
  5.6 2.4 %prepare.1 = (bf16[384,1920]{1,0:T(8,128)(2,1)S(1)}, bf16[1920,384]{1,0:T(8,128)(2,1)S(1)}, f32[384,256]{1,0:T(8,128)S(1)}, f32[384,256]{1,0:T(8,128)S(1)}, f32[...) custom-call(s32[24]{0:T(128)} %tile_dst_hbm.1, ...), custom_call_target="tpu_custom_call" | custom-call | flops 150994944 | bytes 6291456 | tf_op jit(solution)/shard_map/prepare/pallas_call | solution.py:267
  8.1 1.0 %collective-permute-done.5.rest_5_.rest_6_ = bf16[272,256]{1,0:T(8,128)(2,1)S(1)} collective-permute-done((bf16[272,256]{1,0:T(8,128)(2,1)S(1)}, bf16[272,256]{1,0:T(8,128)(2,1)S(1)}, u32[]{:S(2)}, u32[]{:S(2)}) %collective-permute-start.5) | collective-permute-done | bytes 139296 | tf_op jit(solution)/shard_map/ppermute | solution.py:198
  9.1 2.6 %collective-permute-done.3.rest_3_.rest_4_ = bf16[272,256]{1,0:T(8,128)(2,1)S(1)} collective-permute-done((bf16[272,256]{1,0:T(8,128)(2,1)S(1)}, bf16[272,256]{1,0:T(8,128)(2,1)S(1)}, u32[]{:S(2)}, u32[]{:S(2)}) %collective-permute-start.3) | collective-permute-done | bytes 139296 | tf_op jit(solution)/shard_map/ppermute | solution.py:198
  11.6 0.3 collective-permute-done.1.rest_1_.rest_2_
  11.9 0.0 collective-permute-start.2
  11.9 0.5 %collective-permute-start.4 = (bf16[272,256]{1,0:T(8,128)(2,1)S(1)}, bf16[272,256]{1,0:T(8,128)(2,1)S(1)}, u32[]{:S(2)}, u32[]{:S(2)}) collective-permute-start(bf16[272,256]{1,0:T(8,128)(2,1)S(1)} %collective-permute-done.3.rest_3_.rest_4_), channel_id=1, source_target_pairs={{0,1},{1,0},{2,3},{3,2},{4,5},{5,4},{6,7},{7,6},{8,9},{9,8},{10,11... | collective-permute-start | bytes 417800 | tf_op jit(solution)/shard_map/ppermute | solution.py:198
  12.4 0.0 collective-permute-start.6
  12.4 17.0 %all-gather = bf16[1088,256]{1,0:T(8,128)(2,1)S(1)} all-gather(bf16[272,256]{1,0:T(8,128)(2,1)S(1)} %edge.1), channel_id=2, replica_groups=mesh['cluster'=4,'sub'=8] {'cluster'}, dimensions={0}, use_global_device_ids=true | all-gather | bytes 696320 | tf_op jit(solution)/shard_map/all_gather | solution.py:265
  29.4 0.0 collective-permute-done.rest_0_.rest_1_
  29.4 0.0 collective-permute-done.2.rest_2_.rest_3_
  29.4 0.0 collective-permute-done.4.rest_4_.rest_5_
  29.4 0.0 collective-permute-done.6.rest_6_.rest_7_
  29.4 0.5 near.1.near_sum
  29.9 1.3 %middle.1 = (bf16[128,256]{1,0:T(8,128)(2,1)S(1)}, bf16[128,256]{1,0:T(8,128)(2,1)S(1)}, bf16[128,256]{1,0:T(8,128)(2,1)S(1)}, bf16[128,256]{1,0:T(8,128)(2,1)S(...) custom-call(f32[12,256]{1,0:T(8,128)S(1)} %get-tuple-element.32.choi, ...), custom_call_target="tpu_custom_call" | custom-call | flops 377487360 | bytes 6291456 | tf_op jit(solution)/shard_map/middle/pallas_call | solution.py:311
  31.2 3.3 %collective-permute-start.7 = (bf16[128,256]{1,0:T(8,128)(2,1)S(1)}, bf16[128,256]{1,0:T(8,128)(2,1)S(1)}, u32[]{:S(2)}, u32[]{:S(2)}) collective-permute-start(bf16[128,256]{1,0:T(8,128)(2,1)S(1)} %get-tuple-element.49), channel_id=1, source_target_pairs={{0,24},{8,16},{16,8},{24,0},{1,25},{9,17},{17,9},{25,1},{2,26},{10... | collective-permute-start | bytes 196616 | tf_op jit(solution)/shard_map/ppermute | solution.py:198
  34.5 1.7 %collective-permute-start.8 = (bf16[128,256]{1,0:T(8,128)(2,1)S(1)}, bf16[128,256]{1,0:T(8,128)(2,1)S(1)}, u32[]{:S(2)}, u32[]{:S(2)}) collective-permute-start(bf16[128,256]{1,0:T(8,128)(2,1)S(1)} %get-tuple-element.50), channel_id=1, source_target_pairs={{0,6},{1,7},{2,4},{3,5},{4,2},{5,3},{6,0},{7,1},{8,14},{9,15},{10,... | collective-permute-start | bytes 196616 | tf_op jit(solution)/shard_map/ppermute | solution.py:198
  36.2 0.0 collective-permute-start.9
  36.2 1.3 %collective-permute-start.10 = (bf16[128,256]{1,0:T(8,128)(2,1)S(1)}, bf16[128,256]{1,0:T(8,128)(2,1)S(1)}, u32[]{:S(2)}, u32[]{:S(2)}) collective-permute-start(bf16[128,256]{1,0:T(8,128)(2,1)S(1)} %get-tuple-element.52), channel_id=1, source_target_pairs={{0,4},{1,5},{2,6},{3,7},{4,0},{5,1},{6,2},{7,3},{8,12},{9,13},{10,... | collective-permute-start | bytes 196616 | tf_op jit(solution)/shard_map/ppermute | solution.py:198
  37.5 1.4 %collective-permute-start.11 = (bf16[128,256]{1,0:T(8,128)(2,1)S(1)}, bf16[128,256]{1,0:T(8,128)(2,1)S(1)}, u32[]{:S(2)}, u32[]{:S(2)}) collective-permute-start(bf16[128,256]{1,0:T(8,128)(2,1)S(1)} %get-tuple-element.53), channel_id=1, source_target_pairs={{0,5},{1,4},{2,7},{3,6},{4,1},{5,0},{6,3},{7,2},{8,13},{9,12},{10,... | collective-permute-start | bytes 196616 | tf_op jit(solution)/shard_map/ppermute | solution.py:198
  38.9 0.0 collective-permute-done.7.rest_0_
  38.9 0.0 collective-permute-start.12
  38.9 0.8 %collective-permute-done.8.rest_1_ = bf16[128,256]{1,0:T(8,128)(2,1)S(1)} collective-permute-done((bf16[128,256]{1,0:T(8,128)(2,1)S(1)}, bf16[128,256]{1,0:T(8,128)(2,1)S(1)}, u32[]{:S(2)}, u32[]{:S(2)}) %collective-permute-start.8) | collective-permute-done | bytes 65568 | tf_op jit(solution)/shard_map/ppermute | solution.py:198
  39.6 1.5 %collective-permute-start.13 = (bf16[128,256]{1,0:T(8,128)(2,1)S(1)}, bf16[128,256]{1,0:T(8,128)(2,1)S(1)}, u32[]{:S(2)}, u32[]{:S(2)}) collective-permute-start(bf16[128,256]{1,0:T(8,128)(2,1)S(1)} %get-tuple-element.55), channel_id=1, source_target_pairs={{0,8},{8,0},{16,24},{24,16},{1,9},{9,1},{17,25},{25,17},{2,10},{10... | collective-permute-start | bytes 196616 | tf_op jit(solution)/shard_map/ppermute | solution.py:198
  41.1 0.0 collective-permute-done.9.rest_2_
  41.2 1.5 %collective-permute-start.14 = (bf16[128,256]{1,0:T(8,128)(2,1)S(1)}, bf16[128,256]{1,0:T(8,128)(2,1)S(1)}, u32[]{:S(2)}, u32[]{:S(2)}) collective-permute-start(bf16[128,256]{1,0:T(8,128)(2,1)S(1)} %get-tuple-element.56), channel_id=1, source_target_pairs={{0,2},{1,3},{2,0},{3,1},{4,6},{5,7},{6,4},{7,5},{8,10},{9,11},{10,... | collective-permute-start | bytes 196616 | tf_op jit(solution)/shard_map/ppermute | solution.py:198
  42.7 0.0 collective-permute-done.10.rest_3_
  42.7 1.0 %collective-permute-start.15 = (bf16[128,256]{1,0:T(8,128)(2,1)S(1)}, bf16[128,256]{1,0:T(8,128)(2,1)S(1)}, u32[]{:S(2)}, u32[]{:S(2)}) collective-permute-start(bf16[128,256]{1,0:T(8,128)(2,1)S(1)} %get-tuple-element.57), channel_id=1, source_target_pairs={{0,3},{1,2},{2,1},{3,0},{4,7},{5,6},{6,5},{7,4},{8,11},{9,10},{10,... | collective-permute-start | bytes 196616 | tf_op jit(solution)/shard_map/ppermute | solution.py:198
  43.6 0.2 collective-permute-done.11.rest_4_
  43.9 0.2 collective-permute-start.16
  44.0 0.3 own.1
  44.4 0.0 collective-permute-done.12.rest_5_
  44.4 0.5 %collective-permute-done.13.rest_6_ = bf16[128,256]{1,0:T(8,128)(2,1)S(1)} collective-permute-done((bf16[128,256]{1,0:T(8,128)(2,1)S(1)}, bf16[128,256]{1,0:T(8,128)(2,1)S(1)}, u32[]{:S(2)}, u32[]{:S(2)}) %collective-permute-start.13) | collective-permute-done | bytes 65568 | tf_op jit(solution)/shard_map/ppermute | solution.py:198
  44.9 0.5 %collective-permute-done.14.rest_7_ = bf16[128,256]{1,0:T(8,128)(2,1)S(1)} collective-permute-done((bf16[128,256]{1,0:T(8,128)(2,1)S(1)}, bf16[128,256]{1,0:T(8,128)(2,1)S(1)}, u32[]{:S(2)}, u32[]{:S(2)}) %collective-permute-start.14) | collective-permute-done | bytes 65568 | tf_op jit(solution)/shard_map/ppermute | solution.py:198
  45.4 1.6 %collective-permute-done.15.rest_8_ = bf16[128,256]{1,0:T(8,128)(2,1)S(1)} collective-permute-done((bf16[128,256]{1,0:T(8,128)(2,1)S(1)}, bf16[128,256]{1,0:T(8,128)(2,1)S(1)}, u32[]{:S(2)}, u32[]{:S(2)}) %collective-permute-start.15) | collective-permute-done | bytes 65568 | tf_op jit(solution)/shard_map/ppermute | solution.py:198
  47.0 0.0 collective-permute-done.16.rest_9_
  47.0 1.0 %final.1 = bf16[384,256]{1,0:T(8,128)(2,1)} custom-call(f32[12,256]{1,0:T(8,128)S(1)} %get-tuple-element.47.owner, f32[384,256]{1,0:T(8,128)S(1)} %get-tuple-element.48.total, bf16[128,256]{1,0:T(8,128)(2,1)S(1)} %collective-permute-done.7.rest_0_, bf16[128,256]{1,0:T(8,128)(2,1)S(1)} %collective-permute-done.8.rest_1_, ...), custom_call_target="tpu_custom_call" | custom-call | flops 393216 | bytes 2097152 | tf_op jit(solution)/shard_map/final/pallas_call | solution.py:336
Async XLA Ops:
  1.0 8.0 %collective-permute-start.5 = (bf16[272,256]{1,0:T(8,128)(2,1)S(1)}, bf16[272,256]{1,0:T(8,128)(2,1)S(1)}, u32[]{:S(2)}, u32[]{:S(2)}) collective-permute-start(bf16[272,256]{1,0:T(8,128)(2,1)S(1)} %edge.1), channel_id=1, source_target_pairs={{0,6},{1,7},{2,4},{3,5},{4,2},{5,3},{6,0},{7,1},{8,14},{9,15},{10,... | collective-permute-start | bytes 417800 | tf_op jit(solution)/shard_map/ppermute | solution.py:198
  5.0 6.7 %collective-permute-start.3 = (bf16[272,256]{1,0:T(8,128)(2,1)S(1)}, bf16[272,256]{1,0:T(8,128)(2,1)S(1)}, u32[]{:S(2)}, u32[]{:S(2)}) collective-permute-start(bf16[272,256]{1,0:T(8,128)(2,1)S(1)} %edge.1), channel_id=1, source_target_pairs={{0,4},{1,5},{2,6},{3,7},{4,0},{5,1},{6,2},{7,3},{8,12},{9,13},{10,... | collective-permute-start | bytes 417800 | tf_op jit(solution)/shard_map/ppermute | solution.py:198
  5.5 6.4 %collective-permute-start.1 = (bf16[272,256]{1,0:T(8,128)(2,1)S(1)}, bf16[272,256]{1,0:T(8,128)(2,1)S(1)}, u32[]{:S(2)}, u32[]{:S(2)}) collective-permute-start(bf16[272,256]{1,0:T(8,128)(2,1)S(1)} %edge.1), channel_id=1, source_target_pairs={{0,2},{1,3},{2,0},{3,1},{4,6},{5,7},{6,4},{7,5},{8,10},{9,11},{10,... | collective-permute-start | bytes 417800 | tf_op jit(solution)/shard_map/ppermute | solution.py:198
  5.6 23.8 %collective-permute-start = (bf16[272,256]{1,0:T(8,128)(2,1)S(1)}, bf16[272,256]{1,0:T(8,128)(2,1)S(1)}, u32[]{:S(2)}, u32[]{:S(2)}) collective-permute-start(bf16[272,256]{1,0:T(8,128)(2,1)S(1)} %edge.1), channel_id=1, source_target_pairs={{0,1},{1,0},{2,3},{3,2},{4,5},{5,4},{6,7},{7,6},{8,9},{9,8},{10,11... | collective-permute-start | bytes 417800 | tf_op jit(solution)/shard_map/ppermute | solution.py:198
  11.9 17.5 %collective-permute-start.2 = (bf16[272,256]{1,0:T(8,128)(2,1)S(1)}, bf16[272,256]{1,0:T(8,128)(2,1)S(1)}, u32[]{:S(2)}, u32[]{:S(2)}) collective-permute-start(bf16[272,256]{1,0:T(8,128)(2,1)S(1)} %collective-permute-done.1.rest_1_.rest_2_), channel_id=1, source_target_pairs={{0,1},{1,0},{2,3},{3,2},{4,5},{5,4},{6,7},{7,6},{8,9},{9,8},{10,11... | collective-permute-start | bytes 417800 | tf_op jit(solution)/shard_map/ppermute | solution.py:198
  11.9 17.5 %collective-permute-start.4 = (bf16[272,256]{1,0:T(8,128)(2,1)S(1)}, bf16[272,256]{1,0:T(8,128)(2,1)S(1)}, u32[]{:S(2)}, u32[]{:S(2)}) collective-permute-start(bf16[272,256]{1,0:T(8,128)(2,1)S(1)} %collective-permute-done.3.rest_3_.rest_4_), channel_id=1, source_target_pairs={{0,1},{1,0},{2,3},{3,2},{4,5},{5,4},{6,7},{7,6},{8,9},{9,8},{10,11... | collective-permute-start | bytes 417800 | tf_op jit(solution)/shard_map/ppermute | solution.py:198
  12.4 17.0 %collective-permute-start.6 = (bf16[272,256]{1,0:T(8,128)(2,1)S(1)}, bf16[272,256]{1,0:T(8,128)(2,1)S(1)}, u32[]{:S(2)}, u32[]{:S(2)}) collective-permute-start(bf16[272,256]{1,0:T(8,128)(2,1)S(1)} %collective-permute-done.5.rest_5_.rest_6_), channel_id=1, source_target_pairs={{0,1},{1,0},{2,3},{3,2},{4,5},{5,4},{6,7},{7,6},{8,9},{9,8},{10,11... | collective-permute-start | bytes 417800 | tf_op jit(solution)/shard_map/ppermute | solution.py:198
  31.2 7.6 %collective-permute-start.7 = (bf16[128,256]{1,0:T(8,128)(2,1)S(1)}, bf16[128,256]{1,0:T(8,128)(2,1)S(1)}, u32[]{:S(2)}, u32[]{:S(2)}) collective-permute-start(bf16[128,256]{1,0:T(8,128)(2,1)S(1)} %get-tuple-element.49), channel_id=1, source_target_pairs={{0,24},{8,16},{16,8},{24,0},{1,25},{9,17},{17,9},{25,1},{2,26},{10... | collective-permute-start | bytes 196616 | tf_op jit(solution)/shard_map/ppermute | solution.py:198
  34.5 5.2 %collective-permute-start.8 = (bf16[128,256]{1,0:T(8,128)(2,1)S(1)}, bf16[128,256]{1,0:T(8,128)(2,1)S(1)}, u32[]{:S(2)}, u32[]{:S(2)}) collective-permute-start(bf16[128,256]{1,0:T(8,128)(2,1)S(1)} %get-tuple-element.50), channel_id=1, source_target_pairs={{0,6},{1,7},{2,4},{3,5},{4,2},{5,3},{6,0},{7,1},{8,14},{9,15},{10,... | collective-permute-start | bytes 196616 | tf_op jit(solution)/shard_map/ppermute | solution.py:198
  36.2 5.0 %collective-permute-start.9 = (bf16[128,256]{1,0:T(8,128)(2,1)S(1)}, bf16[128,256]{1,0:T(8,128)(2,1)S(1)}, u32[]{:S(2)}, u32[]{:S(2)}) collective-permute-start(bf16[128,256]{1,0:T(8,128)(2,1)S(1)} %get-tuple-element.51), channel_id=1, source_target_pairs={{0,7},{1,6},{2,5},{3,4},{4,3},{5,2},{6,1},{7,0},{8,15},{9,14},{10,... | collective-permute-start | bytes 196616 | tf_op jit(solution)/shard_map/ppermute | solution.py:198
  36.2 6.5 %collective-permute-start.10 = (bf16[128,256]{1,0:T(8,128)(2,1)S(1)}, bf16[128,256]{1,0:T(8,128)(2,1)S(1)}, u32[]{:S(2)}, u32[]{:S(2)}) collective-permute-start(bf16[128,256]{1,0:T(8,128)(2,1)S(1)} %get-tuple-element.52), channel_id=1, source_target_pairs={{0,4},{1,5},{2,6},{3,7},{4,0},{5,1},{6,2},{7,3},{8,12},{9,13},{10,... | collective-permute-start | bytes 196616 | tf_op jit(solution)/shard_map/ppermute | solution.py:198
  37.5 6.4 %collective-permute-start.11 = (bf16[128,256]{1,0:T(8,128)(2,1)S(1)}, bf16[128,256]{1,0:T(8,128)(2,1)S(1)}, u32[]{:S(2)}, u32[]{:S(2)}) collective-permute-start(bf16[128,256]{1,0:T(8,128)(2,1)S(1)} %get-tuple-element.53), channel_id=1, source_target_pairs={{0,5},{1,4},{2,7},{3,6},{4,1},{5,0},{6,3},{7,2},{8,13},{9,12},{10,... | collective-permute-start | bytes 196616 | tf_op jit(solution)/shard_map/ppermute | solution.py:198
  38.9 5.5 %collective-permute-start.12 = (bf16[128,256]{1,0:T(8,128)(2,1)S(1)}, bf16[128,256]{1,0:T(8,128)(2,1)S(1)}, u32[]{:S(2)}, u32[]{:S(2)}) collective-permute-start(bf16[128,256]{1,0:T(8,128)(2,1)S(1)} %get-tuple-element.54), channel_id=1, source_target_pairs={{0,16},{8,24},{16,0},{24,8},{1,17},{9,25},{17,1},{25,9},{2,18},{10... | collective-permute-start | bytes 196616 | tf_op jit(solution)/shard_map/ppermute | solution.py:198
  39.6 5.2 %collective-permute-start.13 = (bf16[128,256]{1,0:T(8,128)(2,1)S(1)}, bf16[128,256]{1,0:T(8,128)(2,1)S(1)}, u32[]{:S(2)}, u32[]{:S(2)}) collective-permute-start(bf16[128,256]{1,0:T(8,128)(2,1)S(1)} %get-tuple-element.55), channel_id=1, source_target_pairs={{0,8},{8,0},{16,24},{24,16},{1,9},{9,1},{17,25},{25,17},{2,10},{10... | collective-permute-start | bytes 196616 | tf_op jit(solution)/shard_map/ppermute | solution.py:198
  41.2 4.3 %collective-permute-start.14 = (bf16[128,256]{1,0:T(8,128)(2,1)S(1)}, bf16[128,256]{1,0:T(8,128)(2,1)S(1)}, u32[]{:S(2)}, u32[]{:S(2)}) collective-permute-start(bf16[128,256]{1,0:T(8,128)(2,1)S(1)} %get-tuple-element.56), channel_id=1, source_target_pairs={{0,2},{1,3},{2,0},{3,1},{4,6},{5,7},{6,4},{7,5},{8,10},{9,11},{10,... | collective-permute-start | bytes 196616 | tf_op jit(solution)/shard_map/ppermute | solution.py:198
  42.7 4.4 %collective-permute-start.15 = (bf16[128,256]{1,0:T(8,128)(2,1)S(1)}, bf16[128,256]{1,0:T(8,128)(2,1)S(1)}, u32[]{:S(2)}, u32[]{:S(2)}) collective-permute-start(bf16[128,256]{1,0:T(8,128)(2,1)S(1)} %get-tuple-element.57), channel_id=1, source_target_pairs={{0,3},{1,2},{2,1},{3,0},{4,7},{5,6},{6,5},{7,4},{8,11},{9,10},{10,... | collective-permute-start | bytes 196616 | tf_op jit(solution)/shard_map/ppermute | solution.py:198
  43.9 3.2 %collective-permute-start.16 = (bf16[128,256]{1,0:T(8,128)(2,1)S(1)}, bf16[128,256]{1,0:T(8,128)(2,1)S(1)}, u32[]{:S(2)}, u32[]{:S(2)}) collective-permute-start(bf16[128,256]{1,0:T(8,128)(2,1)S(1)} %get-tuple-element.58), channel_id=1, source_target_pairs={{0,1},{1,0},{2,3},{3,2},{4,5},{5,4},{6,7},{7,6},{8,9},{9,8},{10,11... | collective-permute-start | bytes 196616 | tf_op jit(solution)/shard_map/ppermute | solution.py:198

commit v5 on v3

v5 whole, which is shorter than its diff:
```python
import functools

import jax
import jax.numpy as jnp
from jax import lax
from jax.experimental import pallas as pl
from jax.experimental.pallas import tpu as pltpu
from jax.sharding import PartitionSpec as P

BF = jnp.bfloat16
F32 = jnp.float32
BOUNDARY = 2
EXTRA = 16
VMEM = pl.BlockSpec(memory_space=pltpu.VMEM)
HBM = pl.BlockSpec(memory_space=pltpu.HBM)
PARAMS = pltpu.CompilerParams(vmem_limit_bytes=24 * 1024 * 1024)


def dot(left, right):
    return jnp.dot(left, right, preferred_element_type=F32)


def dot_right_transposed(left, right):
    return lax.dot_general(left, right, (((1,), (1,)), ((), ())), preferred_element_type=F32)


def gelu_slope(v):
    scale = 0.7978845608028654
    t = jnp.tanh(scale * (v + 0.044715 * v * v * v))
    return 0.5 * (1.0 + t) + (0.5 * scale) * v * (1.0 - t * t) * (1.0 + 3.0 * 0.044715 * v * v)


def edge_kernel(recv_sub, recv_cluster, features, edge, first, second, sub_row, cluster_row, sems):
    size = first.shape[0]
    copies = [
        pltpu.make_async_copy(features.at[0:size, :], first, sems.at[0]),
        pltpu.make_async_copy(features.at[size : 2 * size, :], second.at[0:size, :], sems.at[1]),
        pltpu.make_async_copy(features.at[0 : 2 * size, :], edge.at[0 : 2 * size, :], sems.at[2]),
        pltpu.make_async_copy(recv_sub, sub_row, sems.at[3]),
        pltpu.make_async_copy(recv_cluster, cluster_row, sems.at[4]),
    ]
    for copy in copies:
        copy.start()
    for copy in copies:
        copy.wait()
    sub_count, cluster_count = sub_row.shape[1], cluster_row.shape[1]
    pad = jnp.zeros((1, edge.shape[1] - sub_count - cluster_count), F32)
    row = jnp.concatenate([sub_row[...].astype(F32), cluster_row[...].astype(F32), pad], axis=1)
    rows = jnp.broadcast_to(row, (EXTRA, edge.shape[1])).astype(BF)
    edge[2 * size :, :] = rows
    second[size:, :] = rows


def prepare_kernel(
    own, sub_count, cluster_count,
    tile_dst_hbm, tile_src_hbm, recv_sub_hbm, recv_cluster_hbm, tile_weight_hbm,
    features_hbm, w_self_hbm, w_neigh_hbm, grad_out_hbm, bias_hbm,
    dense, dense_t, inverse, choice, features, w_self, w_neigh, grad_out, bias,
    tile_dst, tile_src, recv_sub, recv_cluster, tile_weight, sems,
):
    size = tile_weight.shape[1]
    pairs = (
        (tile_dst_hbm, tile_dst), (tile_src_hbm, tile_src), (recv_sub_hbm, recv_sub),
        (recv_cluster_hbm, recv_cluster), (tile_weight_hbm, tile_weight),
        (features_hbm, features), (w_self_hbm, w_self), (w_neigh_hbm, w_neigh),
        (grad_out_hbm, grad_out), (bias_hbm, bias),
    )
    copies = [pltpu.make_async_copy(a, b, sems.at[i]) for i, (a, b) in enumerate(pairs)]
    for copy in copies:
        copy.start()
    sub_id = lax.axis_index("sub")
    cluster_id = lax.axis_index("cluster")
    dense[...] = jnp.zeros_like(dense)
    dense_t[...] = jnp.zeros_like(dense_t)
    for copy in copies[:5]:
        copy.wait()

    def place(t, carry):
        src = tile_src[t]
        from_sub = own + ((src - own) ^ sub_id)
        from_cluster = own + sub_count + ((src - own - sub_count) ^ cluster_id)
        slot = jnp.where(src < own, src, jnp.where(src < own + sub_count, from_sub, from_cluster))
        dst = pl.ds(pl.multiple_of(tile_dst[t] * size, size), size)
        col = pl.ds(pl.multiple_of(slot * size, size), size)
        tile = tile_weight[t]
        dense[dst, col] = dense[dst, col] + tile
        dense_t[col, dst] = dense_t[col, dst] + tile.T
        return carry

    lax.fori_loop(0, tile_weight.shape[0], place, 0, unroll=4)
    for d in range(sub_count):
        index = recv_sub[0, sub_id ^ d].astype(F32)
        choice[d : d + 1, :] = jnp.full((1, choice.shape[1]), index, F32)
    for d in range(cluster_count):
        index = recv_cluster[0, cluster_id ^ d].astype(F32)
        choice[sub_count + d : sub_count + d + 1, :] = jnp.full((1, choice.shape[1]), index, F32)
    slots = own + sub_count + cluster_count
    total = dense[:, 0:size].astype(F32)
    for slot in range(1, slots):
        total = total + dense[:, slot * size : (slot + 1) * size].astype(F32)
    degree = jnp.sum(total, axis=1, keepdims=True)
    inverse[...] = jnp.broadcast_to(1.0 / (degree + 1.0), inverse.shape)
    for copy in copies[5:]:
        copy.wait()


def halo_sum(choice, dense, own, shape, refs, halo):
    size = dense.shape[0] // own
    columns, at = [], 0
    for i, (slot, count) in enumerate(shape.items()):
        if count == 1:
            first, second = refs[at][0:size, :], refs[at][size : 2 * size, :]
        else:
            first, second = refs[at][0:size, :], refs[at + 1][0:size, :]
        at += count
        halo[i * size : (i + 1) * size, :] = jnp.where(
            choice[slot : slot + 1, :] > 0.5, second.astype(F32), first.astype(F32)
        ).astype(BF)
        columns.append(dense[:, (own + slot) * size : (own + slot + 1) * size])
    return dot(jnp.concatenate(columns, axis=1), halo[...])


def first_kernel(own, shape, choice, dense, features, w_self, bias, *rest):
    refs, (total, own_pre, halo) = rest[:-3], rest[-3:]
    size = dense.shape[0] // own
    total[...] = dot(dense[:, 0 : own * size], features[...]) + halo_sum(
        choice, dense, own, shape, refs, halo
    )
    own_pre[...] = dot(features[...], w_self[...]) + bias[...].reshape(1, -1)


def near_kernel(own, shape, choice, dense, before, *rest):
    refs, (total, halo) = rest[:-2], rest[-2:]
    total[...] = before[...] + halo_sum(choice, dense, own, shape, refs, halo)


def middle_kernel(
    own, sub_count, cluster_count, shape,
    choice, grad_out, w_neigh, dense, dense_t, before, own_pre, inverse,
    *rest,
):
    received = sum(shape.values())
    refs, rest = rest[:received], rest[received:]
    pairs, rest = rest[: sub_count // 2 - 1], rest[sub_count // 2 - 1 :]
    along, (sibling, kept, spread, grad_pre, halo) = rest[:-5], rest[-5:]
    size = dense.shape[0] // own
    aggregate = before[...] + halo_sum(choice, dense, own, shape, refs, halo)
    inv = jnp.concatenate([inverse[...]] * (grad_out.shape[1] // size), axis=1)
    mean = (aggregate * inv).astype(BF)
    pre = own_pre[...] + dot(mean, w_neigh[...])
    grad = (grad_out[...].astype(F32) * gelu_slope(pre)).astype(BF)
    grad_pre[...] = grad
    spread[...] = (dot_right_transposed(grad, w_neigh[...]) * inv).astype(BF)

    def partial(slot, count=1):
        rows = slice((own + slot) * size, (own + slot + count) * size)
        return dot(dense_t[rows, :], spread[...]).astype(BF)

    for i, target in enumerate(pairs):
        target[...] = partial(2 * (i + 1), 2)
    for i, target in enumerate(along):
        target[...] = partial(sub_count + 1 + i)
    sibling[...] = partial(1)
    kept[0] = partial(0)
    kept[1] = partial(sub_count)


def split(total, value, second, size):
    zero = jnp.zeros_like(value)
    total[0:size, :] = total[0:size, :] + jnp.where(second, zero, value)
    total[size : 2 * size, :] = total[size : 2 * size, :] + jnp.where(second, value, zero)


def own_kernel(own, sub_count, order, parts, *rest):
    back, rest = rest[: len(parts)], rest[len(parts) :]
    received, rest = rest[: len(order)], rest[len(order) :]
    choice, w_self, dense_t, kept, spread, grad_pre, total, owner = rest
    size = kept.shape[1]
    width = total.shape[1]
    total[...] = dot_right_transposed(grad_pre[...], w_self[...]) + dot(
        dense_t[0 : own * size, :], spread[...]
    )
    for i, slot in enumerate((0, sub_count)):
        split(total, kept[i].astype(F32), choice[slot : slot + 1, :] > 0.5, size)
    lanes = lax.broadcasted_iota(jnp.int32, (1, width), 1)
    for message, slot in zip(received, order):
        lane = lax.axis_index("sub")
        if slot > sub_count:
            lane = sub_count + lax.axis_index("cluster")
        last = message.shape[0] - EXTRA
        row = message[last : last + EXTRA, :].astype(F32)[0:1, :]
        index = jnp.sum(jnp.where(lanes == lane, row, 0.0), axis=1, keepdims=True)
        owner[slot : slot + 1, :] = jnp.broadcast_to(index, (1, width))
    for message, (slot, row) in zip(back, parts):
        value = message[row : row + size, :].astype(F32)
        split(total, value, owner[slot : slot + 1, :] > 0.5, size)


def final_kernel(own, parts, owner, total, *rest):
    received, out = rest[:-1], rest[-1]
    size = total.shape[0] // own
    first = total[0:size, :]
    second = total[size : 2 * size, :]
    for message, (slot, row) in zip(received, parts):
        value = message[row : row + size, :].astype(F32)
        to_second = owner[slot : slot + 1, :] > 0.5
        first = first + jnp.where(to_second, 0.0, value)
        second = second + jnp.where(to_second, value, 0.0)
    out[0:size, :] = first.astype(BF)
    out[size : 2 * size, :] = second.astype(BF)
    out[2 * size :, :] = total[2 * size :, :].astype(BF)


def swap(value, axis, count, d):
    return lax.ppermute(value, axis, [(i, i ^ d) for i in range(count)])


def after(value, other):
    return lax.optimization_barrier((value, other))[0]


def in_hbm(value):
    return pltpu.with_memory_space_constraint(value, pltpu.HBM)


def cost(flops, moved):
    return pl.CostEstimate(flops=flops, bytes_accessed=moved, transcendentals=0)


def shards(
    features, grad_out, w_self, w_neigh, bias, tile_dst, tile_src, tile_weight, recv_sub, recv_cluster
):
    sub_count = lax.axis_size("sub")
    cluster_count = lax.axis_size("cluster")
    peers = sub_count + cluster_count - 2
    size = tile_weight.shape[1]
    rows, width = features.shape
    own = rows // size
    slots = own + sub_count + cluster_count
    counts = (own, sub_count, cluster_count)

    wide = jax.ShapeDtypeStruct((rows, width), F32)
    narrow = jax.ShapeDtypeStruct((rows, width), BF)
    square = jax.ShapeDtypeStruct((width, width), BF)
    block = jax.ShapeDtypeStruct((size, width), BF)
    marks = jax.ShapeDtypeStruct((sub_count + cluster_count, width), F32)

    edge, *halves = pl.pallas_call(
        edge_kernel,
        out_shape=[
            jax.ShapeDtypeStruct((BOUNDARY * size + EXTRA, width), BF),
            block,
            jax.ShapeDtypeStruct((size + EXTRA, width), BF),
        ],
        in_specs=[HBM] * 3,
        out_specs=[VMEM] * 3,
        scratch_shapes=[
            pltpu.VMEM(recv_sub.shape, jnp.int32),
            pltpu.VMEM(recv_cluster.shape, jnp.int32),
            pltpu.SemaphoreType.DMA((5,)),
        ],
        compiler_params=PARAMS,
        cost_estimate=cost(1024, 256 * 1024),
        name="edge",
    )(in_hbm(recv_sub), in_hbm(recv_cluster), in_hbm(features))

    def along(value, d):
        return swap(value, "cluster", cluster_count, d)

    def across(value, d):
        return swap(value, "sub", sub_count, d)

    direct = [d for d in range(2, cluster_count) if not d & (d - 1)]
    relayed = [d for d in range(2, cluster_count) if d & (d - 1)]
    got = {sub_count + d: tuple(along(half, d) for half in halves) for d in direct}
    got[1] = (across(edge, 1),)
    early = (got[1][0], *(got[sub_count + d][0] for d in direct[-1:]))
    start = after(tile_dst, early)

    dense, dense_t, inverse, choice, features, w_self, w_neigh, grad_out, bias = pl.pallas_call(
        functools.partial(prepare_kernel, *counts),
        out_shape=[
            jax.ShapeDtypeStruct((rows, slots * size), BF),
            jax.ShapeDtypeStruct((slots * size, rows), BF),
            jax.ShapeDtypeStruct((rows, size), F32),
            marks,
            narrow,
            square,
            square,
            narrow,
            jax.ShapeDtypeStruct(bias.shape, F32),
        ],
        in_specs=[HBM] * 10,
        out_specs=[VMEM] * 9,
        scratch_shapes=[
            pltpu.SMEM(tile_dst.shape, jnp.int32),
            pltpu.SMEM(tile_src.shape, jnp.int32),
            pltpu.SMEM(recv_sub.shape, jnp.int32),
            pltpu.SMEM(recv_cluster.shape, jnp.int32),
            pltpu.VMEM(tile_weight.shape, BF),
            pltpu.SemaphoreType.DMA((10,)),
        ],
        compiler_params=PARAMS,
        cost_estimate=cost(10**6, 6 * 1024 * 1024),
        name="prepare",
    )(
        *map(in_hbm, (start, tile_src, recv_sub, recv_cluster, tile_weight)),
        *map(in_hbm, (features, w_self, w_neigh, grad_out, bias)),
    )

    def sum_call(kernel, out_shape, name, slots, *operands):
        shape = {slot: len(got[slot]) for slot in slots}
        refs = [part for slot in slots for part in got[slot]]
        return pl.pallas_call(
            functools.partial(kernel, own, shape),
            out_shape=out_shape,
            in_specs=[VMEM] * (len(operands) + len(refs)),
            out_specs=jax.tree.map(lambda _: VMEM, out_shape),
            scratch_shapes=[pltpu.VMEM((len(shape) * size, width), BF)],
            compiler_params=PARAMS,
            cost_estimate=cost(10**10, 3 * 1024 * 1024),
            name=name,
        )(*operands, *refs)

    got[0] = got[sub_count] = (edge,)
    got[sub_count + 1] = (along(edge, 1),)
    first_sum, own_pre = sum_call(
        first_kernel, [wide, wide], "first", [0, sub_count, *(sub_count + d for d in direct), sub_count + 1],
        choice, dense, features, w_self, bias,
    )
    even = list(range(2, sub_count, 2))
    for d in relayed:
        low = d & -d
        one, two = got[sub_count + d - low]
        got[sub_count + d] = (along(one, low), along(two, low))
    for d in even:
        got[d] = (across(edge, d),)
        got[d + 1] = (across(after(got[d][0], own_pre), 1),)
    near_sum = sum_call(near_kernel, wide, "near", [*even, 1], choice, dense, first_sum)

    late = [*(sub_count + d for d in relayed), *(d + 1 for d in even)]
    shape = {slot: len(got[slot]) for slot in late}
    refs = [part for slot in late for part in got[slot]]
    outs = pl.pallas_call(
        functools.partial(middle_kernel, *counts, shape),
        out_shape=[jax.ShapeDtypeStruct((2 * size, width), BF)] * len(even)
        + [block] * cluster_count
        + [jax.ShapeDtypeStruct((2, size, width), BF), narrow, narrow],
        in_specs=[VMEM] * (8 + len(refs)),
        out_specs=[VMEM] * (len(even) + cluster_count + 3),
        scratch_shapes=[pltpu.VMEM((len(shape) * size, width), BF)],
        compiler_params=PARAMS,
        cost_estimate=cost(2 * rows * slots * size * width, 6 * 1024 * 1024),
        name="middle",
    )(choice, grad_out, w_neigh, dense, dense_t, near_sum, own_pre, inverse, *refs)
    *sent, sibling, kept, spread, grad_pre = outs

    back = [(along(sent[len(even) + d - 1], d), sub_count + d, 0) for d in range(1, cluster_count)]
    direct_back, swapped_back = [], []
    for d, value in zip(even, sent):
        value = across(value, d)
        direct_back.append((value, d, 0))
        swapped_back.append((across(value, 1), d + 1, size))
    sibling_back = [(across(sibling, 1), 1, 0)]
    early_back, back = back[::-1], [*direct_back, *swapped_back, *sibling_back]

    order = [*even, *(sub_count + d for d in direct), *(d + 1 for d in even), 1, sub_count + 1, *(sub_count + d for d in relayed)]
    total, owner = pl.pallas_call(
        functools.partial(
            own_kernel, own, sub_count, order, [(slot, row) for _, slot, row in early_back]
        ),
        out_shape=[wide, marks],
        in_specs=[VMEM] * (6 + peers + len(early_back)),
        out_specs=[VMEM] * 2,
        compiler_params=PARAMS,
        cost_estimate=cost(10**10, 2 * 1024 * 1024),
        name="own",
    )(
        *[value for value, _, _ in early_back],
        *[got[slot][-1] for slot in order],
        choice, w_self, dense_t, kept, spread, grad_pre,
    )

    return pl.pallas_call(
        functools.partial(final_kernel, own, [(slot, row) for _, slot, row in back]),
        out_shape=narrow,
        in_specs=[VMEM] * (2 + len(back)),
        out_specs=VMEM,
        compiler_params=PARAMS,
        cost_estimate=cost(rows * width * 4, 2 * 1024 * 1024),
        name="final",
    )(owner, total, *[value for value, _, _ in back])


def solution(mesh):
    placed = (
        P(("cluster", "sub"), None),
        P(("cluster", "sub"), None),
        P(),
        P(),
        P(),
        P(("cluster", "sub")),
        P(("cluster", "sub")),
        P(("cluster", "sub"), None, None),
        P(("cluster", "sub"), None),
        P(("cluster", "sub"), None),
    )
    return jax.shard_map(
        shards, mesh=mesh, in_specs=placed, out_specs=P(("cluster", "sub"), None), check_vma=False
    )
```

time: 39.3 us -> 40.5 us (1.031)
  waiting for transfers between devices: 9.31 us -> 10.5 us
    ppermute x20 -> x22, waiting for transfers between devices: 9.31 us -> 10.5 us  [swap(): return lax.ppermute(value, axis, [(i, i ^ d) for i in range(count)])]
    pallas_call x4 -> x6, Pallas kernels: 4.2 us -> 4.37 us  [the longest x1 1.26 us: shards(): pl.pallas_call(functools.partial(middle_kernel, *counts, shape), out_shap...]
    ppermute x20 -> x22, starting transfers between devices: 23.1 us -> 23.2 us  [swap(): return lax.ppermute(value, axis, [(i, i ^ d) for i in range(count)])]
  transfers between devices with their start and end apart: 20 -> 22, of which waited for: 7 -> 7; matrix products, arithmetic and copies ran while one was open for 0% -> 0% of each run, Pallas kernels for 7% -> 8%
where the time goes in v5:
time: 40.5 us; the launch traced here: 40.3 us
  starting transfers between devices  23.2 us (57%)
  waiting for transfers between devices  10.5 us (26%)
  Pallas kernels  6.48 us (16%)
    ppermute x22, starting transfers between devices, swap(): return lax.ppermute(value, axis, [(i, i ^ d) for i in range(count)])  23.2 us
    ppermute x22, waiting for transfers between devices, swap(): return lax.ppermute(value, axis, [(i, i ^ d) for i in range(count)])  10.5 us
    pallas_call x1, Pallas kernels, shards(): pl.pallas_call(functools.partial(prepare_kernel, *counts), out_shape=[jax...  2.11 us
    pallas_call x1, Pallas kernels, shards(): pl.pallas_call(functools.partial(middle_kernel, *counts, shape), out_shap...  1.26 us
    pallas_call x1, Pallas kernels, shards(): pl.pallas_call(edge_kernel, out_shape=[jax.ShapeDtypeStruct((BOUNDARY * s...  1.11 us
    pallas_call x1, Pallas kernels, shards(): pl.pallas_call(functools.partial(final_kernel, own, [(slot, row) for _, s...  0.87 us
  transfers between devices with their start and end apart: 22, of which 7 were waited for; matrix products, arithmetic and copies ran while one was open for 0% of the time, Pallas kernels for 8%

profile of v5, /device:TPU:0, one launch (start us, length us, event | category | flops | bytes accessed | tf_op | source)
XLA Modules:
  0.0 40.3 jit_solution(7941912378062925339)
XLA Ops:
  0.0 1.1 %edge.1 = (bf16[272,256]{1,0:T(8,128)(2,1)S(1)}, bf16[128,256]{1,0:T(8,128)(2,1)S(1)}, bf16[144,256]{1,0:T(8,128)(2,1)S(1)}) custom-call(s32[1,8]{1,0:T(1,128)} %recv_sub_hbm.1, s32[1,4]{1,0:T(1,128)} %recv_cluster_hbm.1, bf16[384,256]{1,0:T(8,128)(2,1)} %features_hbm.1), custom_call_target="tpu_custom_call" | custom-call | flops 1024 | bytes 262144 | tf_op jit(solution)/shard_map/edge/pallas_call | solution.py:248
  1.1 0.5 %collective-permute-start = (bf16[272,256]{1,0:T(8,128)(2,1)S(1)}, bf16[272,256]{1,0:T(8,128)(2,1)S(1)}, u32[]{:S(2)}, u32[]{:S(2)}) collective-permute-start(bf16[272,256]{1,0:T(8,128)(2,1)S(1)} %get-tuple-element.35.rest_0_.rest_1_), channel_id=1, source_target_pairs={{0,1},{1,0},{2,3},{3,2},{4,5},{5,4},{6,7},{7,6},{8,9},{9,8},{10,11... | collective-permute-start | bytes 417800 | tf_op jit(solution)/shard_map/ppermute | solution.py:215
  1.6 2.6 %collective-permute-start.3 = (bf16[272,256]{1,0:T(8,128)(2,1)S(1)}, bf16[272,256]{1,0:T(8,128)(2,1)S(1)}, u32[]{:S(2)}, u32[]{:S(2)}) collective-permute-start(bf16[272,256]{1,0:T(8,128)(2,1)S(1)} %get-tuple-element.35.rest_0_.rest_1_), channel_id=1, source_target_pairs={{0,8},{8,0},{16,24},{24,16},{1,9},{9,1},{17,25},{25,17},{2,10},{10... | collective-permute-start | bytes 417800 | tf_op jit(solution)/shard_map/ppermute | solution.py:215
  4.3 2.6 %collective-permute-start.2 = (bf16[144,256]{1,0:T(8,128)(2,1)S(1)}, bf16[144,256]{1,0:T(8,128)(2,1)S(1)}, u32[]{:S(2)}, u32[]{:S(2)}) collective-permute-start(bf16[144,256]{1,0:T(8,128)(2,1)S(1)} %get-tuple-element.46), channel_id=1, source_target_pairs={{0,16},{8,24},{16,0},{24,8},{1,17},{9,25},{17,1},{25,9},{2,18},{10... | collective-permute-start | bytes 221192 | tf_op jit(solution)/shard_map/ppermute | solution.py:215
  6.9 0.3 collective-permute-start.1
  7.2 2.4 %collective-permute-start.6 = (bf16[272,256]{1,0:T(8,128)(2,1)S(1)}, bf16[272,256]{1,0:T(8,128)(2,1)S(1)}, u32[]{:S(2)}, u32[]{:S(2)}) collective-permute-start(bf16[272,256]{1,0:T(8,128)(2,1)S(1)} %get-tuple-element.35.rest_0_.rest_1_), channel_id=1, source_target_pairs={{0,6},{1,7},{2,4},{3,5},{4,2},{5,3},{6,0},{7,1},{8,14},{9,15},{10,... | collective-permute-start | bytes 417800 | tf_op jit(solution)/shard_map/ppermute | solution.py:215
  9.7 5.0 %collective-permute-done.1.rest_2_ = bf16[128,256]{1,0:T(8,128)(2,1)S(1)} collective-permute-done((bf16[128,256]{1,0:T(8,128)(2,1)S(1)}, bf16[128,256]{1,0:T(8,128)(2,1)S(1)}, u32[]{:S(2)}, u32[]{:S(2)}) %collective-permute-start.1) | collective-permute-done | bytes 65568 | tf_op jit(solution)/shard_map/ppermute | solution.py:215
  14.6 1.5 %collective-permute-start.5 = (bf16[272,256]{1,0:T(8,128)(2,1)S(1)}, bf16[272,256]{1,0:T(8,128)(2,1)S(1)}, u32[]{:S(2)}, u32[]{:S(2)}) collective-permute-start(bf16[272,256]{1,0:T(8,128)(2,1)S(1)} %get-tuple-element.35.rest_0_.rest_1_), channel_id=1, source_target_pairs={{0,4},{1,5},{2,6},{3,7},{4,0},{5,1},{6,2},{7,3},{8,12},{9,13},{10,... | collective-permute-start | bytes 417800 | tf_op jit(solution)/shard_map/ppermute | solution.py:215
  16.2 0.0 collective-permute-done.rest_3_.rest_10_
  16.2 1.5 %collective-permute-start.4 = (bf16[272,256]{1,0:T(8,128)(2,1)S(1)}, bf16[272,256]{1,0:T(8,128)(2,1)S(1)}, u32[]{:S(2)}, u32[]{:S(2)}) collective-permute-start(bf16[272,256]{1,0:T(8,128)(2,1)S(1)} %get-tuple-element.35.rest_0_.rest_1_), channel_id=1, source_target_pairs={{0,2},{1,3},{2,0},{3,1},{4,6},{5,7},{6,4},{7,5},{8,10},{9,11},{10,... | collective-permute-start | bytes 417800 | tf_op jit(solution)/shard_map/ppermute | solution.py:215
  17.7 2.1 %prepare.1 = (bf16[384,1920]{1,0:T(8,128)(2,1)S(1)}, bf16[1920,384]{1,0:T(8,128)(2,1)S(1)}, f32[384,128]{1,0:T(8,128)S(1)}, f32[12,256]{1,0:T(8,128)S(1)}, bf16[...) custom-call(s32[24]{0:T(128)} %tile_dst_hbm, ...), custom_call_target="tpu_custom_call" | custom-call | flops 1000000 | bytes 6291456 | tf_op jit(solution)/shard_map/prepare/pallas_call | solution.py:280
  19.8 0.0 collective-permute-done.2.rest_3_.rest_6_
  19.8 0.1 collective-permute-start.7
  19.9 0.0 collective-permute-done.3.rest_4_.rest_11_
  19.9 2.0 %collective-permute-start.8 = (bf16[144,256]{1,0:T(8,128)(2,1)S(1)}, bf16[144,256]{1,0:T(8,128)(2,1)S(1)}, u32[]{:S(2)}, u32[]{:S(2)}) collective-permute-start(bf16[144,256]{1,0:T(8,128)(2,1)S(1)} %collective-permute-done.2.rest_3_.rest_6_), channel_id=1, source_target_pairs={{0,8},{8,0},{16,24},{24,16},{1,9},{9,1},{17,25},{25,17},{2,10},{10... | collective-permute-start | bytes 221192 | tf_op jit(solution)/shard_map/ppermute | solution.py:215
  21.9 0.5 %first.1 = (f32[384,256]{1,0:T(8,128)S(1)}, f32[384,256]{1,0:T(8,128)S(1)}) custom-call(f32[12,256]{1,0:T(8,128)S(1)} %get-tuple-element.38.choice.rest_13_, bf16[384,1920]{1,0:T(8,128)(2,1)S(1)} %get-tuple-element.41.dense, bf16[384,256]{1,0:T(8,128)(2,1)S(1)} %get-tuple-element.43.features, bf16[256,256]{1,0:T(8,128)(2,1)S(1)} %get-tuple-element.44.w_self.rest_14_, ...), custom_call_target="tpu_custom_call" | custom-call | flops 10000000000 | bytes 3145728 | tf_op jit(solution)/shard_map/first/pallas_call | solution.py:314
  22.3 0.0 collective-permute-done.6.rest_2_.rest_5_
  22.4 0.0 collective-permute-done.5.rest_1_.rest_4_
  22.4 0.0 collective-permute-done.4.rest_0_.rest_3_
  22.4 0.1 collective-permute-start.9
  22.5 0.5 %collective-permute-start.10 = (bf16[272,256]{1,0:T(8,128)(2,1)S(1)}, bf16[272,256]{1,0:T(8,128)(2,1)S(1)}, u32[]{:S(2)}, u32[]{:S(2)}) collective-permute-start(bf16[272,256]{1,0:T(8,128)(2,1)S(1)} %collective-permute-done.5.rest_1_.rest_4_), channel_id=1, source_target_pairs={{0,1},{1,0},{2,3},{3,2},{4,5},{5,4},{6,7},{7,6},{8,9},{9,8},{10,11... | collective-permute-start | bytes 417800 | tf_op jit(solution)/shard_map/ppermute | solution.py:215
  23.0 0.1 collective-permute-start.11
  23.0 0.3 near.1.before
  23.3 0.8 %collective-permute-done.7.rest_0_ = bf16[128,256]{1,0:T(8,128)(2,1)S(1)} collective-permute-done((bf16[128,256]{1,0:T(8,128)(2,1)S(1)}, bf16[128,256]{1,0:T(8,128)(2,1)S(1)}, u32[]{:S(2)}, u32[]{:S(2)}) %collective-permute-start.7) | collective-permute-done | bytes 65568 | tf_op jit(solution)/shard_map/ppermute | solution.py:215
  24.1 0.8 %collective-permute-done.8.rest_1_.rest_12_ = bf16[144,256]{1,0:T(8,128)(2,1)S(1)} collective-permute-done((bf16[144,256]{1,0:T(8,128)(2,1)S(1)}, bf16[144,256]{1,0:T(8,128)(2,1)S(1)}, u32[]{:S(2)}, u32[]{:S(2)}) %collective-permute-start.8) | collective-permute-done | bytes 73760 | tf_op jit(solution)/shard_map/ppermute | solution.py:215
  24.9 0.0 collective-permute-done.9.rest_2_.rest_7_
  24.9 0.0 collective-permute-done.10.rest_3_.rest_8_
  24.9 0.0 collective-permute-done.11.rest_4_.rest_9_
  24.9 1.3 %middle.1 = (bf16[256,256]{1,0:T(8,128)(2,1)S(1)}, bf16[256,256]{1,0:T(8,128)(2,1)S(1)}, bf16[256,256]{1,0:T(8,128)(2,1)S(1)}, bf16[128,256]{1,0:T(8,128)(2,1)S(...) custom-call(f32[12,256]{1,0:T(8,128)S(1)} %get-tuple-element.38.choi, ...), custom_call_target="tpu_custom_call" | custom-call | flops 377487360 | bytes 6291456 | tf_op jit(solution)/shard_map/middle/pallas_call | solution.py:344
  26.2 1.8 %collective-permute-start.12 = (bf16[128,256]{1,0:T(8,128)(2,1)S(1)}, bf16[128,256]{1,0:T(8,128)(2,1)S(1)}, u32[]{:S(2)}, u32[]{:S(2)}) collective-permute-start(bf16[128,256]{1,0:T(8,128)(2,1)S(1)} %get-tuple-element.53), channel_id=1, source_target_pairs={{0,24},{8,16},{16,8},{24,0},{1,25},{9,17},{17,9},{25,1},{2,26},{10... | collective-permute-start | bytes 196616 | tf_op jit(solution)/shard_map/ppermute | solution.py:215
  28.0 0.5 %collective-permute-start.15 = (bf16[256,256]{1,0:T(8,128)(2,1)S(1)}, bf16[256,256]{1,0:T(8,128)(2,1)S(1)}, u32[]{:S(2)}, u32[]{:S(2)}) collective-permute-start(bf16[256,256]{1,0:T(8,128)(2,1)S(1)} %get-tuple-element.61), channel_id=1, source_target_pairs={{0,2},{1,3},{2,0},{3,1},{4,6},{5,7},{6,4},{7,5},{8,10},{9,11},{10,... | collective-permute-start | bytes 393224 | tf_op jit(solution)/shard_map/ppermute | solution.py:215
  28.6 0.5 %collective-permute-start.16 = (bf16[256,256]{1,0:T(8,128)(2,1)S(1)}, bf16[256,256]{1,0:T(8,128)(2,1)S(1)}, u32[]{:S(2)}, u32[]{:S(2)}) collective-permute-start(bf16[256,256]{1,0:T(8,128)(2,1)S(1)} %get-tuple-element.62), channel_id=1, source_target_pairs={{0,4},{1,5},{2,6},{3,7},{4,0},{5,1},{6,2},{7,3},{8,12},{9,13},{10,... | collective-permute-start | bytes 393224 | tf_op jit(solution)/shard_map/ppermute | solution.py:215
  29.1 2.4 %collective-permute-start.17 = (bf16[256,256]{1,0:T(8,128)(2,1)S(1)}, bf16[256,256]{1,0:T(8,128)(2,1)S(1)}, u32[]{:S(2)}, u32[]{:S(2)}) collective-permute-start(bf16[256,256]{1,0:T(8,128)(2,1)S(1)} %get-tuple-element.63), channel_id=1, source_target_pairs={{0,6},{1,7},{2,4},{3,5},{4,2},{5,3},{6,0},{7,1},{8,14},{9,15},{10,... | collective-permute-start | bytes 393224 | tf_op jit(solution)/shard_map/ppermute | solution.py:215
  31.5 1.0 %collective-permute-start.13 = (bf16[128,256]{1,0:T(8,128)(2,1)S(1)}, bf16[128,256]{1,0:T(8,128)(2,1)S(1)}, u32[]{:S(2)}, u32[]{:S(2)}) collective-permute-start(bf16[128,256]{1,0:T(8,128)(2,1)S(1)} %get-tuple-element.54), channel_id=1, source_target_pairs={{0,16},{8,24},{16,0},{24,8},{1,17},{9,25},{17,1},{25,9},{2,18},{10... | collective-permute-start | bytes 196616 | tf_op jit(solution)/shard_map/ppermute | solution.py:215
  32.5 0.0 collective-permute-done.12.rest_0_
  32.5 1.6 %collective-permute-start.14 = (bf16[128,256]{1,0:T(8,128)(2,1)S(1)}, bf16[128,256]{1,0:T(8,128)(2,1)S(1)}, u32[]{:S(2)}, u32[]{:S(2)}) collective-permute-start(bf16[128,256]{1,0:T(8,128)(2,1)S(1)} %get-tuple-element.55), channel_id=1, source_target_pairs={{0,8},{8,0},{16,24},{24,16},{1,9},{9,1},{17,25},{25,17},{2,10},{10... | collective-permute-start | bytes 196616 | tf_op jit(solution)/shard_map/ppermute | solution.py:215
  34.1 3.2 %collective-permute-done.13.rest_1_ = bf16[128,256]{1,0:T(8,128)(2,1)S(1)} collective-permute-done((bf16[128,256]{1,0:T(8,128)(2,1)S(1)}, bf16[128,256]{1,0:T(8,128)(2,1)S(1)}, u32[]{:S(2)}, u32[]{:S(2)}) %collective-permute-start.13) | collective-permute-done | bytes 65568 | tf_op jit(solution)/shard_map/ppermute | solution.py:215
  37.4 0.0 collective-permute-start.21
  37.4 0.0 collective-permute-done.15.rest_0_
  37.4 0.5 %collective-permute-start.18 = (bf16[256,256]{1,0:T(8,128)(2,1)S(1)}, bf16[256,256]{1,0:T(8,128)(2,1)S(1)}, u32[]{:S(2)}, u32[]{:S(2)}) collective-permute-start(bf16[256,256]{1,0:T(8,128)(2,1)S(1)} %collective-permute-done.15.rest_0_), channel_id=1, source_target_pairs={{0,1},{1,0},{2,3},{3,2},{4,5},{5,4},{6,7},{7,6},{8,9},{9,8},{10,11... | collective-permute-start | bytes 393224 | tf_op jit(solution)/shard_map/ppermute | solution.py:215
  37.9 0.0 collective-permute-done.16.rest_1_
  37.9 0.1 collective-permute-start.19
  38.0 0.0 collective-permute-done.17.rest_2_
  38.0 0.4 %collective-permute-start.20 = (bf16[256,256]{1,0:T(8,128)(2,1)S(1)}, bf16[256,256]{1,0:T(8,128)(2,1)S(1)}, u32[]{:S(2)}, u32[]{:S(2)}) collective-permute-start(bf16[256,256]{1,0:T(8,128)(2,1)S(1)} %collective-permute-done.17.rest_2_), channel_id=1, source_target_pairs={{0,1},{1,0},{2,3},{3,2},{4,5},{5,4},{6,7},{7,6},{8,9},{9,8},{10,11... | collective-permute-start | bytes 393224 | tf_op jit(solution)/shard_map/ppermute | solution.py:215
  38.4 0.0 collective-permute-done.14.rest_2_
  38.4 0.4 own.1
  38.8 0.0 collective-permute-done.21.rest_6_
  38.8 0.1 collective-permute-done.18.rest_3_
  38.9 0.4 collective-permute-done.19.rest_4_
  39.2 0.2 collective-permute-done.20.rest_5_
  39.4 0.9 %final.1 = bf16[384,256]{1,0:T(8,128)(2,1)} custom-call(f32[12,256]{1,0:T(8,128)S(1)} %get-tuple-element.59.owner, f32[384,256]{1,0:T(8,128)S(1)} %get-tuple-element.60.total, bf16[256,256]{1,0:T(8,128)(2,1)S(1)} %collective-permute-done.15.rest_0_, bf16[256,256]{1,0:T(8,128)(2,1)S(1)} %collective-permute-done.16.rest_1_, ...), custom_call_target="tpu_custom_call" | custom-call | flops 393216 | bytes 2097152 | tf_op jit(solution)/shard_map/final/pallas_call | solution.py:384
Async XLA Ops:
  1.1 15.0 %collective-permute-start = (bf16[272,256]{1,0:T(8,128)(2,1)S(1)}, bf16[272,256]{1,0:T(8,128)(2,1)S(1)}, u32[]{:S(2)}, u32[]{:S(2)}) collective-permute-start(bf16[272,256]{1,0:T(8,128)(2,1)S(1)} %get-tuple-element.35.rest_0_.rest_1_), channel_id=1, source_target_pairs={{0,1},{1,0},{2,3},{3,2},{4,5},{5,4},{6,7},{7,6},{8,9},{9,8},{10,11... | collective-permute-start | bytes 417800 | tf_op jit(solution)/shard_map/ppermute | solution.py:215
  1.6 18.2 %collective-permute-start.3 = (bf16[272,256]{1,0:T(8,128)(2,1)S(1)}, bf16[272,256]{1,0:T(8,128)(2,1)S(1)}, u32[]{:S(2)}, u32[]{:S(2)}) collective-permute-start(bf16[272,256]{1,0:T(8,128)(2,1)S(1)} %get-tuple-element.35.rest_0_.rest_1_), channel_id=1, source_target_pairs={{0,8},{8,0},{16,24},{24,16},{1,9},{9,1},{17,25},{25,17},{2,10},{10... | collective-permute-start | bytes 417800 | tf_op jit(solution)/shard_map/ppermute | solution.py:215
  4.3 15.5 %collective-permute-start.2 = (bf16[144,256]{1,0:T(8,128)(2,1)S(1)}, bf16[144,256]{1,0:T(8,128)(2,1)S(1)}, u32[]{:S(2)}, u32[]{:S(2)}) collective-permute-start(bf16[144,256]{1,0:T(8,128)(2,1)S(1)} %get-tuple-element.46), channel_id=1, source_target_pairs={{0,16},{8,24},{16,0},{24,8},{1,17},{9,25},{17,1},{25,9},{2,18},{10... | collective-permute-start | bytes 221192 | tf_op jit(solution)/shard_map/ppermute | solution.py:215
  6.9 7.8 %collective-permute-start.1 = (bf16[128,256]{1,0:T(8,128)(2,1)S(1)}, bf16[128,256]{1,0:T(8,128)(2,1)S(1)}, u32[]{:S(2)}, u32[]{:S(2)}) collective-permute-start(bf16[128,256]{1,0:T(8,128)(2,1)S(1)} %get-tuple-element.36), channel_id=1, source_target_pairs={{0,16},{8,24},{16,0},{24,8},{1,17},{9,25},{17,1},{25,9},{2,18},{10... | collective-permute-start | bytes 196616 | tf_op jit(solution)/shard_map/ppermute | solution.py:215
  7.2 15.1 %collective-permute-start.6 = (bf16[272,256]{1,0:T(8,128)(2,1)S(1)}, bf16[272,256]{1,0:T(8,128)(2,1)S(1)}, u32[]{:S(2)}, u32[]{:S(2)}) collective-permute-start(bf16[272,256]{1,0:T(8,128)(2,1)S(1)} %get-tuple-element.35.rest_0_.rest_1_), channel_id=1, source_target_pairs={{0,6},{1,7},{2,4},{3,5},{4,2},{5,3},{6,0},{7,1},{8,14},{9,15},{10,... | collective-permute-start | bytes 417800 | tf_op jit(solution)/shard_map/ppermute | solution.py:215
  14.6 7.7 %collective-permute-start.5 = (bf16[272,256]{1,0:T(8,128)(2,1)S(1)}, bf16[272,256]{1,0:T(8,128)(2,1)S(1)}, u32[]{:S(2)}, u32[]{:S(2)}) collective-permute-start(bf16[272,256]{1,0:T(8,128)(2,1)S(1)} %get-tuple-element.35.rest_0_.rest_1_), channel_id=1, source_target_pairs={{0,4},{1,5},{2,6},{3,7},{4,0},{5,1},{6,2},{7,3},{8,12},{9,13},{10,... | collective-permute-start | bytes 417800 | tf_op jit(solution)/shard_map/ppermute | solution.py:215
  16.2 6.2 %collective-permute-start.4 = (bf16[272,256]{1,0:T(8,128)(2,1)S(1)}, bf16[272,256]{1,0:T(8,128)(2,1)S(1)}, u32[]{:S(2)}, u32[]{:S(2)}) collective-permute-start(bf16[272,256]{1,0:T(8,128)(2,1)S(1)} %get-tuple-element.35.rest_0_.rest_1_), channel_id=1, source_target_pairs={{0,2},{1,3},{2,0},{3,1},{4,6},{5,7},{6,4},{7,5},{8,10},{9,11},{10,... | collective-permute-start | bytes 417800 | tf_op jit(solution)/shard_map/ppermute | solution.py:215
  19.8 4.3 %collective-permute-start.7 = (bf16[128,256]{1,0:T(8,128)(2,1)S(1)}, bf16[128,256]{1,0:T(8,128)(2,1)S(1)}, u32[]{:S(2)}, u32[]{:S(2)}) collective-permute-start(bf16[128,256]{1,0:T(8,128)(2,1)S(1)} %collective-permute-done.1.rest_2_), channel_id=1, source_target_pairs={{0,8},{8,0},{16,24},{24,16},{1,9},{9,1},{17,25},{25,17},{2,10},{10... | collective-permute-start | bytes 196616 | tf_op jit(solution)/shard_map/ppermute | solution.py:215
  19.9 5.0 %collective-permute-start.8 = (bf16[144,256]{1,0:T(8,128)(2,1)S(1)}, bf16[144,256]{1,0:T(8,128)(2,1)S(1)}, u32[]{:S(2)}, u32[]{:S(2)}) collective-permute-start(bf16[144,256]{1,0:T(8,128)(2,1)S(1)} %collective-permute-done.2.rest_3_.rest_6_), channel_id=1, source_target_pairs={{0,8},{8,0},{16,24},{24,16},{1,9},{9,1},{17,25},{25,17},{2,10},{10... | collective-permute-start | bytes 221192 | tf_op jit(solution)/shard_map/ppermute | solution.py:215
  22.4 2.5 %collective-permute-start.9 = (bf16[272,256]{1,0:T(8,128)(2,1)S(1)}, bf16[272,256]{1,0:T(8,128)(2,1)S(1)}, u32[]{:S(2)}, u32[]{:S(2)}) collective-permute-start(bf16[272,256]{1,0:T(8,128)(2,1)S(1)} %collective-permute-done.4.rest_0_.rest_3_), channel_id=1, source_target_pairs={{0,1},{1,0},{2,3},{3,2},{4,5},{5,4},{6,7},{7,6},{8,9},{9,8},{10,11... | collective-permute-start | bytes 417800 | tf_op jit(solution)/shard_map/ppermute | solution.py:215
  22.5 2.5 %collective-permute-start.10 = (bf16[272,256]{1,0:T(8,128)(2,1)S(1)}, bf16[272,256]{1,0:T(8,128)(2,1)S(1)}, u32[]{:S(2)}, u32[]{:S(2)}) collective-permute-start(bf16[272,256]{1,0:T(8,128)(2,1)S(1)} %collective-permute-done.5.rest_1_.rest_4_), channel_id=1, source_target_pairs={{0,1},{1,0},{2,3},{3,2},{4,5},{5,4},{6,7},{7,6},{8,9},{9,8},{10,11... | collective-permute-start | bytes 417800 | tf_op jit(solution)/shard_map/ppermute | solution.py:215
  23.0 2.0 %collective-permute-start.11 = (bf16[272,256]{1,0:T(8,128)(2,1)S(1)}, bf16[272,256]{1,0:T(8,128)(2,1)S(1)}, u32[]{:S(2)}, u32[]{:S(2)}) collective-permute-start(bf16[272,256]{1,0:T(8,128)(2,1)S(1)} %collective-permute-done.6.rest_2_.rest_5_), channel_id=1, source_target_pairs={{0,1},{1,0},{2,3},{3,2},{4,5},{5,4},{6,7},{7,6},{8,9},{9,8},{10,11... | collective-permute-start | bytes 417800 | tf_op jit(solution)/shard_map/ppermute | solution.py:215
  26.2 6.3 %collective-permute-start.12 = (bf16[128,256]{1,0:T(8,128)(2,1)S(1)}, bf16[128,256]{1,0:T(8,128)(2,1)S(1)}, u32[]{:S(2)}, u32[]{:S(2)}) collective-permute-start(bf16[128,256]{1,0:T(8,128)(2,1)S(1)} %get-tuple-element.53), channel_id=1, source_target_pairs={{0,24},{8,16},{16,8},{24,0},{1,25},{9,17},{17,9},{25,1},{2,26},{10... | collective-permute-start | bytes 196616 | tf_op jit(solution)/shard_map/ppermute | solution.py:215
  28.0 9.3 %collective-permute-start.15 = (bf16[256,256]{1,0:T(8,128)(2,1)S(1)}, bf16[256,256]{1,0:T(8,128)(2,1)S(1)}, u32[]{:S(2)}, u32[]{:S(2)}) collective-permute-start(bf16[256,256]{1,0:T(8,128)(2,1)S(1)} %get-tuple-element.61), channel_id=1, source_target_pairs={{0,2},{1,3},{2,0},{3,1},{4,6},{5,7},{6,4},{7,5},{8,10},{9,11},{10,... | collective-permute-start | bytes 393224 | tf_op jit(solution)/shard_map/ppermute | solution.py:215
  28.6 9.3 %collective-permute-start.16 = (bf16[256,256]{1,0:T(8,128)(2,1)S(1)}, bf16[256,256]{1,0:T(8,128)(2,1)S(1)}, u32[]{:S(2)}, u32[]{:S(2)}) collective-permute-start(bf16[256,256]{1,0:T(8,128)(2,1)S(1)} %get-tuple-element.62), channel_id=1, source_target_pairs={{0,4},{1,5},{2,6},{3,7},{4,0},{5,1},{6,2},{7,3},{8,12},{9,13},{10,... | collective-permute-start | bytes 393224 | tf_op jit(solution)/shard_map/ppermute | solution.py:215
  29.1 8.9 %collective-permute-start.17 = (bf16[256,256]{1,0:T(8,128)(2,1)S(1)}, bf16[256,256]{1,0:T(8,128)(2,1)S(1)}, u32[]{:S(2)}, u32[]{:S(2)}) collective-permute-start(bf16[256,256]{1,0:T(8,128)(2,1)S(1)} %get-tuple-element.63), channel_id=1, source_target_pairs={{0,6},{1,7},{2,4},{3,5},{4,2},{5,3},{6,0},{7,1},{8,14},{9,15},{10,... | collective-permute-start | bytes 393224 | tf_op jit(solution)/shard_map/ppermute | solution.py:215
  31.5 5.9 %collective-permute-start.13 = (bf16[128,256]{1,0:T(8,128)(2,1)S(1)}, bf16[128,256]{1,0:T(8,128)(2,1)S(1)}, u32[]{:S(2)}, u32[]{:S(2)}) collective-permute-start(bf16[128,256]{1,0:T(8,128)(2,1)S(1)} %get-tuple-element.54), channel_id=1, source_target_pairs={{0,16},{8,24},{16,0},{24,8},{1,17},{9,25},{17,1},{25,9},{2,18},{10... | collective-permute-start | bytes 196616 | tf_op jit(solution)/shard_map/ppermute | solution.py:215
  32.5 5.9 %collective-permute-start.14 = (bf16[128,256]{1,0:T(8,128)(2,1)S(1)}, bf16[128,256]{1,0:T(8,128)(2,1)S(1)}, u32[]{:S(2)}, u32[]{:S(2)}) collective-permute-start(bf16[128,256]{1,0:T(8,128)(2,1)S(1)} %get-tuple-element.55), channel_id=1, source_target_pairs={{0,8},{8,0},{16,24},{24,16},{1,9},{9,1},{17,25},{25,17},{2,10},{10... | collective-permute-start | bytes 196616 | tf_op jit(solution)/shard_map/ppermute | solution.py:215
  37.4 1.4 %collective-permute-start.21 = (bf16[128,256]{1,0:T(8,128)(2,1)S(1)}, bf16[128,256]{1,0:T(8,128)(2,1)S(1)}, u32[]{:S(2)}, u32[]{:S(2)}) collective-permute-start(bf16[128,256]{1,0:T(8,128)(2,1)S(1)} %get-tuple-element.64), channel_id=1, source_target_pairs={{0,1},{1,0},{2,3},{3,2},{4,5},{5,4},{6,7},{7,6},{8,9},{9,8},{10,11... | collective-permute-start | bytes 196616 | tf_op jit(solution)/shard_map/ppermute | solution.py:215
  37.4 1.5 %collective-permute-start.18 = (bf16[256,256]{1,0:T(8,128)(2,1)S(1)}, bf16[256,256]{1,0:T(8,128)(2,1)S(1)}, u32[]{:S(2)}, u32[]{:S(2)}) collective-permute-start(bf16[256,256]{1,0:T(8,128)(2,1)S(1)} %collective-permute-done.15.rest_0_), channel_id=1, source_target_pairs={{0,1},{1,0},{2,3},{3,2},{4,5},{5,4},{6,7},{7,6},{8,9},{9,8},{10,11... | collective-permute-start | bytes 393224 | tf_op jit(solution)/shard_map/ppermute | solution.py:215
  37.9 1.3 %collective-permute-start.19 = (bf16[256,256]{1,0:T(8,128)(2,1)S(1)}, bf16[256,256]{1,0:T(8,128)(2,1)S(1)}, u32[]{:S(2)}, u32[]{:S(2)}) collective-permute-start(bf16[256,256]{1,0:T(8,128)(2,1)S(1)} %collective-permute-done.16.rest_1_), channel_id=1, source_target_pairs={{0,1},{1,0},{2,3},{3,2},{4,5},{5,4},{6,7},{7,6},{8,9},{9,8},{10,11... | collective-permute-start | bytes 393224 | tf_op jit(solution)/shard_map/ppermute | solution.py:215
  38.0 1.5 %collective-permute-start.20 = (bf16[256,256]{1,0:T(8,128)(2,1)S(1)}, bf16[256,256]{1,0:T(8,128)(2,1)S(1)}, u32[]{:S(2)}, u32[]{:S(2)}) collective-permute-start(bf16[256,256]{1,0:T(8,128)(2,1)S(1)} %collective-permute-done.17.rest_2_), channel_id=1, source_target_pairs={{0,1},{1,0},{2,3},{3,2},{4,5},{5,4},{6,7},{7,6},{8,9},{9,8},{10,11... | collective-permute-start | bytes 393224 | tf_op jit(solution)/shard_map/ppermute | solution.py:215

commit v6 on v5

--- a/solution.py
+++ b/solution.py
@@ -30,14 +30,12 @@
     return 0.5 * (1.0 + t) + (0.5 * scale) * v * (1.0 - t * t) * (1.0 + 3.0 * 0.044715 * v * v)
 
 
-def edge_kernel(recv_sub, recv_cluster, features, edge, first, second, sub_row, cluster_row, sems):
-    size = first.shape[0]
+def edge_kernel(recv_sub, recv_cluster, features, edge, sub_row, cluster_row, sems):
+    count = edge.shape[0] - EXTRA
     copies = [
-        pltpu.make_async_copy(features.at[0:size, :], first, sems.at[0]),
-        pltpu.make_async_copy(features.at[size : 2 * size, :], second.at[0:size, :], sems.at[1]),
-        pltpu.make_async_copy(features.at[0 : 2 * size, :], edge.at[0 : 2 * size, :], sems.at[2]),
-        pltpu.make_async_copy(recv_sub, sub_row, sems.at[3]),
-        pltpu.make_async_copy(recv_cluster, cluster_row, sems.at[4]),
+        pltpu.make_async_copy(features.at[0:count, :], edge.at[0:count, :], sems.at[0]),
+        pltpu.make_async_copy(recv_sub, sub_row, sems.at[1]),
+        pltpu.make_async_copy(recv_cluster, cluster_row, sems.at[2]),
     ]
     for copy in copies:
         copy.start()
@@ -46,9 +44,7 @@
     sub_count, cluster_count = sub_row.shape[1], cluster_row.shape[1]
     pad = jnp.zeros((1, edge.shape[1] - sub_count - cluster_count), F32)
     row = jnp.concatenate([sub_row[...].astype(F32), cluster_row[...].astype(F32), pad], axis=1)
-    rows = jnp.broadcast_to(row, (EXTRA, edge.shape[1])).astype(BF)
-    edge[2 * size :, :] = rows
-    second[size:, :] = rows
+    edge[count:, :] = jnp.broadcast_to(row, (EXTRA, edge.shape[1])).astype(BF)
 
 
 def prepare_kernel(
@@ -104,47 +100,58 @@
         copy.wait()
 
 
-def halo_sum(choice, dense, own, shape, refs, halo):
+def relay_kernel(sub_count, d, near, far, out):
+    size = out.shape[0] - EXTRA
+    lanes = lax.broadcasted_iota(jnp.int32, (1, out.shape[1]), 1)
+    lane = sub_count + (lax.axis_index("cluster") ^ d)
+    row = near[2 * size : 2 * size + EXTRA, :].astype(F32)[0:1, :]
+    index = jnp.sum(jnp.where(lanes == lane, row, 0.0), axis=1, keepdims=True)
+    out[0:size, :] = jnp.where(
+        index > 0.5, far[size : 2 * size, :].astype(F32), far[0:size, :].astype(F32)
+    ).astype(BF)
+    out[size:, :] = far[2 * size :, :]
+
+
+def halo_sum(choice, dense, own, slots, messages, halo):
     size = dense.shape[0] // own
-    columns, at = [], 0
-    for i, (slot, count) in enumerate(shape.items()):
-        if count == 1:
-            first, second = refs[at][0:size, :], refs[at][size : 2 * size, :]
-        else:
-            first, second = refs[at][0:size, :], refs[at + 1][0:size, :]
-        at += count
-        halo[i * size : (i + 1) * size, :] = jnp.where(
-            choice[slot : slot + 1, :] > 0.5, second.astype(F32), first.astype(F32)
-        ).astype(BF)
+    columns = []
+    for i, (slot, message) in enumerate(zip(slots, messages)):
+        block = message[0:size, :]
+        if message.shape[0] > 2 * size:
+            block = jnp.where(
+                choice[slot : slot + 1, :] > 0.5,
+                message[size : 2 * size, :].astype(F32),
+                block.astype(F32),
+            ).astype(BF)
+        halo[i * size : (i + 1) * size, :] = block
         columns.append(dense[:, (own + slot) * size : (own + slot + 1) * size])
     return dot(jnp.concatenate(columns, axis=1), halo[...])
 
 
-def first_kernel(own, shape, choice, dense, features, w_self, bias, *rest):
+def first_kernel(own, slots, choice, dense, features, w_self, bias, *rest):
     refs, (total, own_pre, halo) = rest[:-3], rest[-3:]
     size = dense.shape[0] // own
     total[...] = dot(dense[:, 0 : own * size], features[...]) + halo_sum(
-        choice, dense, own, shape, refs, halo
+        choice, dense, own, slots, refs, halo
     )
     own_pre[...] = dot(features[...], w_self[...]) + bias[...].reshape(1, -1)
 
 
-def near_kernel(own, shape, choice, dense, before, *rest):
+def near_kernel(own, slots, choice, dense, before, *rest):
     refs, (total, halo) = rest[:-2], rest[-2:]
-    total[...] = before[...] + halo_sum(choice, dense, own, shape, refs, halo)
+    total[...] = before[...] + halo_sum(choice, dense, own, slots, refs, halo)
 
 
 def middle_kernel(
-    own, sub_count, cluster_count, shape,
+    own, sub_count, cluster_count, slots,
     choice, grad_out, w_neigh, dense, dense_t, before, own_pre, inverse,
     *rest,
 ):
-    received = sum(shape.values())
-    refs, rest = rest[:received], rest[received:]
+    refs, rest = rest[: len(slots)], rest[len(slots) :]
     pairs, rest = rest[: sub_count // 2 - 1], rest[sub_count // 2 - 1 :]
     along, (sibling, kept, spread, grad_pre, halo) = rest[:-5], rest[-5:]
     size = dense.shape[0] // own
-    aggregate = before[...] + halo_sum(choice, dense, own, shape, refs, halo)
+    aggregate = before[...] + halo_sum(choice, dense, own, slots, refs, halo)
     inv = jnp.concatenate([inverse[...]] * (grad_out.shape[1] // size), axis=1)
     mean = (aggregate * inv).astype(BF)
     pre = own_pre[...] + dot(mean, w_neigh[...])
@@ -196,6 +203,15 @@
         split(total, value, owner[slot : slot + 1, :] > 0.5, size)
 
 
+def add_kernel(own, parts, owner, total, *rest):
+    received, out = rest[:-1], rest[-1]
+    size = total.shape[0] // own
+    out[...] = total[...]
+    for message, (slot, row) in zip(received, parts):
+        value = message[row : row + size, :].astype(F32)
+        split(out, value, owner[slot : slot + 1, :] > 0.5, size)
+
+
 def final_kernel(own, parts, owner, total, *rest):
     received, out = rest[:-1], rest[-1]
     size = total.shape[0] // own
@@ -245,19 +261,15 @@
     block = jax.ShapeDtypeStruct((size, width), BF)
     marks = jax.ShapeDtypeStruct((sub_count + cluster_count, width), F32)
 
-    edge, *halves = pl.pallas_call(
+    edge = pl.pallas_call(
         edge_kernel,
-        out_shape=[
-            jax.ShapeDtypeStruct((BOUNDARY * size + EXTRA, width), BF),
-            block,
-            jax.ShapeDtypeStruct((size + EXTRA, width), BF),
-        ],
+        out_shape=jax.ShapeDtypeStruct((BOUNDARY * size + EXTRA, width), BF),
         in_specs=[HBM] * 3,
-        out_specs=[VMEM] * 3,
+        out_specs=VMEM,
         scratch_shapes=[
             pltpu.VMEM(recv_sub.shape, jnp.int32),
             pltpu.VMEM(recv_cluster.shape, jnp.int32),
-            pltpu.SemaphoreType.DMA((5,)),
+            pltpu.SemaphoreType.DMA((3,)),
         ],
         compiler_params=PARAMS,
         cost_estimate=cost(1024, 256 * 1024),
@@ -270,12 +282,17 @@
     def across(value, d):
         return swap(value, "sub", sub_count, d)
 
-    direct = [d for d in range(2, cluster_count) if not d & (d - 1)]
-    relayed = [d for d in range(2, cluster_count) if d & (d - 1)]
-    got = {sub_count + d: tuple(along(half, d) for half in halves) for d in direct}
-    got[1] = (across(edge, 1),)
-    early = (got[1][0], *(got[sub_count + d][0] for d in direct[-1:]))
-    start = after(tile_dst, early)
+    even = list(range(2, sub_count, 2))
+    direct = list(range(2, cluster_count, 2))
+    relayed = list(range(3, cluster_count, 2))
+    got = {0: edge, sub_count: edge}
+    for d in direct:
+        got[sub_count + d] = along(edge, d)
+    for d in even:
+        got[d] = across(edge, d)
+    got[sub_count + 1] = along(edge, 1)
+    got[1] = across(edge, 1)
+    start = tile_dst
 
     dense, dense_t, inverse, choice, features, w_self, w_neigh, grad_out, bias = pl.pallas_call(
         functools.partial(prepare_kernel, *counts),
@@ -301,7 +318,7 @@
             pltpu.SemaphoreType.DMA((10,)),
         ],
         compiler_params=PARAMS,
-        cost_estimate=cost(10**6, 6 * 1024 * 1024),
+        cost_estimate=cost(10**9, 6 * 1024 * 1024),
         name="prepare",
     )(
         *map(in_hbm, (start, tile_src, recv_sub, recv_cluster, tile_weight)),
@@ -309,60 +326,58 @@
     )
 
     def sum_call(kernel, out_shape, name, slots, *operands):
-        shape = {slot: len(got[slot]) for slot in slots}
-        refs = [part for slot in slots for part in got[slot]]
         return pl.pallas_call(
-            functools.partial(kernel, own, shape),
+            functools.partial(kernel, own, slots),
             out_shape=out_shape,
-            in_specs=[VMEM] * (len(operands) + len(refs)),
+            in_specs=[VMEM] * (len(operands) + len(slots)),
             out_specs=jax.tree.map(lambda _: VMEM, out_shape),
-            scratch_shapes=[pltpu.VMEM((len(shape) * size, width), BF)],
+            scratch_shapes=[pltpu.VMEM((len(slots) * size, width), BF)],
             compiler_params=PARAMS,
-            cost_estimate=cost(10**10, 3 * 1024 * 1024),
+            cost_estimate=cost(dict(first=10**9, near=10**9)[name], 3 * 1024 * 1024),
             name=name,
-        )(*operands, *refs)
-
-    got[0] = got[sub_count] = (edge,)
-    got[sub_count + 1] = (along(edge, 1),)
+        )(*operands, *[got[slot] for slot in slots])
+
+    for d in relayed:
+        value = pl.pallas_call(
+            functools.partial(relay_kernel, sub_count, d - 1),
+            out_shape=jax.ShapeDtypeStruct((size + EXTRA, width), BF),
+            in_specs=[VMEM] * 2,
+            out_specs=VMEM,
+            compiler_params=PARAMS,
+            cost_estimate=cost(10**6, 256 * 1024),
+            name="relay",
+        )(got[sub_count + 1], got[sub_count + d - 1])
+        got[sub_count + d] = along(value, 1)
     first_sum, own_pre = sum_call(
         first_kernel, [wide, wide], "first", [0, sub_count, *(sub_count + d for d in direct), sub_count + 1],
         choice, dense, features, w_self, bias,
     )
-    even = list(range(2, sub_count, 2))
-    for d in relayed:
-        low = d & -d
-        one, two = got[sub_count + d - low]
-        got[sub_count + d] = (along(one, low), along(two, low))
     for d in even:
-        got[d] = (across(edge, d),)
-        got[d + 1] = (across(after(got[d][0], own_pre), 1),)
-    near_sum = sum_call(near_kernel, wide, "near", [*even, 1], choice, dense, first_sum)
-
-    late = [*(sub_count + d for d in relayed), *(d + 1 for d in even)]
-    shape = {slot: len(got[slot]) for slot in late}
-    refs = [part for slot in late for part in got[slot]]
+        got[d + 1] = across(after(got[d], choice), 1)
+    near_sum = sum_call(near_kernel, wide, "near", even, choice, dense, first_sum)
+
+    late = [*(sub_count + d for d in relayed), *(d + 1 for d in even), 1]
     outs = pl.pallas_call(
-        functools.partial(middle_kernel, *counts, shape),
+        functools.partial(middle_kernel, *counts, late),
         out_shape=[jax.ShapeDtypeStruct((2 * size, width), BF)] * len(even)
         + [block] * cluster_count
         + [jax.ShapeDtypeStruct((2, size, width), BF), narrow, narrow],
-        in_specs=[VMEM] * (8 + len(refs)),
+        in_specs=[VMEM] * (8 + len(late)),
         out_specs=[VMEM] * (len(even) + cluster_count + 3),
-        scratch_shapes=[pltpu.VMEM((len(shape) * size, width), BF)],
+        scratch_shapes=[pltpu.VMEM((len(late) * size, width), BF)],
         compiler_params=PARAMS,
         cost_estimate=cost(2 * rows * slots * size * width, 6 * 1024 * 1024),
         name="middle",
-    )(choice, grad_out, w_neigh, dense, dense_t, near_sum, own_pre, inverse, *refs)
+    )(
+        choice, grad_out, w_neigh, dense, dense_t, near_sum, own_pre, inverse,
+        *[got[slot] for slot in late],
+    )
     *sent, sibling, kept, spread, grad_pre = outs
 
     back = [(along(sent[len(even) + d - 1], d), sub_count + d, 0) for d in range(1, cluster_count)]
-    direct_back, swapped_back = [], []
-    for d, value in zip(even, sent):
-        value = across(value, d)
-        direct_back.append((value, d, 0))
-        swapped_back.append((across(value, 1), d + 1, size))
+    direct_back = [(across(value, d), d, 0) for d, value in zip(even, sent)]
     sibling_back = [(across(sibling, 1), 1, 0)]
-    early_back, back = back[::-1], [*direct_back, *swapped_back, *sibling_back]
+    early_back = back[::-1]
 
     order = [*even, *(sub_count + d for d in direct), *(d + 1 for d in even), 1, sub_count + 1, *(sub_count + d for d in relayed)]
     total, owner = pl.pallas_call(
@@ -377,10 +392,25 @@
         name="own",
     )(
         *[value for value, _, _ in early_back],
-        *[got[slot][-1] for slot in order],
+        *[got[slot] for slot in order],
         choice, w_self, dense_t, kept, spread, grad_pre,
     )
 
+    swapped_back = [
+        (across(after(value, total), 1), d + 1, size) for value, d, _ in direct_back
+    ]
+    middle_back = []
+    if middle_back:
+        total = pl.pallas_call(
+            functools.partial(add_kernel, own, [(slot, row) for _, slot, row in middle_back]),
+            out_shape=wide,
+            in_specs=[VMEM] * (2 + len(middle_back)),
+            out_specs=VMEM,
+            compiler_params=PARAMS,
+            cost_estimate=cost(10**9, 2 * 1024 * 1024),
+            name="add",
+        )(owner, total, *[value for value, _, _ in middle_back])
+    back = [*direct_back[::-1], *swapped_back[::-1], *sibling_back]
     return pl.pallas_call(
         functools.partial(final_kernel, own, [(slot, row) for _, slot, row in back]),
         out_shape=narrow,

time: 40.5 us -> 34.5 us (0.85)
  starting transfers between devices: 23.2 us -> 19.1 us
  waiting for transfers between devices: 10.5 us -> 8.53 us
    ppermute x22 -> x20, starting transfers between devices: 23.2 us -> 19.1 us  [swap(): return lax.ppermute(value, axis, [(i, i ^ d) for i in range(count)])]
    ppermute x22 -> x20, waiting for transfers between devices: 10.5 us -> 8.53 us  [swap(): return lax.ppermute(value, axis, [(i, i ^ d) for i in range(count)])]
    pallas_call x4 -> x5, Pallas kernels: 3.12 us -> 3.27 us  [the longest x1 1.43 us: shards(): pl.pallas_call(functools.partial(middle_kernel, *counts, late), out_shape...]
  transfers between devices with their start and end apart: 22 -> 20, of which waited for: 7 -> 9; matrix products, arithmetic and copies ran while one was open for 0% -> 0% of each run, Pallas kernels for 8% -> 10%
where the time goes in v6:
time: 34.5 us; the launch traced here: 34.4 us
  starting transfers between devices  19.1 us (55%)
  waiting for transfers between devices  8.53 us (25%)
  Pallas kernels  6.64 us (19%)
    ppermute x20, starting transfers between devices, swap(): return lax.ppermute(value, axis, [(i, i ^ d) for i in range(count)])  19.1 us
    ppermute x20, waiting for transfers between devices, swap(): return lax.ppermute(value, axis, [(i, i ^ d) for i in range(count)])  8.53 us
    pallas_call x1, Pallas kernels, shards(): pl.pallas_call(functools.partial(prepare_kernel, *counts), out_shape=[jax...  2.11 us
    pallas_call x1, Pallas kernels, shards(): pl.pallas_call(functools.partial(middle_kernel, *counts, late), out_shape...  1.43 us
    pallas_call x1, Pallas kernels, shards(): pl.pallas_call(edge_kernel, out_shape=jax.ShapeDtypeStruct((BOUNDARY * si...  1.01 us
    pallas_call x1, Pallas kernels, shards(): pl.pallas_call(functools.partial(final_kernel, own, [(slot, row) for _, s...  0.87 us
    pallas_call x2, Pallas kernels, sum_call(): pl.pallas_call(functools.partial(kernel, own, slots), out_shape=out_shape...  0.73 us
  transfers between devices with their start and end apart: 20, of which 9 were waited for; matrix products, arithmetic and copies ran while one was open for 0% of the time, Pallas kernels for 10%

profile of v6, /device:TPU:0, one launch (start us, length us, event | category | flops | bytes accessed | tf_op | source)
XLA Modules:
  0.0 34.4 jit_solution(12939930279972083809)
XLA Ops:
  0.0 1.0 %edge.1.rest_0_.rest_1_ = bf16[272,256]{1,0:T(8,128)(2,1)S(1)} custom-call(s32[1,8]{1,0:T(1,128)} %recv_sub.1, s32[1,4]{1,0:T(1,128)} %recv_cluster.1, bf16[384,256]{1,0:T(8,128)(2,1)} %features.1), custom_call_target="tpu_custom_call" | custom-call | flops 1024 | bytes 262144 | tf_op jit(solution)/shard_map/edge/pallas_call | solution.py:264
  1.0 3.1 %collective-permute-start.1 = (bf16[272,256]{1,0:T(8,128)(2,1)S(1)}, bf16[272,256]{1,0:T(8,128)(2,1)S(1)}, u32[]{:S(2)}, u32[]{:S(2)}) collective-permute-start(bf16[272,256]{1,0:T(8,128)(2,1)S(1)} %edge.1.rest_0_.rest_1_), channel_id=1, source_target_pairs={{0,8},{8,0},{16,24},{24,16},{1,9},{9,1},{17,25},{25,17},{2,10},{10... | collective-permute-start | bytes 417800 | tf_op jit(solution)/shard_map/ppermute | solution.py:231
  4.1 2.6 %collective-permute-start = (bf16[272,256]{1,0:T(8,128)(2,1)S(1)}, bf16[272,256]{1,0:T(8,128)(2,1)S(1)}, u32[]{:S(2)}, u32[]{:S(2)}) collective-permute-start(bf16[272,256]{1,0:T(8,128)(2,1)S(1)} %edge.1.rest_0_.rest_1_), channel_id=1, source_target_pairs={{0,16},{8,24},{16,0},{24,8},{1,17},{9,25},{17,1},{25,9},{2,18},{10... | collective-permute-start | bytes 417800 | tf_op jit(solution)/shard_map/ppermute | solution.py:231
  6.7 2.4 %collective-permute-start.4 = (bf16[272,256]{1,0:T(8,128)(2,1)S(1)}, bf16[272,256]{1,0:T(8,128)(2,1)S(1)}, u32[]{:S(2)}, u32[]{:S(2)}) collective-permute-start(bf16[272,256]{1,0:T(8,128)(2,1)S(1)} %edge.1.rest_0_.rest_1_), channel_id=1, source_target_pairs={{0,6},{1,7},{2,4},{3,5},{4,2},{5,3},{6,0},{7,1},{8,14},{9,15},{10,... | collective-permute-start | bytes 417800 | tf_op jit(solution)/shard_map/ppermute | solution.py:231
  9.1 0.5 %collective-permute-start.3 = (bf16[272,256]{1,0:T(8,128)(2,1)S(1)}, bf16[272,256]{1,0:T(8,128)(2,1)S(1)}, u32[]{:S(2)}, u32[]{:S(2)}) collective-permute-start(bf16[272,256]{1,0:T(8,128)(2,1)S(1)} %edge.1.rest_0_.rest_1_), channel_id=1, source_target_pairs={{0,4},{1,5},{2,6},{3,7},{4,0},{5,1},{6,2},{7,3},{8,12},{9,13},{10,... | collective-permute-start | bytes 417800 | tf_op jit(solution)/shard_map/ppermute | solution.py:231
  9.6 0.5 %collective-permute-start.2 = (bf16[272,256]{1,0:T(8,128)(2,1)S(1)}, bf16[272,256]{1,0:T(8,128)(2,1)S(1)}, u32[]{:S(2)}, u32[]{:S(2)}) collective-permute-start(bf16[272,256]{1,0:T(8,128)(2,1)S(1)} %edge.1.rest_0_.rest_1_), channel_id=1, source_target_pairs={{0,2},{1,3},{2,0},{3,1},{4,6},{5,7},{6,4},{7,5},{8,10},{9,11},{10,... | collective-permute-start | bytes 417800 | tf_op jit(solution)/shard_map/ppermute | solution.py:231
  10.2 2.1 %prepare.1 = (bf16[384,1920]{1,0:T(8,128)(2,1)S(1)}, bf16[1920,384]{1,0:T(8,128)(2,1)S(1)}, f32[384,128]{1,0:T(8,128)S(1)}, f32[12,256]{1,0:T(8,128)S(1)}, bf16[...) custom-call(s32[24]{0:T(128)} %tile_dst_hbm.1, ...), custom_call_target="tpu_custom_call" | custom-call | flops 1000000000 | bytes 6291456 | tf_op jit(solution)/shard_map/prepare/pallas_call | solution.py:297
  12.3 0.0 collective-permute-done.1.rest_3_.near.rest_11_
  12.3 0.1 collective-permute-start.9
  12.4 0.8 %collective-permute-done.rest_2_.far.rest_6_ = bf16[272,256]{1,0:T(8,128)(2,1)S(1)} collective-permute-done((bf16[272,256]{1,0:T(8,128)(2,1)S(1)}, bf16[272,256]{1,0:T(8,128)(2,1)S(1)}, u32[]{:S(2)}, u32[]{:S(2)}) %collective-permute-start) | collective-permute-done | bytes 139296 | tf_op jit(solution)/shard_map/ppermute | solution.py:231
  13.2 0.1 relay.1
  13.3 0.5 %collective-permute-start.5 = (bf16[144,256]{1,0:T(8,128)(2,1)S(1)}, bf16[144,256]{1,0:T(8,128)(2,1)S(1)}, u32[]{:S(2)}, u32[]{:S(2)}) collective-permute-start(bf16[144,256]{1,0:T(8,128)(2,1)S(1)} %relay.1), channel_id=1, source_target_pairs={{0,8},{8,0},{16,24},{24,16},{1,9},{9,1},{17,25},{25,17},{2,10},{10... | collective-permute-start | bytes 221192 | tf_op jit(solution)/shard_map/ppermute | solution.py:231
  13.8 0.0 collective-permute-done.4.rest_2_.rest_5_
  13.8 1.6 %collective-permute-done.3.rest_1_.rest_4_ = bf16[272,256]{1,0:T(8,128)(2,1)S(1)} collective-permute-done((bf16[272,256]{1,0:T(8,128)(2,1)S(1)}, bf16[272,256]{1,0:T(8,128)(2,1)S(1)}, u32[]{:S(2)}, u32[]{:S(2)}) %collective-permute-start.3) | collective-permute-done | bytes 139296 | tf_op jit(solution)/shard_map/ppermute | solution.py:231
  15.4 0.1 collective-permute-done.2.rest_0_.rest_3_
  15.5 0.0 collective-permute-start.6
  15.5 0.5 %collective-permute-start.7 = (bf16[272,256]{1,0:T(8,128)(2,1)S(1)}, bf16[272,256]{1,0:T(8,128)(2,1)S(1)}, u32[]{:S(2)}, u32[]{:S(2)}) collective-permute-start(bf16[272,256]{1,0:T(8,128)(2,1)S(1)} %collective-permute-done.3.rest_1_.rest_4_), channel_id=1, source_target_pairs={{0,1},{1,0},{2,3},{3,2},{4,5},{5,4},{6,7},{7,6},{8,9},{9,8},{10,11... | collective-permute-start | bytes 417800 | tf_op jit(solution)/shard_map/ppermute | solution.py:231
  16.0 0.0 collective-permute-start.8
  16.0 0.5 %first.1 = (f32[384,256]{1,0:T(8,128)S(1)}, f32[384,256]{1,0:T(8,128)S(1)}) custom-call(f32[12,256]{1,0:T(8,128)S(1)} %get-tuple-element.34.choice.rest_13_, bf16[384,1920]{1,0:T(8,128)(2,1)S(1)} %get-tuple-element.37.dense, bf16[384,256]{1,0:T(8,128)(2,1)S(1)} %get-tuple-element.39.features, bf16[256,256]{1,0:T(8,128)(2,1)S(1)} %get-tuple-element.40.w_self.rest_14_, ...), custom_call_target="tpu_custom_call" | custom-call | flops 1000000000 | bytes 3145728 | tf_op jit(solution)/shard_map/first/pallas_call | solution.py:329
  16.5 0.3 near.1.before
  16.8 0.0 collective-permute-done.9.rest_4_.rest_10_
  16.8 0.9 %collective-permute-done.5.rest_0_.rest_12_ = bf16[144,256]{1,0:T(8,128)(2,1)S(1)} collective-permute-done((bf16[144,256]{1,0:T(8,128)(2,1)S(1)}, bf16[144,256]{1,0:T(8,128)(2,1)S(1)}, u32[]{:S(2)}, u32[]{:S(2)}) %collective-permute-start.5) | collective-permute-done | bytes 73760 | tf_op jit(solution)/shard_map/ppermute | solution.py:231
  17.7 0.0 collective-permute-done.6.rest_1_.rest_7_
  17.7 0.0 collective-permute-done.7.rest_2_.rest_8_
  17.7 0.0 collective-permute-done.8.rest_3_.rest_9_
  17.7 1.4 %middle.1 = (bf16[256,256]{1,0:T(8,128)(2,1)S(1)}, bf16[256,256]{1,0:T(8,128)(2,1)S(1)}, bf16[256,256]{1,0:T(8,128)(2,1)S(1)}, bf16[128,256]{1,0:T(8,128)(2,1)S(...) custom-call(f32[12,256]{1,0:T(8,128)S(1)} %get-tuple-element.34.choi, ...), custom_call_target="tpu_custom_call" | custom-call | flops 377487360 | bytes 6291456 | tf_op jit(solution)/shard_map/middle/pallas_call | solution.py:360
  19.1 2.5 %collective-permute-start.10 = (bf16[128,256]{1,0:T(8,128)(2,1)S(1)}, bf16[128,256]{1,0:T(8,128)(2,1)S(1)}, u32[]{:S(2)}, u32[]{:S(2)}) collective-permute-start(bf16[128,256]{1,0:T(8,128)(2,1)S(1)} %get-tuple-element.48), channel_id=1, source_target_pairs={{0,24},{8,16},{16,8},{24,0},{1,25},{9,17},{17,9},{25,1},{2,26},{10... | collective-permute-start | bytes 196616 | tf_op jit(solution)/shard_map/ppermute | solution.py:231
  21.7 0.0 collective-permute-start.11
  21.7 1.9 %collective-permute-start.12 = (bf16[128,256]{1,0:T(8,128)(2,1)S(1)}, bf16[128,256]{1,0:T(8,128)(2,1)S(1)}, u32[]{:S(2)}, u32[]{:S(2)}) collective-permute-start(bf16[128,256]{1,0:T(8,128)(2,1)S(1)} %get-tuple-element.50), channel_id=1, source_target_pairs={{0,8},{8,0},{16,24},{24,16},{1,9},{9,1},{17,25},{25,17},{2,10},{10... | collective-permute-start | bytes 196616 | tf_op jit(solution)/shard_map/ppermute | solution.py:231
  23.6 2.4 %collective-permute-start.13 = (bf16[256,256]{1,0:T(8,128)(2,1)S(1)}, bf16[256,256]{1,0:T(8,128)(2,1)S(1)}, u32[]{:S(2)}, u32[]{:S(2)}) collective-permute-start(bf16[256,256]{1,0:T(8,128)(2,1)S(1)} %get-tuple-element.56), channel_id=1, source_target_pairs={{0,6},{1,7},{2,4},{3,5},{4,2},{5,3},{6,0},{7,1},{8,14},{9,15},{10,... | collective-permute-start | bytes 393224 | tf_op jit(solution)/shard_map/ppermute | solution.py:231
  26.0 0.5 %collective-permute-start.14 = (bf16[256,256]{1,0:T(8,128)(2,1)S(1)}, bf16[256,256]{1,0:T(8,128)(2,1)S(1)}, u32[]{:S(2)}, u32[]{:S(2)}) collective-permute-start(bf16[256,256]{1,0:T(8,128)(2,1)S(1)} %get-tuple-element.57), channel_id=1, source_target_pairs={{0,4},{1,5},{2,6},{3,7},{4,0},{5,1},{6,2},{7,3},{8,12},{9,13},{10,... | collective-permute-start | bytes 393224 | tf_op jit(solution)/shard_map/ppermute | solution.py:231
  26.5 0.0 collective-permute-done.10.rest_0_
  26.5 0.9 %collective-permute-start.15 = (bf16[256,256]{1,0:T(8,128)(2,1)S(1)}, bf16[256,256]{1,0:T(8,128)(2,1)S(1)}, u32[]{:S(2)}, u32[]{:S(2)}) collective-permute-start(bf16[256,256]{1,0:T(8,128)(2,1)S(1)} %get-tuple-element.58), channel_id=1, source_target_pairs={{0,2},{1,3},{2,0},{3,1},{4,6},{5,7},{6,4},{7,5},{8,10},{9,11},{10,... | collective-permute-start | bytes 393224 | tf_op jit(solution)/shard_map/ppermute | solution.py:231
  27.5 0.1 collective-permute-done.11.rest_1_
  27.6 0.0 collective-permute-done.12.rest_2_
  27.6 0.4 %own.1 = (f32[384,256]{1,0:T(8,128)S(1)}, f32[12,256]{1,0:T(8,128)S(1)}) custom-call(bf16[128,256]{1,0:T(8,128)(2,1)S(1)} %collective-permute-done.10.rest_0_, bf16[128,256]{1,0:T(8,128)(2,1)S(1)} %collective-permute-done.11.rest_1_, bf16[128,256]{1,0:T(8,128)(2,1)S(1)} %collective-permute-done.12.rest_2_, ...), custom_call_target="tpu_custom_call" | custom-call | flops 10000000000 | bytes 2097152 | tf_op jit(solution)/shard_map/own/pallas_call | solution.py:383
  28.0 2.7 %collective-permute-done.13.rest_0_ = bf16[256,256]{1,0:T(8,128)(2,1)S(1)} collective-permute-done((bf16[256,256]{1,0:T(8,128)(2,1)S(1)}, bf16[256,256]{1,0:T(8,128)(2,1)S(1)}, u32[]{:S(2)}, u32[]{:S(2)}) %collective-permute-start.13) | collective-permute-done | bytes 131104 | tf_op jit(solution)/shard_map/ppermute | solution.py:231
  30.7 0.0 collective-permute-start.16
  30.7 1.0 %collective-permute-done.14.rest_1_ = bf16[256,256]{1,0:T(8,128)(2,1)S(1)} collective-permute-done((bf16[256,256]{1,0:T(8,128)(2,1)S(1)}, bf16[256,256]{1,0:T(8,128)(2,1)S(1)}, u32[]{:S(2)}, u32[]{:S(2)}) %collective-permute-start.14) | collective-permute-done | bytes 131104 | tf_op jit(solution)/shard_map/ppermute | solution.py:231
  31.7 0.0 collective-permute-start.17
  31.7 0.1 collective-permute-done.15.rest_2_
  31.8 0.4 %collective-permute-start.18 = (bf16[256,256]{1,0:T(8,128)(2,1)S(1)}, bf16[256,256]{1,0:T(8,128)(2,1)S(1)}, u32[]{:S(2)}, u32[]{:S(2)}) collective-permute-start(bf16[256,256]{1,0:T(8,128)(2,1)S(1)} %collective-permute-done.15.rest_2_), channel_id=1, source_target_pairs={{0,1},{1,0},{2,3},{3,2},{4,5},{5,4},{6,7},{7,6},{8,9},{9,8},{10,11... | collective-permute-start | bytes 393224 | tf_op jit(solution)/shard_map/ppermute | solution.py:231
  32.2 0.1 collective-permute-start.19
  32.4 1.1 %collective-permute-done.19.rest_6_ = bf16[128,256]{1,0:T(8,128)(2,1)S(1)} collective-permute-done((bf16[128,256]{1,0:T(8,128)(2,1)S(1)}, bf16[128,256]{1,0:T(8,128)(2,1)S(1)}, u32[]{:S(2)}, u32[]{:S(2)}) %collective-permute-start.19) | collective-permute-done | bytes 65568 | tf_op jit(solution)/shard_map/ppermute | solution.py:231
  33.5 0.0 collective-permute-done.16.rest_3_
  33.5 0.0 collective-permute-done.17.rest_4_
  33.5 0.0 collective-permute-done.18.rest_5_
  33.5 0.9 %final.1 = bf16[384,256]{1,0:T(8,128)(2,1)} custom-call(f32[12,256]{1,0:T(8,128)S(1)} %get-tuple-element.54.owner, f32[384,256]{1,0:T(8,128)S(1)} %get-tuple-element.55.total, bf16[256,256]{1,0:T(8,128)(2,1)S(1)} %collective-permute-done.13.rest_0_, bf16[256,256]{1,0:T(8,128)(2,1)S(1)} %collective-permute-done.14.rest_1_, ...), custom_call_target="tpu_custom_call" | custom-call | flops 393216 | bytes 2097152 | tf_op jit(solution)/shard_map/final/pallas_call | solution.py:414
Async XLA Ops:
  1.0 11.3 %collective-permute-start.1 = (bf16[272,256]{1,0:T(8,128)(2,1)S(1)}, bf16[272,256]{1,0:T(8,128)(2,1)S(1)}, u32[]{:S(2)}, u32[]{:S(2)}) collective-permute-start(bf16[272,256]{1,0:T(8,128)(2,1)S(1)} %edge.1.rest_0_.rest_1_), channel_id=1, source_target_pairs={{0,8},{8,0},{16,24},{24,16},{1,9},{9,1},{17,25},{25,17},{2,10},{10... | collective-permute-start | bytes 417800 | tf_op jit(solution)/shard_map/ppermute | solution.py:231
  4.1 9.1 %collective-permute-start = (bf16[272,256]{1,0:T(8,128)(2,1)S(1)}, bf16[272,256]{1,0:T(8,128)(2,1)S(1)}, u32[]{:S(2)}, u32[]{:S(2)}) collective-permute-start(bf16[272,256]{1,0:T(8,128)(2,1)S(1)} %edge.1.rest_0_.rest_1_), channel_id=1, source_target_pairs={{0,16},{8,24},{16,0},{24,8},{1,17},{9,25},{17,1},{25,9},{2,18},{10... | collective-permute-start | bytes 417800 | tf_op jit(solution)/shard_map/ppermute | solution.py:231
  6.7 7.1 %collective-permute-start.4 = (bf16[272,256]{1,0:T(8,128)(2,1)S(1)}, bf16[272,256]{1,0:T(8,128)(2,1)S(1)}, u32[]{:S(2)}, u32[]{:S(2)}) collective-permute-start(bf16[272,256]{1,0:T(8,128)(2,1)S(1)} %edge.1.rest_0_.rest_1_), channel_id=1, source_target_pairs={{0,6},{1,7},{2,4},{3,5},{4,2},{5,3},{6,0},{7,1},{8,14},{9,15},{10,... | collective-permute-start | bytes 417800 | tf_op jit(solution)/shard_map/ppermute | solution.py:231
  9.1 6.3 %collective-permute-start.3 = (bf16[272,256]{1,0:T(8,128)(2,1)S(1)}, bf16[272,256]{1,0:T(8,128)(2,1)S(1)}, u32[]{:S(2)}, u32[]{:S(2)}) collective-permute-start(bf16[272,256]{1,0:T(8,128)(2,1)S(1)} %edge.1.rest_0_.rest_1_), channel_id=1, source_target_pairs={{0,4},{1,5},{2,6},{3,7},{4,0},{5,1},{6,2},{7,3},{8,12},{9,13},{10,... | collective-permute-start | bytes 417800 | tf_op jit(solution)/shard_map/ppermute | solution.py:231
  9.6 5.8 %collective-permute-start.2 = (bf16[272,256]{1,0:T(8,128)(2,1)S(1)}, bf16[272,256]{1,0:T(8,128)(2,1)S(1)}, u32[]{:S(2)}, u32[]{:S(2)}) collective-permute-start(bf16[272,256]{1,0:T(8,128)(2,1)S(1)} %edge.1.rest_0_.rest_1_), channel_id=1, source_target_pairs={{0,2},{1,3},{2,0},{3,1},{4,6},{5,7},{6,4},{7,5},{8,10},{9,11},{10,... | collective-permute-start | bytes 417800 | tf_op jit(solution)/shard_map/ppermute | solution.py:231
  12.3 4.4 %collective-permute-start.9 = (bf16[272,256]{1,0:T(8,128)(2,1)S(1)}, bf16[272,256]{1,0:T(8,128)(2,1)S(1)}, u32[]{:S(2)}, u32[]{:S(2)}) collective-permute-start(bf16[272,256]{1,0:T(8,128)(2,1)S(1)} %edge.1.rest_0_.rest_1_), channel_id=1, source_target_pairs={{0,1},{1,0},{2,3},{3,2},{4,5},{5,4},{6,7},{7,6},{8,9},{9,8},{10,11... | collective-permute-start | bytes 417800 | tf_op jit(solution)/shard_map/ppermute | solution.py:231
  13.3 4.4 %collective-permute-start.5 = (bf16[144,256]{1,0:T(8,128)(2,1)S(1)}, bf16[144,256]{1,0:T(8,128)(2,1)S(1)}, u32[]{:S(2)}, u32[]{:S(2)}) collective-permute-start(bf16[144,256]{1,0:T(8,128)(2,1)S(1)} %relay.1), channel_id=1, source_target_pairs={{0,8},{8,0},{16,24},{24,16},{1,9},{9,1},{17,25},{25,17},{2,10},{10... | collective-permute-start | bytes 221192 | tf_op jit(solution)/shard_map/ppermute | solution.py:231
  15.5 2.2 %collective-permute-start.6 = (bf16[272,256]{1,0:T(8,128)(2,1)S(1)}, bf16[272,256]{1,0:T(8,128)(2,1)S(1)}, u32[]{:S(2)}, u32[]{:S(2)}) collective-permute-start(bf16[272,256]{1,0:T(8,128)(2,1)S(1)} %collective-permute-done.2.rest_0_.rest_3_), channel_id=1, source_target_pairs={{0,1},{1,0},{2,3},{3,2},{4,5},{5,4},{6,7},{7,6},{8,9},{9,8},{10,11... | collective-permute-start | bytes 417800 | tf_op jit(solution)/shard_map/ppermute | solution.py:231
  15.5 2.2 %collective-permute-start.7 = (bf16[272,256]{1,0:T(8,128)(2,1)S(1)}, bf16[272,256]{1,0:T(8,128)(2,1)S(1)}, u32[]{:S(2)}, u32[]{:S(2)}) collective-permute-start(bf16[272,256]{1,0:T(8,128)(2,1)S(1)} %collective-permute-done.3.rest_1_.rest_4_), channel_id=1, source_target_pairs={{0,1},{1,0},{2,3},{3,2},{4,5},{5,4},{6,7},{7,6},{8,9},{9,8},{10,11... | collective-permute-start | bytes 417800 | tf_op jit(solution)/shard_map/ppermute | solution.py:231
  16.0 1.7 %collective-permute-start.8 = (bf16[272,256]{1,0:T(8,128)(2,1)S(1)}, bf16[272,256]{1,0:T(8,128)(2,1)S(1)}, u32[]{:S(2)}, u32[]{:S(2)}) collective-permute-start(bf16[272,256]{1,0:T(8,128)(2,1)S(1)} %collective-permute-done.4.rest_2_.rest_5_), channel_id=1, source_target_pairs={{0,1},{1,0},{2,3},{3,2},{4,5},{5,4},{6,7},{7,6},{8,9},{9,8},{10,11... | collective-permute-start | bytes 417800 | tf_op jit(solution)/shard_map/ppermute | solution.py:231
  19.1 7.4 %collective-permute-start.10 = (bf16[128,256]{1,0:T(8,128)(2,1)S(1)}, bf16[128,256]{1,0:T(8,128)(2,1)S(1)}, u32[]{:S(2)}, u32[]{:S(2)}) collective-permute-start(bf16[128,256]{1,0:T(8,128)(2,1)S(1)} %get-tuple-element.48), channel_id=1, source_target_pairs={{0,24},{8,16},{16,8},{24,0},{1,25},{9,17},{17,9},{25,1},{2,26},{10... | collective-permute-start | bytes 196616 | tf_op jit(solution)/shard_map/ppermute | solution.py:231
  21.7 5.9 %collective-permute-start.11 = (bf16[128,256]{1,0:T(8,128)(2,1)S(1)}, bf16[128,256]{1,0:T(8,128)(2,1)S(1)}, u32[]{:S(2)}, u32[]{:S(2)}) collective-permute-start(bf16[128,256]{1,0:T(8,128)(2,1)S(1)} %get-tuple-element.49), channel_id=1, source_target_pairs={{0,16},{8,24},{16,0},{24,8},{1,17},{9,25},{17,1},{25,9},{2,18},{10... | collective-permute-start | bytes 196616 | tf_op jit(solution)/shard_map/ppermute | solution.py:231
  21.7 5.9 %collective-permute-start.12 = (bf16[128,256]{1,0:T(8,128)(2,1)S(1)}, bf16[128,256]{1,0:T(8,128)(2,1)S(1)}, u32[]{:S(2)}, u32[]{:S(2)}) collective-permute-start(bf16[128,256]{1,0:T(8,128)(2,1)S(1)} %get-tuple-element.50), channel_id=1, source_target_pairs={{0,8},{8,0},{16,24},{24,16},{1,9},{9,1},{17,25},{25,17},{2,10},{10... | collective-permute-start | bytes 196616 | tf_op jit(solution)/shard_map/ppermute | solution.py:231
  23.6 7.1 %collective-permute-start.13 = (bf16[256,256]{1,0:T(8,128)(2,1)S(1)}, bf16[256,256]{1,0:T(8,128)(2,1)S(1)}, u32[]{:S(2)}, u32[]{:S(2)}) collective-permute-start(bf16[256,256]{1,0:T(8,128)(2,1)S(1)} %get-tuple-element.56), channel_id=1, source_target_pairs={{0,6},{1,7},{2,4},{3,5},{4,2},{5,3},{6,0},{7,1},{8,14},{9,15},{10,... | collective-permute-start | bytes 393224 | tf_op jit(solution)/shard_map/ppermute | solution.py:231
  26.0 5.7 %collective-permute-start.14 = (bf16[256,256]{1,0:T(8,128)(2,1)S(1)}, bf16[256,256]{1,0:T(8,128)(2,1)S(1)}, u32[]{:S(2)}, u32[]{:S(2)}) collective-permute-start(bf16[256,256]{1,0:T(8,128)(2,1)S(1)} %get-tuple-element.57), channel_id=1, source_target_pairs={{0,4},{1,5},{2,6},{3,7},{4,0},{5,1},{6,2},{7,3},{8,12},{9,13},{10,... | collective-permute-start | bytes 393224 | tf_op jit(solution)/shard_map/ppermute | solution.py:231
  26.5 5.3 %collective-permute-start.15 = (bf16[256,256]{1,0:T(8,128)(2,1)S(1)}, bf16[256,256]{1,0:T(8,128)(2,1)S(1)}, u32[]{:S(2)}, u32[]{:S(2)}) collective-permute-start(bf16[256,256]{1,0:T(8,128)(2,1)S(1)} %get-tuple-element.58), channel_id=1, source_target_pairs={{0,2},{1,3},{2,0},{3,1},{4,6},{5,7},{6,4},{7,5},{8,10},{9,11},{10,... | collective-permute-start | bytes 393224 | tf_op jit(solution)/shard_map/ppermute | solution.py:231
  30.7 2.8 %collective-permute-start.16 = (bf16[256,256]{1,0:T(8,128)(2,1)S(1)}, bf16[256,256]{1,0:T(8,128)(2,1)S(1)}, u32[]{:S(2)}, u32[]{:S(2)}) collective-permute-start(bf16[256,256]{1,0:T(8,128)(2,1)S(1)} %collective-permute-done.13.rest_0_), channel_id=1, source_target_pairs={{0,1},{1,0},{2,3},{3,2},{4,5},{5,4},{6,7},{7,6},{8,9},{9,8},{10,11... | collective-permute-start | bytes 393224 | tf_op jit(solution)/shard_map/ppermute | solution.py:231
  31.7 1.8 %collective-permute-start.17 = (bf16[256,256]{1,0:T(8,128)(2,1)S(1)}, bf16[256,256]{1,0:T(8,128)(2,1)S(1)}, u32[]{:S(2)}, u32[]{:S(2)}) collective-permute-start(bf16[256,256]{1,0:T(8,128)(2,1)S(1)} %collective-permute-done.14.rest_1_), channel_id=1, source_target_pairs={{0,1},{1,0},{2,3},{3,2},{4,5},{5,4},{6,7},{7,6},{8,9},{9,8},{10,11... | collective-permute-start | bytes 393224 | tf_op jit(solution)/shard_map/ppermute | solution.py:231
  31.8 1.6 %collective-permute-start.18 = (bf16[256,256]{1,0:T(8,128)(2,1)S(1)}, bf16[256,256]{1,0:T(8,128)(2,1)S(1)}, u32[]{:S(2)}, u32[]{:S(2)}) collective-permute-start(bf16[256,256]{1,0:T(8,128)(2,1)S(1)} %collective-permute-done.15.rest_2_), channel_id=1, source_target_pairs={{0,1},{1,0},{2,3},{3,2},{4,5},{5,4},{6,7},{7,6},{8,9},{9,8},{10,11... | collective-permute-start | bytes 393224 | tf_op jit(solution)/shard_map/ppermute | solution.py:231
  32.2 1.3 %collective-permute-start.19 = (bf16[128,256]{1,0:T(8,128)(2,1)S(1)}, bf16[128,256]{1,0:T(8,128)(2,1)S(1)}, u32[]{:S(2)}, u32[]{:S(2)}) collective-permute-start(bf16[128,256]{1,0:T(8,128)(2,1)S(1)} %get-tuple-element.62), channel_id=1, source_target_pairs={{0,1},{1,0},{2,3},{3,2},{4,5},{5,4},{6,7},{7,6},{8,9},{9,8},{10,11... | collective-permute-start | bytes 196616 | tf_op jit(solution)/shard_map/ppermute | solution.py:231

commit v7 on v6

--- a/solution.py
+++ b/solution.py
@@ -100,58 +100,84 @@
         copy.wait()
 
 
-def relay_kernel(sub_count, d, near, far, out):
+def index_row(message, size):
+    return message[2 * size : 2 * size + EXTRA, :].astype(F32)[0:1, :]
+
+
+def lane_of(row, lane):
+    lanes = lax.broadcasted_iota(jnp.int32, row.shape, 1)
+    return jnp.sum(jnp.where(lanes == lane, row, 0.0), axis=1, keepdims=True)
+
+
+def pick(message, index, size):
+    return jnp.where(
+        index > 0.5, message[size : 2 * size, :].astype(F32), message[0:size, :].astype(F32)
+    ).astype(BF)
+
+
+def relay_kernel(sub_count, d, far, near, out):
     size = out.shape[0] - EXTRA
-    lanes = lax.broadcasted_iota(jnp.int32, (1, out.shape[1]), 1)
-    lane = sub_count + (lax.axis_index("cluster") ^ d)
-    row = near[2 * size : 2 * size + EXTRA, :].astype(F32)[0:1, :]
-    index = jnp.sum(jnp.where(lanes == lane, row, 0.0), axis=1, keepdims=True)
-    out[0:size, :] = jnp.where(
-        index > 0.5, far[size : 2 * size, :].astype(F32), far[0:size, :].astype(F32)
-    ).astype(BF)
+    index = lane_of(index_row(near, size), sub_count + (lax.axis_index("cluster") ^ d))
+    out[0:size, :] = pick(far, index, size)
     out[size:, :] = far[2 * size :, :]
 
 
-def halo_sum(choice, dense, own, slots, messages, halo):
+def trade_kernel(even, sibling, *rest):
+    messages, out = rest[:-1], rest[-1]
+    size = out.shape[0] // len(even) - EXTRA
+    row = index_row(sibling, size)
+    for i, (d, message) in enumerate(zip(even, messages)):
+        index = lane_of(row, lax.axis_index("sub") ^ d)
+        out[i * size : (i + 1) * size, :] = pick(message, index, size)
+        at = len(even) * size + i * EXTRA
+        out[at : at + EXTRA, :] = message[2 * size :, :]
+
+
+def turn_kernel(sibling, *rest):
+    messages, out = rest[:-1], rest[-1]
+    size = sibling.shape[0]
+    out[0:size, :] = sibling[...]
+    for i, message in enumerate(messages):
+        out[(i + 1) * size : (i + 2) * size, :] = message[size : 2 * size, :]
+
+
+def halo_sum(choice, dense, own, halos, refs, halo):
     size = dense.shape[0] // own
     columns = []
-    for i, (slot, message) in enumerate(zip(slots, messages)):
-        block = message[0:size, :]
-        if message.shape[0] > 2 * size:
-            block = jnp.where(
-                choice[slot : slot + 1, :] > 0.5,
-                message[size : 2 * size, :].astype(F32),
-                block.astype(F32),
-            ).astype(BF)
+    for i, (slot, at, row, picked) in enumerate(halos):
+        if picked:
+            block = refs[at][row : row + size, :]
+        else:
+            block = pick(refs[at], choice[slot : slot + 1, :], size)
         halo[i * size : (i + 1) * size, :] = block
         columns.append(dense[:, (own + slot) * size : (own + slot + 1) * size])
     return dot(jnp.concatenate(columns, axis=1), halo[...])
 
 
-def first_kernel(own, slots, choice, dense, features, w_self, bias, *rest):
+def first_kernel(own, halos, choice, dense, features, w_self, bias, *rest):
     refs, (total, own_pre, halo) = rest[:-3], rest[-3:]
     size = dense.shape[0] // own
     total[...] = dot(dense[:, 0 : own * size], features[...]) + halo_sum(
-        choice, dense, own, slots, refs, halo
+        choice, dense, own, halos, refs, halo
     )
     own_pre[...] = dot(features[...], w_self[...]) + bias[...].reshape(1, -1)
 
 
-def near_kernel(own, slots, choice, dense, before, *rest):
+def near_kernel(own, halos, choice, dense, before, *rest):
     refs, (total, halo) = rest[:-2], rest[-2:]
-    total[...] = before[...] + halo_sum(choice, dense, own, slots, refs, halo)
+    total[...] = before[...] + halo_sum(choice, dense, own, halos, refs, halo)
 
 
 def middle_kernel(
-    own, sub_count, cluster_count, slots,
+    own, sub_count, cluster_count, halos, received,
     choice, grad_out, w_neigh, dense, dense_t, before, own_pre, inverse,
     *rest,
 ):
-    refs, rest = rest[: len(slots)], rest[len(slots) :]
+    refs, rest = rest[:received], rest[received:]
     pairs, rest = rest[: sub_count // 2 - 1], rest[sub_count // 2 - 1 :]
     along, (sibling, kept, spread, grad_pre, halo) = rest[:-5], rest[-5:]
     size = dense.shape[0] // own
-    aggregate = before[...] + halo_sum(choice, dense, own, slots, refs, halo)
+    aggregate = before[...] + halo_sum(choice, dense, own, halos, refs, halo)
     inv = jnp.concatenate([inverse[...]] * (grad_out.shape[1] // size), axis=1)
     mean = (aggregate * inv).astype(BF)
     pre = own_pre[...] + dot(mean, w_neigh[...])
@@ -178,9 +204,9 @@
     total[size : 2 * size, :] = total[size : 2 * size, :] + jnp.where(second, value, zero)
 
 
-def own_kernel(own, sub_count, order, parts, *rest):
+def own_kernel(own, sub_count, rows, received, parts, *rest):
     back, rest = rest[: len(parts)], rest[len(parts) :]
-    received, rest = rest[: len(order)], rest[len(order) :]
+    messages, rest = rest[:received], rest[received:]
     choice, w_self, dense_t, kept, spread, grad_pre, total, owner = rest
     size = kept.shape[1]
     width = total.shape[1]
@@ -189,27 +215,24 @@
     )
     for i, slot in enumerate((0, sub_count)):
         split(total, kept[i].astype(F32), choice[slot : slot + 1, :] > 0.5, size)
-    lanes = lax.broadcasted_iota(jnp.int32, (1, width), 1)
-    for message, slot in zip(received, order):
+    for slot, at, row in rows:
         lane = lax.axis_index("sub")
         if slot > sub_count:
             lane = sub_count + lax.axis_index("cluster")
-        last = message.shape[0] - EXTRA
-        row = message[last : last + EXTRA, :].astype(F32)[0:1, :]
-        index = jnp.sum(jnp.where(lanes == lane, row, 0.0), axis=1, keepdims=True)
+        index = lane_of(messages[at][row : row + EXTRA, :].astype(F32)[0:1, :], lane)
         owner[slot : slot + 1, :] = jnp.broadcast_to(index, (1, width))
-    for message, (slot, row) in zip(back, parts):
-        value = message[row : row + size, :].astype(F32)
+    for slot, at, row in parts:
+        value = back[at][row : row + size, :].astype(F32)
         split(total, value, owner[slot : slot + 1, :] > 0.5, size)
 
 
-def add_kernel(own, parts, owner, total, *rest):
-    received, out = rest[:-1], rest[-1]
+def add_kernel(own, parts, owner, before, *rest):
+    received, total = rest[:-1], rest[-1]
     size = total.shape[0] // own
-    out[...] = total[...]
-    for message, (slot, row) in zip(received, parts):
-        value = message[row : row + size, :].astype(F32)
-        split(out, value, owner[slot : slot + 1, :] > 0.5, size)
+    total[...] = before[...]
+    for slot, at, row in parts:
+        value = received[at][row : row + size, :].astype(F32)
+        split(total, value, owner[slot : slot + 1, :] > 0.5, size)
 
 
 def final_kernel(own, parts, owner, total, *rest):
@@ -217,8 +240,8 @@
     size = total.shape[0] // own
     first = total[0:size, :]
     second = total[size : 2 * size, :]
-    for message, (slot, row) in zip(received, parts):
-        value = message[row : row + size, :].astype(F32)
+    for slot, at, row in parts:
+        value = received[at][row : row + size, :].astype(F32)
         to_second = owner[slot : slot + 1, :] > 0.5
         first = first + jnp.where(to_second, 0.0, value)
         second = second + jnp.where(to_second, value, 0.0)
@@ -285,15 +308,14 @@
     even = list(range(2, sub_count, 2))
     direct = list(range(2, cluster_count, 2))
     relayed = list(range(3, cluster_count, 2))
-    got = {0: edge, sub_count: edge}
+    rows_at = BOUNDARY * size
+    got = {0: (edge, 0, False, rows_at), sub_count: (edge, 0, False, rows_at)}
     for d in direct:
-        got[sub_count + d] = along(edge, d)
+        got[sub_count + d] = (along(edge, d), 0, False, rows_at)
     for d in even:
-        got[d] = across(edge, d)
-    got[sub_count + 1] = along(edge, 1)
-    got[1] = across(edge, 1)
-    start = tile_dst
-
+        got[d] = (across(edge, d), 0, False, rows_at)
+    got[sub_count + 1] = (along(edge, 1), 0, False, rows_at)
+    got[1] = (across(edge, 1), 0, False, rows_at)
     dense, dense_t, inverse, choice, features, w_self, w_neigh, grad_out, bias = pl.pallas_call(
         functools.partial(prepare_kernel, *counts),
         out_shape=[
@@ -318,51 +340,77 @@
             pltpu.SemaphoreType.DMA((10,)),
         ],
         compiler_params=PARAMS,
-        cost_estimate=cost(10**9, 6 * 1024 * 1024),
+        cost_estimate=cost(10**8, 6 * 1024 * 1024),
         name="prepare",
     )(
-        *map(in_hbm, (start, tile_src, recv_sub, recv_cluster, tile_weight)),
+        *map(in_hbm, (tile_dst, tile_src, recv_sub, recv_cluster, tile_weight)),
         *map(in_hbm, (features, w_self, w_neigh, grad_out, bias)),
     )
 
+    def call(kernel, out_shape, name, flops, *operands):
+        return pl.pallas_call(
+            kernel,
+            out_shape=out_shape,
+            in_specs=[VMEM] * len(operands),
+            out_specs=jax.tree.map(lambda _: VMEM, out_shape),
+            compiler_params=PARAMS,
+            cost_estimate=cost(flops, 1024 * 1024),
+            name=name,
+        )(*operands)
+
+    def unique(slots):
+        arrays, at = [], {}
+        for slot in slots:
+            known = [i for i, array in enumerate(arrays) if array is got[slot][0]]
+            at[slot] = known[0] if known else len(arrays)
+            if not known:
+                arrays.append(got[slot][0])
+        return arrays, at
+
     def sum_call(kernel, out_shape, name, slots, *operands):
+        arrays, at = unique(slots)
+        halos = [(slot, at[slot], got[slot][1], got[slot][2]) for slot in slots]
         return pl.pallas_call(
-            functools.partial(kernel, own, slots),
+            functools.partial(kernel, own, halos),
             out_shape=out_shape,
-            in_specs=[VMEM] * (len(operands) + len(slots)),
+            in_specs=[VMEM] * (len(operands) + len(arrays)),
             out_specs=jax.tree.map(lambda _: VMEM, out_shape),
             scratch_shapes=[pltpu.VMEM((len(slots) * size, width), BF)],
             compiler_params=PARAMS,
-            cost_estimate=cost(dict(first=10**9, near=10**9)[name], 3 * 1024 * 1024),
+            cost_estimate=cost(dict(first=10**9, near=10**10)[name], 3 * 1024 * 1024),
             name=name,
-        )(*operands, *[got[slot] for slot in slots])
+        )(*operands, *arrays)
 
     for d in relayed:
-        value = pl.pallas_call(
+        value = call(
             functools.partial(relay_kernel, sub_count, d - 1),
-            out_shape=jax.ShapeDtypeStruct((size + EXTRA, width), BF),
-            in_specs=[VMEM] * 2,
-            out_specs=VMEM,
-            compiler_params=PARAMS,
-            cost_estimate=cost(10**6, 256 * 1024),
-            name="relay",
-        )(got[sub_count + 1], got[sub_count + d - 1])
-        got[sub_count + d] = along(value, 1)
+            jax.ShapeDtypeStruct((size + EXTRA, width), BF),
+            "relay", 10**6, got[sub_count + d - 1][0], got[sub_count + 1][0],
+        )
+        got[sub_count + d] = (along(value, 1), 0, True, size)
     first_sum, own_pre = sum_call(
         first_kernel, [wide, wide], "first", [0, sub_count, *(sub_count + d for d in direct), sub_count + 1],
         choice, dense, features, w_self, bias,
     )
-    for d in even:
-        got[d + 1] = across(after(got[d], choice), 1)
-    near_sum = sum_call(near_kernel, wide, "near", even, choice, dense, first_sum)
-
-    late = [*(sub_count + d for d in relayed), *(d + 1 for d in even), 1]
+    value = call(
+        functools.partial(trade_kernel, even),
+        jax.ShapeDtypeStruct((len(even) * (size + EXTRA), width), BF),
+        "trade", 10**6, after(got[1][0], (own_pre, value)), *[got[d][0] for d in even],
+    )
+    value = across(value, 1)
+    for i, d in enumerate(even):
+        got[d + 1] = (value, i * size, True, len(even) * size + i * EXTRA)
+    near_sum = sum_call(near_kernel, wide, "near", [*even, 1, *(sub_count + d for d in relayed)], choice, dense, first_sum)
+
+    late = [d + 1 for d in even]
+    late_arrays, late_at = unique(late)
+    late_halos = [(slot, late_at[slot], got[slot][1], got[slot][2]) for slot in late]
     outs = pl.pallas_call(
-        functools.partial(middle_kernel, *counts, late),
+        functools.partial(middle_kernel, *counts, late_halos, len(late_arrays)),
         out_shape=[jax.ShapeDtypeStruct((2 * size, width), BF)] * len(even)
         + [block] * cluster_count
         + [jax.ShapeDtypeStruct((2, size, width), BF), narrow, narrow],
-        in_specs=[VMEM] * (8 + len(late)),
+        in_specs=[VMEM] * (8 + len(late_arrays)),
         out_specs=[VMEM] * (len(even) + cluster_count + 3),
         scratch_shapes=[pltpu.VMEM((len(late) * size, width), BF)],
         compiler_params=PARAMS,
@@ -370,56 +418,52 @@
         name="middle",
     )(
         choice, grad_out, w_neigh, dense, dense_t, near_sum, own_pre, inverse,
-        *[got[slot] for slot in late],
+        *late_arrays,
     )
     *sent, sibling, kept, spread, grad_pre = outs
 
-    back = [(along(sent[len(even) + d - 1], d), sub_count + d, 0) for d in range(1, cluster_count)]
-    direct_back = [(across(value, d), d, 0) for d, value in zip(even, sent)]
-    sibling_back = [(across(sibling, 1), 1, 0)]
-    early_back = back[::-1]
-
+    far = [(sub_count + d, along(sent[len(even) + d - 1], d)) for d in range(1, cluster_count)]
+    near = [(d, across(value, d)) for d, value in zip(even, sent)]
     order = [*even, *(sub_count + d for d in direct), *(d + 1 for d in even), 1, sub_count + 1, *(sub_count + d for d in relayed)]
+    arrays, at = unique(order)
+    early = far[:1:-1]
     total, owner = pl.pallas_call(
         functools.partial(
-            own_kernel, own, sub_count, order, [(slot, row) for _, slot, row in early_back]
+            own_kernel, own, sub_count, [(slot, at[slot], got[slot][3]) for slot in order],
+            len(arrays), [(slot, i, 0) for i, (slot, _) in enumerate(early)],
         ),
         out_shape=[wide, marks],
-        in_specs=[VMEM] * (6 + peers + len(early_back)),
+        in_specs=[VMEM] * (6 + len(arrays) + len(early)),
         out_specs=[VMEM] * 2,
         compiler_params=PARAMS,
-        cost_estimate=cost(10**10, 2 * 1024 * 1024),
+        cost_estimate=cost(10**9, 2 * 1024 * 1024),
         name="own",
     )(
-        *[value for value, _, _ in early_back],
-        *[got[slot] for slot in order],
+        *[value for _, value in early], *arrays,
         choice, w_self, dense_t, kept, spread, grad_pre,
     )
 
-    swapped_back = [
-        (across(after(value, total), 1), d + 1, size) for value, d, _ in direct_back
-    ]
-    middle_back = []
-    if middle_back:
-        total = pl.pallas_call(
-            functools.partial(add_kernel, own, [(slot, row) for _, slot, row in middle_back]),
-            out_shape=wide,
-            in_specs=[VMEM] * (2 + len(middle_back)),
-            out_specs=VMEM,
-            compiler_params=PARAMS,
-            cost_estimate=cost(10**9, 2 * 1024 * 1024),
-            name="add",
-        )(owner, total, *[value for value, _, _ in middle_back])
-    back = [*direct_back[::-1], *swapped_back[::-1], *sibling_back]
-    return pl.pallas_call(
-        functools.partial(final_kernel, own, [(slot, row) for _, slot, row in back]),
-        out_shape=narrow,
-        in_specs=[VMEM] * (2 + len(back)),
-        out_specs=VMEM,
-        compiler_params=PARAMS,
-        cost_estimate=cost(rows * width * 4, 2 * 1024 * 1024),
-        name="final",
-    )(owner, total, *[value for value, _, _ in back])
+    turned = call(
+        turn_kernel,
+        jax.ShapeDtypeStruct(((1 + len(even)) * size, width), BF),
+        "turn", 10**6, after(sibling, total), *[value for _, value in near],
+    )
+    turned = across(turned, 1)
+
+    more = [far[1], far[0]]
+    if more:
+        total = call(
+            functools.partial(add_kernel, own, [(slot, i, 0) for i, (slot, _) in enumerate(more)]),
+            wide, "add", 10**10, owner, total, *[value for _, value in more],
+        )
+    last = near[::-1]
+    parts = [(slot, i, 0) for i, (slot, _) in enumerate(last)]
+    parts += [(d + 1, len(last), (i + 1) * size) for i, d in enumerate(even)]
+    parts += [(1, len(last), 0)]
+    return call(
+        functools.partial(final_kernel, own, parts), narrow, "final", rows * width * 4,
+        owner, total, *[value for _, value in last], turned,
+    )
 
 
 def solution(mesh):

time: 34.5 us -> 33.3 us (0.965)
  waiting for transfers between devices: 8.53 us -> 7.68 us
  starting transfers between devices: 19.1 us -> 18.6 us
    ppermute x20 -> x15, waiting for transfers between devices: 8.53 us -> 7.68 us  [swap(): return lax.ppermute(value, axis, [(i, i ^ d) for i in range(count)])]
    ppermute x20 -> x15, starting transfers between devices: 19.1 us -> 18.6 us  [swap(): return lax.ppermute(value, axis, [(i, i ^ d) for i in range(count)])]
    pallas_call x6 -> x9, Pallas kernels: 3.52 us -> 3.62 us  [the longest x1 1.27 us: shards(): pl.pallas_call(functools.partial(middle_kernel, *counts, late_halos, len(...]
  transfers between devices with their start and end apart: 20 -> 15, of which waited for: 9 -> 8; matrix products, arithmetic and copies ran while one was open for 0% -> 0% of each run, Pallas kernels for 10% -> 11%
where the time goes in v7:
time: 33.3 us; the launch traced here: 33.2 us
  starting transfers between devices  18.6 us (56%)
  waiting for transfers between devices  7.68 us (23%)
  Pallas kernels  6.74 us (20%)
    ppermute x15, starting transfers between devices, swap(): return lax.ppermute(value, axis, [(i, i ^ d) for i in range(count)])  18.6 us
    ppermute x15, waiting for transfers between devices, swap(): return lax.ppermute(value, axis, [(i, i ^ d) for i in range(count)])  7.68 us
    pallas_call x1, Pallas kernels, shards(): pl.pallas_call(functools.partial(prepare_kernel, *counts), out_shape=[jax...  2.11 us
    pallas_call x1, Pallas kernels, shards(): pl.pallas_call(functools.partial(middle_kernel, *counts, late_halos, len(...  1.27 us
    pallas_call x5, Pallas kernels, call(): pl.pallas_call(kernel, out_shape=out_shape, in_specs=[VMEM] * len(operand...  1.2 us
    pallas_call x1, Pallas kernels, shards(): pl.pallas_call(edge_kernel, out_shape=jax.ShapeDtypeStruct((BOUNDARY * si...  1.01 us
    pallas_call x2, Pallas kernels, sum_call(): pl.pallas_call(functools.partial(kernel, own, halos), out_shape=out_shape...  0.81 us
  transfers between devices with their start and end apart: 15, of which 8 were waited for; matrix products, arithmetic and copies ran while one was open for 0% of the time, Pallas kernels for 11%

profile of v7, /device:TPU:0, one launch (start us, length us, event | category | flops | bytes accessed | tf_op | source)
XLA Modules:
  0.0 33.2 jit_solution(15450649057052883111)
XLA Ops:
  0.0 1.0 %edge.1.rest_0_ = bf16[272,256]{1,0:T(8,128)(2,1)S(1)} custom-call(s32[1,8]{1,0:T(1,128)} %recv_sub.1, s32[1,4]{1,0:T(1,128)} %recv_cluster.1, bf16[384,256]{1,0:T(8,128)(2,1)} %features.1), custom_call_target="tpu_custom_call" | custom-call | flops 1024 | bytes 262144 | tf_op jit(solution)/shard_map/edge/pallas_call | solution.py:287
  1.0 3.1 %collective-permute-start.1 = (bf16[272,256]{1,0:T(8,128)(2,1)S(1)}, bf16[272,256]{1,0:T(8,128)(2,1)S(1)}, u32[]{:S(2)}, u32[]{:S(2)}) collective-permute-start(bf16[272,256]{1,0:T(8,128)(2,1)S(1)} %edge.1.rest_0_), channel_id=1, source_target_pairs={{0,8},{8,0},{16,24},{24,16},{1,9},{9,1},{17,25},{25,17},{2,10},{10... | collective-permute-start | bytes 417800 | tf_op jit(solution)/shard_map/ppermute | solution.py:254
  4.1 2.6 %collective-permute-start = (bf16[272,256]{1,0:T(8,128)(2,1)S(1)}, bf16[272,256]{1,0:T(8,128)(2,1)S(1)}, u32[]{:S(2)}, u32[]{:S(2)}) collective-permute-start(bf16[272,256]{1,0:T(8,128)(2,1)S(1)} %edge.1.rest_0_), channel_id=1, source_target_pairs={{0,16},{8,24},{16,0},{24,8},{1,17},{9,25},{17,1},{25,9},{2,18},{10... | collective-permute-start | bytes 417800 | tf_op jit(solution)/shard_map/ppermute | solution.py:254
  6.7 0.0 collective-permute-start.5
  6.7 2.4 %collective-permute-start.4 = (bf16[272,256]{1,0:T(8,128)(2,1)S(1)}, bf16[272,256]{1,0:T(8,128)(2,1)S(1)}, u32[]{:S(2)}, u32[]{:S(2)}) collective-permute-start(bf16[272,256]{1,0:T(8,128)(2,1)S(1)} %edge.1.rest_0_), channel_id=1, source_target_pairs={{0,6},{1,7},{2,4},{3,5},{4,2},{5,3},{6,0},{7,1},{8,14},{9,15},{10,... | collective-permute-start | bytes 417800 | tf_op jit(solution)/shard_map/ppermute | solution.py:254
  9.1 0.5 %collective-permute-start.3 = (bf16[272,256]{1,0:T(8,128)(2,1)S(1)}, bf16[272,256]{1,0:T(8,128)(2,1)S(1)}, u32[]{:S(2)}, u32[]{:S(2)}) collective-permute-start(bf16[272,256]{1,0:T(8,128)(2,1)S(1)} %edge.1.rest_0_), channel_id=1, source_target_pairs={{0,4},{1,5},{2,6},{3,7},{4,0},{5,1},{6,2},{7,3},{8,12},{9,13},{10,... | collective-permute-start | bytes 417800 | tf_op jit(solution)/shard_map/ppermute | solution.py:254
  9.7 0.3 collective-permute-done.1.rest_2_.near.rest_7_
  10.0 1.8 %collective-permute-start.2 = (bf16[272,256]{1,0:T(8,128)(2,1)S(1)}, bf16[272,256]{1,0:T(8,128)(2,1)S(1)}, u32[]{:S(2)}, u32[]{:S(2)}) collective-permute-start(bf16[272,256]{1,0:T(8,128)(2,1)S(1)} %edge.1.rest_0_), channel_id=1, source_target_pairs={{0,2},{1,3},{2,0},{3,1},{4,6},{5,7},{6,4},{7,5},{8,10},{9,11},{10,... | collective-permute-start | bytes 417800 | tf_op jit(solution)/shard_map/ppermute | solution.py:254
  11.8 2.1 %prepare.1 = (bf16[384,1920]{1,0:T(8,128)(2,1)S(1)}, bf16[1920,384]{1,0:T(8,128)(2,1)S(1)}, f32[384,128]{1,0:T(8,128)S(1)}, f32[12,256]{1,0:T(8,128)S(1)}, bf16[...) custom-call(s32[24]{0:T(128)} %tile_dst_hbm.1, ...), custom_call_target="tpu_custom_call" | custom-call | flops 100000000 | bytes 6291456 | tf_op jit(solution)/shard_map/prepare/pallas_call | solution.py:319
  13.9 0.0 collective-permute-done.rest_1_.far.rest_4_
  13.9 0.1 relay.1
  14.0 0.1 collective-permute-start.6
  14.1 0.5 %first.1 = (f32[384,256]{1,0:T(8,128)S(1)}, f32[384,256]{1,0:T(8,128)S(1)}) custom-call(f32[12,256]{1,0:T(8,128)S(1)} %get-tuple-element.30.choice.rest_9_, bf16[384,1920]{1,0:T(8,128)(2,1)S(1)} %get-tuple-element.33.dense, bf16[384,256]{1,0:T(8,128)(2,1)S(1)} %get-tuple-element.35.features, bf16[256,256]{1,0:T(8,128)(2,1)S(1)} %get-tuple-element.36.w_self.rest_10_, ...), custom_call_target="tpu_custom_call" | custom-call | flops 1000000000 | bytes 3145728 | tf_op jit(solution)/shard_map/first/pallas_call | solution.py:373
  14.6 0.0 collective-permute-done.5.rest_3_.sibling.rest_6_
  14.6 0.0 collective-permute-done.4.rest_2_.rest_3_
  14.6 2.1 %collective-permute-done.3.rest_1_.rest_2_ = bf16[272,256]{1,0:T(8,128)(2,1)S(1)} collective-permute-done((bf16[272,256]{1,0:T(8,128)(2,1)S(1)}, bf16[272,256]{1,0:T(8,128)(2,1)S(1)}, u32[]{:S(2)}, u32[]{:S(2)}) %collective-permute-start.3) | collective-permute-done | bytes 139296 | tf_op jit(solution)/shard_map/ppermute | solution.py:254
  16.7 0.1 collective-permute-done.2.rest_0_.rest_1_
  16.8 0.1 trade.1
  16.9 0.1 collective-permute-start.7
  17.0 1.5 %collective-permute-done.6.rest_4_.rest_8_ = bf16[144,256]{1,0:T(8,128)(2,1)S(1)} collective-permute-done((bf16[144,256]{1,0:T(8,128)(2,1)S(1)}, bf16[144,256]{1,0:T(8,128)(2,1)S(1)}, u32[]{:S(2)}, u32[]{:S(2)}) %collective-permute-start.6) | collective-permute-done | bytes 73760 | tf_op jit(solution)/shard_map/ppermute | solution.py:254
  18.4 0.3 %near.1.before = f32[384,256]{1,0:T(8,128)S(1)} custom-call(f32[12,256]{1,0:T(8,128)S(1)} %get-tuple-element.30.choice.rest_9_, bf16[384,1920]{1,0:T(8,128)(2,1)S(1)} %get-tuple-element.33.dense, f32[384,256]{1,0:T(8,128)S(1)} %get-tuple-element.38.before, bf16[272,256]{1,0:T(8,128)(2,1)S(1)} %collective-permute-done.2.rest_0_.rest_1_, ...), custom_call_target="tpu_custom_call" | custom-call | flops 10000000000 | bytes 3145728 | tf_op jit(solution)/shard_map/near/pallas_call | solution.py:373
  18.8 0.0 collective-permute-done.7.rest_0_.rest_5_
  18.8 1.3 %middle.1 = (bf16[256,256]{1,0:T(8,128)(2,1)S(1)}, bf16[256,256]{1,0:T(8,128)(2,1)S(1)}, bf16[256,256]{1,0:T(8,128)(2,1)S(1)}, bf16[128,256]{1,0:T(8,128)(2,1)S(...) custom-call(f32[12,256]{1,0:T(8,128)S(1)} %get-tuple-element.30.choi, ...), custom_call_target="tpu_custom_call" | custom-call | flops 377487360 | bytes 6291456 | tf_op jit(solution)/shard_map/middle/pallas_call | solution.py:408
  20.1 3.1 %collective-permute-start.8 = (bf16[128,256]{1,0:T(8,128)(2,1)S(1)}, bf16[128,256]{1,0:T(8,128)(2,1)S(1)}, u32[]{:S(2)}, u32[]{:S(2)}) collective-permute-start(bf16[128,256]{1,0:T(8,128)(2,1)S(1)} %get-tuple-element.42), channel_id=1, source_target_pairs={{0,24},{8,16},{16,8},{24,0},{1,25},{9,17},{17,9},{25,1},{2,26},{10... | collective-permute-start | bytes 196616 | tf_op jit(solution)/shard_map/ppermute | solution.py:254
  23.1 1.5 %collective-permute-start.11 = (bf16[256,256]{1,0:T(8,128)(2,1)S(1)}, bf16[256,256]{1,0:T(8,128)(2,1)S(1)}, u32[]{:S(2)}, u32[]{:S(2)}) collective-permute-start(bf16[256,256]{1,0:T(8,128)(2,1)S(1)} %get-tuple-element.50), channel_id=1, source_target_pairs={{0,6},{1,7},{2,4},{3,5},{4,2},{5,3},{6,0},{7,1},{8,14},{9,15},{10,... | collective-permute-start | bytes 393224 | tf_op jit(solution)/shard_map/ppermute | solution.py:254
  24.6 0.5 %collective-permute-start.12 = (bf16[256,256]{1,0:T(8,128)(2,1)S(1)}, bf16[256,256]{1,0:T(8,128)(2,1)S(1)}, u32[]{:S(2)}, u32[]{:S(2)}) collective-permute-start(bf16[256,256]{1,0:T(8,128)(2,1)S(1)} %get-tuple-element.51), channel_id=1, source_target_pairs={{0,4},{1,5},{2,6},{3,7},{4,0},{5,1},{6,2},{7,3},{8,12},{9,13},{10,... | collective-permute-start | bytes 393224 | tf_op jit(solution)/shard_map/ppermute | solution.py:254
  25.1 1.5 %collective-permute-start.13 = (bf16[256,256]{1,0:T(8,128)(2,1)S(1)}, bf16[256,256]{1,0:T(8,128)(2,1)S(1)}, u32[]{:S(2)}, u32[]{:S(2)}) collective-permute-start(bf16[256,256]{1,0:T(8,128)(2,1)S(1)} %get-tuple-element.52), channel_id=1, source_target_pairs={{0,2},{1,3},{2,0},{3,1},{4,6},{5,7},{6,4},{7,5},{8,10},{9,11},{10,... | collective-permute-start | bytes 393224 | tf_op jit(solution)/shard_map/ppermute | solution.py:254
  26.6 0.0 collective-permute-start.9
  26.6 0.0 collective-permute-done.8.rest_0_
  26.6 1.4 %collective-permute-start.10 = (bf16[128,256]{1,0:T(8,128)(2,1)S(1)}, bf16[128,256]{1,0:T(8,128)(2,1)S(1)}, u32[]{:S(2)}, u32[]{:S(2)}) collective-permute-start(bf16[128,256]{1,0:T(8,128)(2,1)S(1)} %get-tuple-element.49), channel_id=1, source_target_pairs={{0,8},{8,0},{16,24},{24,16},{1,9},{9,1},{17,25},{25,17},{2,10},{10... | collective-permute-start | bytes 196616 | tf_op jit(solution)/shard_map/ppermute | solution.py:254
  28.0 0.3 %own.1 = (f32[384,256]{1,0:T(8,128)S(1)}, f32[12,256]{1,0:T(8,128)S(1)}) custom-call(bf16[128,256]{1,0:T(8,128)(2,1)S(1)} %collective-permute-done.8.rest_0_, bf16[272,256]{1,0:T(8,128)(2,1)S(1)} %collective-permute-done.2.rest_0_.rest_1_, bf16[272,256]{1,0:T(8,128)(2,1)S(1)} %collective-permute-done.3.rest_1_.rest_2_, ...), custom_call_target="tpu_custom_call" | custom-call | flops 1000000000 | bytes 2097152 | tf_op jit(solution)/shard_map/own/pallas_call | solution.py:430
  28.4 1.7 %collective-permute-done.11.rest_2_.rest_0_ = bf16[256,256]{1,0:T(8,128)(2,1)S(1)} collective-permute-done((bf16[256,256]{1,0:T(8,128)(2,1)S(1)}, bf16[256,256]{1,0:T(8,128)(2,1)S(1)}, u32[]{:S(2)}, u32[]{:S(2)}) %collective-permute-start.11) | collective-permute-done | bytes 131104 | tf_op jit(solution)/shard_map/ppermute | solution.py:254
  30.1 0.6 %collective-permute-done.12.rest_1_ = bf16[256,256]{1,0:T(8,128)(2,1)S(1)} collective-permute-done((bf16[256,256]{1,0:T(8,128)(2,1)S(1)}, bf16[256,256]{1,0:T(8,128)(2,1)S(1)}, u32[]{:S(2)}, u32[]{:S(2)}) %collective-permute-start.12) | collective-permute-done | bytes 131104 | tf_op jit(solution)/shard_map/ppermute | solution.py:254
  30.7 0.0 collective-permute-done.13.rest_0_.rest_2_
  30.7 0.1 collective-permute-start.14
  30.8 1.0 %collective-permute-done.9.rest_0_ = bf16[128,256]{1,0:T(8,128)(2,1)S(1)} collective-permute-done((bf16[128,256]{1,0:T(8,128)(2,1)S(1)}, bf16[128,256]{1,0:T(8,128)(2,1)S(1)}, u32[]{:S(2)}, u32[]{:S(2)}) %collective-permute-start.9) | collective-permute-done | bytes 65568 | tf_op jit(solution)/shard_map/ppermute | solution.py:254
  31.8 0.0 collective-permute-done.10.rest_1_
  31.8 0.1 add.1.total
  31.9 0.4 %collective-permute-done.14.rest_3_ = bf16[512,256]{1,0:T(8,128)(2,1)S(1)} collective-permute-done((bf16[512,256]{1,0:T(8,128)(2,1)S(1)}, bf16[512,256]{1,0:T(8,128)(2,1)S(1)}, u32[]{:S(2)}, u32[]{:S(2)}) %collective-permute-start.14) | collective-permute-done | bytes 262176 | tf_op jit(solution)/shard_map/ppermute | solution.py:254
  32.3 0.9 %final.1 = bf16[384,256]{1,0:T(8,128)(2,1)} custom-call(f32[12,256]{1,0:T(8,128)S(1)} %get-tuple-element.46.owner, f32[384,256]{1,0:T(8,128)S(1)} %add.1.total, bf16[256,256]{1,0:T(8,128)(2,1)S(1)} %collective-permute-done.11.rest_2_.rest_0_, bf16[256,256]{1,0:T(8,128)(2,1)S(1)} %collective-permute-done.12.rest_1_, ...), custom_call_target="tpu_custom_call" | custom-call | flops 393216 | bytes 1048576 | tf_op jit(solution)/shard_map/final/pallas_call | solution.py:351
  (1 shorter events, 0.0 us)
Async XLA Ops:
  1.0 9.0 %collective-permute-start.1 = (bf16[272,256]{1,0:T(8,128)(2,1)S(1)}, bf16[272,256]{1,0:T(8,128)(2,1)S(1)}, u32[]{:S(2)}, u32[]{:S(2)}) collective-permute-start(bf16[272,256]{1,0:T(8,128)(2,1)S(1)} %edge.1.rest_0_), channel_id=1, source_target_pairs={{0,8},{8,0},{16,24},{24,16},{1,9},{9,1},{17,25},{25,17},{2,10},{10... | collective-permute-start | bytes 417800 | tf_op jit(solution)/shard_map/ppermute | solution.py:254
  4.1 9.8 %collective-permute-start = (bf16[272,256]{1,0:T(8,128)(2,1)S(1)}, bf16[272,256]{1,0:T(8,128)(2,1)S(1)}, u32[]{:S(2)}, u32[]{:S(2)}) collective-permute-start(bf16[272,256]{1,0:T(8,128)(2,1)S(1)} %edge.1.rest_0_), channel_id=1, source_target_pairs={{0,16},{8,24},{16,0},{24,8},{1,17},{9,25},{17,1},{25,9},{2,18},{10... | collective-permute-start | bytes 417800 | tf_op jit(solution)/shard_map/ppermute | solution.py:254
  6.7 7.9 %collective-permute-start.5 = (bf16[272,256]{1,0:T(8,128)(2,1)S(1)}, bf16[272,256]{1,0:T(8,128)(2,1)S(1)}, u32[]{:S(2)}, u32[]{:S(2)}) collective-permute-start(bf16[272,256]{1,0:T(8,128)(2,1)S(1)} %edge.1.rest_0_), channel_id=1, source_target_pairs={{0,1},{1,0},{2,3},{3,2},{4,5},{5,4},{6,7},{7,6},{8,9},{9,8},{10,11... | collective-permute-start | bytes 417800 | tf_op jit(solution)/shard_map/ppermute | solution.py:254
  6.7 7.9 %collective-permute-start.4 = (bf16[272,256]{1,0:T(8,128)(2,1)S(1)}, bf16[272,256]{1,0:T(8,128)(2,1)S(1)}, u32[]{:S(2)}, u32[]{:S(2)}) collective-permute-start(bf16[272,256]{1,0:T(8,128)(2,1)S(1)} %edge.1.rest_0_), channel_id=1, source_target_pairs={{0,6},{1,7},{2,4},{3,5},{4,2},{5,3},{6,0},{7,1},{8,14},{9,15},{10,... | collective-permute-start | bytes 417800 | tf_op jit(solution)/shard_map/ppermute | solution.py:254
  9.1 7.5 %collective-permute-start.3 = (bf16[272,256]{1,0:T(8,128)(2,1)S(1)}, bf16[272,256]{1,0:T(8,128)(2,1)S(1)}, u32[]{:S(2)}, u32[]{:S(2)}) collective-permute-start(bf16[272,256]{1,0:T(8,128)(2,1)S(1)} %edge.1.rest_0_), channel_id=1, source_target_pairs={{0,4},{1,5},{2,6},{3,7},{4,0},{5,1},{6,2},{7,3},{8,12},{9,13},{10,... | collective-permute-start | bytes 417800 | tf_op jit(solution)/shard_map/ppermute | solution.py:254
  10.0 6.8 %collective-permute-start.2 = (bf16[272,256]{1,0:T(8,128)(2,1)S(1)}, bf16[272,256]{1,0:T(8,128)(2,1)S(1)}, u32[]{:S(2)}, u32[]{:S(2)}) collective-permute-start(bf16[272,256]{1,0:T(8,128)(2,1)S(1)} %edge.1.rest_0_), channel_id=1, source_target_pairs={{0,2},{1,3},{2,0},{3,1},{4,6},{5,7},{6,4},{7,5},{8,10},{9,11},{10,... | collective-permute-start | bytes 417800 | tf_op jit(solution)/shard_map/ppermute | solution.py:254
  14.0 4.4 %collective-permute-start.6 = (bf16[144,256]{1,0:T(8,128)(2,1)S(1)}, bf16[144,256]{1,0:T(8,128)(2,1)S(1)}, u32[]{:S(2)}, u32[]{:S(2)}) collective-permute-start(bf16[144,256]{1,0:T(8,128)(2,1)S(1)} %relay.1), channel_id=1, source_target_pairs={{0,8},{8,0},{16,24},{24,16},{1,9},{9,1},{17,25},{25,17},{2,10},{10... | collective-permute-start | bytes 221192 | tf_op jit(solution)/shard_map/ppermute | solution.py:254
  16.9 1.9 %collective-permute-start.7 = (bf16[432,256]{1,0:T(8,128)(2,1)S(1)}, bf16[432,256]{1,0:T(8,128)(2,1)S(1)}, u32[]{:S(2)}, u32[]{:S(2)}) collective-permute-start(bf16[432,256]{1,0:T(8,128)(2,1)S(1)} %trade.1), channel_id=1, source_target_pairs={{0,1},{1,0},{2,3},{3,2},{4,5},{5,4},{6,7},{7,6},{8,9},{9,8},{10,11... | collective-permute-start | bytes 663560 | tf_op jit(solution)/shard_map/ppermute | solution.py:254
  20.1 6.6 %collective-permute-start.8 = (bf16[128,256]{1,0:T(8,128)(2,1)S(1)}, bf16[128,256]{1,0:T(8,128)(2,1)S(1)}, u32[]{:S(2)}, u32[]{:S(2)}) collective-permute-start(bf16[128,256]{1,0:T(8,128)(2,1)S(1)} %get-tuple-element.42), channel_id=1, source_target_pairs={{0,24},{8,16},{16,8},{24,0},{1,25},{9,17},{17,9},{25,1},{2,26},{10... | collective-permute-start | bytes 196616 | tf_op jit(solution)/shard_map/ppermute | solution.py:254
  23.1 6.9 %collective-permute-start.11 = (bf16[256,256]{1,0:T(8,128)(2,1)S(1)}, bf16[256,256]{1,0:T(8,128)(2,1)S(1)}, u32[]{:S(2)}, u32[]{:S(2)}) collective-permute-start(bf16[256,256]{1,0:T(8,128)(2,1)S(1)} %get-tuple-element.50), channel_id=1, source_target_pairs={{0,6},{1,7},{2,4},{3,5},{4,2},{5,3},{6,0},{7,1},{8,14},{9,15},{10,... | collective-permute-start | bytes 393224 | tf_op jit(solution)/shard_map/ppermute | solution.py:254
  24.6 6.0 %collective-permute-start.12 = (bf16[256,256]{1,0:T(8,128)(2,1)S(1)}, bf16[256,256]{1,0:T(8,128)(2,1)S(1)}, u32[]{:S(2)}, u32[]{:S(2)}) collective-permute-start(bf16[256,256]{1,0:T(8,128)(2,1)S(1)} %get-tuple-element.51), channel_id=1, source_target_pairs={{0,4},{1,5},{2,6},{3,7},{4,0},{5,1},{6,2},{7,3},{8,12},{9,13},{10,... | collective-permute-start | bytes 393224 | tf_op jit(solution)/shard_map/ppermute | solution.py:254
  25.1 5.5 %collective-permute-start.13 = (bf16[256,256]{1,0:T(8,128)(2,1)S(1)}, bf16[256,256]{1,0:T(8,128)(2,1)S(1)}, u32[]{:S(2)}, u32[]{:S(2)}) collective-permute-start(bf16[256,256]{1,0:T(8,128)(2,1)S(1)} %get-tuple-element.52), channel_id=1, source_target_pairs={{0,2},{1,3},{2,0},{3,1},{4,6},{5,7},{6,4},{7,5},{8,10},{9,11},{10,... | collective-permute-start | bytes 393224 | tf_op jit(solution)/shard_map/ppermute | solution.py:254
  26.6 5.2 %collective-permute-start.9 = (bf16[128,256]{1,0:T(8,128)(2,1)S(1)}, bf16[128,256]{1,0:T(8,128)(2,1)S(1)}, u32[]{:S(2)}, u32[]{:S(2)}) collective-permute-start(bf16[128,256]{1,0:T(8,128)(2,1)S(1)} %get-tuple-element.48), channel_id=1, source_target_pairs={{0,16},{8,24},{16,0},{24,8},{1,17},{9,25},{17,1},{25,9},{2,18},{10... | collective-permute-start | bytes 196616 | tf_op jit(solution)/shard_map/ppermute | solution.py:254
  26.6 5.2 %collective-permute-start.10 = (bf16[128,256]{1,0:T(8,128)(2,1)S(1)}, bf16[128,256]{1,0:T(8,128)(2,1)S(1)}, u32[]{:S(2)}, u32[]{:S(2)}) collective-permute-start(bf16[128,256]{1,0:T(8,128)(2,1)S(1)} %get-tuple-element.49), channel_id=1, source_target_pairs={{0,8},{8,0},{16,24},{24,16},{1,9},{9,1},{17,25},{25,17},{2,10},{10... | collective-permute-start | bytes 196616 | tf_op jit(solution)/shard_map/ppermute | solution.py:254
  30.7 1.6 %collective-permute-start.14 = (bf16[512,256]{1,0:T(8,128)(2,1)S(1)}, bf16[512,256]{1,0:T(8,128)(2,1)S(1)}, u32[]{:S(2)}, u32[]{:S(2)}) collective-permute-start(bf16[512,256]{1,0:T(8,128)(2,1)S(1)} %turn.1), channel_id=1, source_target_pairs={{0,1},{1,0},{2,3},{3,2},{4,5},{5,4},{6,7},{7,6},{8,9},{9,8},{10,11... | collective-permute-start | bytes 786440 | tf_op jit(solution)/shard_map/ppermute | solution.py:254

commit v8 on v7

--- a/solution.py
+++ b/solution.py
@@ -30,7 +30,7 @@
     return 0.5 * (1.0 + t) + (0.5 * scale) * v * (1.0 - t * t) * (1.0 + 3.0 * 0.044715 * v * v)
 
 
-def edge_kernel(recv_sub, recv_cluster, features, edge, sub_row, cluster_row, sems):
+def edge_kernel(recv_sub, recv_cluster, features, edge, rows, sub_row, cluster_row, sems):
     count = edge.shape[0] - EXTRA
     copies = [
         pltpu.make_async_copy(features.at[0:count, :], edge.at[0:count, :], sems.at[0]),
@@ -39,12 +39,15 @@
     ]
     for copy in copies:
         copy.start()
-    for copy in copies:
-        copy.wait()
+    copies[1].wait()
+    copies[2].wait()
     sub_count, cluster_count = sub_row.shape[1], cluster_row.shape[1]
     pad = jnp.zeros((1, edge.shape[1] - sub_count - cluster_count), F32)
     row = jnp.concatenate([sub_row[...].astype(F32), cluster_row[...].astype(F32), pad], axis=1)
-    edge[count:, :] = jnp.broadcast_to(row, (EXTRA, edge.shape[1])).astype(BF)
+    value = jnp.broadcast_to(row, rows.shape).astype(BF)
+    edge[count:, :] = value
+    rows[...] = value
+    copies[0].wait()
 
 
 def prepare_kernel(
@@ -122,10 +125,10 @@
     out[size:, :] = far[2 * size :, :]
 
 
-def trade_kernel(even, sibling, *rest):
-    messages, out = rest[:-1], rest[-1]
+def trade_kernel(even, *rest):
+    messages, (sibling, out) = rest[:-2], rest[-2:]
     size = out.shape[0] // len(even) - EXTRA
-    row = index_row(sibling, size)
+    row = sibling[...].astype(F32)[0:1, :]
     for i, (d, message) in enumerate(zip(even, messages)):
         index = lane_of(row, lax.axis_index("sub") ^ d)
         out[i * size : (i + 1) * size, :] = pick(message, index, size)
@@ -133,12 +136,11 @@
         out[at : at + EXTRA, :] = message[2 * size :, :]
 
 
-def turn_kernel(sibling, *rest):
+def turn_kernel(*rest):
     messages, out = rest[:-1], rest[-1]
-    size = sibling.shape[0]
-    out[0:size, :] = sibling[...]
+    size = out.shape[0] // len(messages)
     for i, message in enumerate(messages):
-        out[(i + 1) * size : (i + 2) * size, :] = message[size : 2 * size, :]
+        out[i * size : (i + 1) * size, :] = message[size : 2 * size, :]
 
 
 def halo_sum(choice, dense, own, halos, refs, halo):
@@ -284,11 +286,14 @@
     block = jax.ShapeDtypeStruct((size, width), BF)
     marks = jax.ShapeDtypeStruct((sub_count + cluster_count, width), F32)
 
-    edge = pl.pallas_call(
+    edge, rows_only = pl.pallas_call(
         edge_kernel,
-        out_shape=jax.ShapeDtypeStruct((BOUNDARY * size + EXTRA, width), BF),
+        out_shape=[
+            jax.ShapeDtypeStruct((BOUNDARY * size + EXTRA, width), BF),
+            jax.ShapeDtypeStruct((EXTRA, width), BF),
+        ],
         in_specs=[HBM] * 3,
-        out_specs=VMEM,
+        out_specs=[VMEM] * 2,
         scratch_shapes=[
             pltpu.VMEM(recv_sub.shape, jnp.int32),
             pltpu.VMEM(recv_cluster.shape, jnp.int32),
@@ -315,7 +320,7 @@
     for d in even:
         got[d] = (across(edge, d), 0, False, rows_at)
     got[sub_count + 1] = (along(edge, 1), 0, False, rows_at)
-    got[1] = (across(edge, 1), 0, False, rows_at)
+    sibling_rows = across(rows_only, 1)
     dense, dense_t, inverse, choice, features, w_self, w_neigh, grad_out, bias = pl.pallas_call(
         functools.partial(prepare_kernel, *counts),
         out_shape=[
@@ -377,7 +382,7 @@
             out_specs=jax.tree.map(lambda _: VMEM, out_shape),
             scratch_shapes=[pltpu.VMEM((len(slots) * size, width), BF)],
             compiler_params=PARAMS,
-            cost_estimate=cost(dict(first=10**9, near=10**10)[name], 3 * 1024 * 1024),
+            cost_estimate=cost(dict(first=10**9, near=10**9, late=10**10)[name], 3 * 1024 * 1024),
             name=name,
         )(*operands, *arrays)
 
@@ -392,17 +397,21 @@
         first_kernel, [wide, wide], "first", [0, sub_count, *(sub_count + d for d in direct), sub_count + 1],
         choice, dense, features, w_self, bias,
     )
+    traded = [0, *even]
     value = call(
-        functools.partial(trade_kernel, even),
-        jax.ShapeDtypeStruct((len(even) * (size + EXTRA), width), BF),
-        "trade", 10**6, after(got[1][0], (own_pre, value)), *[got[d][0] for d in even],
+        functools.partial(trade_kernel, traded),
+        jax.ShapeDtypeStruct((len(traded) * (size + EXTRA), width), BF),
+        "trade", 10**6, *[got[d][0] for d in traded], after(sibling_rows, (own_pre, value)),
     )
     value = across(value, 1)
-    for i, d in enumerate(even):
-        got[d + 1] = (value, i * size, True, len(even) * size + i * EXTRA)
-    near_sum = sum_call(near_kernel, wide, "near", [*even, 1, *(sub_count + d for d in relayed)], choice, dense, first_sum)
-
-    late = [d + 1 for d in even]
+    for i, d in enumerate(traded):
+        got[d + 1] = (value, i * size, True, len(traded) * size + i * EXTRA)
+    near_sum = sum_call(near_kernel, wide, "near", even, choice, dense, first_sum)
+    if relayed:
+        slots_late = [sub_count + d for d in relayed]
+        near_sum = sum_call(near_kernel, wide, "late", slots_late, choice, dense, near_sum)
+
+    late = [1, *(d + 1 for d in even)]
     late_arrays, late_at = unique(late)
     late_halos = [(slot, late_at[slot], got[slot][1], got[slot][2]) for slot in late]
     outs = pl.pallas_call(
@@ -424,7 +433,8 @@
 
     far = [(sub_count + d, along(sent[len(even) + d - 1], d)) for d in range(1, cluster_count)]
     near = [(d, across(value, d)) for d, value in zip(even, sent)]
-    order = [*even, *(sub_count + d for d in direct), *(d + 1 for d in even), 1, sub_count + 1, *(sub_count + d for d in relayed)]
+    beside = (1, across(sibling, 1))
+    order = [sub_count + 1, *(sub_count + d for d in direct), *even, *(d + 1 for d in even), 1, *(sub_count + d for d in relayed)]
     arrays, at = unique(order)
     early = far[:1:-1]
     total, owner = pl.pallas_call(
@@ -445,21 +455,20 @@
 
     turned = call(
         turn_kernel,
-        jax.ShapeDtypeStruct(((1 + len(even)) * size, width), BF),
-        "turn", 10**6, after(sibling, total), *[value for _, value in near],
+        jax.ShapeDtypeStruct((len(even) * size, width), BF),
+        "turn", 10**6, *[after(value, total) for _, value in near],
     )
     turned = across(turned, 1)
 
-    more = [far[1], far[0]]
+    more = [far[1], far[0], beside, *near[::-1]]
     if more:
         total = call(
             functools.partial(add_kernel, own, [(slot, i, 0) for i, (slot, _) in enumerate(more)]),
             wide, "add", 10**10, owner, total, *[value for _, value in more],
         )
-    last = near[::-1]
+    last = []
     parts = [(slot, i, 0) for i, (slot, _) in enumerate(last)]
-    parts += [(d + 1, len(last), (i + 1) * size) for i, d in enumerate(even)]
-    parts += [(1, len(last), 0)]
+    parts += [(d + 1, len(last), i * size) for i, d in enumerate(even)]
     return call(
         functools.partial(final_kernel, own, parts), narrow, "final", rows * width * 4,
         owner, total, *[value for _, value in last], turned,

time: 33.3 us -> 33.1 us (level)
  starting transfers between devices: 18.6 us -> 16.6 us
  waiting for transfers between devices: 7.68 us -> 9.36 us
    ppermute x15 -> x16, starting transfers between devices: 18.6 us -> 16.6 us  [swap(): return lax.ppermute(value, axis, [(i, i ^ d) for i in range(count)])]
    ppermute x15 -> x16, waiting for transfers between devices: 7.68 us -> 9.36 us  [swap(): return lax.ppermute(value, axis, [(i, i ^ d) for i in range(count)])]
    pallas_call x2 -> x3, Pallas kernels: 0.81 us -> 0.93 us  [sum_call(): pl.pallas_call(functools.partial(kernel, own, halos), out_shape=out_shape...]
  transfers between devices with their start and end apart: 15 -> 16, of which waited for: 8 -> 9; matrix products, arithmetic and copies ran while one was open for 0% -> 0% of each run, Pallas kernels for 11% -> 12%
where the time goes in v8:
time: 33.1 us; the launch traced here: 32.9 us
  starting transfers between devices  16.6 us (50%)
  waiting for transfers between devices  9.36 us (28%)
  Pallas kernels  6.79 us (21%)
    ppermute x16, starting transfers between devices, swap(): return lax.ppermute(value, axis, [(i, i ^ d) for i in range(count)])  16.6 us
    ppermute x16, waiting for transfers between devices, swap(): return lax.ppermute(value, axis, [(i, i ^ d) for i in range(count)])  9.36 us
    pallas_call x1, Pallas kernels, shards(): pl.pallas_call(functools.partial(prepare_kernel, *counts), out_shape=[jax...  2.11 us
    pallas_call x1, Pallas kernels, shards(): pl.pallas_call(functools.partial(middle_kernel, *counts, late_halos, len(...  1.25 us
    pallas_call x5, Pallas kernels, call(): pl.pallas_call(kernel, out_shape=out_shape, in_specs=[VMEM] * len(operand...  1.22 us
    pallas_call x3, Pallas kernels, sum_call(): pl.pallas_call(functools.partial(kernel, own, halos), out_shape=out_shape...  0.93 us
    pallas_call x1, Pallas kernels, shards(): pl.pallas_call(edge_kernel, out_shape=[jax.ShapeDtypeStruct((BOUNDARY * s...  0.93 us
  transfers between devices with their start and end apart: 16, of which 9 were waited for; matrix products, arithmetic and copies ran while one was open for 0% of the time, Pallas kernels for 12%

profile of v8, /device:TPU:0, one launch (start us, length us, event | category | flops | bytes accessed | tf_op | source)
XLA Modules:
  0.0 32.9 jit_solution(15302659074995760205)
XLA Ops:
  0.0 0.9 %edge.1 = (bf16[272,256]{1,0:T(8,128)(2,1)S(1)}, bf16[16,256]{1,0:T(8,128)(2,1)S(1)}) custom-call(s32[1,8]{1,0:T(1,128)} %recv_sub.1, s32[1,4]{1,0:T(1,128)} %recv_cluster.1, bf16[384,256]{1,0:T(8,128)(2,1)} %features.1), custom_call_target="tpu_custom_call" | custom-call | flops 1024 | bytes 262144 | tf_op jit(solution)/shard_map/edge/pallas_call | solution.py:289
  0.9 3.1 %collective-permute-start.1 = (bf16[272,256]{1,0:T(8,128)(2,1)S(1)}, bf16[272,256]{1,0:T(8,128)(2,1)S(1)}, u32[]{:S(2)}, u32[]{:S(2)}) collective-permute-start(bf16[272,256]{1,0:T(8,128)(2,1)S(1)} %get-tuple-element.42.rest_0_), channel_id=1, source_target_pairs={{0,8},{8,0},{16,24},{24,16},{1,9},{9,1},{17,25},{25,17},{2,10},{10... | collective-permute-start | bytes 417800 | tf_op jit(solution)/shard_map/ppermute | solution.py:256
  4.0 2.6 %collective-permute-start = (bf16[272,256]{1,0:T(8,128)(2,1)S(1)}, bf16[272,256]{1,0:T(8,128)(2,1)S(1)}, u32[]{:S(2)}, u32[]{:S(2)}) collective-permute-start(bf16[272,256]{1,0:T(8,128)(2,1)S(1)} %get-tuple-element.42.rest_0_), channel_id=1, source_target_pairs={{0,16},{8,24},{16,0},{24,8},{1,17},{9,25},{17,1},{25,9},{2,18},{10... | collective-permute-start | bytes 417800 | tf_op jit(solution)/shard_map/ppermute | solution.py:256
  6.6 2.4 %collective-permute-start.4 = (bf16[272,256]{1,0:T(8,128)(2,1)S(1)}, bf16[272,256]{1,0:T(8,128)(2,1)S(1)}, u32[]{:S(2)}, u32[]{:S(2)}) collective-permute-start(bf16[272,256]{1,0:T(8,128)(2,1)S(1)} %get-tuple-element.42.rest_0_), channel_id=1, source_target_pairs={{0,6},{1,7},{2,4},{3,5},{4,2},{5,3},{6,0},{7,1},{8,14},{9,15},{10,... | collective-permute-start | bytes 417800 | tf_op jit(solution)/shard_map/ppermute | solution.py:256
  9.1 0.5 %collective-permute-start.3 = (bf16[272,256]{1,0:T(8,128)(2,1)S(1)}, bf16[272,256]{1,0:T(8,128)(2,1)S(1)}, u32[]{:S(2)}, u32[]{:S(2)}) collective-permute-start(bf16[272,256]{1,0:T(8,128)(2,1)S(1)} %get-tuple-element.42.rest_0_), channel_id=1, source_target_pairs={{0,4},{1,5},{2,6},{3,7},{4,0},{5,1},{6,2},{7,3},{8,12},{9,13},{10,... | collective-permute-start | bytes 417800 | tf_op jit(solution)/shard_map/ppermute | solution.py:256
  9.6 0.5 %collective-permute-start.2 = (bf16[272,256]{1,0:T(8,128)(2,1)S(1)}, bf16[272,256]{1,0:T(8,128)(2,1)S(1)}, u32[]{:S(2)}, u32[]{:S(2)}) collective-permute-start(bf16[272,256]{1,0:T(8,128)(2,1)S(1)} %get-tuple-element.42.rest_0_), channel_id=1, source_target_pairs={{0,2},{1,3},{2,0},{3,1},{4,6},{5,7},{6,4},{7,5},{8,10},{9,11},{10,... | collective-permute-start | bytes 417800 | tf_op jit(solution)/shard_map/ppermute | solution.py:256
  10.1 2.1 %prepare.1 = (bf16[384,1920]{1,0:T(8,128)(2,1)S(1)}, bf16[1920,384]{1,0:T(8,128)(2,1)S(1)}, f32[384,128]{1,0:T(8,128)S(1)}, f32[12,256]{1,0:T(8,128)S(1)}, bf16[...) custom-call(s32[24]{0:T(128)} %tile_dst_hbm.1, ...), custom_call_target="tpu_custom_call" | custom-call | flops 100000000 | bytes 6291456 | tf_op jit(solution)/shard_map/prepare/pallas_call | solution.py:324
  12.2 0.0 collective-permute-done.1.rest_2_.near.rest_1_
  12.2 0.1 collective-permute-start.6
  12.3 0.8 %collective-permute-done.rest_1_.far.rest_2_ = bf16[272,256]{1,0:T(8,128)(2,1)S(1)} collective-permute-done((bf16[272,256]{1,0:T(8,128)(2,1)S(1)}, bf16[272,256]{1,0:T(8,128)(2,1)S(1)}, u32[]{:S(2)}, u32[]{:S(2)}) %collective-permute-start) | collective-permute-done | bytes 139296 | tf_op jit(solution)/shard_map/ppermute | solution.py:256
  13.1 0.1 relay.1
  13.2 0.5 %collective-permute-start.5 = (bf16[144,256]{1,0:T(8,128)(2,1)S(1)}, bf16[144,256]{1,0:T(8,128)(2,1)S(1)}, u32[]{:S(2)}, u32[]{:S(2)}) collective-permute-start(bf16[144,256]{1,0:T(8,128)(2,1)S(1)} %relay.1), channel_id=1, source_target_pairs={{0,8},{8,0},{16,24},{24,16},{1,9},{9,1},{17,25},{25,17},{2,10},{10... | collective-permute-start | bytes 221192 | tf_op jit(solution)/shard_map/ppermute | solution.py:256
  13.7 0.5 %first.1 = (f32[384,256]{1,0:T(8,128)S(1)}, f32[384,256]{1,0:T(8,128)S(1)}) custom-call(f32[12,256]{1,0:T(8,128)S(1)} %get-tuple-element.34.choice.rest_8_, bf16[384,1920]{1,0:T(8,128)(2,1)S(1)} %get-tuple-element.37.dense, bf16[384,256]{1,0:T(8,128)(2,1)S(1)} %get-tuple-element.39.features, bf16[256,256]{1,0:T(8,128)(2,1)S(1)} %get-tuple-element.40.w_self.rest_9_, ...), custom_call_target="tpu_custom_call" | custom-call | flops 1000000000 | bytes 3145728 | tf_op jit(solution)/shard_map/first/pallas_call | solution.py:378
  14.2 0.0 collective-permute-done.6.rest_4_
  14.2 0.0 collective-permute-done.4.rest_2_.rest_3_.rest_5_
  14.2 1.2 %collective-permute-done.3.rest_1_.rest_2_.rest_4_ = bf16[272,256]{1,0:T(8,128)(2,1)S(1)} collective-permute-done((bf16[272,256]{1,0:T(8,128)(2,1)S(1)}, bf16[272,256]{1,0:T(8,128)(2,1)S(1)}, u32[]{:S(2)}, u32[]{:S(2)}) %collective-permute-start.3) | collective-permute-done | bytes 139296 | tf_op jit(solution)/shard_map/ppermute | solution.py:256
  15.4 0.1 collective-permute-done.2.rest_0_.rest_1_.rest_3_
  15.4 0.2 trade.1
  15.6 0.1 collective-permute-start.7
  15.6 0.3 near.1.before
  15.9 1.7 %collective-permute-done.5.rest_0_.rest_7_ = bf16[144,256]{1,0:T(8,128)(2,1)S(1)} collective-permute-done((bf16[144,256]{1,0:T(8,128)(2,1)S(1)}, bf16[144,256]{1,0:T(8,128)(2,1)S(1)}, u32[]{:S(2)}, u32[]{:S(2)}) %collective-permute-start.5) | collective-permute-done | bytes 73760 | tf_op jit(solution)/shard_map/ppermute | solution.py:256
  17.6 0.2 late.1.before
  17.8 0.0 collective-permute-done.7.rest_0_.rest_6_
  17.8 1.3 %middle.1 = (bf16[256,256]{1,0:T(8,128)(2,1)S(1)}, bf16[256,256]{1,0:T(8,128)(2,1)S(1)}, bf16[256,256]{1,0:T(8,128)(2,1)S(1)}, bf16[128,256]{1,0:T(8,128)(2,1)S(...) custom-call(f32[12,256]{1,0:T(8,128)S(1)} %get-tuple-element.34.choi, ...), custom_call_target="tpu_custom_call" | custom-call | flops 377487360 | bytes 6291456 | tf_op jit(solution)/shard_map/middle/pallas_call | solution.py:417
  19.1 2.5 %collective-permute-start.12 = (bf16[256,256]{1,0:T(8,128)(2,1)S(1)}, bf16[256,256]{1,0:T(8,128)(2,1)S(1)}, u32[]{:S(2)}, u32[]{:S(2)}) collective-permute-start(bf16[256,256]{1,0:T(8,128)(2,1)S(1)} %get-tuple-element.57), channel_id=1, source_target_pairs={{0,6},{1,7},{2,4},{3,5},{4,2},{5,3},{6,0},{7,1},{8,14},{9,15},{10,... | collective-permute-start | bytes 393224 | tf_op jit(solution)/shard_map/ppermute | solution.py:256
  21.6 2.5 %collective-permute-start.8 = (bf16[128,256]{1,0:T(8,128)(2,1)S(1)}, bf16[128,256]{1,0:T(8,128)(2,1)S(1)}, u32[]{:S(2)}, u32[]{:S(2)}) collective-permute-start(bf16[128,256]{1,0:T(8,128)(2,1)S(1)} %get-tuple-element.48), channel_id=1, source_target_pairs={{0,24},{8,16},{16,8},{24,0},{1,25},{9,17},{17,9},{25,1},{2,26},{10... | collective-permute-start | bytes 196616 | tf_op jit(solution)/shard_map/ppermute | solution.py:256
  24.1 0.5 %collective-permute-start.13 = (bf16[256,256]{1,0:T(8,128)(2,1)S(1)}, bf16[256,256]{1,0:T(8,128)(2,1)S(1)}, u32[]{:S(2)}, u32[]{:S(2)}) collective-permute-start(bf16[256,256]{1,0:T(8,128)(2,1)S(1)} %get-tuple-element.58), channel_id=1, source_target_pairs={{0,4},{1,5},{2,6},{3,7},{4,0},{5,1},{6,2},{7,3},{8,12},{9,13},{10,... | collective-permute-start | bytes 393224 | tf_op jit(solution)/shard_map/ppermute | solution.py:256
  24.6 0.5 %collective-permute-start.14 = (bf16[256,256]{1,0:T(8,128)(2,1)S(1)}, bf16[256,256]{1,0:T(8,128)(2,1)S(1)}, u32[]{:S(2)}, u32[]{:S(2)}) collective-permute-start(bf16[256,256]{1,0:T(8,128)(2,1)S(1)} %get-tuple-element.59), channel_id=1, source_target_pairs={{0,2},{1,3},{2,0},{3,1},{4,6},{5,7},{6,4},{7,5},{8,10},{9,11},{10,... | collective-permute-start | bytes 393224 | tf_op jit(solution)/shard_map/ppermute | solution.py:256
  25.1 0.0 collective-permute-start.9
  25.1 2.5 %collective-permute-done.8.rest_0_ = bf16[128,256]{1,0:T(8,128)(2,1)S(1)} collective-permute-done((bf16[128,256]{1,0:T(8,128)(2,1)S(1)}, bf16[128,256]{1,0:T(8,128)(2,1)S(1)}, u32[]{:S(2)}, u32[]{:S(2)}) %collective-permute-start.8) | collective-permute-done | bytes 65568 | tf_op jit(solution)/shard_map/ppermute | solution.py:256
  27.7 0.7 %collective-permute-start.10 = (bf16[128,256]{1,0:T(8,128)(2,1)S(1)}, bf16[128,256]{1,0:T(8,128)(2,1)S(1)}, u32[]{:S(2)}, u32[]{:S(2)}) collective-permute-start(bf16[128,256]{1,0:T(8,128)(2,1)S(1)} %get-tuple-element.55), channel_id=1, source_target_pairs={{0,8},{8,0},{16,24},{24,16},{1,9},{9,1},{17,25},{25,17},{2,10},{10... | collective-permute-start | bytes 196616 | tf_op jit(solution)/shard_map/ppermute | solution.py:256
  28.4 0.0 collective-permute-done.12.rest_3_.rest_2_
  28.4 0.0 collective-permute-start.11
  28.4 0.3 %own.1 = (f32[384,256]{1,0:T(8,128)S(1)}, f32[12,256]{1,0:T(8,128)S(1)}) custom-call(bf16[128,256]{1,0:T(8,128)(2,1)S(1)} %collective-permute-done.8.rest_0_, bf16[272,256]{1,0:T(8,128)(2,1)S(1)} %collective-permute-done.1.rest_2_.near.rest_1_, bf16[272,256]{1,0:T(8,128)(2,1)S(1)} %collective-permute-done.rest_1_.far.rest_2_, ...), custom_call_target="tpu_custom_call" | custom-call | flops 1000000000 | bytes 2097152 | tf_op jit(solution)/shard_map/own/pallas_call | solution.py:440
  28.7 0.3 %collective-permute-done.13.rest_4_.rest_1_ = bf16[256,256]{1,0:T(8,128)(2,1)S(1)} collective-permute-done((bf16[256,256]{1,0:T(8,128)(2,1)S(1)}, bf16[256,256]{1,0:T(8,128)(2,1)S(1)}, u32[]{:S(2)}, u32[]{:S(2)}) %collective-permute-start.13) | collective-permute-done | bytes 131104 | tf_op jit(solution)/shard_map/ppermute | solution.py:256
  29.0 0.5 %collective-permute-done.14.rest_5_.rest_0_ = bf16[256,256]{1,0:T(8,128)(2,1)S(1)} collective-permute-done((bf16[256,256]{1,0:T(8,128)(2,1)S(1)}, bf16[256,256]{1,0:T(8,128)(2,1)S(1)}, u32[]{:S(2)}, u32[]{:S(2)}) %collective-permute-start.14) | collective-permute-done | bytes 131104 | tf_op jit(solution)/shard_map/ppermute | solution.py:256
  29.6 0.1 collective-permute-start.15
  29.6 0.6 %collective-permute-done.9.rest_0_ = bf16[128,256]{1,0:T(8,128)(2,1)S(1)} collective-permute-done((bf16[128,256]{1,0:T(8,128)(2,1)S(1)}, bf16[128,256]{1,0:T(8,128)(2,1)S(1)}, u32[]{:S(2)}, u32[]{:S(2)}) %collective-permute-start.9) | collective-permute-done | bytes 65568 | tf_op jit(solution)/shard_map/ppermute | solution.py:256
  30.3 1.7 %collective-permute-done.10.rest_1_ = bf16[128,256]{1,0:T(8,128)(2,1)S(1)} collective-permute-done((bf16[128,256]{1,0:T(8,128)(2,1)S(1)}, bf16[128,256]{1,0:T(8,128)(2,1)S(1)}, u32[]{:S(2)}, u32[]{:S(2)}) %collective-permute-start.10) | collective-permute-done | bytes 65568 | tf_op jit(solution)/shard_map/ppermute | solution.py:256
  31.9 0.0 collective-permute-done.11.rest_2_
  31.9 0.2 add.1.total
  32.1 0.0 collective-permute-done.15.rest_0_
  32.1 0.8 %final.1 = bf16[384,256]{1,0:T(8,128)(2,1)} custom-call(f32[12,256]{1,0:T(8,128)S(1)} %get-tuple-element.52.owner, f32[384,256]{1,0:T(8,128)S(1)} %add.1.total, bf16[384,256]{1,0:T(8,128)(2,1)S(1)} %collective-permute-done.15.rest_0_), custom_call_target="tpu_custom_call" | custom-call | flops 393216 | bytes 1048576 | tf_op jit(solution)/shard_map/final/pallas_call | solution.py:356
  (1 shorter events, 0.0 us)
Async XLA Ops:
  0.9 11.3 %collective-permute-start.1 = (bf16[272,256]{1,0:T(8,128)(2,1)S(1)}, bf16[272,256]{1,0:T(8,128)(2,1)S(1)}, u32[]{:S(2)}, u32[]{:S(2)}) collective-permute-start(bf16[272,256]{1,0:T(8,128)(2,1)S(1)} %get-tuple-element.42.rest_0_), channel_id=1, source_target_pairs={{0,8},{8,0},{16,24},{24,16},{1,9},{9,1},{17,25},{25,17},{2,10},{10... | collective-permute-start | bytes 417800 | tf_op jit(solution)/shard_map/ppermute | solution.py:256
  4.0 9.1 %collective-permute-start = (bf16[272,256]{1,0:T(8,128)(2,1)S(1)}, bf16[272,256]{1,0:T(8,128)(2,1)S(1)}, u32[]{:S(2)}, u32[]{:S(2)}) collective-permute-start(bf16[272,256]{1,0:T(8,128)(2,1)S(1)} %get-tuple-element.42.rest_0_), channel_id=1, source_target_pairs={{0,16},{8,24},{16,0},{24,8},{1,17},{9,25},{17,1},{25,9},{2,18},{10... | collective-permute-start | bytes 417800 | tf_op jit(solution)/shard_map/ppermute | solution.py:256
  6.6 7.6 %collective-permute-start.4 = (bf16[272,256]{1,0:T(8,128)(2,1)S(1)}, bf16[272,256]{1,0:T(8,128)(2,1)S(1)}, u32[]{:S(2)}, u32[]{:S(2)}) collective-permute-start(bf16[272,256]{1,0:T(8,128)(2,1)S(1)} %get-tuple-element.42.rest_0_), channel_id=1, source_target_pairs={{0,6},{1,7},{2,4},{3,5},{4,2},{5,3},{6,0},{7,1},{8,14},{9,15},{10,... | collective-permute-start | bytes 417800 | tf_op jit(solution)/shard_map/ppermute | solution.py:256
  9.1 6.3 %collective-permute-start.3 = (bf16[272,256]{1,0:T(8,128)(2,1)S(1)}, bf16[272,256]{1,0:T(8,128)(2,1)S(1)}, u32[]{:S(2)}, u32[]{:S(2)}) collective-permute-start(bf16[272,256]{1,0:T(8,128)(2,1)S(1)} %get-tuple-element.42.rest_0_), channel_id=1, source_target_pairs={{0,4},{1,5},{2,6},{3,7},{4,0},{5,1},{6,2},{7,3},{8,12},{9,13},{10,... | collective-permute-start | bytes 417800 | tf_op jit(solution)/shard_map/ppermute | solution.py:256
  9.6 5.8 %collective-permute-start.2 = (bf16[272,256]{1,0:T(8,128)(2,1)S(1)}, bf16[272,256]{1,0:T(8,128)(2,1)S(1)}, u32[]{:S(2)}, u32[]{:S(2)}) collective-permute-start(bf16[272,256]{1,0:T(8,128)(2,1)S(1)} %get-tuple-element.42.rest_0_), channel_id=1, source_target_pairs={{0,2},{1,3},{2,0},{3,1},{4,6},{5,7},{6,4},{7,5},{8,10},{9,11},{10,... | collective-permute-start | bytes 417800 | tf_op jit(solution)/shard_map/ppermute | solution.py:256
  12.2 1.9 %collective-permute-start.6 = (bf16[16,256]{1,0:T(8,128)(2,1)S(1)}, bf16[16,256]{1,0:T(8,128)(2,1)S(1)}, u32[]{:S(2)}, u32[]{:S(2)}) collective-permute-start(bf16[16,256]{1,0:T(8,128)(2,1)S(1)} %get-tuple-element.46), channel_id=1, source_target_pairs={{0,1},{1,0},{2,3},{3,2},{4,5},{5,4},{6,7},{7,6},{8,9},{9,8},{10,11... | collective-permute-start | bytes 24584 | tf_op jit(solution)/shard_map/ppermute | solution.py:256
  13.2 4.4 %collective-permute-start.5 = (bf16[144,256]{1,0:T(8,128)(2,1)S(1)}, bf16[144,256]{1,0:T(8,128)(2,1)S(1)}, u32[]{:S(2)}, u32[]{:S(2)}) collective-permute-start(bf16[144,256]{1,0:T(8,128)(2,1)S(1)} %relay.1), channel_id=1, source_target_pairs={{0,8},{8,0},{16,24},{24,16},{1,9},{9,1},{17,25},{25,17},{2,10},{10... | collective-permute-start | bytes 221192 | tf_op jit(solution)/shard_map/ppermute | solution.py:256
  15.6 2.2 %collective-permute-start.7 = (bf16[576,256]{1,0:T(8,128)(2,1)S(1)}, bf16[576,256]{1,0:T(8,128)(2,1)S(1)}, u32[]{:S(2)}, u32[]{:S(2)}) collective-permute-start(bf16[576,256]{1,0:T(8,128)(2,1)S(1)} %trade.1), channel_id=1, source_target_pairs={{0,1},{1,0},{2,3},{3,2},{4,5},{5,4},{6,7},{7,6},{8,9},{9,8},{10,11... | collective-permute-start | bytes 884744 | tf_op jit(solution)/shard_map/ppermute | solution.py:256
  19.1 9.3 %collective-permute-start.12 = (bf16[256,256]{1,0:T(8,128)(2,1)S(1)}, bf16[256,256]{1,0:T(8,128)(2,1)S(1)}, u32[]{:S(2)}, u32[]{:S(2)}) collective-permute-start(bf16[256,256]{1,0:T(8,128)(2,1)S(1)} %get-tuple-element.57), channel_id=1, source_target_pairs={{0,6},{1,7},{2,4},{3,5},{4,2},{5,3},{6,0},{7,1},{8,14},{9,15},{10,... | collective-permute-start | bytes 393224 | tf_op jit(solution)/shard_map/ppermute | solution.py:256
  21.6 6.1 %collective-permute-start.8 = (bf16[128,256]{1,0:T(8,128)(2,1)S(1)}, bf16[128,256]{1,0:T(8,128)(2,1)S(1)}, u32[]{:S(2)}, u32[]{:S(2)}) collective-permute-start(bf16[128,256]{1,0:T(8,128)(2,1)S(1)} %get-tuple-element.48), channel_id=1, source_target_pairs={{0,24},{8,16},{16,8},{24,0},{1,25},{9,17},{17,9},{25,1},{2,26},{10... | collective-permute-start | bytes 196616 | tf_op jit(solution)/shard_map/ppermute | solution.py:256
  24.1 5.0 %collective-permute-start.13 = (bf16[256,256]{1,0:T(8,128)(2,1)S(1)}, bf16[256,256]{1,0:T(8,128)(2,1)S(1)}, u32[]{:S(2)}, u32[]{:S(2)}) collective-permute-start(bf16[256,256]{1,0:T(8,128)(2,1)S(1)} %get-tuple-element.58), channel_id=1, source_target_pairs={{0,4},{1,5},{2,6},{3,7},{4,0},{5,1},{6,2},{7,3},{8,12},{9,13},{10,... | collective-permute-start | bytes 393224 | tf_op jit(solution)/shard_map/ppermute | solution.py:256
  24.6 5.0 %collective-permute-start.14 = (bf16[256,256]{1,0:T(8,128)(2,1)S(1)}, bf16[256,256]{1,0:T(8,128)(2,1)S(1)}, u32[]{:S(2)}, u32[]{:S(2)}) collective-permute-start(bf16[256,256]{1,0:T(8,128)(2,1)S(1)} %get-tuple-element.59), channel_id=1, source_target_pairs={{0,2},{1,3},{2,0},{3,1},{4,6},{5,7},{6,4},{7,5},{8,10},{9,11},{10,... | collective-permute-start | bytes 393224 | tf_op jit(solution)/shard_map/ppermute | solution.py:256
  25.1 5.2 %collective-permute-start.9 = (bf16[128,256]{1,0:T(8,128)(2,1)S(1)}, bf16[128,256]{1,0:T(8,128)(2,1)S(1)}, u32[]{:S(2)}, u32[]{:S(2)}) collective-permute-start(bf16[128,256]{1,0:T(8,128)(2,1)S(1)} %get-tuple-element.54), channel_id=1, source_target_pairs={{0,16},{8,24},{16,0},{24,8},{1,17},{9,25},{17,1},{25,9},{2,18},{10... | collective-permute-start | bytes 196616 | tf_op jit(solution)/shard_map/ppermute | solution.py:256
  27.7 4.3 %collective-permute-start.10 = (bf16[128,256]{1,0:T(8,128)(2,1)S(1)}, bf16[128,256]{1,0:T(8,128)(2,1)S(1)}, u32[]{:S(2)}, u32[]{:S(2)}) collective-permute-start(bf16[128,256]{1,0:T(8,128)(2,1)S(1)} %get-tuple-element.55), channel_id=1, source_target_pairs={{0,8},{8,0},{16,24},{24,16},{1,9},{9,1},{17,25},{25,17},{2,10},{10... | collective-permute-start | bytes 196616 | tf_op jit(solution)/shard_map/ppermute | solution.py:256
  28.4 3.6 %collective-permute-start.11 = (bf16[128,256]{1,0:T(8,128)(2,1)S(1)}, bf16[128,256]{1,0:T(8,128)(2,1)S(1)}, u32[]{:S(2)}, u32[]{:S(2)}) collective-permute-start(bf16[128,256]{1,0:T(8,128)(2,1)S(1)} %get-tuple-element.56), channel_id=1, source_target_pairs={{0,1},{1,0},{2,3},{3,2},{4,5},{5,4},{6,7},{7,6},{8,9},{9,8},{10,11... | collective-permute-start | bytes 196616 | tf_op jit(solution)/shard_map/ppermute | solution.py:256
  29.6 2.6 %collective-permute-start.15 = (bf16[384,256]{1,0:T(8,128)(2,1)S(1)}, bf16[384,256]{1,0:T(8,128)(2,1)S(1)}, u32[]{:S(2)}, u32[]{:S(2)}) collective-permute-start(bf16[384,256]{1,0:T(8,128)(2,1)S(1)} %turn.1), channel_id=1, source_target_pairs={{0,1},{1,0},{2,3},{3,2},{4,5},{5,4},{6,7},{7,6},{8,9},{9,8},{10,11... | collective-permute-start | bytes 589832 | tf_op jit(solution)/shard_map/ppermute | solution.py:256

commit v9 on v8

--- a/solution.py
+++ b/solution.py
@@ -118,11 +118,15 @@
     ).astype(BF)
 
 
-def relay_kernel(sub_count, d, far, near, out):
+def rows_kernel(message, out):
+    out[...] = message[message.shape[0] - EXTRA :, :]
+
+
+def relay_kernel(sub_count, d, far, rows, near, out):
     size = out.shape[0] - EXTRA
     index = lane_of(index_row(near, size), sub_count + (lax.axis_index("cluster") ^ d))
     out[0:size, :] = pick(far, index, size)
-    out[size:, :] = far[2 * size :, :]
+    out[size:, :] = rows[...]
 
 
 def trade_kernel(even, *rest):
@@ -387,26 +391,30 @@
         )(*operands, *arrays)
 
     for d in relayed:
+        far = got[sub_count + d - 1][0]
+        far_rows = call(
+            rows_kernel, jax.ShapeDtypeStruct((EXTRA, width), BF), "rows", 10**9, far
+        )
         value = call(
             functools.partial(relay_kernel, sub_count, d - 1),
             jax.ShapeDtypeStruct((size + EXTRA, width), BF),
-            "relay", 10**6, got[sub_count + d - 1][0], got[sub_count + 1][0],
+            "relay", 10**6, far, far_rows, got[sub_count + 1][0],
         )
         got[sub_count + d] = (along(value, 1), 0, True, size)
     first_sum, own_pre = sum_call(
-        first_kernel, [wide, wide], "first", [0, sub_count, *(sub_count + d for d in direct), sub_count + 1],
+        first_kernel, [wide, wide], "first", [0, sub_count, *(sub_count + d for d in direct)],
         choice, dense, features, w_self, bias,
     )
     traded = [0, *even]
     value = call(
         functools.partial(trade_kernel, traded),
         jax.ShapeDtypeStruct((len(traded) * (size + EXTRA), width), BF),
-        "trade", 10**6, *[got[d][0] for d in traded], after(sibling_rows, (own_pre, value)),
+        "trade", 10**6, *[got[d][0] for d in traded], after(sibling_rows, (choice, value)),
     )
     value = across(value, 1)
     for i, d in enumerate(traded):
         got[d + 1] = (value, i * size, True, len(traded) * size + i * EXTRA)
-    near_sum = sum_call(near_kernel, wide, "near", even, choice, dense, first_sum)
+    near_sum = sum_call(near_kernel, wide, "near", [sub_count + 1, *even], choice, dense, first_sum)
     if relayed:
         slots_late = [sub_count + d for d in relayed]
         near_sum = sum_call(near_kernel, wide, "late", slots_late, choice, dense, near_sum)
@@ -460,13 +468,13 @@
     )
     turned = across(turned, 1)
 
-    more = [far[1], far[0], beside, *near[::-1]]
+    more = [far[1], far[0], *near[::-1]]
     if more:
         total = call(
             functools.partial(add_kernel, own, [(slot, i, 0) for i, (slot, _) in enumerate(more)]),
             wide, "add", 10**10, owner, total, *[value for _, value in more],
         )
-    last = []
+    last = [beside]
     parts = [(slot, i, 0) for i, (slot, _) in enumerate(last)]
     parts += [(d + 1, len(last), i * size) for i, d in enumerate(even)]
     return call(

time: 33.1 us -> 32.8 us (level)
  waiting for transfers between devices: 9.36 us -> 7.15 us
  starting transfers between devices: 16.6 us -> 18.5 us
    ppermute x16, waiting for transfers between devices: 9.36 us -> 7.15 us  [swap(): return lax.ppermute(value, axis, [(i, i ^ d) for i in range(count)])]
    ppermute x16, starting transfers between devices: 16.6 us -> 18.5 us  [swap(): return lax.ppermute(value, axis, [(i, i ^ d) for i in range(count)])]
    pallas_call x5 -> x6, Pallas kernels: 1.22 us -> 1.23 us  [call(): pl.pallas_call(kernel, out_shape=out_shape, in_specs=[VMEM] * len(operand...]
  transfers between devices with their start and end apart: 16 -> 16, of which waited for: 9 -> 7; matrix products, arithmetic and copies ran while one was open for 0% -> 0% of each run, Pallas kernels for 12% -> 12%
where the time goes in v9:
time: 32.8 us; the launch traced here: 32.6 us
  starting transfers between devices  18.5 us (56%)
  waiting for transfers between devices  7.15 us (22%)
  Pallas kernels  6.78 us (21%)
    ppermute x16, starting transfers between devices, swap(): return lax.ppermute(value, axis, [(i, i ^ d) for i in range(count)])  18.5 us
    ppermute x16, waiting for transfers between devices, swap(): return lax.ppermute(value, axis, [(i, i ^ d) for i in range(count)])  7.15 us
    pallas_call x1, Pallas kernels, shards(): pl.pallas_call(functools.partial(prepare_kernel, *counts), out_shape=[jax...  2.11 us
    pallas_call x1, Pallas kernels, shards(): pl.pallas_call(functools.partial(middle_kernel, *counts, late_halos, len(...  1.26 us
    pallas_call x6, Pallas kernels, call(): pl.pallas_call(kernel, out_shape=out_shape, in_specs=[VMEM] * len(operand...  1.23 us
    pallas_call x1, Pallas kernels, shards(): pl.pallas_call(edge_kernel, out_shape=[jax.ShapeDtypeStruct((BOUNDARY * s...  0.93 us
    pallas_call x3, Pallas kernels, sum_call(): pl.pallas_call(functools.partial(kernel, own, halos), out_shape=out_shape...  0.91 us
  transfers between devices with their start and end apart: 16, of which 7 were waited for; matrix products, arithmetic and copies ran while one was open for 0% of the time, Pallas kernels for 12%

profile of v9, /device:TPU:0, one launch (start us, length us, event | category | flops | bytes accessed | tf_op | source)
XLA Modules:
  0.0 32.6 jit_solution(14624275812559255633)
XLA Ops:
  0.0 0.9 %edge.1 = (bf16[272,256]{1,0:T(8,128)(2,1)S(1)}, bf16[16,256]{1,0:T(8,128)(2,1)S(1)}) custom-call(s32[1,8]{1,0:T(1,128)} %recv_sub.1, s32[1,4]{1,0:T(1,128)} %recv_cluster.1, bf16[384,256]{1,0:T(8,128)(2,1)} %features.1), custom_call_target="tpu_custom_call" | custom-call | flops 1024 | bytes 262144 | tf_op jit(solution)/shard_map/edge/pallas_call | solution.py:293
  0.9 4.1 %collective-permute-start = (bf16[272,256]{1,0:T(8,128)(2,1)S(1)}, bf16[272,256]{1,0:T(8,128)(2,1)S(1)}, u32[]{:S(2)}, u32[]{:S(2)}) collective-permute-start(bf16[272,256]{1,0:T(8,128)(2,1)S(1)} %get-tuple-element.42.rest_0_), channel_id=1, source_target_pairs={{0,16},{8,24},{16,0},{24,8},{1,17},{9,25},{17,1},{25,9},{2,18},{10... | collective-permute-start | bytes 417800 | tf_op jit(solution)/shard_map/ppermute | solution.py:260
  5.0 1.6 %collective-permute-start.1 = (bf16[272,256]{1,0:T(8,128)(2,1)S(1)}, bf16[272,256]{1,0:T(8,128)(2,1)S(1)}, u32[]{:S(2)}, u32[]{:S(2)}) collective-permute-start(bf16[272,256]{1,0:T(8,128)(2,1)S(1)} %get-tuple-element.42.rest_0_), channel_id=1, source_target_pairs={{0,8},{8,0},{16,24},{24,16},{1,9},{9,1},{17,25},{25,17},{2,10},{10... | collective-permute-start | bytes 417800 | tf_op jit(solution)/shard_map/ppermute | solution.py:260
  6.6 2.4 %collective-permute-start.4 = (bf16[272,256]{1,0:T(8,128)(2,1)S(1)}, bf16[272,256]{1,0:T(8,128)(2,1)S(1)}, u32[]{:S(2)}, u32[]{:S(2)}) collective-permute-start(bf16[272,256]{1,0:T(8,128)(2,1)S(1)} %get-tuple-element.42.rest_0_), channel_id=1, source_target_pairs={{0,6},{1,7},{2,4},{3,5},{4,2},{5,3},{6,0},{7,1},{8,14},{9,15},{10,... | collective-permute-start | bytes 417800 | tf_op jit(solution)/shard_map/ppermute | solution.py:260
  9.1 0.5 %collective-permute-start.3 = (bf16[272,256]{1,0:T(8,128)(2,1)S(1)}, bf16[272,256]{1,0:T(8,128)(2,1)S(1)}, u32[]{:S(2)}, u32[]{:S(2)}) collective-permute-start(bf16[272,256]{1,0:T(8,128)(2,1)S(1)} %get-tuple-element.42.rest_0_), channel_id=1, source_target_pairs={{0,4},{1,5},{2,6},{3,7},{4,0},{5,1},{6,2},{7,3},{8,12},{9,13},{10,... | collective-permute-start | bytes 417800 | tf_op jit(solution)/shard_map/ppermute | solution.py:260
  9.6 0.5 %collective-permute-start.2 = (bf16[272,256]{1,0:T(8,128)(2,1)S(1)}, bf16[272,256]{1,0:T(8,128)(2,1)S(1)}, u32[]{:S(2)}, u32[]{:S(2)}) collective-permute-start(bf16[272,256]{1,0:T(8,128)(2,1)S(1)} %get-tuple-element.42.rest_0_), channel_id=1, source_target_pairs={{0,2},{1,3},{2,0},{3,1},{4,6},{5,7},{6,4},{7,5},{8,10},{9,11},{10,... | collective-permute-start | bytes 417800 | tf_op jit(solution)/shard_map/ppermute | solution.py:260
  10.1 2.1 %prepare.1 = (bf16[384,1920]{1,0:T(8,128)(2,1)S(1)}, bf16[1920,384]{1,0:T(8,128)(2,1)S(1)}, f32[384,128]{1,0:T(8,128)S(1)}, f32[12,256]{1,0:T(8,128)S(1)}, bf16[...) custom-call(s32[24]{0:T(128)} %tile_dst_hbm.1, ...), custom_call_target="tpu_custom_call" | custom-call | flops 100000000 | bytes 6291456 | tf_op jit(solution)/shard_map/prepare/pallas_call | solution.py:328
  12.2 0.0 collective-permute-done.rest_1_.message.far.rest_2_
  12.2 0.1 collective-permute-start.6
  12.3 0.0 collective-permute-done.1.rest_0_.near.rest_1_
  12.3 0.1 relay.1
  12.4 1.2 %collective-permute-start.5 = (bf16[144,256]{1,0:T(8,128)(2,1)S(1)}, bf16[144,256]{1,0:T(8,128)(2,1)S(1)}, u32[]{:S(2)}, u32[]{:S(2)}) collective-permute-start(bf16[144,256]{1,0:T(8,128)(2,1)S(1)} %relay.1), channel_id=1, source_target_pairs={{0,8},{8,0},{16,24},{24,16},{1,9},{9,1},{17,25},{25,17},{2,10},{10... | collective-permute-start | bytes 221192 | tf_op jit(solution)/shard_map/ppermute | solution.py:260
  13.6 0.0 collective-permute-done.6.rest_4_
  13.6 0.0 collective-permute-done.4.rest_3_.rest_5_
  13.6 1.7 %collective-permute-done.3.rest_2_.rest_4_ = bf16[272,256]{1,0:T(8,128)(2,1)S(1)} collective-permute-done((bf16[272,256]{1,0:T(8,128)(2,1)S(1)}, bf16[272,256]{1,0:T(8,128)(2,1)S(1)}, u32[]{:S(2)}, u32[]{:S(2)}) %collective-permute-start.3) | collective-permute-done | bytes 139296 | tf_op jit(solution)/shard_map/ppermute | solution.py:260
  15.4 0.1 collective-permute-done.2.rest_1_.rest_3_
  15.4 0.2 trade.1
  15.6 0.1 collective-permute-start.7
  15.6 0.4 %first.1 = (f32[384,256]{1,0:T(8,128)S(1)}, f32[384,256]{1,0:T(8,128)S(1)}) custom-call(f32[12,256]{1,0:T(8,128)S(1)} %get-tuple-element.34.choice.rest_8_, bf16[384,1920]{1,0:T(8,128)(2,1)S(1)} %get-tuple-element.37.dense, bf16[384,256]{1,0:T(8,128)(2,1)S(1)} %get-tuple-element.39.features, bf16[256,256]{1,0:T(8,128)(2,1)S(1)} %get-tuple-element.40.w_self.rest_9_, ...), custom_call_target="tpu_custom_call" | custom-call | flops 1000000000 | bytes 3145728 | tf_op jit(solution)/shard_map/first/pallas_call | solution.py:382
  16.1 0.3 near.1.before
  16.4 0.8 %collective-permute-done.5.rest_0_.rest_7_ = bf16[144,256]{1,0:T(8,128)(2,1)S(1)} collective-permute-done((bf16[144,256]{1,0:T(8,128)(2,1)S(1)}, bf16[144,256]{1,0:T(8,128)(2,1)S(1)}, u32[]{:S(2)}, u32[]{:S(2)}) %collective-permute-start.5) | collective-permute-done | bytes 73760 | tf_op jit(solution)/shard_map/ppermute | solution.py:260
  17.2 0.2 late.1.before
  17.4 0.0 collective-permute-done.7.rest_0_.rest_6_
  17.4 1.3 %middle.1 = (bf16[256,256]{1,0:T(8,128)(2,1)S(1)}, bf16[256,256]{1,0:T(8,128)(2,1)S(1)}, bf16[256,256]{1,0:T(8,128)(2,1)S(1)}, bf16[128,256]{1,0:T(8,128)(2,1)S(...) custom-call(f32[12,256]{1,0:T(8,128)S(1)} %get-tuple-element.34.choi, ...), custom_call_target="tpu_custom_call" | custom-call | flops 377487360 | bytes 6291456 | tf_op jit(solution)/shard_map/middle/pallas_call | solution.py:425
  18.6 3.0 %collective-permute-start.8 = (bf16[128,256]{1,0:T(8,128)(2,1)S(1)}, bf16[128,256]{1,0:T(8,128)(2,1)S(1)}, u32[]{:S(2)}, u32[]{:S(2)}) collective-permute-start(bf16[128,256]{1,0:T(8,128)(2,1)S(1)} %get-tuple-element.48), channel_id=1, source_target_pairs={{0,24},{8,16},{16,8},{24,0},{1,25},{9,17},{17,9},{25,1},{2,26},{10... | collective-permute-start | bytes 196616 | tf_op jit(solution)/shard_map/ppermute | solution.py:260
  21.6 2.5 %collective-permute-start.11 = (bf16[256,256]{1,0:T(8,128)(2,1)S(1)}, bf16[256,256]{1,0:T(8,128)(2,1)S(1)}, u32[]{:S(2)}, u32[]{:S(2)}) collective-permute-start(bf16[256,256]{1,0:T(8,128)(2,1)S(1)} %get-tuple-element.56), channel_id=1, source_target_pairs={{0,6},{1,7},{2,4},{3,5},{4,2},{5,3},{6,0},{7,1},{8,14},{9,15},{10,... | collective-permute-start | bytes 393224 | tf_op jit(solution)/shard_map/ppermute | solution.py:260
  24.1 0.5 %collective-permute-start.12 = (bf16[256,256]{1,0:T(8,128)(2,1)S(1)}, bf16[256,256]{1,0:T(8,128)(2,1)S(1)}, u32[]{:S(2)}, u32[]{:S(2)}) collective-permute-start(bf16[256,256]{1,0:T(8,128)(2,1)S(1)} %get-tuple-element.57), channel_id=1, source_target_pairs={{0,4},{1,5},{2,6},{3,7},{4,0},{5,1},{6,2},{7,3},{8,12},{9,13},{10,... | collective-permute-start | bytes 393224 | tf_op jit(solution)/shard_map/ppermute | solution.py:260
  24.6 0.5 %collective-permute-start.13 = (bf16[256,256]{1,0:T(8,128)(2,1)S(1)}, bf16[256,256]{1,0:T(8,128)(2,1)S(1)}, u32[]{:S(2)}, u32[]{:S(2)}) collective-permute-start(bf16[256,256]{1,0:T(8,128)(2,1)S(1)} %get-tuple-element.58), channel_id=1, source_target_pairs={{0,2},{1,3},{2,0},{3,1},{4,6},{5,7},{6,4},{7,5},{8,10},{9,11},{10,... | collective-permute-start | bytes 393224 | tf_op jit(solution)/shard_map/ppermute | solution.py:260
  25.1 0.0 collective-permute-start.9
  25.1 0.0 collective-permute-done.8.rest_0_
  25.1 1.5 %collective-permute-start.10 = (bf16[128,256]{1,0:T(8,128)(2,1)S(1)}, bf16[128,256]{1,0:T(8,128)(2,1)S(1)}, u32[]{:S(2)}, u32[]{:S(2)}) collective-permute-start(bf16[128,256]{1,0:T(8,128)(2,1)S(1)} %get-tuple-element.55), channel_id=1, source_target_pairs={{0,8},{8,0},{16,24},{24,16},{1,9},{9,1},{17,25},{25,17},{2,10},{10... | collective-permute-start | bytes 196616 | tf_op jit(solution)/shard_map/ppermute | solution.py:260
  26.6 0.3 %own.1 = (f32[384,256]{1,0:T(8,128)S(1)}, f32[12,256]{1,0:T(8,128)S(1)}) custom-call(bf16[128,256]{1,0:T(8,128)(2,1)S(1)} %collective-permute-done.8.rest_0_, bf16[272,256]{1,0:T(8,128)(2,1)S(1)} %collective-permute-done.1.rest_0_.near.rest_1_, bf16[272,256]{1,0:T(8,128)(2,1)S(1)} %collective-permute-done.rest_1_.message.far.rest_2_, ...), custom_call_target="tpu_custom_call" | custom-call | flops 1000000000 | bytes 2097152 | tf_op jit(solution)/shard_map/own/pallas_call | solution.py:448
  26.9 1.1 %collective-permute-done.11.rest_2_ = bf16[256,256]{1,0:T(8,128)(2,1)S(1)} collective-permute-done((bf16[256,256]{1,0:T(8,128)(2,1)S(1)}, bf16[256,256]{1,0:T(8,128)(2,1)S(1)}, u32[]{:S(2)}, u32[]{:S(2)}) %collective-permute-start.11) | collective-permute-done | bytes 131104 | tf_op jit(solution)/shard_map/ppermute | solution.py:260
  28.0 0.0 collective-permute-start.14
  28.0 2.2 %collective-permute-done.12.rest_3_.rest_1_ = bf16[256,256]{1,0:T(8,128)(2,1)S(1)} collective-permute-done((bf16[256,256]{1,0:T(8,128)(2,1)S(1)}, bf16[256,256]{1,0:T(8,128)(2,1)S(1)}, u32[]{:S(2)}, u32[]{:S(2)}) %collective-permute-start.12) | collective-permute-done | bytes 131104 | tf_op jit(solution)/shard_map/ppermute | solution.py:260
  30.2 0.1 collective-permute-done.13.rest_4_.rest_0_
  30.3 0.1 collective-permute-start.15
  30.4 0.0 collective-permute-done.9.rest_0_
  30.4 0.0 collective-permute-done.10.rest_1_
  30.4 0.2 add.1.total
  30.6 0.0 collective-permute-done.14.rest_0_
  30.6 1.2 %collective-permute-done.15.rest_1_ = bf16[384,256]{1,0:T(8,128)(2,1)S(1)} collective-permute-done((bf16[384,256]{1,0:T(8,128)(2,1)S(1)}, bf16[384,256]{1,0:T(8,128)(2,1)S(1)}, u32[]{:S(2)}, u32[]{:S(2)}) %collective-permute-start.15) | collective-permute-done | bytes 196640 | tf_op jit(solution)/shard_map/ppermute | solution.py:260
  31.8 0.8 %final.1 = bf16[384,256]{1,0:T(8,128)(2,1)} custom-call(f32[12,256]{1,0:T(8,128)S(1)} %get-tuple-element.52.owner, f32[384,256]{1,0:T(8,128)S(1)} %add.1.total, bf16[128,256]{1,0:T(8,128)(2,1)S(1)} %collective-permute-done.14.rest_0_, bf16[384,256]{1,0:T(8,128)(2,1)S(1)} %collective-permute-done.15.rest_1_), custom_call_target="tpu_custom_call" | custom-call | flops 393216 | bytes 1048576 | tf_op jit(solution)/shard_map/final/pallas_call | solution.py:360
  (2 shorter events, 0.0 us)
Async XLA Ops:
  0.9 11.3 %collective-permute-start = (bf16[272,256]{1,0:T(8,128)(2,1)S(1)}, bf16[272,256]{1,0:T(8,128)(2,1)S(1)}, u32[]{:S(2)}, u32[]{:S(2)}) collective-permute-start(bf16[272,256]{1,0:T(8,128)(2,1)S(1)} %get-tuple-element.42.rest_0_), channel_id=1, source_target_pairs={{0,16},{8,24},{16,0},{24,8},{1,17},{9,25},{17,1},{25,9},{2,18},{10... | collective-permute-start | bytes 417800 | tf_op jit(solution)/shard_map/ppermute | solution.py:260
  5.0 7.3 %collective-permute-start.1 = (bf16[272,256]{1,0:T(8,128)(2,1)S(1)}, bf16[272,256]{1,0:T(8,128)(2,1)S(1)}, u32[]{:S(2)}, u32[]{:S(2)}) collective-permute-start(bf16[272,256]{1,0:T(8,128)(2,1)S(1)} %get-tuple-element.42.rest_0_), channel_id=1, source_target_pairs={{0,8},{8,0},{16,24},{24,16},{1,9},{9,1},{17,25},{25,17},{2,10},{10... | collective-permute-start | bytes 417800 | tf_op jit(solution)/shard_map/ppermute | solution.py:260
  6.6 7.0 %collective-permute-start.4 = (bf16[272,256]{1,0:T(8,128)(2,1)S(1)}, bf16[272,256]{1,0:T(8,128)(2,1)S(1)}, u32[]{:S(2)}, u32[]{:S(2)}) collective-permute-start(bf16[272,256]{1,0:T(8,128)(2,1)S(1)} %get-tuple-element.42.rest_0_), channel_id=1, source_target_pairs={{0,6},{1,7},{2,4},{3,5},{4,2},{5,3},{6,0},{7,1},{8,14},{9,15},{10,... | collective-permute-start | bytes 417800 | tf_op jit(solution)/shard_map/ppermute | solution.py:260
  9.1 6.3 %collective-permute-start.3 = (bf16[272,256]{1,0:T(8,128)(2,1)S(1)}, bf16[272,256]{1,0:T(8,128)(2,1)S(1)}, u32[]{:S(2)}, u32[]{:S(2)}) collective-permute-start(bf16[272,256]{1,0:T(8,128)(2,1)S(1)} %get-tuple-element.42.rest_0_), channel_id=1, source_target_pairs={{0,4},{1,5},{2,6},{3,7},{4,0},{5,1},{6,2},{7,3},{8,12},{9,13},{10,... | collective-permute-start | bytes 417800 | tf_op jit(solution)/shard_map/ppermute | solution.py:260
  9.6 5.8 %collective-permute-start.2 = (bf16[272,256]{1,0:T(8,128)(2,1)S(1)}, bf16[272,256]{1,0:T(8,128)(2,1)S(1)}, u32[]{:S(2)}, u32[]{:S(2)}) collective-permute-start(bf16[272,256]{1,0:T(8,128)(2,1)S(1)} %get-tuple-element.42.rest_0_), channel_id=1, source_target_pairs={{0,2},{1,3},{2,0},{3,1},{4,6},{5,7},{6,4},{7,5},{8,10},{9,11},{10,... | collective-permute-start | bytes 417800 | tf_op jit(solution)/shard_map/ppermute | solution.py:260
  12.2 1.4 %collective-permute-start.6 = (bf16[16,256]{1,0:T(8,128)(2,1)S(1)}, bf16[16,256]{1,0:T(8,128)(2,1)S(1)}, u32[]{:S(2)}, u32[]{:S(2)}) collective-permute-start(bf16[16,256]{1,0:T(8,128)(2,1)S(1)} %get-tuple-element.46), channel_id=1, source_target_pairs={{0,1},{1,0},{2,3},{3,2},{4,5},{5,4},{6,7},{7,6},{8,9},{9,8},{10,11... | collective-permute-start | bytes 24584 | tf_op jit(solution)/shard_map/ppermute | solution.py:260
  12.4 4.7 %collective-permute-start.5 = (bf16[144,256]{1,0:T(8,128)(2,1)S(1)}, bf16[144,256]{1,0:T(8,128)(2,1)S(1)}, u32[]{:S(2)}, u32[]{:S(2)}) collective-permute-start(bf16[144,256]{1,0:T(8,128)(2,1)S(1)} %relay.1), channel_id=1, source_target_pairs={{0,8},{8,0},{16,24},{24,16},{1,9},{9,1},{17,25},{25,17},{2,10},{10... | collective-permute-start | bytes 221192 | tf_op jit(solution)/shard_map/ppermute | solution.py:260
  15.6 1.8 %collective-permute-start.7 = (bf16[576,256]{1,0:T(8,128)(2,1)S(1)}, bf16[576,256]{1,0:T(8,128)(2,1)S(1)}, u32[]{:S(2)}, u32[]{:S(2)}) collective-permute-start(bf16[576,256]{1,0:T(8,128)(2,1)S(1)} %trade.1), channel_id=1, source_target_pairs={{0,1},{1,0},{2,3},{3,2},{4,5},{5,4},{6,7},{7,6},{8,9},{9,8},{10,11... | collective-permute-start | bytes 884744 | tf_op jit(solution)/shard_map/ppermute | solution.py:260
  18.6 6.5 %collective-permute-start.8 = (bf16[128,256]{1,0:T(8,128)(2,1)S(1)}, bf16[128,256]{1,0:T(8,128)(2,1)S(1)}, u32[]{:S(2)}, u32[]{:S(2)}) collective-permute-start(bf16[128,256]{1,0:T(8,128)(2,1)S(1)} %get-tuple-element.48), channel_id=1, source_target_pairs={{0,24},{8,16},{16,8},{24,0},{1,25},{9,17},{17,9},{25,1},{2,26},{10... | collective-permute-start | bytes 196616 | tf_op jit(solution)/shard_map/ppermute | solution.py:260
  21.6 6.4 %collective-permute-start.11 = (bf16[256,256]{1,0:T(8,128)(2,1)S(1)}, bf16[256,256]{1,0:T(8,128)(2,1)S(1)}, u32[]{:S(2)}, u32[]{:S(2)}) collective-permute-start(bf16[256,256]{1,0:T(8,128)(2,1)S(1)} %get-tuple-element.56), channel_id=1, source_target_pairs={{0,6},{1,7},{2,4},{3,5},{4,2},{5,3},{6,0},{7,1},{8,14},{9,15},{10,... | collective-permute-start | bytes 393224 | tf_op jit(solution)/shard_map/ppermute | solution.py:260
  24.1 6.1 %collective-permute-start.12 = (bf16[256,256]{1,0:T(8,128)(2,1)S(1)}, bf16[256,256]{1,0:T(8,128)(2,1)S(1)}, u32[]{:S(2)}, u32[]{:S(2)}) collective-permute-start(bf16[256,256]{1,0:T(8,128)(2,1)S(1)} %get-tuple-element.57), channel_id=1, source_target_pairs={{0,4},{1,5},{2,6},{3,7},{4,0},{5,1},{6,2},{7,3},{8,12},{9,13},{10,... | collective-permute-start | bytes 393224 | tf_op jit(solution)/shard_map/ppermute | solution.py:260
  24.6 5.7 %collective-permute-start.13 = (bf16[256,256]{1,0:T(8,128)(2,1)S(1)}, bf16[256,256]{1,0:T(8,128)(2,1)S(1)}, u32[]{:S(2)}, u32[]{:S(2)}) collective-permute-start(bf16[256,256]{1,0:T(8,128)(2,1)S(1)} %get-tuple-element.58), channel_id=1, source_target_pairs={{0,2},{1,3},{2,0},{3,1},{4,6},{5,7},{6,4},{7,5},{8,10},{9,11},{10,... | collective-permute-start | bytes 393224 | tf_op jit(solution)/shard_map/ppermute | solution.py:260
  25.1 5.3 %collective-permute-start.9 = (bf16[128,256]{1,0:T(8,128)(2,1)S(1)}, bf16[128,256]{1,0:T(8,128)(2,1)S(1)}, u32[]{:S(2)}, u32[]{:S(2)}) collective-permute-start(bf16[128,256]{1,0:T(8,128)(2,1)S(1)} %get-tuple-element.54), channel_id=1, source_target_pairs={{0,16},{8,24},{16,0},{24,8},{1,17},{9,25},{17,1},{25,9},{2,18},{10... | collective-permute-start | bytes 196616 | tf_op jit(solution)/shard_map/ppermute | solution.py:260
  25.1 5.3 %collective-permute-start.10 = (bf16[128,256]{1,0:T(8,128)(2,1)S(1)}, bf16[128,256]{1,0:T(8,128)(2,1)S(1)}, u32[]{:S(2)}, u32[]{:S(2)}) collective-permute-start(bf16[128,256]{1,0:T(8,128)(2,1)S(1)} %get-tuple-element.55), channel_id=1, source_target_pairs={{0,8},{8,0},{16,24},{24,16},{1,9},{9,1},{17,25},{25,17},{2,10},{10... | collective-permute-start | bytes 196616 | tf_op jit(solution)/shard_map/ppermute | solution.py:260
  28.0 2.6 %collective-permute-start.14 = (bf16[128,256]{1,0:T(8,128)(2,1)S(1)}, bf16[128,256]{1,0:T(8,128)(2,1)S(1)}, u32[]{:S(2)}, u32[]{:S(2)}) collective-permute-start(bf16[128,256]{1,0:T(8,128)(2,1)S(1)} %get-tuple-element.59), channel_id=1, source_target_pairs={{0,1},{1,0},{2,3},{3,2},{4,5},{5,4},{6,7},{7,6},{8,9},{9,8},{10,11... | collective-permute-start | bytes 196616 | tf_op jit(solution)/shard_map/ppermute | solution.py:260
  30.3 1.5 %collective-permute-start.15 = (bf16[384,256]{1,0:T(8,128)(2,1)S(1)}, bf16[384,256]{1,0:T(8,128)(2,1)S(1)}, u32[]{:S(2)}, u32[]{:S(2)}) collective-permute-start(bf16[384,256]{1,0:T(8,128)(2,1)S(1)} %turn.1), channel_id=1, source_target_pairs={{0,1},{1,0},{2,3},{3,2},{4,5},{5,4},{6,7},{7,6},{8,9},{9,8},{10,11... | collective-permute-start | bytes 589832 | tf_op jit(solution)/shard_map/ppermute | solution.py:260

commit v10 on v9

--- a/solution.py
+++ b/solution.py
@@ -242,18 +242,29 @@
 
 
 def final_kernel(own, parts, owner, total, *rest):
-    received, out = rest[:-1], rest[-1]
+    received, (out, done, sems) = rest[:-3], rest[-3:]
     size = total.shape[0] // own
-    first = total[0:size, :]
-    second = total[size : 2 * size, :]
-    for slot, at, row in parts:
-        value = received[at][row : row + size, :].astype(F32)
-        to_second = owner[slot : slot + 1, :] > 0.5
-        first = first + jnp.where(to_second, 0.0, value)
-        second = second + jnp.where(to_second, value, 0.0)
-    out[0:size, :] = first.astype(BF)
-    out[size : 2 * size, :] = second.astype(BF)
-    out[2 * size :, :] = total[2 * size :, :].astype(BF)
+    copies = []
+
+    def leave(first, last, value):
+        done[first:last, :] = value.astype(BF)
+        copies.append(
+            pltpu.make_async_copy(
+                done.at[first:last, :], out.at[first:last, :], sems.at[len(copies)]
+            )
+        )
+        copies[-1].start()
+
+    leave(2 * size, own * size, total[2 * size :, :])
+    for block in range(2):
+        value = total[block * size : (block + 1) * size, :]
+        for slot, at, row in parts:
+            index = owner[slot : slot + 1, :]
+            mine = index > 0.5 if block else index <= 0.5
+            value = value + jnp.where(mine, received[at][row : row + size, :].astype(F32), 0.0)
+        leave(block * size, (block + 1) * size, value)
+    for copy in copies:
+        copy.wait()
 
 
 def swap(value, axis, count, d):
@@ -324,7 +335,6 @@
     for d in even:
         got[d] = (across(edge, d), 0, False, rows_at)
     got[sub_count + 1] = (along(edge, 1), 0, False, rows_at)
-    sibling_rows = across(rows_only, 1)
     dense, dense_t, inverse, choice, features, w_self, w_neigh, grad_out, bias = pl.pallas_call(
         functools.partial(prepare_kernel, *counts),
         out_shape=[
@@ -406,15 +416,19 @@
         choice, dense, features, w_self, bias,
     )
     traded = [0, *even]
+    sibling_rows = across(after(rows_only, value), 1)
     value = call(
         functools.partial(trade_kernel, traded),
         jax.ShapeDtypeStruct((len(traded) * (size + EXTRA), width), BF),
         "trade", 10**6, *[got[d][0] for d in traded], after(sibling_rows, (choice, value)),
     )
+    trade_value = value
     value = across(value, 1)
     for i, d in enumerate(traded):
         got[d + 1] = (value, i * size, True, len(traded) * size + i * EXTRA)
-    near_sum = sum_call(near_kernel, wide, "near", [sub_count + 1, *even], choice, dense, first_sum)
+    near_sum = sum_call(
+        near_kernel, wide, "near", [sub_count + 1, *even], after(choice, trade_value), dense, first_sum
+    )
     if relayed:
         slots_late = [sub_count + d for d in relayed]
         near_sum = sum_call(near_kernel, wide, "late", slots_late, choice, dense, near_sum)
@@ -444,7 +458,7 @@
     beside = (1, across(sibling, 1))
     order = [sub_count + 1, *(sub_count + d for d in direct), *even, *(d + 1 for d in even), 1, *(sub_count + d for d in relayed)]
     arrays, at = unique(order)
-    early = far[:1:-1]
+    early = []
     total, owner = pl.pallas_call(
         functools.partial(
             own_kernel, own, sub_count, [(slot, at[slot], got[slot][3]) for slot in order],
@@ -454,7 +468,7 @@
         in_specs=[VMEM] * (6 + len(arrays) + len(early)),
         out_specs=[VMEM] * 2,
         compiler_params=PARAMS,
-        cost_estimate=cost(10**9, 2 * 1024 * 1024),
+        cost_estimate=cost(2*10**9, 2 * 1024 * 1024),
         name="own",
     )(
         *[value for _, value in early], *arrays,
@@ -468,7 +482,7 @@
     )
     turned = across(turned, 1)
 
-    more = [far[1], far[0], *near[::-1]]
+    more = [far[2], far[1], far[0], *near[::-1]]
     if more:
         total = call(
             functools.partial(add_kernel, own, [(slot, i, 0) for i, (slot, _) in enumerate(more)]),
@@ -477,10 +491,17 @@
     last = [beside]
     parts = [(slot, i, 0) for i, (slot, _) in enumerate(last)]
     parts += [(d + 1, len(last), i * size) for i, d in enumerate(even)]
-    return call(
-        functools.partial(final_kernel, own, parts), narrow, "final", rows * width * 4,
-        owner, total, *[value for _, value in last], turned,
-    )
+    values = [value for _, value in last]
+    return pl.pallas_call(
+        functools.partial(final_kernel, own, parts),
+        out_shape=narrow,
+        in_specs=[VMEM] * (3 + len(values)),
+        out_specs=HBM,
+        scratch_shapes=[pltpu.VMEM((rows, width), BF), pltpu.SemaphoreType.DMA((3,))],
+        compiler_params=PARAMS,
+        cost_estimate=cost(rows * width * 4, 1024 * 1024),
+        name="final",
+    )(owner, total, *values, turned)
 
 
 def solution(mesh):

time: 32.8 us -> 33.4 us (1.018)
  waiting for transfers between devices: 7.15 us -> 7.68 us
    pallas_call x0 -> x1, Pallas kernels: none -> 0.78 us  [shards(): pl.pallas_call(functools.partial(final_kernel, own, parts), out_shape=nar...]
    pallas_call x6 -> x5, Pallas kernels: 1.23 us -> 0.47 us  [call(): pl.pallas_call(kernel, out_shape=out_shape, in_specs=[VMEM] * len(operand...]
    ppermute x16, waiting for transfers between devices: 7.15 us -> 7.68 us  [swap(): return lax.ppermute(value, axis, [(i, i ^ d) for i in range(count)])]
  transfers between devices with their start and end apart: 16 -> 16, of which waited for: 7 -> 9; matrix products, arithmetic and copies ran while one was open for 0% -> 0% of each run, Pallas kernels for 12% -> 11%
where the time goes in v10:
time: 33.4 us; the launch traced here: 33.2 us
  starting transfers between devices  18.6 us (56%)
  waiting for transfers between devices  7.68 us (23%)
  Pallas kernels  6.76 us (20%)
    ppermute x16, starting transfers between devices, swap(): return lax.ppermute(value, axis, [(i, i ^ d) for i in range(count)])  18.6 us
    ppermute x16, waiting for transfers between devices, swap(): return lax.ppermute(value, axis, [(i, i ^ d) for i in range(count)])  7.68 us
    pallas_call x1, Pallas kernels, shards(): pl.pallas_call(functools.partial(prepare_kernel, *counts), out_shape=[jax...  2.11 us
    pallas_call x1, Pallas kernels, shards(): pl.pallas_call(functools.partial(middle_kernel, *counts, late_halos, len(...  1.26 us
    pallas_call x1, Pallas kernels, shards(): pl.pallas_call(edge_kernel, out_shape=[jax.ShapeDtypeStruct((BOUNDARY * s...  0.93 us
    pallas_call x3, Pallas kernels, sum_call(): pl.pallas_call(functools.partial(kernel, own, halos), out_shape=out_shape...  0.91 us
    pallas_call x1, Pallas kernels, shards(): pl.pallas_call(functools.partial(final_kernel, own, parts), out_shape=nar...  0.78 us
  transfers between devices with their start and end apart: 16, of which 9 were waited for; matrix products, arithmetic and copies ran while one was open for 0% of the time, Pallas kernels for 11%

profile of v10, /device:TPU:0, one launch (start us, length us, event | category | flops | bytes accessed | tf_op | source)
XLA Modules:
  0.0 33.2 jit_solution(12427192781130887464)
XLA Ops:
  0.0 0.9 %edge.1 = (bf16[272,256]{1,0:T(8,128)(2,1)S(1)}, bf16[16,256]{1,0:T(8,128)(2,1)S(1)}) custom-call(s32[1,8]{1,0:T(1,128)} %recv_sub_hbm.1, s32[1,4]{1,0:T(1,128)} %recv_cluster_hbm.1, bf16[384,256]{1,0:T(8,128)(2,1)} %features_hbm.1), custom_call_target="tpu_custom_call" | custom-call | flops 1024 | bytes 262144 | tf_op jit(solution)/shard_map/edge/pallas_call | solution.py:304
  0.9 4.1 %collective-permute-start.1 = (bf16[272,256]{1,0:T(8,128)(2,1)S(1)}, bf16[272,256]{1,0:T(8,128)(2,1)S(1)}, u32[]{:S(2)}, u32[]{:S(2)}) collective-permute-start(bf16[272,256]{1,0:T(8,128)(2,1)S(1)} %get-tuple-element.36.rest_0_), channel_id=1, source_target_pairs={{0,16},{8,24},{16,0},{24,8},{1,17},{9,25},{17,1},{25,9},{2,18},{10... | collective-permute-start | bytes 417800 | tf_op jit(solution)/shard_map/ppermute | solution.py:271
  5.0 1.6 %collective-permute-start = (bf16[272,256]{1,0:T(8,128)(2,1)S(1)}, bf16[272,256]{1,0:T(8,128)(2,1)S(1)}, u32[]{:S(2)}, u32[]{:S(2)}) collective-permute-start(bf16[272,256]{1,0:T(8,128)(2,1)S(1)} %get-tuple-element.36.rest_0_), channel_id=1, source_target_pairs={{0,8},{8,0},{16,24},{24,16},{1,9},{9,1},{17,25},{25,17},{2,10},{10... | collective-permute-start | bytes 417800 | tf_op jit(solution)/shard_map/ppermute | solution.py:271
  6.6 2.4 %collective-permute-start.4 = (bf16[272,256]{1,0:T(8,128)(2,1)S(1)}, bf16[272,256]{1,0:T(8,128)(2,1)S(1)}, u32[]{:S(2)}, u32[]{:S(2)}) collective-permute-start(bf16[272,256]{1,0:T(8,128)(2,1)S(1)} %get-tuple-element.36.rest_0_), channel_id=1, source_target_pairs={{0,6},{1,7},{2,4},{3,5},{4,2},{5,3},{6,0},{7,1},{8,14},{9,15},{10,... | collective-permute-start | bytes 417800 | tf_op jit(solution)/shard_map/ppermute | solution.py:271
  9.1 0.5 %collective-permute-start.3 = (bf16[272,256]{1,0:T(8,128)(2,1)S(1)}, bf16[272,256]{1,0:T(8,128)(2,1)S(1)}, u32[]{:S(2)}, u32[]{:S(2)}) collective-permute-start(bf16[272,256]{1,0:T(8,128)(2,1)S(1)} %get-tuple-element.36.rest_0_), channel_id=1, source_target_pairs={{0,4},{1,5},{2,6},{3,7},{4,0},{5,1},{6,2},{7,3},{8,12},{9,13},{10,... | collective-permute-start | bytes 417800 | tf_op jit(solution)/shard_map/ppermute | solution.py:271
  9.6 0.5 %collective-permute-start.2 = (bf16[272,256]{1,0:T(8,128)(2,1)S(1)}, bf16[272,256]{1,0:T(8,128)(2,1)S(1)}, u32[]{:S(2)}, u32[]{:S(2)}) collective-permute-start(bf16[272,256]{1,0:T(8,128)(2,1)S(1)} %get-tuple-element.36.rest_0_), channel_id=1, source_target_pairs={{0,2},{1,3},{2,0},{3,1},{4,6},{5,7},{6,4},{7,5},{8,10},{9,11},{10,... | collective-permute-start | bytes 417800 | tf_op jit(solution)/shard_map/ppermute | solution.py:271
  10.1 2.1 %prepare.1 = (bf16[384,1920]{1,0:T(8,128)(2,1)S(1)}, bf16[1920,384]{1,0:T(8,128)(2,1)S(1)}, f32[384,128]{1,0:T(8,128)S(1)}, f32[12,256]{1,0:T(8,128)S(1)}, bf16[...) custom-call(s32[24]{0:T(128)} %tile_dst_hbm.1, ...), custom_call_target="tpu_custom_call" | custom-call | flops 100000000 | bytes 6291456 | tf_op jit(solution)/shard_map/prepare/pallas_call | solution.py:338
  12.2 0.0 collective-permute-done.1.message.far.rest_1_
  12.2 0.0 collective-permute-done.near.rest_0_
  12.3 0.1 relay.1
  12.4 1.3 %collective-permute-start.7 = (bf16[144,256]{1,0:T(8,128)(2,1)S(1)}, bf16[144,256]{1,0:T(8,128)(2,1)S(1)}, u32[]{:S(2)}, u32[]{:S(2)}) collective-permute-start(bf16[144,256]{1,0:T(8,128)(2,1)S(1)} %relay.1), channel_id=1, source_target_pairs={{0,8},{8,0},{16,24},{24,16},{1,9},{9,1},{17,25},{25,17},{2,10},{10... | collective-permute-start | bytes 221192 | tf_op jit(solution)/shard_map/ppermute | solution.py:271
  13.6 0.0 collective-permute-start.5
  13.6 0.4 %first.1 = (f32[384,256]{1,0:T(8,128)S(1)}, f32[384,256]{1,0:T(8,128)S(1)}) custom-call(f32[12,256]{1,0:T(8,128)S(1)} %get-tuple-element.46.choice.rest_7_, bf16[384,1920]{1,0:T(8,128)(2,1)S(1)} %get-tuple-element.45.dense, bf16[384,256]{1,0:T(8,128)(2,1)S(1)} %get-tuple-element.47.features, bf16[256,256]{1,0:T(8,128)(2,1)S(1)} %get-tuple-element.41.w_self.rest_8_, ...), custom_call_target="tpu_custom_call" | custom-call | flops 1000000000 | bytes 3145728 | tf_op jit(solution)/shard_map/first/pallas_call | solution.py:392
  14.1 0.7 %collective-permute-done.5.rest_4_ = bf16[16,256]{1,0:T(8,128)(2,1)S(1)} collective-permute-done((bf16[16,256]{1,0:T(8,128)(2,1)S(1)}, bf16[16,256]{1,0:T(8,128)(2,1)S(1)}, u32[]{:S(2)}, u32[]{:S(2)}) %collective-permute-start.5) | collective-permute-done | bytes 8224 | tf_op jit(solution)/shard_map/ppermute | solution.py:271
  14.8 0.0 collective-permute-done.4.rest_3_.rest_4_
  14.8 0.5 %collective-permute-done.3.rest_2_.rest_3_ = bf16[272,256]{1,0:T(8,128)(2,1)S(1)} collective-permute-done((bf16[272,256]{1,0:T(8,128)(2,1)S(1)}, bf16[272,256]{1,0:T(8,128)(2,1)S(1)}, u32[]{:S(2)}, u32[]{:S(2)}) %collective-permute-start.3) | collective-permute-done | bytes 139296 | tf_op jit(solution)/shard_map/ppermute | solution.py:271
  15.4 0.1 collective-permute-done.2.rest_1_.rest_2_
  15.4 0.2 trade.1
  15.6 0.1 collective-permute-start.6
  15.6 0.3 near.1.before
  16.0 0.8 %collective-permute-done.7.rest_0_.rest_6_ = bf16[144,256]{1,0:T(8,128)(2,1)S(1)} collective-permute-done((bf16[144,256]{1,0:T(8,128)(2,1)S(1)}, bf16[144,256]{1,0:T(8,128)(2,1)S(1)}, u32[]{:S(2)}, u32[]{:S(2)}) %collective-permute-start.7) | collective-permute-done | bytes 73760 | tf_op jit(solution)/shard_map/ppermute | solution.py:271
  16.8 0.2 late.1.before
  17.0 0.2 collective-permute-done.6.rest_0_.rest_5_
  17.2 1.3 %middle.1 = (bf16[256,256]{1,0:T(8,128)(2,1)S(1)}, bf16[256,256]{1,0:T(8,128)(2,1)S(1)}, bf16[256,256]{1,0:T(8,128)(2,1)S(1)}, bf16[128,256]{1,0:T(8,128)(2,1)S(...) custom-call(f32[12,256]{1,0:T(8,128)S(1)} %get-tuple-element.46.choi, ...), custom_call_target="tpu_custom_call" | custom-call | flops 377487360 | bytes 6291456 | tf_op jit(solution)/shard_map/middle/pallas_call | solution.py:439
  18.5 2.3 %collective-permute-start.11 = (bf16[256,256]{1,0:T(8,128)(2,1)S(1)}, bf16[256,256]{1,0:T(8,128)(2,1)S(1)}, u32[]{:S(2)}, u32[]{:S(2)}) collective-permute-start(bf16[256,256]{1,0:T(8,128)(2,1)S(1)} %get-tuple-element.60), channel_id=1, source_target_pairs={{0,6},{1,7},{2,4},{3,5},{4,2},{5,3},{6,0},{7,1},{8,14},{9,15},{10,... | collective-permute-start | bytes 393224 | tf_op jit(solution)/shard_map/ppermute | solution.py:271
  20.8 3.0 %collective-permute-start.8 = (bf16[128,256]{1,0:T(8,128)(2,1)S(1)}, bf16[128,256]{1,0:T(8,128)(2,1)S(1)}, u32[]{:S(2)}, u32[]{:S(2)}) collective-permute-start(bf16[128,256]{1,0:T(8,128)(2,1)S(1)} %get-tuple-element.57), channel_id=1, source_target_pairs={{0,24},{8,16},{16,8},{24,0},{1,25},{9,17},{17,9},{25,1},{2,26},{10... | collective-permute-start | bytes 196616 | tf_op jit(solution)/shard_map/ppermute | solution.py:271
  23.8 0.0 collective-permute-start.9
  23.8 1.4 %collective-permute-start.10 = (bf16[128,256]{1,0:T(8,128)(2,1)S(1)}, bf16[128,256]{1,0:T(8,128)(2,1)S(1)}, u32[]{:S(2)}, u32[]{:S(2)}) collective-permute-start(bf16[128,256]{1,0:T(8,128)(2,1)S(1)} %get-tuple-element.59), channel_id=1, source_target_pairs={{0,8},{8,0},{16,24},{24,16},{1,9},{9,1},{17,25},{25,17},{2,10},{10... | collective-permute-start | bytes 196616 | tf_op jit(solution)/shard_map/ppermute | solution.py:271
  25.2 0.8 %collective-permute-start.12 = (bf16[256,256]{1,0:T(8,128)(2,1)S(1)}, bf16[256,256]{1,0:T(8,128)(2,1)S(1)}, u32[]{:S(2)}, u32[]{:S(2)}) collective-permute-start(bf16[256,256]{1,0:T(8,128)(2,1)S(1)} %get-tuple-element.61), channel_id=1, source_target_pairs={{0,4},{1,5},{2,6},{3,7},{4,0},{5,1},{6,2},{7,3},{8,12},{9,13},{10,... | collective-permute-start | bytes 393224 | tf_op jit(solution)/shard_map/ppermute | solution.py:271
  25.9 0.0 collective-permute-done.11.rest_3_.rest_2_
  25.9 0.6 %collective-permute-start.13 = (bf16[256,256]{1,0:T(8,128)(2,1)S(1)}, bf16[256,256]{1,0:T(8,128)(2,1)S(1)}, u32[]{:S(2)}, u32[]{:S(2)}) collective-permute-start(bf16[256,256]{1,0:T(8,128)(2,1)S(1)} %get-tuple-element.62), channel_id=1, source_target_pairs={{0,2},{1,3},{2,0},{3,1},{4,6},{5,7},{6,4},{7,5},{8,10},{9,11},{10,... | collective-permute-start | bytes 393224 | tf_op jit(solution)/shard_map/ppermute | solution.py:271
  26.5 0.3 own.1
  26.8 3.3 %collective-permute-done.12.rest_4_.rest_1_ = bf16[256,256]{1,0:T(8,128)(2,1)S(1)} collective-permute-done((bf16[256,256]{1,0:T(8,128)(2,1)S(1)}, bf16[256,256]{1,0:T(8,128)(2,1)S(1)}, u32[]{:S(2)}, u32[]{:S(2)}) %collective-permute-start.12) | collective-permute-done | bytes 131104 | tf_op jit(solution)/shard_map/ppermute | solution.py:271
  30.1 0.0 collective-permute-start.14
  30.1 0.8 %collective-permute-done.13.rest_5_.rest_0_ = bf16[256,256]{1,0:T(8,128)(2,1)S(1)} collective-permute-done((bf16[256,256]{1,0:T(8,128)(2,1)S(1)}, bf16[256,256]{1,0:T(8,128)(2,1)S(1)}, u32[]{:S(2)}, u32[]{:S(2)}) %collective-permute-start.13) | collective-permute-done | bytes 131104 | tf_op jit(solution)/shard_map/ppermute | solution.py:271
  30.9 0.1 collective-permute-start.15
  31.0 0.0 collective-permute-done.8.rest_0_
  31.0 0.0 collective-permute-done.9.rest_1_
  31.0 0.0 collective-permute-done.10.rest_2_
  31.0 0.2 add.1.total
  31.2 0.2 collective-permute-done.14.rest_0_
  31.4 1.0 %collective-permute-done.15.rest_1_ = bf16[384,256]{1,0:T(8,128)(2,1)S(1)} collective-permute-done((bf16[384,256]{1,0:T(8,128)(2,1)S(1)}, bf16[384,256]{1,0:T(8,128)(2,1)S(1)}, u32[]{:S(2)}, u32[]{:S(2)}) %collective-permute-start.15) | collective-permute-done | bytes 196640 | tf_op jit(solution)/shard_map/ppermute | solution.py:271
  32.4 0.8 %final.1 = bf16[384,256]{1,0:T(8,128)(2,1)} custom-call(f32[12,256]{1,0:T(8,128)S(1)} %get-tuple-element.55.owner, f32[384,256]{1,0:T(8,128)S(1)} %add.1.total, bf16[128,256]{1,0:T(8,128)(2,1)S(1)} %collective-permute-done.14.rest_0_, bf16[384,256]{1,0:T(8,128)(2,1)S(1)} %collective-permute-done.15.rest_1_), custom_call_target="tpu_custom_call" | custom-call | flops 393216 | bytes 1048576 | tf_op jit(solution)/shard_map/final/pallas_call | solution.py:495
  (2 shorter events, 0.0 us)
Async XLA Ops:
  0.9 11.3 %collective-permute-start.1 = (bf16[272,256]{1,0:T(8,128)(2,1)S(1)}, bf16[272,256]{1,0:T(8,128)(2,1)S(1)}, u32[]{:S(2)}, u32[]{:S(2)}) collective-permute-start(bf16[272,256]{1,0:T(8,128)(2,1)S(1)} %get-tuple-element.36.rest_0_), channel_id=1, source_target_pairs={{0,16},{8,24},{16,0},{24,8},{1,17},{9,25},{17,1},{25,9},{2,18},{10... | collective-permute-start | bytes 417800 | tf_op jit(solution)/shard_map/ppermute | solution.py:271
  5.0 7.2 %collective-permute-start = (bf16[272,256]{1,0:T(8,128)(2,1)S(1)}, bf16[272,256]{1,0:T(8,128)(2,1)S(1)}, u32[]{:S(2)}, u32[]{:S(2)}) collective-permute-start(bf16[272,256]{1,0:T(8,128)(2,1)S(1)} %get-tuple-element.36.rest_0_), channel_id=1, source_target_pairs={{0,8},{8,0},{16,24},{24,16},{1,9},{9,1},{17,25},{25,17},{2,10},{10... | collective-permute-start | bytes 417800 | tf_op jit(solution)/shard_map/ppermute | solution.py:271
  6.6 8.2 %collective-permute-start.4 = (bf16[272,256]{1,0:T(8,128)(2,1)S(1)}, bf16[272,256]{1,0:T(8,128)(2,1)S(1)}, u32[]{:S(2)}, u32[]{:S(2)}) collective-permute-start(bf16[272,256]{1,0:T(8,128)(2,1)S(1)} %get-tuple-element.36.rest_0_), channel_id=1, source_target_pairs={{0,6},{1,7},{2,4},{3,5},{4,2},{5,3},{6,0},{7,1},{8,14},{9,15},{10,... | collective-permute-start | bytes 417800 | tf_op jit(solution)/shard_map/ppermute | solution.py:271
  9.1 6.3 %collective-permute-start.3 = (bf16[272,256]{1,0:T(8,128)(2,1)S(1)}, bf16[272,256]{1,0:T(8,128)(2,1)S(1)}, u32[]{:S(2)}, u32[]{:S(2)}) collective-permute-start(bf16[272,256]{1,0:T(8,128)(2,1)S(1)} %get-tuple-element.36.rest_0_), channel_id=1, source_target_pairs={{0,4},{1,5},{2,6},{3,7},{4,0},{5,1},{6,2},{7,3},{8,12},{9,13},{10,... | collective-permute-start | bytes 417800 | tf_op jit(solution)/shard_map/ppermute | solution.py:271
  9.6 5.8 %collective-permute-start.2 = (bf16[272,256]{1,0:T(8,128)(2,1)S(1)}, bf16[272,256]{1,0:T(8,128)(2,1)S(1)}, u32[]{:S(2)}, u32[]{:S(2)}) collective-permute-start(bf16[272,256]{1,0:T(8,128)(2,1)S(1)} %get-tuple-element.36.rest_0_), channel_id=1, source_target_pairs={{0,2},{1,3},{2,0},{3,1},{4,6},{5,7},{6,4},{7,5},{8,10},{9,11},{10,... | collective-permute-start | bytes 417800 | tf_op jit(solution)/shard_map/ppermute | solution.py:271
  12.4 4.4 %collective-permute-start.7 = (bf16[144,256]{1,0:T(8,128)(2,1)S(1)}, bf16[144,256]{1,0:T(8,128)(2,1)S(1)}, u32[]{:S(2)}, u32[]{:S(2)}) collective-permute-start(bf16[144,256]{1,0:T(8,128)(2,1)S(1)} %relay.1), channel_id=1, source_target_pairs={{0,8},{8,0},{16,24},{24,16},{1,9},{9,1},{17,25},{25,17},{2,10},{10... | collective-permute-start | bytes 221192 | tf_op jit(solution)/shard_map/ppermute | solution.py:271
  13.6 1.2 %collective-permute-start.5 = (bf16[16,256]{1,0:T(8,128)(2,1)S(1)}, bf16[16,256]{1,0:T(8,128)(2,1)S(1)}, u32[]{:S(2)}, u32[]{:S(2)}) collective-permute-start(bf16[16,256]{1,0:T(8,128)(2,1)S(1)} %get-tuple-element.38), channel_id=1, source_target_pairs={{0,1},{1,0},{2,3},{3,2},{4,5},{5,4},{6,7},{7,6},{8,9},{9,8},{10,11... | collective-permute-start | bytes 24584 | tf_op jit(solution)/shard_map/ppermute | solution.py:271
  15.6 1.6 %collective-permute-start.6 = (bf16[576,256]{1,0:T(8,128)(2,1)S(1)}, bf16[576,256]{1,0:T(8,128)(2,1)S(1)}, u32[]{:S(2)}, u32[]{:S(2)}) collective-permute-start(bf16[576,256]{1,0:T(8,128)(2,1)S(1)} %trade.1), channel_id=1, source_target_pairs={{0,1},{1,0},{2,3},{3,2},{4,5},{5,4},{6,7},{7,6},{8,9},{9,8},{10,11... | collective-permute-start | bytes 884744 | tf_op jit(solution)/shard_map/ppermute | solution.py:271
  18.5 7.4 %collective-permute-start.11 = (bf16[256,256]{1,0:T(8,128)(2,1)S(1)}, bf16[256,256]{1,0:T(8,128)(2,1)S(1)}, u32[]{:S(2)}, u32[]{:S(2)}) collective-permute-start(bf16[256,256]{1,0:T(8,128)(2,1)S(1)} %get-tuple-element.60), channel_id=1, source_target_pairs={{0,6},{1,7},{2,4},{3,5},{4,2},{5,3},{6,0},{7,1},{8,14},{9,15},{10,... | collective-permute-start | bytes 393224 | tf_op jit(solution)/shard_map/ppermute | solution.py:271
  20.8 10.2 %collective-permute-start.8 = (bf16[128,256]{1,0:T(8,128)(2,1)S(1)}, bf16[128,256]{1,0:T(8,128)(2,1)S(1)}, u32[]{:S(2)}, u32[]{:S(2)}) collective-permute-start(bf16[128,256]{1,0:T(8,128)(2,1)S(1)} %get-tuple-element.57), channel_id=1, source_target_pairs={{0,24},{8,16},{16,8},{24,0},{1,25},{9,17},{17,9},{25,1},{2,26},{10... | collective-permute-start | bytes 196616 | tf_op jit(solution)/shard_map/ppermute | solution.py:271
  23.8 7.3 %collective-permute-start.9 = (bf16[128,256]{1,0:T(8,128)(2,1)S(1)}, bf16[128,256]{1,0:T(8,128)(2,1)S(1)}, u32[]{:S(2)}, u32[]{:S(2)}) collective-permute-start(bf16[128,256]{1,0:T(8,128)(2,1)S(1)} %get-tuple-element.58), channel_id=1, source_target_pairs={{0,16},{8,24},{16,0},{24,8},{1,17},{9,25},{17,1},{25,9},{2,18},{10... | collective-permute-start | bytes 196616 | tf_op jit(solution)/shard_map/ppermute | solution.py:271
  23.8 7.3 %collective-permute-start.10 = (bf16[128,256]{1,0:T(8,128)(2,1)S(1)}, bf16[128,256]{1,0:T(8,128)(2,1)S(1)}, u32[]{:S(2)}, u32[]{:S(2)}) collective-permute-start(bf16[128,256]{1,0:T(8,128)(2,1)S(1)} %get-tuple-element.59), channel_id=1, source_target_pairs={{0,8},{8,0},{16,24},{24,16},{1,9},{9,1},{17,25},{25,17},{2,10},{10... | collective-permute-start | bytes 196616 | tf_op jit(solution)/shard_map/ppermute | solution.py:271
  25.2 5.0 %collective-permute-start.12 = (bf16[256,256]{1,0:T(8,128)(2,1)S(1)}, bf16[256,256]{1,0:T(8,128)(2,1)S(1)}, u32[]{:S(2)}, u32[]{:S(2)}) collective-permute-start(bf16[256,256]{1,0:T(8,128)(2,1)S(1)} %get-tuple-element.61), channel_id=1, source_target_pairs={{0,4},{1,5},{2,6},{3,7},{4,0},{5,1},{6,2},{7,3},{8,12},{9,13},{10,... | collective-permute-start | bytes 393224 | tf_op jit(solution)/shard_map/ppermute | solution.py:271
  25.9 5.0 %collective-permute-start.13 = (bf16[256,256]{1,0:T(8,128)(2,1)S(1)}, bf16[256,256]{1,0:T(8,128)(2,1)S(1)}, u32[]{:S(2)}, u32[]{:S(2)}) collective-permute-start(bf16[256,256]{1,0:T(8,128)(2,1)S(1)} %get-tuple-element.62), channel_id=1, source_target_pairs={{0,2},{1,3},{2,0},{3,1},{4,6},{5,7},{6,4},{7,5},{8,10},{9,11},{10,... | collective-permute-start | bytes 393224 | tf_op jit(solution)/shard_map/ppermute | solution.py:271
  30.1 1.3 %collective-permute-start.14 = (bf16[128,256]{1,0:T(8,128)(2,1)S(1)}, bf16[128,256]{1,0:T(8,128)(2,1)S(1)}, u32[]{:S(2)}, u32[]{:S(2)}) collective-permute-start(bf16[128,256]{1,0:T(8,128)(2,1)S(1)} %get-tuple-element.63), channel_id=1, source_target_pairs={{0,1},{1,0},{2,3},{3,2},{4,5},{5,4},{6,7},{7,6},{8,9},{9,8},{10,11... | collective-permute-start | bytes 196616 | tf_op jit(solution)/shard_map/ppermute | solution.py:271
  30.9 1.5 %collective-permute-start.15 = (bf16[384,256]{1,0:T(8,128)(2,1)S(1)}, bf16[384,256]{1,0:T(8,128)(2,1)S(1)}, u32[]{:S(2)}, u32[]{:S(2)}) collective-permute-start(bf16[384,256]{1,0:T(8,128)(2,1)S(1)} %turn.1), channel_id=1, source_target_pairs={{0,1},{1,0},{2,3},{3,2},{4,5},{5,4},{6,7},{7,6},{8,9},{9,8},{10,11... | collective-permute-start | bytes 589832 | tf_op jit(solution)/shard_map/ppermute | solution.py:271

commit v11 on v10

--- a/solution.py
+++ b/solution.py
@@ -11,6 +11,7 @@
 F32 = jnp.float32
 BOUNDARY = 2
 EXTRA = 16
+CHUNKS = 4
 VMEM = pl.BlockSpec(memory_space=pltpu.VMEM)
 HBM = pl.BlockSpec(memory_space=pltpu.HBM)
 PARAMS = pltpu.CompilerParams(vmem_limit_bytes=24 * 1024 * 1024)
@@ -32,22 +33,29 @@
 
 def edge_kernel(recv_sub, recv_cluster, features, edge, rows, sub_row, cluster_row, sems):
     count = edge.shape[0] - EXTRA
-    copies = [
-        pltpu.make_async_copy(features.at[0:count, :], edge.at[0:count, :], sems.at[0]),
-        pltpu.make_async_copy(recv_sub, sub_row, sems.at[1]),
-        pltpu.make_async_copy(recv_cluster, cluster_row, sems.at[2]),
+    step = count // CHUNKS
+    small = [
+        pltpu.make_async_copy(recv_sub, sub_row, sems.at[0]),
+        pltpu.make_async_copy(recv_cluster, cluster_row, sems.at[1]),
     ]
-    for copy in copies:
+    large = []
+    for i in range(CHUNKS):
+        part = slice(i * step, (i + 1) * step)
+        large.append(
+            pltpu.make_async_copy(features.at[part, :], edge.at[part, :], sems.at[2 + i])
+        )
+    for copy in small + large:
         copy.start()
-    copies[1].wait()
-    copies[2].wait()
+    for copy in small:
+        copy.wait()
     sub_count, cluster_count = sub_row.shape[1], cluster_row.shape[1]
     pad = jnp.zeros((1, edge.shape[1] - sub_count - cluster_count), F32)
     row = jnp.concatenate([sub_row[...].astype(F32), cluster_row[...].astype(F32), pad], axis=1)
     value = jnp.broadcast_to(row, rows.shape).astype(BF)
     edge[count:, :] = value
     rows[...] = value
-    copies[0].wait()
+    for copy in large:
+        copy.wait()
 
 
 def prepare_kernel(
@@ -58,9 +66,14 @@
     tile_dst, tile_src, recv_sub, recv_cluster, tile_weight, sems,
 ):
     size = tile_weight.shape[1]
+    step = tile_weight.shape[0] // CHUNKS
     pairs = (
         (tile_dst_hbm, tile_dst), (tile_src_hbm, tile_src), (recv_sub_hbm, recv_sub),
-        (recv_cluster_hbm, recv_cluster), (tile_weight_hbm, tile_weight),
+        (recv_cluster_hbm, recv_cluster),
+        *(
+            (tile_weight_hbm.at[i * step : (i + 1) * step], tile_weight.at[i * step : (i + 1) * step])
+            for i in range(CHUNKS)
+        ),
         (features_hbm, features), (w_self_hbm, w_self), (w_neigh_hbm, w_neigh),
         (grad_out_hbm, grad_out), (bias_hbm, bias),
     )
@@ -71,7 +84,7 @@
     cluster_id = lax.axis_index("cluster")
     dense[...] = jnp.zeros_like(dense)
     dense_t[...] = jnp.zeros_like(dense_t)
-    for copy in copies[:5]:
+    for copy in copies[: 4 + CHUNKS]:
         copy.wait()
 
     def place(t, carry):
@@ -99,7 +112,7 @@
         total = total + dense[:, slot * size : (slot + 1) * size].astype(F32)
     degree = jnp.sum(total, axis=1, keepdims=True)
     inverse[...] = jnp.broadcast_to(1.0 / (degree + 1.0), inverse.shape)
-    for copy in copies[5:]:
+    for copy in copies[4 + CHUNKS :]:
         copy.wait()
 
 
@@ -123,10 +136,9 @@
 
 
 def relay_kernel(sub_count, d, far, rows, near, out):
-    size = out.shape[0] - EXTRA
+    size = out.shape[0]
     index = lane_of(index_row(near, size), sub_count + (lax.axis_index("cluster") ^ d))
-    out[0:size, :] = pick(far, index, size)
-    out[size:, :] = rows[...]
+    out[...] = pick(far, index, size)
 
 
 def trade_kernel(even, *rest):
@@ -144,7 +156,8 @@
     messages, out = rest[:-1], rest[-1]
     size = out.shape[0] // len(messages)
     for i, message in enumerate(messages):
-        out[i * size : (i + 1) * size, :] = message[size : 2 * size, :]
+        last = message.shape[0]
+        out[i * size : (i + 1) * size, :] = message[last - size : last, :]
 
 
 def halo_sum(choice, dense, own, halos, refs, halo):
@@ -175,11 +188,12 @@
 
 
 def middle_kernel(
-    own, sub_count, cluster_count, halos, received,
+    own, sub_count, cluster_count, halos, received, carried,
     choice, grad_out, w_neigh, dense, dense_t, before, own_pre, inverse,
     *rest,
 ):
     refs, rest = rest[:received], rest[received:]
+    rows, rest = rest[:carried], rest[carried:]
     pairs, rest = rest[: sub_count // 2 - 1], rest[sub_count // 2 - 1 :]
     along, (sibling, kept, spread, grad_pre, halo) = rest[:-5], rest[-5:]
     size = dense.shape[0] // own
@@ -198,7 +212,9 @@
     for i, target in enumerate(pairs):
         target[...] = partial(2 * (i + 1), 2)
     for i, target in enumerate(along):
-        target[...] = partial(sub_count + 1 + i)
+        target[0:size, :] = partial(sub_count + 1 + i)
+    for i, value in enumerate(rows):
+        along[0][size + i * EXTRA : size + (i + 1) * EXTRA, :] = value[...]
     sibling[...] = partial(1)
     kept[0] = partial(0)
     kept[1] = partial(sub_count)
@@ -210,8 +226,7 @@
     total[size : 2 * size, :] = total[size : 2 * size, :] + jnp.where(second, value, zero)
 
 
-def own_kernel(own, sub_count, rows, received, parts, *rest):
-    back, rest = rest[: len(parts)], rest[len(parts) :]
+def own_kernel(own, sub_count, rows, received, *rest):
     messages, rest = rest[:received], rest[received:]
     choice, w_self, dense_t, kept, spread, grad_pre, total, owner = rest
     size = kept.shape[1]
@@ -227,18 +242,20 @@
             lane = sub_count + lax.axis_index("cluster")
         index = lane_of(messages[at][row : row + EXTRA, :].astype(F32)[0:1, :], lane)
         owner[slot : slot + 1, :] = jnp.broadcast_to(index, (1, width))
-    for slot, at, row in parts:
-        value = back[at][row : row + size, :].astype(F32)
-        split(total, value, owner[slot : slot + 1, :] > 0.5, size)
-
-
-def add_kernel(own, parts, owner, before, *rest):
+
+
+def add_kernel(own, sub_count, parts, rows, owner, before, *rest):
     received, total = rest[:-1], rest[-1]
     size = total.shape[0] // own
     total[...] = before[...]
     for slot, at, row in parts:
         value = received[at][row : row + size, :].astype(F32)
-        split(total, value, owner[slot : slot + 1, :] > 0.5, size)
+        index = owner[slot : slot + 1, :]
+        if slot in rows:
+            where, first = rows[slot]
+            indices = received[where][first : first + EXTRA, :].astype(F32)[0:1, :]
+            index = lane_of(indices, sub_count + lax.axis_index("cluster"))
+        split(total, value, index > 0.5, size)
 
 
 def final_kernel(own, parts, owner, total, *rest):
@@ -312,7 +329,7 @@
         scratch_shapes=[
             pltpu.VMEM(recv_sub.shape, jnp.int32),
             pltpu.VMEM(recv_cluster.shape, jnp.int32),
-            pltpu.SemaphoreType.DMA((3,)),
+            pltpu.SemaphoreType.DMA((2 + CHUNKS,)),
         ],
         compiler_params=PARAMS,
         cost_estimate=cost(1024, 256 * 1024),
@@ -356,7 +373,7 @@
             pltpu.SMEM(recv_sub.shape, jnp.int32),
             pltpu.SMEM(recv_cluster.shape, jnp.int32),
             pltpu.VMEM(tile_weight.shape, BF),
-            pltpu.SemaphoreType.DMA((10,)),
+            pltpu.SemaphoreType.DMA((9 + CHUNKS,)),
         ],
         compiler_params=PARAMS,
         cost_estimate=cost(10**8, 6 * 1024 * 1024),
@@ -400,6 +417,7 @@
             name=name,
         )(*operands, *arrays)
 
+    carried = []
     for d in relayed:
         far = got[sub_count + d - 1][0]
         far_rows = call(
@@ -407,10 +425,11 @@
         )
         value = call(
             functools.partial(relay_kernel, sub_count, d - 1),
-            jax.ShapeDtypeStruct((size + EXTRA, width), BF),
+            block,
             "relay", 10**6, far, far_rows, got[sub_count + 1][0],
         )
-        got[sub_count + d] = (along(value, 1), 0, True, size)
+        carried.append(far_rows)
+        got[sub_count + d] = (along(value, 1), 0, True, None)
     first_sum, own_pre = sum_call(
         first_kernel, [wide, wide], "first", [0, sub_count, *(sub_count + d for d in direct)],
         choice, dense, features, w_self, bias,
@@ -437,11 +456,12 @@
     late_arrays, late_at = unique(late)
     late_halos = [(slot, late_at[slot], got[slot][1], got[slot][2]) for slot in late]
     outs = pl.pallas_call(
-        functools.partial(middle_kernel, *counts, late_halos, len(late_arrays)),
+        functools.partial(middle_kernel, *counts, late_halos, len(late_arrays), len(carried)),
         out_shape=[jax.ShapeDtypeStruct((2 * size, width), BF)] * len(even)
-        + [block] * cluster_count
+        + [jax.ShapeDtypeStruct((size + len(carried) * EXTRA, width), BF)]
+        + [block] * (cluster_count - 1)
         + [jax.ShapeDtypeStruct((2, size, width), BF), narrow, narrow],
-        in_specs=[VMEM] * (8 + len(late_arrays)),
+        in_specs=[VMEM] * (8 + len(late_arrays) + len(carried)),
         out_specs=[VMEM] * (len(even) + cluster_count + 3),
         scratch_shapes=[pltpu.VMEM((len(late) * size, width), BF)],
         compiler_params=PARAMS,
@@ -449,49 +469,49 @@
         name="middle",
     )(
         choice, grad_out, w_neigh, dense, dense_t, near_sum, own_pre, inverse,
-        *late_arrays,
+        *late_arrays, *carried,
     )
     *sent, sibling, kept, spread, grad_pre = outs
 
     far = [(sub_count + d, along(sent[len(even) + d - 1], d)) for d in range(1, cluster_count)]
     near = [(d, across(value, d)) for d, value in zip(even, sent)]
-    beside = (1, across(sibling, 1))
-    order = [sub_count + 1, *(sub_count + d for d in direct), *even, *(d + 1 for d in even), 1, *(sub_count + d for d in relayed)]
+    order = [sub_count + 1, *(sub_count + d for d in direct), *even, *(d + 1 for d in even), 1]
     arrays, at = unique(order)
-    early = []
     total, owner = pl.pallas_call(
         functools.partial(
             own_kernel, own, sub_count, [(slot, at[slot], got[slot][3]) for slot in order],
-            len(arrays), [(slot, i, 0) for i, (slot, _) in enumerate(early)],
+            len(arrays),
         ),
         out_shape=[wide, marks],
-        in_specs=[VMEM] * (6 + len(arrays) + len(early)),
+        in_specs=[VMEM] * (6 + len(arrays)),
         out_specs=[VMEM] * 2,
         compiler_params=PARAMS,
-        cost_estimate=cost(2*10**9, 2 * 1024 * 1024),
+        cost_estimate=cost(10**9, 2 * 1024 * 1024),
         name="own",
-    )(
-        *[value for _, value in early], *arrays,
-        choice, w_self, dense_t, kept, spread, grad_pre,
-    )
-
+    )(*arrays, after(choice, far[-1][1]), w_self, dense_t, kept, spread, grad_pre)
+
+    soon, rest = near[-1:], near[:-1]
+    early = call(
+        turn_kernel, jax.ShapeDtypeStruct((2 * size, width), BF), "early", 10**6,
+        sibling, *[value for _, value in soon],
+    )
+    early = across(early, 1)
     turned = call(
-        turn_kernel,
-        jax.ShapeDtypeStruct((len(even) * size, width), BF),
-        "turn", 10**6, *[after(value, total) for _, value in near],
+        turn_kernel, jax.ShapeDtypeStruct((len(rest) * size, width), BF), "turn", 10**6,
+        *[after(value, total) for _, value in rest],
     )
     turned = across(turned, 1)
-
-    more = [far[2], far[1], far[0], *near[::-1]]
-    if more:
-        total = call(
-            functools.partial(add_kernel, own, [(slot, i, 0) for i, (slot, _) in enumerate(more)]),
-            wide, "add", 10**10, owner, total, *[value for _, value in more],
-        )
-    last = [beside]
-    parts = [(slot, i, 0) for i, (slot, _) in enumerate(last)]
-    parts += [(d + 1, len(last), i * size) for i, d in enumerate(even)]
-    values = [value for _, value in last]
+    more = [*far, *near[::-1]]
+    places = {slot: (0, size + i * EXTRA) for i, slot in enumerate(sub_count + d for d in relayed)}
+    total = call(
+        functools.partial(
+            add_kernel, own, sub_count, [(slot, i, 0) for i, (slot, _) in enumerate(more)], places
+        ),
+        wide, "add", 10**10, owner, total, *[value for _, value in more],
+    )
+    parts = [(1, 0, 0), *[(d + 1, 0, size) for d, _ in soon]]
+    parts += [(d + 1, 1, i * size) for i, (d, _) in enumerate(rest)]
+    values = [early]
     return pl.pallas_call(
         functools.partial(final_kernel, own, parts),
         out_shape=narrow,

time: 33.4 us -> 31.6 us (0.946)
  waiting for transfers between devices: 7.68 us -> 5.92 us
    ppermute x16, waiting for transfers between devices: 7.68 us -> 5.92 us  [swap(): return lax.ppermute(value, axis, [(i, i ^ d) for i in range(count)])]
  transfers between devices with their start and end apart: 16 -> 16, of which waited for: 9 -> 9; matrix products, arithmetic and copies ran while one was open for 0% -> 0% of each run, Pallas kernels for 11% -> 13%
where the time goes in v11:
time: 31.6 us; the launch traced here: 31.4 us
  starting transfers between devices  18.5 us (59%)
  Pallas kernels  6.88 us (22%)
  waiting for transfers between devices  5.92 us (19%)
    ppermute x16, starting transfers between devices, swap(): return lax.ppermute(value, axis, [(i, i ^ d) for i in range(count)])  18.5 us
    ppermute x16, waiting for transfers between devices, swap(): return lax.ppermute(value, axis, [(i, i ^ d) for i in range(count)])  5.92 us
    pallas_call x1, Pallas kernels, shards(): pl.pallas_call(functools.partial(prepare_kernel, *counts), out_shape=[jax...  2.22 us
    pallas_call x1, Pallas kernels, shards(): pl.pallas_call(functools.partial(middle_kernel, *counts, late_halos, len(...  1.28 us
    pallas_call x3, Pallas kernels, sum_call(): pl.pallas_call(functools.partial(kernel, own, halos), out_shape=out_shape...  0.91 us
    pallas_call x1, Pallas kernels, shards(): pl.pallas_call(edge_kernel, out_shape=[jax.ShapeDtypeStruct((BOUNDARY * s...  0.89 us
    pallas_call x1, Pallas kernels, shards(): pl.pallas_call(functools.partial(final_kernel, own, parts), out_shape=nar...  0.78 us
  transfers between devices with their start and end apart: 16, of which 9 were waited for; matrix products, arithmetic and copies ran while one was open for 0% of the time, Pallas kernels for 13%

profile of v11, /device:TPU:0, one launch (start us, length us, event | category | flops | bytes accessed | tf_op | source)
XLA Modules:
  0.0 31.4 jit_solution(11067903613112683288)
XLA Ops:
  0.0 0.9 %edge.1 = (bf16[272,256]{1,0:T(8,128)(2,1)S(1)}, bf16[16,256]{1,0:T(8,128)(2,1)S(1)}) custom-call(s32[1,8]{1,0:T(1,128)} %recv_sub_hbm.1, s32[1,4]{1,0:T(1,128)} %recv_cluster_hbm.1, bf16[384,256]{1,0:T(8,128)(2,1)} %features_hbm.1), custom_call_target="tpu_custom_call" | custom-call | flops 1024 | bytes 262144 | tf_op jit(solution)/shard_map/edge/pallas_call | solution.py:321
  0.9 4.1 %collective-permute-start.1 = (bf16[272,256]{1,0:T(8,128)(2,1)S(1)}, bf16[272,256]{1,0:T(8,128)(2,1)S(1)}, u32[]{:S(2)}, u32[]{:S(2)}) collective-permute-start(bf16[272,256]{1,0:T(8,128)(2,1)S(1)} %get-tuple-element.36.rest_0_), channel_id=1, source_target_pairs={{0,16},{8,24},{16,0},{24,8},{1,17},{9,25},{17,1},{25,9},{2,18},{10... | collective-permute-start | bytes 417800 | tf_op jit(solution)/shard_map/ppermute | solution.py:288
  5.0 1.6 %collective-permute-start = (bf16[272,256]{1,0:T(8,128)(2,1)S(1)}, bf16[272,256]{1,0:T(8,128)(2,1)S(1)}, u32[]{:S(2)}, u32[]{:S(2)}) collective-permute-start(bf16[272,256]{1,0:T(8,128)(2,1)S(1)} %get-tuple-element.36.rest_0_), channel_id=1, source_target_pairs={{0,8},{8,0},{16,24},{24,16},{1,9},{9,1},{17,25},{25,17},{2,10},{10... | collective-permute-start | bytes 417800 | tf_op jit(solution)/shard_map/ppermute | solution.py:288
  6.6 2.4 %collective-permute-start.4 = (bf16[272,256]{1,0:T(8,128)(2,1)S(1)}, bf16[272,256]{1,0:T(8,128)(2,1)S(1)}, u32[]{:S(2)}, u32[]{:S(2)}) collective-permute-start(bf16[272,256]{1,0:T(8,128)(2,1)S(1)} %get-tuple-element.36.rest_0_), channel_id=1, source_target_pairs={{0,6},{1,7},{2,4},{3,5},{4,2},{5,3},{6,0},{7,1},{8,14},{9,15},{10,... | collective-permute-start | bytes 417800 | tf_op jit(solution)/shard_map/ppermute | solution.py:288
  9.0 0.5 %collective-permute-start.3 = (bf16[272,256]{1,0:T(8,128)(2,1)S(1)}, bf16[272,256]{1,0:T(8,128)(2,1)S(1)}, u32[]{:S(2)}, u32[]{:S(2)}) collective-permute-start(bf16[272,256]{1,0:T(8,128)(2,1)S(1)} %get-tuple-element.36.rest_0_), channel_id=1, source_target_pairs={{0,4},{1,5},{2,6},{3,7},{4,0},{5,1},{6,2},{7,3},{8,12},{9,13},{10,... | collective-permute-start | bytes 417800 | tf_op jit(solution)/shard_map/ppermute | solution.py:288
  9.5 0.5 %collective-permute-start.2 = (bf16[272,256]{1,0:T(8,128)(2,1)S(1)}, bf16[272,256]{1,0:T(8,128)(2,1)S(1)}, u32[]{:S(2)}, u32[]{:S(2)}) collective-permute-start(bf16[272,256]{1,0:T(8,128)(2,1)S(1)} %get-tuple-element.36.rest_0_), channel_id=1, source_target_pairs={{0,2},{1,3},{2,0},{3,1},{4,6},{5,7},{6,4},{7,5},{8,10},{9,11},{10,... | collective-permute-start | bytes 417800 | tf_op jit(solution)/shard_map/ppermute | solution.py:288
  10.1 2.2 %prepare.1 = (bf16[384,1920]{1,0:T(8,128)(2,1)S(1)}, bf16[1920,384]{1,0:T(8,128)(2,1)S(1)}, f32[384,128]{1,0:T(8,128)S(1)}, f32[12,256]{1,0:T(8,128)S(1)}, bf16[...) custom-call(s32[24]{0:T(128)} %tile_dst_hbm.1, ...), custom_call_target="tpu_custom_call" | custom-call | flops 100000000 | bytes 6291456 | tf_op jit(solution)/shard_map/prepare/pallas_call | solution.py:355
  12.3 0.0 collective-permute-done.1.message.far.rest_1_
  12.3 0.0 collective-permute-done.near.rest_0_
  12.3 0.1 relay.1
  12.4 1.2 %collective-permute-start.7 = (bf16[128,256]{1,0:T(8,128)(2,1)S(1)}, bf16[128,256]{1,0:T(8,128)(2,1)S(1)}, u32[]{:S(2)}, u32[]{:S(2)}) collective-permute-start(bf16[128,256]{1,0:T(8,128)(2,1)S(1)} %relay.1), channel_id=1, source_target_pairs={{0,8},{8,0},{16,24},{24,16},{1,9},{9,1},{17,25},{25,17},{2,10},{10... | collective-permute-start | bytes 196616 | tf_op jit(solution)/shard_map/ppermute | solution.py:288
  13.6 0.0 collective-permute-start.5
  13.6 0.4 %first.1 = (f32[384,256]{1,0:T(8,128)S(1)}, f32[384,256]{1,0:T(8,128)S(1)}) custom-call(f32[12,256]{1,0:T(8,128)S(1)} %get-tuple-element.53.choice.rest_6_, bf16[384,1920]{1,0:T(8,128)(2,1)S(1)} %get-tuple-element.43.dense, bf16[384,256]{1,0:T(8,128)(2,1)S(1)} %get-tuple-element.46.features, bf16[256,256]{1,0:T(8,128)(2,1)S(1)} %get-tuple-element.47.w_self.rest_7_, ...), custom_call_target="tpu_custom_call" | custom-call | flops 1000000000 | bytes 3145728 | tf_op jit(solution)/shard_map/first/pallas_call | solution.py:409
  14.0 0.7 %collective-permute-done.5.rest_4_ = bf16[16,256]{1,0:T(8,128)(2,1)S(1)} collective-permute-done((bf16[16,256]{1,0:T(8,128)(2,1)S(1)}, bf16[16,256]{1,0:T(8,128)(2,1)S(1)}, u32[]{:S(2)}, u32[]{:S(2)}) %collective-permute-start.5) | collective-permute-done | bytes 8224 | tf_op jit(solution)/shard_map/ppermute | solution.py:288
  14.8 0.0 collective-permute-done.4.rest_3_.rest_4_
  14.8 0.5 %collective-permute-done.3.rest_2_.rest_3_ = bf16[272,256]{1,0:T(8,128)(2,1)S(1)} collective-permute-done((bf16[272,256]{1,0:T(8,128)(2,1)S(1)}, bf16[272,256]{1,0:T(8,128)(2,1)S(1)}, u32[]{:S(2)}, u32[]{:S(2)}) %collective-permute-start.3) | collective-permute-done | bytes 139296 | tf_op jit(solution)/shard_map/ppermute | solution.py:288
  15.3 0.1 collective-permute-done.2.rest_1_.rest_2_
  15.4 0.2 trade.1
  15.5 0.1 collective-permute-start.6
  15.6 0.3 near.1.before
  15.9 0.9 %collective-permute-done.7.rest_0_ = bf16[128,256]{1,0:T(8,128)(2,1)S(1)} collective-permute-done((bf16[128,256]{1,0:T(8,128)(2,1)S(1)}, bf16[128,256]{1,0:T(8,128)(2,1)S(1)}, u32[]{:S(2)}, u32[]{:S(2)}) %collective-permute-start.7) | collective-permute-done | bytes 65568 | tf_op jit(solution)/shard_map/ppermute | solution.py:288
  16.8 0.2 late.1.before
  17.0 0.2 collective-permute-done.6.rest_0_.rest_5_
  17.2 1.3 %middle.1 = (bf16[256,256]{1,0:T(8,128)(2,1)S(1)}, bf16[256,256]{1,0:T(8,128)(2,1)S(1)}, bf16[256,256]{1,0:T(8,128)(2,1)S(1)}, bf16[144,256]{1,0:T(8,128)(2,1)S(...) custom-call(f32[12,256]{1,0:T(8,128)S(1)} %get-tuple-element.53.choi, ...), custom_call_target="tpu_custom_call" | custom-call | flops 377487360 | bytes 6291456 | tf_op jit(solution)/shard_map/middle/pallas_call | solution.py:458
  18.5 2.7 %collective-permute-start.8 = (bf16[128,256]{1,0:T(8,128)(2,1)S(1)}, bf16[128,256]{1,0:T(8,128)(2,1)S(1)}, u32[]{:S(2)}, u32[]{:S(2)}) collective-permute-start(bf16[128,256]{1,0:T(8,128)(2,1)S(1)} %get-tuple-element.52), channel_id=1, source_target_pairs={{0,24},{8,16},{16,8},{24,0},{1,25},{9,17},{17,9},{25,1},{2,26},{10... | collective-permute-start | bytes 196616 | tf_op jit(solution)/shard_map/ppermute | solution.py:288
  21.2 2.4 %collective-permute-start.11 = (bf16[256,256]{1,0:T(8,128)(2,1)S(1)}, bf16[256,256]{1,0:T(8,128)(2,1)S(1)}, u32[]{:S(2)}, u32[]{:S(2)}) collective-permute-start(bf16[256,256]{1,0:T(8,128)(2,1)S(1)} %get-tuple-element.61), channel_id=1, source_target_pairs={{0,6},{1,7},{2,4},{3,5},{4,2},{5,3},{6,0},{7,1},{8,14},{9,15},{10,... | collective-permute-start | bytes 393224 | tf_op jit(solution)/shard_map/ppermute | solution.py:288
  23.6 0.5 %collective-permute-start.12 = (bf16[256,256]{1,0:T(8,128)(2,1)S(1)}, bf16[256,256]{1,0:T(8,128)(2,1)S(1)}, u32[]{:S(2)}, u32[]{:S(2)}) collective-permute-start(bf16[256,256]{1,0:T(8,128)(2,1)S(1)} %get-tuple-element.62), channel_id=1, source_target_pairs={{0,4},{1,5},{2,6},{3,7},{4,0},{5,1},{6,2},{7,3},{8,12},{9,13},{10,... | collective-permute-start | bytes 393224 | tf_op jit(solution)/shard_map/ppermute | solution.py:288
  24.2 0.5 %collective-permute-start.13 = (bf16[256,256]{1,0:T(8,128)(2,1)S(1)}, bf16[256,256]{1,0:T(8,128)(2,1)S(1)}, u32[]{:S(2)}, u32[]{:S(2)}) collective-permute-start(bf16[256,256]{1,0:T(8,128)(2,1)S(1)} %get-tuple-element.63), channel_id=1, source_target_pairs={{0,2},{1,3},{2,0},{3,1},{4,6},{5,7},{6,4},{7,5},{8,10},{9,11},{10,... | collective-permute-start | bytes 393224 | tf_op jit(solution)/shard_map/ppermute | solution.py:288
  24.7 0.0 collective-permute-start.10
  24.7 0.0 collective-permute-done.8.rest_2_
  24.7 1.7 %collective-permute-start.9 = (bf16[144,256]{1,0:T(8,128)(2,1)S(1)}, bf16[144,256]{1,0:T(8,128)(2,1)S(1)}, u32[]{:S(2)}, u32[]{:S(2)}) collective-permute-start(bf16[144,256]{1,0:T(8,128)(2,1)S(1)} %get-tuple-element.59), channel_id=1, source_target_pairs={{0,8},{8,0},{16,24},{24,16},{1,9},{9,1},{17,25},{25,17},{2,10},{10... | collective-permute-start | bytes 221192 | tf_op jit(solution)/shard_map/ppermute | solution.py:288
  26.4 0.3 own.1
  26.7 1.7 %collective-permute-done.11.rest_3_.rest_1_ = bf16[256,256]{1,0:T(8,128)(2,1)S(1)} collective-permute-done((bf16[256,256]{1,0:T(8,128)(2,1)S(1)}, bf16[256,256]{1,0:T(8,128)(2,1)S(1)}, u32[]{:S(2)}, u32[]{:S(2)}) %collective-permute-start.11) | collective-permute-done | bytes 131104 | tf_op jit(solution)/shard_map/ppermute | solution.py:288
  28.4 0.1 collective-permute-start.14
  28.5 0.7 %collective-permute-done.12.rest_4_.rest_1_ = bf16[256,256]{1,0:T(8,128)(2,1)S(1)} collective-permute-done((bf16[256,256]{1,0:T(8,128)(2,1)S(1)}, bf16[256,256]{1,0:T(8,128)(2,1)S(1)}, u32[]{:S(2)}, u32[]{:S(2)}) %collective-permute-start.12) | collective-permute-done | bytes 131104 | tf_op jit(solution)/shard_map/ppermute | solution.py:288
  29.2 0.0 collective-permute-done.13.rest_5_.rest_0_
  29.2 0.1 collective-permute-start.15
  29.3 0.5 %collective-permute-done.10.rest_1_ = bf16[128,256]{1,0:T(8,128)(2,1)S(1)} collective-permute-done((bf16[128,256]{1,0:T(8,128)(2,1)S(1)}, bf16[128,256]{1,0:T(8,128)(2,1)S(1)}, u32[]{:S(2)}, u32[]{:S(2)}) %collective-permute-start.10) | collective-permute-done | bytes 65568 | tf_op jit(solution)/shard_map/ppermute | solution.py:288
  29.9 0.0 collective-permute-done.9.rest_0_
  29.9 0.2 add.1.total
  30.1 0.0 collective-permute-done.14.rest_0_
  30.1 0.6 %collective-permute-done.15.rest_1_ = bf16[256,256]{1,0:T(8,128)(2,1)S(1)} collective-permute-done((bf16[256,256]{1,0:T(8,128)(2,1)S(1)}, bf16[256,256]{1,0:T(8,128)(2,1)S(1)}, u32[]{:S(2)}, u32[]{:S(2)}) %collective-permute-start.15) | collective-permute-done | bytes 131104 | tf_op jit(solution)/shard_map/ppermute | solution.py:288
  30.6 0.8 %final.1 = bf16[384,256]{1,0:T(8,128)(2,1)} custom-call(f32[12,256]{1,0:T(8,128)S(1)} %get-tuple-element.57.owner, f32[384,256]{1,0:T(8,128)S(1)} %add.1.total, bf16[256,256]{1,0:T(8,128)(2,1)S(1)} %collective-permute-done.14.rest_0_, bf16[256,256]{1,0:T(8,128)(2,1)S(1)} %collective-permute-done.15.rest_1_), custom_call_target="tpu_custom_call" | custom-call | flops 393216 | bytes 1048576 | tf_op jit(solution)/shard_map/final/pallas_call | solution.py:515
  (3 shorter events, 0.0 us)
Async XLA Ops:
  0.9 11.4 %collective-permute-start.1 = (bf16[272,256]{1,0:T(8,128)(2,1)S(1)}, bf16[272,256]{1,0:T(8,128)(2,1)S(1)}, u32[]{:S(2)}, u32[]{:S(2)}) collective-permute-start(bf16[272,256]{1,0:T(8,128)(2,1)S(1)} %get-tuple-element.36.rest_0_), channel_id=1, source_target_pairs={{0,16},{8,24},{16,0},{24,8},{1,17},{9,25},{17,1},{25,9},{2,18},{10... | collective-permute-start | bytes 417800 | tf_op jit(solution)/shard_map/ppermute | solution.py:288
  5.0 7.3 %collective-permute-start = (bf16[272,256]{1,0:T(8,128)(2,1)S(1)}, bf16[272,256]{1,0:T(8,128)(2,1)S(1)}, u32[]{:S(2)}, u32[]{:S(2)}) collective-permute-start(bf16[272,256]{1,0:T(8,128)(2,1)S(1)} %get-tuple-element.36.rest_0_), channel_id=1, source_target_pairs={{0,8},{8,0},{16,24},{24,16},{1,9},{9,1},{17,25},{25,17},{2,10},{10... | collective-permute-start | bytes 417800 | tf_op jit(solution)/shard_map/ppermute | solution.py:288
  6.6 8.2 %collective-permute-start.4 = (bf16[272,256]{1,0:T(8,128)(2,1)S(1)}, bf16[272,256]{1,0:T(8,128)(2,1)S(1)}, u32[]{:S(2)}, u32[]{:S(2)}) collective-permute-start(bf16[272,256]{1,0:T(8,128)(2,1)S(1)} %get-tuple-element.36.rest_0_), channel_id=1, source_target_pairs={{0,6},{1,7},{2,4},{3,5},{4,2},{5,3},{6,0},{7,1},{8,14},{9,15},{10,... | collective-permute-start | bytes 417800 | tf_op jit(solution)/shard_map/ppermute | solution.py:288
  9.0 6.3 %collective-permute-start.3 = (bf16[272,256]{1,0:T(8,128)(2,1)S(1)}, bf16[272,256]{1,0:T(8,128)(2,1)S(1)}, u32[]{:S(2)}, u32[]{:S(2)}) collective-permute-start(bf16[272,256]{1,0:T(8,128)(2,1)S(1)} %get-tuple-element.36.rest_0_), channel_id=1, source_target_pairs={{0,4},{1,5},{2,6},{3,7},{4,0},{5,1},{6,2},{7,3},{8,12},{9,13},{10,... | collective-permute-start | bytes 417800 | tf_op jit(solution)/shard_map/ppermute | solution.py:288
  9.5 5.8 %collective-permute-start.2 = (bf16[272,256]{1,0:T(8,128)(2,1)S(1)}, bf16[272,256]{1,0:T(8,128)(2,1)S(1)}, u32[]{:S(2)}, u32[]{:S(2)}) collective-permute-start(bf16[272,256]{1,0:T(8,128)(2,1)S(1)} %get-tuple-element.36.rest_0_), channel_id=1, source_target_pairs={{0,2},{1,3},{2,0},{3,1},{4,6},{5,7},{6,4},{7,5},{8,10},{9,11},{10,... | collective-permute-start | bytes 417800 | tf_op jit(solution)/shard_map/ppermute | solution.py:288
  12.4 4.3 %collective-permute-start.7 = (bf16[128,256]{1,0:T(8,128)(2,1)S(1)}, bf16[128,256]{1,0:T(8,128)(2,1)S(1)}, u32[]{:S(2)}, u32[]{:S(2)}) collective-permute-start(bf16[128,256]{1,0:T(8,128)(2,1)S(1)} %relay.1), channel_id=1, source_target_pairs={{0,8},{8,0},{16,24},{24,16},{1,9},{9,1},{17,25},{25,17},{2,10},{10... | collective-permute-start | bytes 196616 | tf_op jit(solution)/shard_map/ppermute | solution.py:288
  13.6 1.2 %collective-permute-start.5 = (bf16[16,256]{1,0:T(8,128)(2,1)S(1)}, bf16[16,256]{1,0:T(8,128)(2,1)S(1)}, u32[]{:S(2)}, u32[]{:S(2)}) collective-permute-start(bf16[16,256]{1,0:T(8,128)(2,1)S(1)} %get-tuple-element.38), channel_id=1, source_target_pairs={{0,1},{1,0},{2,3},{3,2},{4,5},{5,4},{6,7},{7,6},{8,9},{9,8},{10,11... | collective-permute-start | bytes 24584 | tf_op jit(solution)/shard_map/ppermute | solution.py:288
  15.5 1.6 %collective-permute-start.6 = (bf16[576,256]{1,0:T(8,128)(2,1)S(1)}, bf16[576,256]{1,0:T(8,128)(2,1)S(1)}, u32[]{:S(2)}, u32[]{:S(2)}) collective-permute-start(bf16[576,256]{1,0:T(8,128)(2,1)S(1)} %trade.1), channel_id=1, source_target_pairs={{0,1},{1,0},{2,3},{3,2},{4,5},{5,4},{6,7},{7,6},{8,9},{9,8},{10,11... | collective-permute-start | bytes 884744 | tf_op jit(solution)/shard_map/ppermute | solution.py:288
  18.5 6.2 %collective-permute-start.8 = (bf16[128,256]{1,0:T(8,128)(2,1)S(1)}, bf16[128,256]{1,0:T(8,128)(2,1)S(1)}, u32[]{:S(2)}, u32[]{:S(2)}) collective-permute-start(bf16[128,256]{1,0:T(8,128)(2,1)S(1)} %get-tuple-element.52), channel_id=1, source_target_pairs={{0,24},{8,16},{16,8},{24,0},{1,25},{9,17},{17,9},{25,1},{2,26},{10... | collective-permute-start | bytes 196616 | tf_op jit(solution)/shard_map/ppermute | solution.py:288
  21.2 7.2 %collective-permute-start.11 = (bf16[256,256]{1,0:T(8,128)(2,1)S(1)}, bf16[256,256]{1,0:T(8,128)(2,1)S(1)}, u32[]{:S(2)}, u32[]{:S(2)}) collective-permute-start(bf16[256,256]{1,0:T(8,128)(2,1)S(1)} %get-tuple-element.61), channel_id=1, source_target_pairs={{0,6},{1,7},{2,4},{3,5},{4,2},{5,3},{6,0},{7,1},{8,14},{9,15},{10,... | collective-permute-start | bytes 393224 | tf_op jit(solution)/shard_map/ppermute | solution.py:288
  23.6 5.6 %collective-permute-start.12 = (bf16[256,256]{1,0:T(8,128)(2,1)S(1)}, bf16[256,256]{1,0:T(8,128)(2,1)S(1)}, u32[]{:S(2)}, u32[]{:S(2)}) collective-permute-start(bf16[256,256]{1,0:T(8,128)(2,1)S(1)} %get-tuple-element.62), channel_id=1, source_target_pairs={{0,4},{1,5},{2,6},{3,7},{4,0},{5,1},{6,2},{7,3},{8,12},{9,13},{10,... | collective-permute-start | bytes 393224 | tf_op jit(solution)/shard_map/ppermute | solution.py:288
  24.2 5.1 %collective-permute-start.13 = (bf16[256,256]{1,0:T(8,128)(2,1)S(1)}, bf16[256,256]{1,0:T(8,128)(2,1)S(1)}, u32[]{:S(2)}, u32[]{:S(2)}) collective-permute-start(bf16[256,256]{1,0:T(8,128)(2,1)S(1)} %get-tuple-element.63), channel_id=1, source_target_pairs={{0,2},{1,3},{2,0},{3,1},{4,6},{5,7},{6,4},{7,5},{8,10},{9,11},{10,... | collective-permute-start | bytes 393224 | tf_op jit(solution)/shard_map/ppermute | solution.py:288
  24.7 5.2 %collective-permute-start.10 = (bf16[128,256]{1,0:T(8,128)(2,1)S(1)}, bf16[128,256]{1,0:T(8,128)(2,1)S(1)}, u32[]{:S(2)}, u32[]{:S(2)}) collective-permute-start(bf16[128,256]{1,0:T(8,128)(2,1)S(1)} %get-tuple-element.60), channel_id=1, source_target_pairs={{0,16},{8,24},{16,0},{24,8},{1,17},{9,25},{17,1},{25,9},{2,18},{10... | collective-permute-start | bytes 196616 | tf_op jit(solution)/shard_map/ppermute | solution.py:288
  24.7 5.2 %collective-permute-start.9 = (bf16[144,256]{1,0:T(8,128)(2,1)S(1)}, bf16[144,256]{1,0:T(8,128)(2,1)S(1)}, u32[]{:S(2)}, u32[]{:S(2)}) collective-permute-start(bf16[144,256]{1,0:T(8,128)(2,1)S(1)} %get-tuple-element.59), channel_id=1, source_target_pairs={{0,8},{8,0},{16,24},{24,16},{1,9},{9,1},{17,25},{25,17},{2,10},{10... | collective-permute-start | bytes 221192 | tf_op jit(solution)/shard_map/ppermute | solution.py:288
  28.4 1.6 %collective-permute-start.14 = (bf16[256,256]{1,0:T(8,128)(2,1)S(1)}, bf16[256,256]{1,0:T(8,128)(2,1)S(1)}, u32[]{:S(2)}, u32[]{:S(2)}) collective-permute-start(bf16[256,256]{1,0:T(8,128)(2,1)S(1)} %early.1), channel_id=1, source_target_pairs={{0,1},{1,0},{2,3},{3,2},{4,5},{5,4},{6,7},{7,6},{8,9},{9,8},{10,11... | collective-permute-start | bytes 393224 | tf_op jit(solution)/shard_map/ppermute | solution.py:288
  29.2 1.4 %collective-permute-start.15 = (bf16[256,256]{1,0:T(8,128)(2,1)S(1)}, bf16[256,256]{1,0:T(8,128)(2,1)S(1)}, u32[]{:S(2)}, u32[]{:S(2)}) collective-permute-start(bf16[256,256]{1,0:T(8,128)(2,1)S(1)} %turn.1), channel_id=1, source_target_pairs={{0,1},{1,0},{2,3},{3,2},{4,5},{5,4},{6,7},{7,6},{8,9},{9,8},{10,11... | collective-permute-start | bytes 393224 | tf_op jit(solution)/shard_map/ppermute | solution.py:288

commit v12 on v11

--- a/solution.py
+++ b/solution.py
@@ -62,7 +62,7 @@
     own, sub_count, cluster_count,
     tile_dst_hbm, tile_src_hbm, recv_sub_hbm, recv_cluster_hbm, tile_weight_hbm,
     features_hbm, w_self_hbm, w_neigh_hbm, grad_out_hbm, bias_hbm,
-    dense, dense_t, inverse, choice, features, w_self, w_neigh, grad_out, bias,
+    dense, choice, features, w_self, w_neigh, grad_out, bias,
     tile_dst, tile_src, recv_sub, recv_cluster, tile_weight, sems,
 ):
     size = tile_weight.shape[1]
@@ -83,7 +83,6 @@
     sub_id = lax.axis_index("sub")
     cluster_id = lax.axis_index("cluster")
     dense[...] = jnp.zeros_like(dense)
-    dense_t[...] = jnp.zeros_like(dense_t)
     for copy in copies[: 4 + CHUNKS]:
         copy.wait()
 
@@ -94,9 +93,7 @@
         slot = jnp.where(src < own, src, jnp.where(src < own + sub_count, from_sub, from_cluster))
         dst = pl.ds(pl.multiple_of(tile_dst[t] * size, size), size)
         col = pl.ds(pl.multiple_of(slot * size, size), size)
-        tile = tile_weight[t]
-        dense[dst, col] = dense[dst, col] + tile
-        dense_t[col, dst] = dense_t[col, dst] + tile.T
+        dense[dst, col] = dense[dst, col] + tile_weight[t]
         return carry
 
     lax.fori_loop(0, tile_weight.shape[0], place, 0, unroll=4)
@@ -106,12 +103,6 @@
     for d in range(cluster_count):
         index = recv_cluster[0, cluster_id ^ d].astype(F32)
         choice[sub_count + d : sub_count + d + 1, :] = jnp.full((1, choice.shape[1]), index, F32)
-    slots = own + sub_count + cluster_count
-    total = dense[:, 0:size].astype(F32)
-    for slot in range(1, slots):
-        total = total + dense[:, slot * size : (slot + 1) * size].astype(F32)
-    degree = jnp.sum(total, axis=1, keepdims=True)
-    inverse[...] = jnp.broadcast_to(1.0 / (degree + 1.0), inverse.shape)
     for copy in copies[4 + CHUNKS :]:
         copy.wait()
 
@@ -173,9 +164,19 @@
     return dot(jnp.concatenate(columns, axis=1), halo[...])
 
 
+def flip_kernel(size, dense, dense_t):
+    for at in range(0, dense.shape[1], size):
+        dense_t[at : at + size, :] = dense[:, at : at + size].T
+
+
 def first_kernel(own, halos, choice, dense, features, w_self, bias, *rest):
-    refs, (total, own_pre, halo) = rest[:-3], rest[-3:]
+    refs, (total, own_pre, inverse, halo) = rest[:-4], rest[-4:]
     size = dense.shape[0] // own
+    count = dense[:, 0:size].astype(F32)
+    for at in range(size, dense.shape[1], size):
+        count = count + dense[:, at : at + size].astype(F32)
+    degree = jnp.sum(count, axis=1, keepdims=True)
+    inverse[...] = jnp.broadcast_to(1.0 / (degree + 1.0), inverse.shape)
     total[...] = dot(dense[:, 0 : own * size], features[...]) + halo_sum(
         choice, dense, own, halos, refs, halo
     )
@@ -352,12 +353,10 @@
     for d in even:
         got[d] = (across(edge, d), 0, False, rows_at)
     got[sub_count + 1] = (along(edge, 1), 0, False, rows_at)
-    dense, dense_t, inverse, choice, features, w_self, w_neigh, grad_out, bias = pl.pallas_call(
+    dense, choice, features, w_self, w_neigh, grad_out, bias = pl.pallas_call(
         functools.partial(prepare_kernel, *counts),
         out_shape=[
             jax.ShapeDtypeStruct((rows, slots * size), BF),
-            jax.ShapeDtypeStruct((slots * size, rows), BF),
-            jax.ShapeDtypeStruct((rows, size), F32),
             marks,
             narrow,
             square,
@@ -366,7 +365,7 @@
             jax.ShapeDtypeStruct(bias.shape, F32),
         ],
         in_specs=[HBM] * 10,
-        out_specs=[VMEM] * 9,
+        out_specs=[VMEM] * 7,
         scratch_shapes=[
             pltpu.SMEM(tile_dst.shape, jnp.int32),
             pltpu.SMEM(tile_src.shape, jnp.int32),
@@ -430,8 +429,8 @@
         )
         carried.append(far_rows)
         got[sub_count + d] = (along(value, 1), 0, True, None)
-    first_sum, own_pre = sum_call(
-        first_kernel, [wide, wide], "first", [0, sub_count, *(sub_count + d for d in direct)],
+    first_sum, own_pre, inverse = sum_call(
+        first_kernel, [wide, wide, jax.ShapeDtypeStruct((rows, size), F32)], "first", [0, sub_count, *(sub_count + d for d in direct)],
         choice, dense, features, w_self, bias,
     )
     traded = [0, *even]
@@ -448,9 +447,15 @@
     near_sum = sum_call(
         near_kernel, wide, "near", [sub_count + 1, *even], after(choice, trade_value), dense, first_sum
     )
+    dense_t = call(
+        functools.partial(flip_kernel, size), jax.ShapeDtypeStruct((slots * size, rows), BF), "flip", 10**7,
+        after(dense, near_sum),
+    )
     if relayed:
         slots_late = [sub_count + d for d in relayed]
-        near_sum = sum_call(near_kernel, wide, "late", slots_late, choice, dense, near_sum)
+        near_sum = sum_call(
+            near_kernel, wide, "late", slots_late, after(choice, dense_t), dense, near_sum
+        )
 
     late = [1, *(d + 1 for d in even)]
     late_arrays, late_at = unique(late)
@@ -475,6 +480,11 @@
 
     far = [(sub_count + d, along(sent[len(even) + d - 1], d)) for d in range(1, cluster_count)]
     near = [(d, across(value, d)) for d, value in zip(even, sent)]
+    soon, rest = near[-1:], near[:-1]
+    early = call(
+        turn_kernel, jax.ShapeDtypeStruct((2 * size, width), BF), "early", 10**8,
+        sibling, *[value for _, value in soon],
+    )
     order = [sub_count + 1, *(sub_count + d for d in direct), *even, *(d + 1 for d in even), 1]
     arrays, at = unique(order)
     total, owner = pl.pallas_call(
@@ -488,13 +498,8 @@
         compiler_params=PARAMS,
         cost_estimate=cost(10**9, 2 * 1024 * 1024),
         name="own",
-    )(*arrays, after(choice, far[-1][1]), w_self, dense_t, kept, spread, grad_pre)
-
-    soon, rest = near[-1:], near[:-1]
-    early = call(
-        turn_kernel, jax.ShapeDtypeStruct((2 * size, width), BF), "early", 10**6,
-        sibling, *[value for _, value in soon],
-    )
+    )(*arrays, after(choice, (far[-1][1], early)), w_self, dense_t, kept, spread, grad_pre)
+
     early = across(early, 1)
     turned = call(
         turn_kernel, jax.ShapeDtypeStruct((len(rest) * size, width), BF), "turn", 10**6,

time: 31.6 us -> 31.5 us (level)
    pallas_call x1, Pallas kernels: 2.22 us -> 1.63 us  [shards(): pl.pallas_call(functools.partial(prepare_kernel, *counts), out_shape=[jax...]
    pallas_call x6 -> x7, Pallas kernels: 0.49 us -> 0.92 us  [call(): pl.pallas_call(kernel, out_shape=out_shape, in_specs=[VMEM] * len(operand...]
  transfers between devices with their start and end apart: 16 -> 16, of which waited for: 9 -> 12; matrix products, arithmetic and copies ran while one was open for 0% -> 0% of each run, Pallas kernels for 13% -> 12%
where the time goes in v12:
time: 31.5 us; the launch traced here: 31.3 us
  starting transfers between devices  18.5 us (59%)
  Pallas kernels  6.76 us (21%)
  waiting for transfers between devices  5.97 us (19%)
    ppermute x16, starting transfers between devices, swap(): return lax.ppermute(value, axis, [(i, i ^ d) for i in range(count)])  18.5 us
    ppermute x16, waiting for transfers between devices, swap(): return lax.ppermute(value, axis, [(i, i ^ d) for i in range(count)])  5.97 us
    pallas_call x1, Pallas kernels, shards(): pl.pallas_call(functools.partial(prepare_kernel, *counts), out_shape=[jax...  1.63 us
    pallas_call x1, Pallas kernels, shards(): pl.pallas_call(functools.partial(middle_kernel, *counts, late_halos, len(...  1.25 us
    pallas_call x3, Pallas kernels, sum_call(): pl.pallas_call(functools.partial(kernel, own, halos), out_shape=out_shape...  0.99 us
    pallas_call x7, Pallas kernels, call(): pl.pallas_call(kernel, out_shape=out_shape, in_specs=[VMEM] * len(operand...  0.92 us
    pallas_call x1, Pallas kernels, shards(): pl.pallas_call(edge_kernel, out_shape=[jax.ShapeDtypeStruct((BOUNDARY * s...  0.89 us
    pallas_call x1, Pallas kernels, shards(): pl.pallas_call(functools.partial(final_kernel, own, parts), out_shape=nar...  0.78 us
  transfers between devices with their start and end apart: 16, of which 12 were waited for; matrix products, arithmetic and copies ran while one was open for 0% of the time, Pallas kernels for 12%

profile of v12, /device:TPU:0, one launch (start us, length us, event | category | flops | bytes accessed | tf_op | source)
XLA Modules:
  0.0 31.3 jit_solution(13115975144916571336)
XLA Ops:
  0.0 0.9 %edge.1 = (bf16[272,256]{1,0:T(8,128)(2,1)S(1)}, bf16[16,256]{1,0:T(8,128)(2,1)S(1)}) custom-call(s32[1,8]{1,0:T(1,128)} %recv_sub_hbm.1, s32[1,4]{1,0:T(1,128)} %recv_cluster_hbm.1, bf16[384,256]{1,0:T(8,128)(2,1)} %features_hbm.1), custom_call_target="tpu_custom_call" | custom-call | flops 1024 | bytes 262144 | tf_op jit(solution)/shard_map/edge/pallas_call | solution.py:322
  0.9 4.1 %collective-permute-start.1 = (bf16[272,256]{1,0:T(8,128)(2,1)S(1)}, bf16[272,256]{1,0:T(8,128)(2,1)S(1)}, u32[]{:S(2)}, u32[]{:S(2)}) collective-permute-start(bf16[272,256]{1,0:T(8,128)(2,1)S(1)} %get-tuple-element.37.rest_0_), channel_id=1, source_target_pairs={{0,16},{8,24},{16,0},{24,8},{1,17},{9,25},{17,1},{25,9},{2,18},{10... | collective-permute-start | bytes 417800 | tf_op jit(solution)/shard_map/ppermute | solution.py:289
  5.0 1.6 %collective-permute-start = (bf16[272,256]{1,0:T(8,128)(2,1)S(1)}, bf16[272,256]{1,0:T(8,128)(2,1)S(1)}, u32[]{:S(2)}, u32[]{:S(2)}) collective-permute-start(bf16[272,256]{1,0:T(8,128)(2,1)S(1)} %get-tuple-element.37.rest_0_), channel_id=1, source_target_pairs={{0,8},{8,0},{16,24},{24,16},{1,9},{9,1},{17,25},{25,17},{2,10},{10... | collective-permute-start | bytes 417800 | tf_op jit(solution)/shard_map/ppermute | solution.py:289
  6.6 2.4 %collective-permute-start.4 = (bf16[272,256]{1,0:T(8,128)(2,1)S(1)}, bf16[272,256]{1,0:T(8,128)(2,1)S(1)}, u32[]{:S(2)}, u32[]{:S(2)}) collective-permute-start(bf16[272,256]{1,0:T(8,128)(2,1)S(1)} %get-tuple-element.37.rest_0_), channel_id=1, source_target_pairs={{0,6},{1,7},{2,4},{3,5},{4,2},{5,3},{6,0},{7,1},{8,14},{9,15},{10,... | collective-permute-start | bytes 417800 | tf_op jit(solution)/shard_map/ppermute | solution.py:289
  9.0 0.5 %collective-permute-start.3 = (bf16[272,256]{1,0:T(8,128)(2,1)S(1)}, bf16[272,256]{1,0:T(8,128)(2,1)S(1)}, u32[]{:S(2)}, u32[]{:S(2)}) collective-permute-start(bf16[272,256]{1,0:T(8,128)(2,1)S(1)} %get-tuple-element.37.rest_0_), channel_id=1, source_target_pairs={{0,4},{1,5},{2,6},{3,7},{4,0},{5,1},{6,2},{7,3},{8,12},{9,13},{10,... | collective-permute-start | bytes 417800 | tf_op jit(solution)/shard_map/ppermute | solution.py:289
  9.5 0.5 %collective-permute-start.2 = (bf16[272,256]{1,0:T(8,128)(2,1)S(1)}, bf16[272,256]{1,0:T(8,128)(2,1)S(1)}, u32[]{:S(2)}, u32[]{:S(2)}) collective-permute-start(bf16[272,256]{1,0:T(8,128)(2,1)S(1)} %get-tuple-element.37.rest_0_), channel_id=1, source_target_pairs={{0,2},{1,3},{2,0},{3,1},{4,6},{5,7},{6,4},{7,5},{8,10},{9,11},{10,... | collective-permute-start | bytes 417800 | tf_op jit(solution)/shard_map/ppermute | solution.py:289
  10.1 1.6 %prepare.1 = (bf16[384,1920]{1,0:T(8,128)(2,1)S(1)}, f32[12,256]{1,0:T(8,128)S(1)}, bf16[384,256]{1,0:T(8,128)(2,1)S(1)}, bf16[256,256]{1,0:T(8,128)(2,1)S(1)}, ...) custom-call(s32[24]{0:T(128)} %tile_dst_hbm.1, s32[24]{0:T(128)} %tile_src_hbm.1, ...), custom_call_target="tpu_custom_call" | custom-call | flops 100000000 | bytes 6291456 | tf_op jit(solution)/shard_map/prepare/pallas_call | solution.py:356
  11.7 0.1 collective-permute-done.1.message.far.rest_1_
  11.8 0.2 collective-permute-done.near.rest_0_
  12.0 0.1 relay.1
  12.1 1.5 %collective-permute-start.7 = (bf16[128,256]{1,0:T(8,128)(2,1)S(1)}, bf16[128,256]{1,0:T(8,128)(2,1)S(1)}, u32[]{:S(2)}, u32[]{:S(2)}) collective-permute-start(bf16[128,256]{1,0:T(8,128)(2,1)S(1)} %relay.1), channel_id=1, source_target_pairs={{0,8},{8,0},{16,24},{24,16},{1,9},{9,1},{17,25},{25,17},{2,10},{10... | collective-permute-start | bytes 196616 | tf_op jit(solution)/shard_map/ppermute | solution.py:289
  13.6 0.0 collective-permute-start.5
  13.6 0.5 %first.1 = (f32[384,256]{1,0:T(8,128)S(1)}, f32[384,256]{1,0:T(8,128)S(1)}, f32[384,128]{1,0:T(8,128)S(1)}) custom-call(f32[12,256]{1,0:T(8,128)S(1)} %get-tuple-element.57.choice.rest_6_, bf16[384,1920]{1,0:T(8,128)(2,1)S(1)} %get-tuple-element.50.dense, bf16[384,256]{1,0:T(8,128)(2,1)S(1)} %get-tuple-element.46.features, ...), custom_call_target="tpu_custom_call" | custom-call | flops 1000000000 | bytes 3145728 | tf_op jit(solution)/shard_map/first/pallas_call | solution.py:408
  14.1 0.7 %collective-permute-done.5.rest_4_ = bf16[16,256]{1,0:T(8,128)(2,1)S(1)} collective-permute-done((bf16[16,256]{1,0:T(8,128)(2,1)S(1)}, bf16[16,256]{1,0:T(8,128)(2,1)S(1)}, u32[]{:S(2)}, u32[]{:S(2)}) %collective-permute-start.5) | collective-permute-done | bytes 8224 | tf_op jit(solution)/shard_map/ppermute | solution.py:289
  14.8 0.0 collective-permute-done.4.rest_3_.rest_4_
  14.8 0.5 %collective-permute-done.3.rest_2_.rest_3_ = bf16[272,256]{1,0:T(8,128)(2,1)S(1)} collective-permute-done((bf16[272,256]{1,0:T(8,128)(2,1)S(1)}, bf16[272,256]{1,0:T(8,128)(2,1)S(1)}, u32[]{:S(2)}, u32[]{:S(2)}) %collective-permute-start.3) | collective-permute-done | bytes 139296 | tf_op jit(solution)/shard_map/ppermute | solution.py:289
  15.3 0.1 collective-permute-done.2.rest_1_.rest_2_
  15.4 0.2 trade.1
  15.5 0.1 collective-permute-start.6
  15.6 0.3 near.1.before
  15.9 0.4 %flip.1.dense_t.rest_8_ = bf16[1920,384]{1,0:T(8,128)(2,1)S(1)} custom-call(bf16[384,1920]{1,0:T(8,128)(2,1)S(1)} %get-tuple-element.50.dense), custom_call_target="tpu_custom_call" | custom-call | flops 10000000 | bytes 1048576 | tf_op jit(solution)/shard_map/flip/pallas_call | solution.py:386
  16.4 0.0 collective-permute-done.7.rest_0_
  16.4 0.2 late.1.before
  16.6 0.6 %collective-permute-done.6.rest_0_.rest_5_ = bf16[576,256]{1,0:T(8,128)(2,1)S(1)} collective-permute-done((bf16[576,256]{1,0:T(8,128)(2,1)S(1)}, bf16[576,256]{1,0:T(8,128)(2,1)S(1)}, u32[]{:S(2)}, u32[]{:S(2)}) %collective-permute-start.6) | collective-permute-done | bytes 294944 | tf_op jit(solution)/shard_map/ppermute | solution.py:289
  17.2 1.2 %middle.1 = (bf16[256,256]{1,0:T(8,128)(2,1)S(1)}, bf16[256,256]{1,0:T(8,128)(2,1)S(1)}, bf16[256,256]{1,0:T(8,128)(2,1)S(1)}, bf16[144,256]{1,0:T(8,128)(2,1)S(...) custom-call(f32[12,256]{1,0:T(8,128)S(1)} %get-tuple-element.57.choi, ...), custom_call_target="tpu_custom_call" | custom-call | flops 377487360 | bytes 6291456 | tf_op jit(solution)/shard_map/middle/pallas_call | solution.py:463
  18.4 2.0 %collective-permute-start.9 = (bf16[256,256]{1,0:T(8,128)(2,1)S(1)}, bf16[256,256]{1,0:T(8,128)(2,1)S(1)}, u32[]{:S(2)}, u32[]{:S(2)}) collective-permute-start(bf16[256,256]{1,0:T(8,128)(2,1)S(1)} %get-tuple-element.56), channel_id=1, source_target_pairs={{0,6},{1,7},{2,4},{3,5},{4,2},{5,3},{6,0},{7,1},{8,14},{9,15},{10,... | collective-permute-start | bytes 393224 | tf_op jit(solution)/shard_map/ppermute | solution.py:289
  20.4 3.2 %collective-permute-start.8 = (bf16[128,256]{1,0:T(8,128)(2,1)S(1)}, bf16[128,256]{1,0:T(8,128)(2,1)S(1)}, u32[]{:S(2)}, u32[]{:S(2)}) collective-permute-start(bf16[128,256]{1,0:T(8,128)(2,1)S(1)} %get-tuple-element.54), channel_id=1, source_target_pairs={{0,24},{8,16},{16,8},{24,0},{1,25},{9,17},{17,9},{25,1},{2,26},{10... | collective-permute-start | bytes 196616 | tf_op jit(solution)/shard_map/ppermute | solution.py:289
  23.6 0.5 %collective-permute-start.12 = (bf16[256,256]{1,0:T(8,128)(2,1)S(1)}, bf16[256,256]{1,0:T(8,128)(2,1)S(1)}, u32[]{:S(2)}, u32[]{:S(2)}) collective-permute-start(bf16[256,256]{1,0:T(8,128)(2,1)S(1)} %get-tuple-element.65), channel_id=1, source_target_pairs={{0,4},{1,5},{2,6},{3,7},{4,0},{5,1},{6,2},{7,3},{8,12},{9,13},{10,... | collective-permute-start | bytes 393224 | tf_op jit(solution)/shard_map/ppermute | solution.py:289
  24.1 0.5 %collective-permute-start.13 = (bf16[256,256]{1,0:T(8,128)(2,1)S(1)}, bf16[256,256]{1,0:T(8,128)(2,1)S(1)}, u32[]{:S(2)}, u32[]{:S(2)}) collective-permute-start(bf16[256,256]{1,0:T(8,128)(2,1)S(1)} %get-tuple-element.66), channel_id=1, source_target_pairs={{0,2},{1,3},{2,0},{3,1},{4,6},{5,7},{6,4},{7,5},{8,10},{9,11},{10,... | collective-permute-start | bytes 393224 | tf_op jit(solution)/shard_map/ppermute | solution.py:289
  24.7 0.0 collective-permute-start.11
  24.7 0.3 %collective-permute-done.9.rest_1_.rest_3_ = bf16[256,256]{1,0:T(8,128)(2,1)S(1)} collective-permute-done((bf16[256,256]{1,0:T(8,128)(2,1)S(1)}, bf16[256,256]{1,0:T(8,128)(2,1)S(1)}, u32[]{:S(2)}, u32[]{:S(2)}) %collective-permute-start.9) | collective-permute-done | bytes 131104 | tf_op jit(solution)/shard_map/ppermute | solution.py:289
  25.0 1.4 %collective-permute-start.10 = (bf16[144,256]{1,0:T(8,128)(2,1)S(1)}, bf16[144,256]{1,0:T(8,128)(2,1)S(1)}, u32[]{:S(2)}, u32[]{:S(2)}) collective-permute-start(bf16[144,256]{1,0:T(8,128)(2,1)S(1)} %get-tuple-element.63), channel_id=1, source_target_pairs={{0,8},{8,0},{16,24},{24,16},{1,9},{9,1},{17,25},{25,17},{2,10},{10... | collective-permute-start | bytes 221192 | tf_op jit(solution)/shard_map/ppermute | solution.py:289
  26.4 0.4 %collective-permute-done.8.rest_2_ = bf16[128,256]{1,0:T(8,128)(2,1)S(1)} collective-permute-done((bf16[128,256]{1,0:T(8,128)(2,1)S(1)}, bf16[128,256]{1,0:T(8,128)(2,1)S(1)}, u32[]{:S(2)}, u32[]{:S(2)}) %collective-permute-start.8) | collective-permute-done | bytes 65568 | tf_op jit(solution)/shard_map/ppermute | solution.py:289
  26.8 0.0 collective-permute-start.14
  26.8 0.3 %own.1 = (f32[384,256]{1,0:T(8,128)S(1)}, f32[12,256]{1,0:T(8,128)S(1)}) custom-call(bf16[272,256]{1,0:T(8,128)(2,1)S(1)} %collective-permute-done.near.rest_0_, bf16[272,256]{1,0:T(8,128)(2,1)S(1)} %collective-permute-done.1.message.far.rest_1_, bf16[272,256]{1,0:T(8,128)(2,1)S(1)} %collective-permute-done.2.rest_1_.rest_2_, ...), custom_call_target="tpu_custom_call" | custom-call | flops 1000000000 | bytes 2097152 | tf_op jit(solution)/shard_map/own/pallas_call | solution.py:490
  27.1 1.5 %collective-permute-done.12.rest_4_.rest_1_ = bf16[256,256]{1,0:T(8,128)(2,1)S(1)} collective-permute-done((bf16[256,256]{1,0:T(8,128)(2,1)S(1)}, bf16[256,256]{1,0:T(8,128)(2,1)S(1)}, u32[]{:S(2)}, u32[]{:S(2)}) %collective-permute-start.12) | collective-permute-done | bytes 131104 | tf_op jit(solution)/shard_map/ppermute | solution.py:289
  28.6 0.5 %collective-permute-done.13.rest_5_.rest_0_ = bf16[256,256]{1,0:T(8,128)(2,1)S(1)} collective-permute-done((bf16[256,256]{1,0:T(8,128)(2,1)S(1)}, bf16[256,256]{1,0:T(8,128)(2,1)S(1)}, u32[]{:S(2)}, u32[]{:S(2)}) %collective-permute-start.13) | collective-permute-done | bytes 131104 | tf_op jit(solution)/shard_map/ppermute | solution.py:289
  29.1 0.1 collective-permute-start.15
  29.2 0.9 %collective-permute-done.11.rest_1_ = bf16[128,256]{1,0:T(8,128)(2,1)S(1)} collective-permute-done((bf16[128,256]{1,0:T(8,128)(2,1)S(1)}, bf16[128,256]{1,0:T(8,128)(2,1)S(1)}, u32[]{:S(2)}, u32[]{:S(2)}) %collective-permute-start.11) | collective-permute-done | bytes 65568 | tf_op jit(solution)/shard_map/ppermute | solution.py:289
  30.1 0.0 collective-permute-done.10.rest_0_
  30.1 0.2 add.1.total
  30.3 0.0 collective-permute-done.14.rest_0_
  30.3 0.2 collective-permute-done.15.rest_1_
  30.5 0.8 %final.1 = bf16[384,256]{1,0:T(8,128)(2,1)} custom-call(f32[12,256]{1,0:T(8,128)S(1)} %get-tuple-element.61.owner, f32[384,256]{1,0:T(8,128)S(1)} %add.1.total, bf16[256,256]{1,0:T(8,128)(2,1)S(1)} %collective-permute-done.14.rest_0_, bf16[256,256]{1,0:T(8,128)(2,1)S(1)} %collective-permute-done.15.rest_1_), custom_call_target="tpu_custom_call" | custom-call | flops 393216 | bytes 1048576 | tf_op jit(solution)/shard_map/final/pallas_call | solution.py:520
  (3 shorter events, 0.0 us)
Async XLA Ops:
  0.9 10.9 %collective-permute-start.1 = (bf16[272,256]{1,0:T(8,128)(2,1)S(1)}, bf16[272,256]{1,0:T(8,128)(2,1)S(1)}, u32[]{:S(2)}, u32[]{:S(2)}) collective-permute-start(bf16[272,256]{1,0:T(8,128)(2,1)S(1)} %get-tuple-element.37.rest_0_), channel_id=1, source_target_pairs={{0,16},{8,24},{16,0},{24,8},{1,17},{9,25},{17,1},{25,9},{2,18},{10... | collective-permute-start | bytes 417800 | tf_op jit(solution)/shard_map/ppermute | solution.py:289
  5.0 7.0 %collective-permute-start = (bf16[272,256]{1,0:T(8,128)(2,1)S(1)}, bf16[272,256]{1,0:T(8,128)(2,1)S(1)}, u32[]{:S(2)}, u32[]{:S(2)}) collective-permute-start(bf16[272,256]{1,0:T(8,128)(2,1)S(1)} %get-tuple-element.37.rest_0_), channel_id=1, source_target_pairs={{0,8},{8,0},{16,24},{24,16},{1,9},{9,1},{17,25},{25,17},{2,10},{10... | collective-permute-start | bytes 417800 | tf_op jit(solution)/shard_map/ppermute | solution.py:289
  6.6 8.2 %collective-permute-start.4 = (bf16[272,256]{1,0:T(8,128)(2,1)S(1)}, bf16[272,256]{1,0:T(8,128)(2,1)S(1)}, u32[]{:S(2)}, u32[]{:S(2)}) collective-permute-start(bf16[272,256]{1,0:T(8,128)(2,1)S(1)} %get-tuple-element.37.rest_0_), channel_id=1, source_target_pairs={{0,6},{1,7},{2,4},{3,5},{4,2},{5,3},{6,0},{7,1},{8,14},{9,15},{10,... | collective-permute-start | bytes 417800 | tf_op jit(solution)/shard_map/ppermute | solution.py:289
  9.0 6.3 %collective-permute-start.3 = (bf16[272,256]{1,0:T(8,128)(2,1)S(1)}, bf16[272,256]{1,0:T(8,128)(2,1)S(1)}, u32[]{:S(2)}, u32[]{:S(2)}) collective-permute-start(bf16[272,256]{1,0:T(8,128)(2,1)S(1)} %get-tuple-element.37.rest_0_), channel_id=1, source_target_pairs={{0,4},{1,5},{2,6},{3,7},{4,0},{5,1},{6,2},{7,3},{8,12},{9,13},{10,... | collective-permute-start | bytes 417800 | tf_op jit(solution)/shard_map/ppermute | solution.py:289
  9.5 5.8 %collective-permute-start.2 = (bf16[272,256]{1,0:T(8,128)(2,1)S(1)}, bf16[272,256]{1,0:T(8,128)(2,1)S(1)}, u32[]{:S(2)}, u32[]{:S(2)}) collective-permute-start(bf16[272,256]{1,0:T(8,128)(2,1)S(1)} %get-tuple-element.37.rest_0_), channel_id=1, source_target_pairs={{0,2},{1,3},{2,0},{3,1},{4,6},{5,7},{6,4},{7,5},{8,10},{9,11},{10,... | collective-permute-start | bytes 417800 | tf_op jit(solution)/shard_map/ppermute | solution.py:289
  12.1 4.3 %collective-permute-start.7 = (bf16[128,256]{1,0:T(8,128)(2,1)S(1)}, bf16[128,256]{1,0:T(8,128)(2,1)S(1)}, u32[]{:S(2)}, u32[]{:S(2)}) collective-permute-start(bf16[128,256]{1,0:T(8,128)(2,1)S(1)} %relay.1), channel_id=1, source_target_pairs={{0,8},{8,0},{16,24},{24,16},{1,9},{9,1},{17,25},{25,17},{2,10},{10... | collective-permute-start | bytes 196616 | tf_op jit(solution)/shard_map/ppermute | solution.py:289
  13.6 1.2 %collective-permute-start.5 = (bf16[16,256]{1,0:T(8,128)(2,1)S(1)}, bf16[16,256]{1,0:T(8,128)(2,1)S(1)}, u32[]{:S(2)}, u32[]{:S(2)}) collective-permute-start(bf16[16,256]{1,0:T(8,128)(2,1)S(1)} %get-tuple-element.39), channel_id=1, source_target_pairs={{0,1},{1,0},{2,3},{3,2},{4,5},{5,4},{6,7},{7,6},{8,9},{9,8},{10,11... | collective-permute-start | bytes 24584 | tf_op jit(solution)/shard_map/ppermute | solution.py:289
  15.5 1.6 %collective-permute-start.6 = (bf16[576,256]{1,0:T(8,128)(2,1)S(1)}, bf16[576,256]{1,0:T(8,128)(2,1)S(1)}, u32[]{:S(2)}, u32[]{:S(2)}) collective-permute-start(bf16[576,256]{1,0:T(8,128)(2,1)S(1)} %trade.1), channel_id=1, source_target_pairs={{0,1},{1,0},{2,3},{3,2},{4,5},{5,4},{6,7},{7,6},{8,9},{9,8},{10,11... | collective-permute-start | bytes 884744 | tf_op jit(solution)/shard_map/ppermute | solution.py:289
  18.4 6.6 %collective-permute-start.9 = (bf16[256,256]{1,0:T(8,128)(2,1)S(1)}, bf16[256,256]{1,0:T(8,128)(2,1)S(1)}, u32[]{:S(2)}, u32[]{:S(2)}) collective-permute-start(bf16[256,256]{1,0:T(8,128)(2,1)S(1)} %get-tuple-element.56), channel_id=1, source_target_pairs={{0,6},{1,7},{2,4},{3,5},{4,2},{5,3},{6,0},{7,1},{8,14},{9,15},{10,... | collective-permute-start | bytes 393224 | tf_op jit(solution)/shard_map/ppermute | solution.py:289
  20.4 6.3 %collective-permute-start.8 = (bf16[128,256]{1,0:T(8,128)(2,1)S(1)}, bf16[128,256]{1,0:T(8,128)(2,1)S(1)}, u32[]{:S(2)}, u32[]{:S(2)}) collective-permute-start(bf16[128,256]{1,0:T(8,128)(2,1)S(1)} %get-tuple-element.54), channel_id=1, source_target_pairs={{0,24},{8,16},{16,8},{24,0},{1,25},{9,17},{17,9},{25,1},{2,26},{10... | collective-permute-start | bytes 196616 | tf_op jit(solution)/shard_map/ppermute | solution.py:289
  23.6 5.0 %collective-permute-start.12 = (bf16[256,256]{1,0:T(8,128)(2,1)S(1)}, bf16[256,256]{1,0:T(8,128)(2,1)S(1)}, u32[]{:S(2)}, u32[]{:S(2)}) collective-permute-start(bf16[256,256]{1,0:T(8,128)(2,1)S(1)} %get-tuple-element.65), channel_id=1, source_target_pairs={{0,4},{1,5},{2,6},{3,7},{4,0},{5,1},{6,2},{7,3},{8,12},{9,13},{10,... | collective-permute-start | bytes 393224 | tf_op jit(solution)/shard_map/ppermute | solution.py:289
  24.1 5.0 %collective-permute-start.13 = (bf16[256,256]{1,0:T(8,128)(2,1)S(1)}, bf16[256,256]{1,0:T(8,128)(2,1)S(1)}, u32[]{:S(2)}, u32[]{:S(2)}) collective-permute-start(bf16[256,256]{1,0:T(8,128)(2,1)S(1)} %get-tuple-element.66), channel_id=1, source_target_pairs={{0,2},{1,3},{2,0},{3,1},{4,6},{5,7},{6,4},{7,5},{8,10},{9,11},{10,... | collective-permute-start | bytes 393224 | tf_op jit(solution)/shard_map/ppermute | solution.py:289
  24.7 5.4 %collective-permute-start.11 = (bf16[128,256]{1,0:T(8,128)(2,1)S(1)}, bf16[128,256]{1,0:T(8,128)(2,1)S(1)}, u32[]{:S(2)}, u32[]{:S(2)}) collective-permute-start(bf16[128,256]{1,0:T(8,128)(2,1)S(1)} %get-tuple-element.64), channel_id=1, source_target_pairs={{0,16},{8,24},{16,0},{24,8},{1,17},{9,25},{17,1},{25,9},{2,18},{10... | collective-permute-start | bytes 196616 | tf_op jit(solution)/shard_map/ppermute | solution.py:289
  25.0 5.1 %collective-permute-start.10 = (bf16[144,256]{1,0:T(8,128)(2,1)S(1)}, bf16[144,256]{1,0:T(8,128)(2,1)S(1)}, u32[]{:S(2)}, u32[]{:S(2)}) collective-permute-start(bf16[144,256]{1,0:T(8,128)(2,1)S(1)} %get-tuple-element.63), channel_id=1, source_target_pairs={{0,8},{8,0},{16,24},{24,16},{1,9},{9,1},{17,25},{25,17},{2,10},{10... | collective-permute-start | bytes 221192 | tf_op jit(solution)/shard_map/ppermute | solution.py:289
  26.8 3.5 %collective-permute-start.14 = (bf16[256,256]{1,0:T(8,128)(2,1)S(1)}, bf16[256,256]{1,0:T(8,128)(2,1)S(1)}, u32[]{:S(2)}, u32[]{:S(2)}) collective-permute-start(bf16[256,256]{1,0:T(8,128)(2,1)S(1)} %early.1), channel_id=1, source_target_pairs={{0,1},{1,0},{2,3},{3,2},{4,5},{5,4},{6,7},{7,6},{8,9},{9,8},{10,11... | collective-permute-start | bytes 393224 | tf_op jit(solution)/shard_map/ppermute | solution.py:289
  29.1 1.4 %collective-permute-start.15 = (bf16[256,256]{1,0:T(8,128)(2,1)S(1)}, bf16[256,256]{1,0:T(8,128)(2,1)S(1)}, u32[]{:S(2)}, u32[]{:S(2)}) collective-permute-start(bf16[256,256]{1,0:T(8,128)(2,1)S(1)} %turn.1), channel_id=1, source_target_pairs={{0,1},{1,0},{2,3},{3,2},{4,5},{5,4},{6,7},{7,6},{8,9},{9,8},{10,11... | collective-permute-start | bytes 393224 | tf_op jit(solution)/shard_map/ppermute | solution.py:289

commit v13 on v12

--- a/solution.py
+++ b/solution.py
@@ -151,17 +151,27 @@
         out[i * size : (i + 1) * size, :] = message[last - size : last, :]
 
 
-def halo_sum(choice, dense, own, halos, refs, halo):
-    size = dense.shape[0] // own
-    columns = []
+def halo_blocks(choice, size, halos, refs, halo):
+    first = halos[0]
+    if all(
+        (at, row, picked) == (first[1], first[2] + i * size, True)
+        for i, (_, at, row, picked) in enumerate(halos)
+    ):
+        return refs[first[1]][first[2] : first[2] + len(halos) * size, :]
     for i, (slot, at, row, picked) in enumerate(halos):
         if picked:
             block = refs[at][row : row + size, :]
         else:
             block = pick(refs[at], choice[slot : slot + 1, :], size)
         halo[i * size : (i + 1) * size, :] = block
-        columns.append(dense[:, (own + slot) * size : (own + slot + 1) * size])
-    return dot(jnp.concatenate(columns, axis=1), halo[...])
+    return halo[...]
+
+
+def halo_sum(choice, dense, own, halos, refs, halo):
+    size = dense.shape[0] // own
+    blocks = halo_blocks(choice, size, halos, refs, halo)
+    columns = [dense[:, (own + slot) * size : (own + slot + 1) * size] for slot, *_ in halos]
+    return dot(jnp.concatenate(columns, axis=1), blocks)
 
 
 def flip_kernel(size, dense, dense_t):
@@ -198,13 +208,17 @@
     pairs, rest = rest[: sub_count // 2 - 1], rest[sub_count // 2 - 1 :]
     along, (sibling, kept, spread, grad_pre, halo) = rest[:-5], rest[-5:]
     size = dense.shape[0] // own
-    aggregate = before[...] + halo_sum(choice, dense, own, halos, refs, halo)
-    inv = jnp.concatenate([inverse[...]] * (grad_out.shape[1] // size), axis=1)
-    mean = (aggregate * inv).astype(BF)
-    pre = own_pre[...] + dot(mean, w_neigh[...])
-    grad = (grad_out[...].astype(F32) * gelu_slope(pre)).astype(BF)
-    grad_pre[...] = grad
-    spread[...] = (dot_right_transposed(grad, w_neigh[...]) * inv).astype(BF)
+    blocks = halo_blocks(choice, size, halos, refs, halo)
+    for at in range(0, own * size, size):
+        part = slice(at, at + size)
+        columns = [dense[part, (own + slot) * size : (own + slot + 1) * size] for slot, *_ in halos]
+        inv = jnp.concatenate([inverse[part, :]] * (grad_out.shape[1] // size), axis=1)
+        aggregate = before[part, :] + dot(jnp.concatenate(columns, axis=1), blocks)
+        mean = (aggregate * inv).astype(BF)
+        pre = own_pre[part, :] + dot(mean, w_neigh[...])
+        grad = (grad_out[part, :].astype(F32) * gelu_slope(pre)).astype(BF)
+        grad_pre[part, :] = grad
+        spread[part, :] = (dot_right_transposed(grad, w_neigh[...]) * inv).astype(BF)
 
     def partial(slot, count=1):
         rows = slice((own + slot) * size, (own + slot + count) * size)
@@ -507,26 +521,26 @@
     )
     turned = across(turned, 1)
     more = [*far, *near[::-1]]
+    parts = [(slot, i, 0) for i, (slot, _) in enumerate(more)]
     places = {slot: (0, size + i * EXTRA) for i, slot in enumerate(sub_count + d for d in relayed)}
     total = call(
         functools.partial(
-            add_kernel, own, sub_count, [(slot, i, 0) for i, (slot, _) in enumerate(more)], places
+            add_kernel, own, sub_count, parts, places
         ),
         wide, "add", 10**10, owner, total, *[value for _, value in more],
     )
     parts = [(1, 0, 0), *[(d + 1, 0, size) for d, _ in soon]]
     parts += [(d + 1, 1, i * size) for i, (d, _) in enumerate(rest)]
-    values = [early]
     return pl.pallas_call(
         functools.partial(final_kernel, own, parts),
         out_shape=narrow,
-        in_specs=[VMEM] * (3 + len(values)),
+        in_specs=[VMEM] * 4,
         out_specs=HBM,
         scratch_shapes=[pltpu.VMEM((rows, width), BF), pltpu.SemaphoreType.DMA((3,))],
         compiler_params=PARAMS,
         cost_estimate=cost(rows * width * 4, 1024 * 1024),
         name="final",
-    )(owner, total, *values, turned)
+    )(owner, total, early, turned)
 
 
 def solution(mesh):

time: 31.5 us -> 31.7 us (level)
  no operation moved by 1% of the time
where the time goes in v13:
time: 31.7 us; the launch traced here: 31.5 us
  starting transfers between devices  18.5 us (58%)
  Pallas kernels  6.98 us (22%)
  waiting for transfers between devices  5.95 us (19%)
    ppermute x16, starting transfers between devices, swap(): return lax.ppermute(value, axis, [(i, i ^ d) for i in range(count)])  18.5 us
    ppermute x16, waiting for transfers between devices, swap(): return lax.ppermute(value, axis, [(i, i ^ d) for i in range(count)])  5.95 us
    pallas_call x1, Pallas kernels, shards(): pl.pallas_call(functools.partial(prepare_kernel, *counts), out_shape=[jax...  1.63 us
    pallas_call x1, Pallas kernels, shards(): pl.pallas_call(functools.partial(middle_kernel, *counts, late_halos, len(...  1.46 us
    pallas_call x3, Pallas kernels, sum_call(): pl.pallas_call(functools.partial(kernel, own, halos), out_shape=out_shape...  0.99 us
    pallas_call x7, Pallas kernels, call(): pl.pallas_call(kernel, out_shape=out_shape, in_specs=[VMEM] * len(operand...  0.92 us
    pallas_call x1, Pallas kernels, shards(): pl.pallas_call(edge_kernel, out_shape=[jax.ShapeDtypeStruct((BOUNDARY * s...  0.89 us
    pallas_call x1, Pallas kernels, shards(): pl.pallas_call(functools.partial(final_kernel, own, parts), out_shape=nar...  0.78 us
  transfers between devices with their start and end apart: 16, of which 12 were waited for; matrix products, arithmetic and copies ran while one was open for 0% of the time, Pallas kernels for 12%

profile of v13, /device:TPU:0, one launch (start us, length us, event | category | flops | bytes accessed | tf_op | source)
XLA Modules:
  0.0 31.5 jit_solution(3030129147038175112)
XLA Ops:
  0.0 0.9 %edge.1 = (bf16[272,256]{1,0:T(8,128)(2,1)S(1)}, bf16[16,256]{1,0:T(8,128)(2,1)S(1)}) custom-call(s32[1,8]{1,0:T(1,128)} %recv_sub_hbm.1, s32[1,4]{1,0:T(1,128)} %recv_cluster_hbm.1, bf16[384,256]{1,0:T(8,128)(2,1)} %features_hbm.1), custom_call_target="tpu_custom_call" | custom-call | flops 1024 | bytes 262144 | tf_op jit(solution)/shard_map/edge/pallas_call | solution.py:336
  0.9 4.1 %collective-permute-start.1 = (bf16[272,256]{1,0:T(8,128)(2,1)S(1)}, bf16[272,256]{1,0:T(8,128)(2,1)S(1)}, u32[]{:S(2)}, u32[]{:S(2)}) collective-permute-start(bf16[272,256]{1,0:T(8,128)(2,1)S(1)} %get-tuple-element.37.rest_0_), channel_id=1, source_target_pairs={{0,16},{8,24},{16,0},{24,8},{1,17},{9,25},{17,1},{25,9},{2,18},{10... | collective-permute-start | bytes 417800 | tf_op jit(solution)/shard_map/ppermute | solution.py:303
  5.0 1.6 %collective-permute-start = (bf16[272,256]{1,0:T(8,128)(2,1)S(1)}, bf16[272,256]{1,0:T(8,128)(2,1)S(1)}, u32[]{:S(2)}, u32[]{:S(2)}) collective-permute-start(bf16[272,256]{1,0:T(8,128)(2,1)S(1)} %get-tuple-element.37.rest_0_), channel_id=1, source_target_pairs={{0,8},{8,0},{16,24},{24,16},{1,9},{9,1},{17,25},{25,17},{2,10},{10... | collective-permute-start | bytes 417800 | tf_op jit(solution)/shard_map/ppermute | solution.py:303
  6.6 2.4 %collective-permute-start.4 = (bf16[272,256]{1,0:T(8,128)(2,1)S(1)}, bf16[272,256]{1,0:T(8,128)(2,1)S(1)}, u32[]{:S(2)}, u32[]{:S(2)}) collective-permute-start(bf16[272,256]{1,0:T(8,128)(2,1)S(1)} %get-tuple-element.37.rest_0_), channel_id=1, source_target_pairs={{0,6},{1,7},{2,4},{3,5},{4,2},{5,3},{6,0},{7,1},{8,14},{9,15},{10,... | collective-permute-start | bytes 417800 | tf_op jit(solution)/shard_map/ppermute | solution.py:303
  9.0 0.5 %collective-permute-start.3 = (bf16[272,256]{1,0:T(8,128)(2,1)S(1)}, bf16[272,256]{1,0:T(8,128)(2,1)S(1)}, u32[]{:S(2)}, u32[]{:S(2)}) collective-permute-start(bf16[272,256]{1,0:T(8,128)(2,1)S(1)} %get-tuple-element.37.rest_0_), channel_id=1, source_target_pairs={{0,4},{1,5},{2,6},{3,7},{4,0},{5,1},{6,2},{7,3},{8,12},{9,13},{10,... | collective-permute-start | bytes 417800 | tf_op jit(solution)/shard_map/ppermute | solution.py:303
  9.5 0.5 %collective-permute-start.2 = (bf16[272,256]{1,0:T(8,128)(2,1)S(1)}, bf16[272,256]{1,0:T(8,128)(2,1)S(1)}, u32[]{:S(2)}, u32[]{:S(2)}) collective-permute-start(bf16[272,256]{1,0:T(8,128)(2,1)S(1)} %get-tuple-element.37.rest_0_), channel_id=1, source_target_pairs={{0,2},{1,3},{2,0},{3,1},{4,6},{5,7},{6,4},{7,5},{8,10},{9,11},{10,... | collective-permute-start | bytes 417800 | tf_op jit(solution)/shard_map/ppermute | solution.py:303
  10.1 1.6 %prepare.1 = (bf16[384,1920]{1,0:T(8,128)(2,1)S(1)}, f32[12,256]{1,0:T(8,128)S(1)}, bf16[384,256]{1,0:T(8,128)(2,1)S(1)}, bf16[256,256]{1,0:T(8,128)(2,1)S(1)}, ...) custom-call(s32[24]{0:T(128)} %tile_dst_hbm.1, s32[24]{0:T(128)} %tile_src_hbm.1, ...), custom_call_target="tpu_custom_call" | custom-call | flops 100000000 | bytes 6291456 | tf_op jit(solution)/shard_map/prepare/pallas_call | solution.py:370
  11.7 0.1 collective-permute-done.1.message.far.rest_1_
  11.8 0.2 collective-permute-done.near.rest_0_
  12.0 0.1 relay.1
  12.1 1.5 %collective-permute-start.7 = (bf16[128,256]{1,0:T(8,128)(2,1)S(1)}, bf16[128,256]{1,0:T(8,128)(2,1)S(1)}, u32[]{:S(2)}, u32[]{:S(2)}) collective-permute-start(bf16[128,256]{1,0:T(8,128)(2,1)S(1)} %relay.1), channel_id=1, source_target_pairs={{0,8},{8,0},{16,24},{24,16},{1,9},{9,1},{17,25},{25,17},{2,10},{10... | collective-permute-start | bytes 196616 | tf_op jit(solution)/shard_map/ppermute | solution.py:303
  13.6 0.0 collective-permute-start.5
  13.6 0.5 %first.1 = (f32[384,256]{1,0:T(8,128)S(1)}, f32[384,256]{1,0:T(8,128)S(1)}, f32[384,128]{1,0:T(8,128)S(1)}) custom-call(f32[12,256]{1,0:T(8,128)S(1)} %get-tuple-element.57.choice.rest_6_, bf16[384,1920]{1,0:T(8,128)(2,1)S(1)} %get-tuple-element.50.dense, bf16[384,256]{1,0:T(8,128)(2,1)S(1)} %get-tuple-element.46.features, ...), custom_call_target="tpu_custom_call" | custom-call | flops 1000000000 | bytes 3145728 | tf_op jit(solution)/shard_map/first/pallas_call | solution.py:422
  14.1 0.7 %collective-permute-done.5.rest_4_ = bf16[16,256]{1,0:T(8,128)(2,1)S(1)} collective-permute-done((bf16[16,256]{1,0:T(8,128)(2,1)S(1)}, bf16[16,256]{1,0:T(8,128)(2,1)S(1)}, u32[]{:S(2)}, u32[]{:S(2)}) %collective-permute-start.5) | collective-permute-done | bytes 8224 | tf_op jit(solution)/shard_map/ppermute | solution.py:303
  14.8 0.0 collective-permute-done.4.rest_3_.rest_4_
  14.8 0.5 %collective-permute-done.3.rest_2_.rest_3_ = bf16[272,256]{1,0:T(8,128)(2,1)S(1)} collective-permute-done((bf16[272,256]{1,0:T(8,128)(2,1)S(1)}, bf16[272,256]{1,0:T(8,128)(2,1)S(1)}, u32[]{:S(2)}, u32[]{:S(2)}) %collective-permute-start.3) | collective-permute-done | bytes 139296 | tf_op jit(solution)/shard_map/ppermute | solution.py:303
  15.3 0.1 collective-permute-done.2.rest_1_.rest_2_
  15.4 0.2 trade.1
  15.5 0.1 collective-permute-start.6
  15.6 0.3 near.1.before
  15.9 0.4 %flip.1.dense_t.rest_8_ = bf16[1920,384]{1,0:T(8,128)(2,1)S(1)} custom-call(bf16[384,1920]{1,0:T(8,128)(2,1)S(1)} %get-tuple-element.50.dense), custom_call_target="tpu_custom_call" | custom-call | flops 10000000 | bytes 1048576 | tf_op jit(solution)/shard_map/flip/pallas_call | solution.py:400
  16.4 0.0 collective-permute-done.7.rest_0_
  16.4 0.2 late.1.before
  16.6 0.6 %collective-permute-done.6.rest_0_.rest_5_ = bf16[576,256]{1,0:T(8,128)(2,1)S(1)} collective-permute-done((bf16[576,256]{1,0:T(8,128)(2,1)S(1)}, bf16[576,256]{1,0:T(8,128)(2,1)S(1)}, u32[]{:S(2)}, u32[]{:S(2)}) %collective-permute-start.6) | collective-permute-done | bytes 294944 | tf_op jit(solution)/shard_map/ppermute | solution.py:303
  17.2 1.5 %middle.1 = (bf16[256,256]{1,0:T(8,128)(2,1)S(1)}, bf16[256,256]{1,0:T(8,128)(2,1)S(1)}, bf16[256,256]{1,0:T(8,128)(2,1)S(1)}, bf16[144,256]{1,0:T(8,128)(2,1)S(...) custom-call(f32[12,256]{1,0:T(8,128)S(1)} %get-tuple-element.57.choi, ...), custom_call_target="tpu_custom_call" | custom-call | flops 377487360 | bytes 6291456 | tf_op jit(solution)/shard_map/middle/pallas_call | solution.py:477
  18.6 2.0 %collective-permute-start.9 = (bf16[256,256]{1,0:T(8,128)(2,1)S(1)}, bf16[256,256]{1,0:T(8,128)(2,1)S(1)}, u32[]{:S(2)}, u32[]{:S(2)}) collective-permute-start(bf16[256,256]{1,0:T(8,128)(2,1)S(1)} %get-tuple-element.56), channel_id=1, source_target_pairs={{0,6},{1,7},{2,4},{3,5},{4,2},{5,3},{6,0},{7,1},{8,14},{9,15},{10,... | collective-permute-start | bytes 393224 | tf_op jit(solution)/shard_map/ppermute | solution.py:303
  20.6 3.2 %collective-permute-start.8 = (bf16[128,256]{1,0:T(8,128)(2,1)S(1)}, bf16[128,256]{1,0:T(8,128)(2,1)S(1)}, u32[]{:S(2)}, u32[]{:S(2)}) collective-permute-start(bf16[128,256]{1,0:T(8,128)(2,1)S(1)} %get-tuple-element.54), channel_id=1, source_target_pairs={{0,24},{8,16},{16,8},{24,0},{1,25},{9,17},{17,9},{25,1},{2,26},{10... | collective-permute-start | bytes 196616 | tf_op jit(solution)/shard_map/ppermute | solution.py:303
  23.8 0.5 %collective-permute-start.12 = (bf16[256,256]{1,0:T(8,128)(2,1)S(1)}, bf16[256,256]{1,0:T(8,128)(2,1)S(1)}, u32[]{:S(2)}, u32[]{:S(2)}) collective-permute-start(bf16[256,256]{1,0:T(8,128)(2,1)S(1)} %get-tuple-element.65), channel_id=1, source_target_pairs={{0,4},{1,5},{2,6},{3,7},{4,0},{5,1},{6,2},{7,3},{8,12},{9,13},{10,... | collective-permute-start | bytes 393224 | tf_op jit(solution)/shard_map/ppermute | solution.py:303
  24.3 0.5 %collective-permute-start.13 = (bf16[256,256]{1,0:T(8,128)(2,1)S(1)}, bf16[256,256]{1,0:T(8,128)(2,1)S(1)}, u32[]{:S(2)}, u32[]{:S(2)}) collective-permute-start(bf16[256,256]{1,0:T(8,128)(2,1)S(1)} %get-tuple-element.66), channel_id=1, source_target_pairs={{0,2},{1,3},{2,0},{3,1},{4,6},{5,7},{6,4},{7,5},{8,10},{9,11},{10,... | collective-permute-start | bytes 393224 | tf_op jit(solution)/shard_map/ppermute | solution.py:303
  24.9 0.0 collective-permute-start.11
  24.9 0.3 %collective-permute-done.9.rest_1_.rest_3_ = bf16[256,256]{1,0:T(8,128)(2,1)S(1)} collective-permute-done((bf16[256,256]{1,0:T(8,128)(2,1)S(1)}, bf16[256,256]{1,0:T(8,128)(2,1)S(1)}, u32[]{:S(2)}, u32[]{:S(2)}) %collective-permute-start.9) | collective-permute-done | bytes 131104 | tf_op jit(solution)/shard_map/ppermute | solution.py:303
  25.2 1.4 %collective-permute-start.10 = (bf16[144,256]{1,0:T(8,128)(2,1)S(1)}, bf16[144,256]{1,0:T(8,128)(2,1)S(1)}, u32[]{:S(2)}, u32[]{:S(2)}) collective-permute-start(bf16[144,256]{1,0:T(8,128)(2,1)S(1)} %get-tuple-element.63), channel_id=1, source_target_pairs={{0,8},{8,0},{16,24},{24,16},{1,9},{9,1},{17,25},{25,17},{2,10},{10... | collective-permute-start | bytes 221192 | tf_op jit(solution)/shard_map/ppermute | solution.py:303
  26.6 0.4 %collective-permute-done.8.rest_2_ = bf16[128,256]{1,0:T(8,128)(2,1)S(1)} collective-permute-done((bf16[128,256]{1,0:T(8,128)(2,1)S(1)}, bf16[128,256]{1,0:T(8,128)(2,1)S(1)}, u32[]{:S(2)}, u32[]{:S(2)}) %collective-permute-start.8) | collective-permute-done | bytes 65568 | tf_op jit(solution)/shard_map/ppermute | solution.py:303
  27.0 0.0 collective-permute-start.14
  27.0 0.3 own.1
  27.3 1.5 %collective-permute-done.12.rest_4_.rest_1_ = bf16[256,256]{1,0:T(8,128)(2,1)S(1)} collective-permute-done((bf16[256,256]{1,0:T(8,128)(2,1)S(1)}, bf16[256,256]{1,0:T(8,128)(2,1)S(1)}, u32[]{:S(2)}, u32[]{:S(2)}) %collective-permute-start.12) | collective-permute-done | bytes 131104 | tf_op jit(solution)/shard_map/ppermute | solution.py:303
  28.8 0.5 %collective-permute-done.13.rest_5_.rest_0_ = bf16[256,256]{1,0:T(8,128)(2,1)S(1)} collective-permute-done((bf16[256,256]{1,0:T(8,128)(2,1)S(1)}, bf16[256,256]{1,0:T(8,128)(2,1)S(1)}, u32[]{:S(2)}, u32[]{:S(2)}) %collective-permute-start.13) | collective-permute-done | bytes 131104 | tf_op jit(solution)/shard_map/ppermute | solution.py:303
  29.3 0.1 collective-permute-start.15
  29.4 0.9 %collective-permute-done.11.rest_1_ = bf16[128,256]{1,0:T(8,128)(2,1)S(1)} collective-permute-done((bf16[128,256]{1,0:T(8,128)(2,1)S(1)}, bf16[128,256]{1,0:T(8,128)(2,1)S(1)}, u32[]{:S(2)}, u32[]{:S(2)}) %collective-permute-start.11) | collective-permute-done | bytes 65568 | tf_op jit(solution)/shard_map/ppermute | solution.py:303
  30.3 0.0 collective-permute-done.10.rest_0_
  30.3 0.2 add.1.total
  30.5 0.0 collective-permute-done.14.rest_0_
  30.5 0.2 collective-permute-done.15.rest_1_
  30.7 0.8 %final.1 = bf16[384,256]{1,0:T(8,128)(2,1)} custom-call(f32[12,256]{1,0:T(8,128)S(1)} %get-tuple-element.61.owner, f32[384,256]{1,0:T(8,128)S(1)} %add.1.total, bf16[256,256]{1,0:T(8,128)(2,1)S(1)} %collective-permute-done.14.rest_0_, bf16[256,256]{1,0:T(8,128)(2,1)S(1)} %collective-permute-done.15.rest_1_), custom_call_target="tpu_custom_call" | custom-call | flops 393216 | bytes 1048576 | tf_op jit(solution)/shard_map/final/pallas_call | solution.py:534
  (3 shorter events, 0.0 us)
Async XLA Ops:
  0.9 10.9 %collective-permute-start.1 = (bf16[272,256]{1,0:T(8,128)(2,1)S(1)}, bf16[272,256]{1,0:T(8,128)(2,1)S(1)}, u32[]{:S(2)}, u32[]{:S(2)}) collective-permute-start(bf16[272,256]{1,0:T(8,128)(2,1)S(1)} %get-tuple-element.37.rest_0_), channel_id=1, source_target_pairs={{0,16},{8,24},{16,0},{24,8},{1,17},{9,25},{17,1},{25,9},{2,18},{10... | collective-permute-start | bytes 417800 | tf_op jit(solution)/shard_map/ppermute | solution.py:303
  5.0 7.0 %collective-permute-start = (bf16[272,256]{1,0:T(8,128)(2,1)S(1)}, bf16[272,256]{1,0:T(8,128)(2,1)S(1)}, u32[]{:S(2)}, u32[]{:S(2)}) collective-permute-start(bf16[272,256]{1,0:T(8,128)(2,1)S(1)} %get-tuple-element.37.rest_0_), channel_id=1, source_target_pairs={{0,8},{8,0},{16,24},{24,16},{1,9},{9,1},{17,25},{25,17},{2,10},{10... | collective-permute-start | bytes 417800 | tf_op jit(solution)/shard_map/ppermute | solution.py:303
  6.6 8.2 %collective-permute-start.4 = (bf16[272,256]{1,0:T(8,128)(2,1)S(1)}, bf16[272,256]{1,0:T(8,128)(2,1)S(1)}, u32[]{:S(2)}, u32[]{:S(2)}) collective-permute-start(bf16[272,256]{1,0:T(8,128)(2,1)S(1)} %get-tuple-element.37.rest_0_), channel_id=1, source_target_pairs={{0,6},{1,7},{2,4},{3,5},{4,2},{5,3},{6,0},{7,1},{8,14},{9,15},{10,... | collective-permute-start | bytes 417800 | tf_op jit(solution)/shard_map/ppermute | solution.py:303
  9.0 6.3 %collective-permute-start.3 = (bf16[272,256]{1,0:T(8,128)(2,1)S(1)}, bf16[272,256]{1,0:T(8,128)(2,1)S(1)}, u32[]{:S(2)}, u32[]{:S(2)}) collective-permute-start(bf16[272,256]{1,0:T(8,128)(2,1)S(1)} %get-tuple-element.37.rest_0_), channel_id=1, source_target_pairs={{0,4},{1,5},{2,6},{3,7},{4,0},{5,1},{6,2},{7,3},{8,12},{9,13},{10,... | collective-permute-start | bytes 417800 | tf_op jit(solution)/shard_map/ppermute | solution.py:303
  9.5 5.8 %collective-permute-start.2 = (bf16[272,256]{1,0:T(8,128)(2,1)S(1)}, bf16[272,256]{1,0:T(8,128)(2,1)S(1)}, u32[]{:S(2)}, u32[]{:S(2)}) collective-permute-start(bf16[272,256]{1,0:T(8,128)(2,1)S(1)} %get-tuple-element.37.rest_0_), channel_id=1, source_target_pairs={{0,2},{1,3},{2,0},{3,1},{4,6},{5,7},{6,4},{7,5},{8,10},{9,11},{10,... | collective-permute-start | bytes 417800 | tf_op jit(solution)/shard_map/ppermute | solution.py:303
  12.1 4.3 %collective-permute-start.7 = (bf16[128,256]{1,0:T(8,128)(2,1)S(1)}, bf16[128,256]{1,0:T(8,128)(2,1)S(1)}, u32[]{:S(2)}, u32[]{:S(2)}) collective-permute-start(bf16[128,256]{1,0:T(8,128)(2,1)S(1)} %relay.1), channel_id=1, source_target_pairs={{0,8},{8,0},{16,24},{24,16},{1,9},{9,1},{17,25},{25,17},{2,10},{10... | collective-permute-start | bytes 196616 | tf_op jit(solution)/shard_map/ppermute | solution.py:303
  13.6 1.2 %collective-permute-start.5 = (bf16[16,256]{1,0:T(8,128)(2,1)S(1)}, bf16[16,256]{1,0:T(8,128)(2,1)S(1)}, u32[]{:S(2)}, u32[]{:S(2)}) collective-permute-start(bf16[16,256]{1,0:T(8,128)(2,1)S(1)} %get-tuple-element.39), channel_id=1, source_target_pairs={{0,1},{1,0},{2,3},{3,2},{4,5},{5,4},{6,7},{7,6},{8,9},{9,8},{10,11... | collective-permute-start | bytes 24584 | tf_op jit(solution)/shard_map/ppermute | solution.py:303
  15.5 1.6 %collective-permute-start.6 = (bf16[576,256]{1,0:T(8,128)(2,1)S(1)}, bf16[576,256]{1,0:T(8,128)(2,1)S(1)}, u32[]{:S(2)}, u32[]{:S(2)}) collective-permute-start(bf16[576,256]{1,0:T(8,128)(2,1)S(1)} %trade.1), channel_id=1, source_target_pairs={{0,1},{1,0},{2,3},{3,2},{4,5},{5,4},{6,7},{7,6},{8,9},{9,8},{10,11... | collective-permute-start | bytes 884744 | tf_op jit(solution)/shard_map/ppermute | solution.py:303
  18.6 6.5 %collective-permute-start.9 = (bf16[256,256]{1,0:T(8,128)(2,1)S(1)}, bf16[256,256]{1,0:T(8,128)(2,1)S(1)}, u32[]{:S(2)}, u32[]{:S(2)}) collective-permute-start(bf16[256,256]{1,0:T(8,128)(2,1)S(1)} %get-tuple-element.56), channel_id=1, source_target_pairs={{0,6},{1,7},{2,4},{3,5},{4,2},{5,3},{6,0},{7,1},{8,14},{9,15},{10,... | collective-permute-start | bytes 393224 | tf_op jit(solution)/shard_map/ppermute | solution.py:303
  20.6 6.4 %collective-permute-start.8 = (bf16[128,256]{1,0:T(8,128)(2,1)S(1)}, bf16[128,256]{1,0:T(8,128)(2,1)S(1)}, u32[]{:S(2)}, u32[]{:S(2)}) collective-permute-start(bf16[128,256]{1,0:T(8,128)(2,1)S(1)} %get-tuple-element.54), channel_id=1, source_target_pairs={{0,24},{8,16},{16,8},{24,0},{1,25},{9,17},{17,9},{25,1},{2,26},{10... | collective-permute-start | bytes 196616 | tf_op jit(solution)/shard_map/ppermute | solution.py:303
  23.8 5.0 %collective-permute-start.12 = (bf16[256,256]{1,0:T(8,128)(2,1)S(1)}, bf16[256,256]{1,0:T(8,128)(2,1)S(1)}, u32[]{:S(2)}, u32[]{:S(2)}) collective-permute-start(bf16[256,256]{1,0:T(8,128)(2,1)S(1)} %get-tuple-element.65), channel_id=1, source_target_pairs={{0,4},{1,5},{2,6},{3,7},{4,0},{5,1},{6,2},{7,3},{8,12},{9,13},{10,... | collective-permute-start | bytes 393224 | tf_op jit(solution)/shard_map/ppermute | solution.py:303
  24.3 5.0 %collective-permute-start.13 = (bf16[256,256]{1,0:T(8,128)(2,1)S(1)}, bf16[256,256]{1,0:T(8,128)(2,1)S(1)}, u32[]{:S(2)}, u32[]{:S(2)}) collective-permute-start(bf16[256,256]{1,0:T(8,128)(2,1)S(1)} %get-tuple-element.66), channel_id=1, source_target_pairs={{0,2},{1,3},{2,0},{3,1},{4,6},{5,7},{6,4},{7,5},{8,10},{9,11},{10,... | collective-permute-start | bytes 393224 | tf_op jit(solution)/shard_map/ppermute | solution.py:303
  24.9 5.4 %collective-permute-start.11 = (bf16[128,256]{1,0:T(8,128)(2,1)S(1)}, bf16[128,256]{1,0:T(8,128)(2,1)S(1)}, u32[]{:S(2)}, u32[]{:S(2)}) collective-permute-start(bf16[128,256]{1,0:T(8,128)(2,1)S(1)} %get-tuple-element.64), channel_id=1, source_target_pairs={{0,16},{8,24},{16,0},{24,8},{1,17},{9,25},{17,1},{25,9},{2,18},{10... | collective-permute-start | bytes 196616 | tf_op jit(solution)/shard_map/ppermute | solution.py:303
  25.2 5.1 %collective-permute-start.10 = (bf16[144,256]{1,0:T(8,128)(2,1)S(1)}, bf16[144,256]{1,0:T(8,128)(2,1)S(1)}, u32[]{:S(2)}, u32[]{:S(2)}) collective-permute-start(bf16[144,256]{1,0:T(8,128)(2,1)S(1)} %get-tuple-element.63), channel_id=1, source_target_pairs={{0,8},{8,0},{16,24},{24,16},{1,9},{9,1},{17,25},{25,17},{2,10},{10... | collective-permute-start | bytes 221192 | tf_op jit(solution)/shard_map/ppermute | solution.py:303
  27.0 3.5 %collective-permute-start.14 = (bf16[256,256]{1,0:T(8,128)(2,1)S(1)}, bf16[256,256]{1,0:T(8,128)(2,1)S(1)}, u32[]{:S(2)}, u32[]{:S(2)}) collective-permute-start(bf16[256,256]{1,0:T(8,128)(2,1)S(1)} %early.1), channel_id=1, source_target_pairs={{0,1},{1,0},{2,3},{3,2},{4,5},{5,4},{6,7},{7,6},{8,9},{9,8},{10,11... | collective-permute-start | bytes 393224 | tf_op jit(solution)/shard_map/ppermute | solution.py:303
  29.3 1.4 %collective-permute-start.15 = (bf16[256,256]{1,0:T(8,128)(2,1)S(1)}, bf16[256,256]{1,0:T(8,128)(2,1)S(1)}, u32[]{:S(2)}, u32[]{:S(2)}) collective-permute-start(bf16[256,256]{1,0:T(8,128)(2,1)S(1)} %turn.1), channel_id=1, source_target_pairs={{0,1},{1,0},{2,3},{3,2},{4,5},{5,4},{6,7},{7,6},{8,9},{9,8},{10,11... | collective-permute-start | bytes 393224 | tf_op jit(solution)/shard_map/ppermute | solution.py:303

commit v14 on v13

--- a/solution.py
+++ b/solution.py
@@ -208,31 +208,27 @@
     pairs, rest = rest[: sub_count // 2 - 1], rest[sub_count // 2 - 1 :]
     along, (sibling, kept, spread, grad_pre, halo) = rest[:-5], rest[-5:]
     size = dense.shape[0] // own
-    blocks = halo_blocks(choice, size, halos, refs, halo)
-    for at in range(0, own * size, size):
-        part = slice(at, at + size)
-        columns = [dense[part, (own + slot) * size : (own + slot + 1) * size] for slot, *_ in halos]
-        inv = jnp.concatenate([inverse[part, :]] * (grad_out.shape[1] // size), axis=1)
-        aggregate = before[part, :] + dot(jnp.concatenate(columns, axis=1), blocks)
-        mean = (aggregate * inv).astype(BF)
-        pre = own_pre[part, :] + dot(mean, w_neigh[...])
-        grad = (grad_out[part, :].astype(F32) * gelu_slope(pre)).astype(BF)
-        grad_pre[part, :] = grad
-        spread[part, :] = (dot_right_transposed(grad, w_neigh[...]) * inv).astype(BF)
-
-    def partial(slot, count=1):
-        rows = slice((own + slot) * size, (own + slot + count) * size)
-        return dot(dense_t[rows, :], spread[...]).astype(BF)
+    aggregate = before[...] + halo_sum(choice, dense, own, halos, refs, halo)
+    inv = jnp.concatenate([inverse[...]] * (grad_out.shape[1] // size), axis=1)
+    mean = (aggregate * inv).astype(BF)
+    pre = own_pre[...] + dot(mean, w_neigh[...])
+    grad = (grad_out[...].astype(F32) * gelu_slope(pre)).astype(BF)
+    grad_pre[...] = grad
+    spread[...] = (dot_right_transposed(grad, w_neigh[...]) * inv).astype(BF)
+    partial = dot(dense_t[own * size :, :], spread[...]).astype(BF)
+
+    def of(slot, count=1):
+        return partial[slot * size : (slot + count) * size, :]
 
     for i, target in enumerate(pairs):
-        target[...] = partial(2 * (i + 1), 2)
+        target[...] = of(2 * (i + 1), 2)
     for i, target in enumerate(along):
-        target[0:size, :] = partial(sub_count + 1 + i)
+        target[0:size, :] = of(sub_count + 1 + i)
     for i, value in enumerate(rows):
         along[0][size + i * EXTRA : size + (i + 1) * EXTRA, :] = value[...]
-    sibling[...] = partial(1)
-    kept[0] = partial(0)
-    kept[1] = partial(sub_count)
+    sibling[...] = of(1)
+    kept[0] = of(0)
+    kept[1] = of(sub_count)
 
 
 def split(total, value, second, size):

time: 31.7 us -> 31.6 us (level)
  no operation moved by 1% of the time
where the time goes in v14:
time: 31.6 us; the launch traced here: 31.4 us
  starting transfers between devices  18.5 us (59%)
  Pallas kernels  6.84 us (22%)
  waiting for transfers between devices  5.95 us (19%)
    ppermute x16, starting transfers between devices, swap(): return lax.ppermute(value, axis, [(i, i ^ d) for i in range(count)])  18.5 us
    ppermute x16, waiting for transfers between devices, swap(): return lax.ppermute(value, axis, [(i, i ^ d) for i in range(count)])  5.95 us
    pallas_call x1, Pallas kernels, shards(): pl.pallas_call(functools.partial(prepare_kernel, *counts), out_shape=[jax...  1.63 us
    pallas_call x1, Pallas kernels, shards(): pl.pallas_call(functools.partial(middle_kernel, *counts, late_halos, len(...  1.32 us
    pallas_call x3, Pallas kernels, sum_call(): pl.pallas_call(functools.partial(kernel, own, halos), out_shape=out_shape...  0.99 us
    pallas_call x7, Pallas kernels, call(): pl.pallas_call(kernel, out_shape=out_shape, in_specs=[VMEM] * len(operand...  0.92 us
    pallas_call x1, Pallas kernels, shards(): pl.pallas_call(edge_kernel, out_shape=[jax.ShapeDtypeStruct((BOUNDARY * s...  0.89 us
    pallas_call x1, Pallas kernels, shards(): pl.pallas_call(functools.partial(final_kernel, own, parts), out_shape=nar...  0.78 us
  transfers between devices with their start and end apart: 16, of which 12 were waited for; matrix products, arithmetic and copies ran while one was open for 0% of the time, Pallas kernels for 12%

profile of v14, /device:TPU:0, one launch (start us, length us, event | category | flops | bytes accessed | tf_op | source)
XLA Modules:
  0.0 31.4 jit_solution(11681064834704678601)
XLA Ops:
  0.0 0.9 %edge.1 = (bf16[272,256]{1,0:T(8,128)(2,1)S(1)}, bf16[16,256]{1,0:T(8,128)(2,1)S(1)}) custom-call(s32[1,8]{1,0:T(1,128)} %recv_sub_hbm.1, s32[1,4]{1,0:T(1,128)} %recv_cluster_hbm.1, bf16[384,256]{1,0:T(8,128)(2,1)} %features_hbm.1), custom_call_target="tpu_custom_call" | custom-call | flops 1024 | bytes 262144 | tf_op jit(solution)/shard_map/edge/pallas_call | solution.py:332
  0.9 4.1 %collective-permute-start.1 = (bf16[272,256]{1,0:T(8,128)(2,1)S(1)}, bf16[272,256]{1,0:T(8,128)(2,1)S(1)}, u32[]{:S(2)}, u32[]{:S(2)}) collective-permute-start(bf16[272,256]{1,0:T(8,128)(2,1)S(1)} %get-tuple-element.37.rest_0_), channel_id=1, source_target_pairs={{0,16},{8,24},{16,0},{24,8},{1,17},{9,25},{17,1},{25,9},{2,18},{10... | collective-permute-start | bytes 417800 | tf_op jit(solution)/shard_map/ppermute | solution.py:299
  5.0 1.6 %collective-permute-start = (bf16[272,256]{1,0:T(8,128)(2,1)S(1)}, bf16[272,256]{1,0:T(8,128)(2,1)S(1)}, u32[]{:S(2)}, u32[]{:S(2)}) collective-permute-start(bf16[272,256]{1,0:T(8,128)(2,1)S(1)} %get-tuple-element.37.rest_0_), channel_id=1, source_target_pairs={{0,8},{8,0},{16,24},{24,16},{1,9},{9,1},{17,25},{25,17},{2,10},{10... | collective-permute-start | bytes 417800 | tf_op jit(solution)/shard_map/ppermute | solution.py:299
  6.6 2.4 %collective-permute-start.4 = (bf16[272,256]{1,0:T(8,128)(2,1)S(1)}, bf16[272,256]{1,0:T(8,128)(2,1)S(1)}, u32[]{:S(2)}, u32[]{:S(2)}) collective-permute-start(bf16[272,256]{1,0:T(8,128)(2,1)S(1)} %get-tuple-element.37.rest_0_), channel_id=1, source_target_pairs={{0,6},{1,7},{2,4},{3,5},{4,2},{5,3},{6,0},{7,1},{8,14},{9,15},{10,... | collective-permute-start | bytes 417800 | tf_op jit(solution)/shard_map/ppermute | solution.py:299
  9.0 0.5 %collective-permute-start.3 = (bf16[272,256]{1,0:T(8,128)(2,1)S(1)}, bf16[272,256]{1,0:T(8,128)(2,1)S(1)}, u32[]{:S(2)}, u32[]{:S(2)}) collective-permute-start(bf16[272,256]{1,0:T(8,128)(2,1)S(1)} %get-tuple-element.37.rest_0_), channel_id=1, source_target_pairs={{0,4},{1,5},{2,6},{3,7},{4,0},{5,1},{6,2},{7,3},{8,12},{9,13},{10,... | collective-permute-start | bytes 417800 | tf_op jit(solution)/shard_map/ppermute | solution.py:299
  9.5 0.5 %collective-permute-start.2 = (bf16[272,256]{1,0:T(8,128)(2,1)S(1)}, bf16[272,256]{1,0:T(8,128)(2,1)S(1)}, u32[]{:S(2)}, u32[]{:S(2)}) collective-permute-start(bf16[272,256]{1,0:T(8,128)(2,1)S(1)} %get-tuple-element.37.rest_0_), channel_id=1, source_target_pairs={{0,2},{1,3},{2,0},{3,1},{4,6},{5,7},{6,4},{7,5},{8,10},{9,11},{10,... | collective-permute-start | bytes 417800 | tf_op jit(solution)/shard_map/ppermute | solution.py:299
  10.1 1.6 %prepare.1 = (bf16[384,1920]{1,0:T(8,128)(2,1)S(1)}, f32[12,256]{1,0:T(8,128)S(1)}, bf16[384,256]{1,0:T(8,128)(2,1)S(1)}, bf16[256,256]{1,0:T(8,128)(2,1)S(1)}, ...) custom-call(s32[24]{0:T(128)} %tile_dst_hbm.1, s32[24]{0:T(128)} %tile_src_hbm.1, ...), custom_call_target="tpu_custom_call" | custom-call | flops 100000000 | bytes 6291456 | tf_op jit(solution)/shard_map/prepare/pallas_call | solution.py:366
  11.7 0.1 collective-permute-done.1.message.far.rest_1_
  11.8 0.2 collective-permute-done.near.rest_0_
  12.0 0.1 relay.1
  12.1 1.5 %collective-permute-start.7 = (bf16[128,256]{1,0:T(8,128)(2,1)S(1)}, bf16[128,256]{1,0:T(8,128)(2,1)S(1)}, u32[]{:S(2)}, u32[]{:S(2)}) collective-permute-start(bf16[128,256]{1,0:T(8,128)(2,1)S(1)} %relay.1), channel_id=1, source_target_pairs={{0,8},{8,0},{16,24},{24,16},{1,9},{9,1},{17,25},{25,17},{2,10},{10... | collective-permute-start | bytes 196616 | tf_op jit(solution)/shard_map/ppermute | solution.py:299
  13.6 0.0 collective-permute-start.5
  13.6 0.5 %first.1 = (f32[384,256]{1,0:T(8,128)S(1)}, f32[384,256]{1,0:T(8,128)S(1)}, f32[384,128]{1,0:T(8,128)S(1)}) custom-call(f32[12,256]{1,0:T(8,128)S(1)} %get-tuple-element.57.choice.rest_6_, bf16[384,1920]{1,0:T(8,128)(2,1)S(1)} %get-tuple-element.50.dense, bf16[384,256]{1,0:T(8,128)(2,1)S(1)} %get-tuple-element.46.features, ...), custom_call_target="tpu_custom_call" | custom-call | flops 1000000000 | bytes 3145728 | tf_op jit(solution)/shard_map/first/pallas_call | solution.py:418
  14.1 0.7 %collective-permute-done.5.rest_4_ = bf16[16,256]{1,0:T(8,128)(2,1)S(1)} collective-permute-done((bf16[16,256]{1,0:T(8,128)(2,1)S(1)}, bf16[16,256]{1,0:T(8,128)(2,1)S(1)}, u32[]{:S(2)}, u32[]{:S(2)}) %collective-permute-start.5) | collective-permute-done | bytes 8224 | tf_op jit(solution)/shard_map/ppermute | solution.py:299
  14.8 0.0 collective-permute-done.4.rest_3_.rest_4_
  14.8 0.5 %collective-permute-done.3.rest_2_.rest_3_ = bf16[272,256]{1,0:T(8,128)(2,1)S(1)} collective-permute-done((bf16[272,256]{1,0:T(8,128)(2,1)S(1)}, bf16[272,256]{1,0:T(8,128)(2,1)S(1)}, u32[]{:S(2)}, u32[]{:S(2)}) %collective-permute-start.3) | collective-permute-done | bytes 139296 | tf_op jit(solution)/shard_map/ppermute | solution.py:299
  15.3 0.1 collective-permute-done.2.rest_1_.rest_2_
  15.4 0.2 trade.1
  15.5 0.1 collective-permute-start.6
  15.6 0.3 near.1.before
  15.9 0.4 %flip.1.dense_t.rest_8_ = bf16[1920,384]{1,0:T(8,128)(2,1)S(1)} custom-call(bf16[384,1920]{1,0:T(8,128)(2,1)S(1)} %get-tuple-element.50.dense), custom_call_target="tpu_custom_call" | custom-call | flops 10000000 | bytes 1048576 | tf_op jit(solution)/shard_map/flip/pallas_call | solution.py:396
  16.4 0.0 collective-permute-done.7.rest_0_
  16.4 0.2 late.1.before
  16.6 0.6 %collective-permute-done.6.rest_0_.rest_5_ = bf16[576,256]{1,0:T(8,128)(2,1)S(1)} collective-permute-done((bf16[576,256]{1,0:T(8,128)(2,1)S(1)}, bf16[576,256]{1,0:T(8,128)(2,1)S(1)}, u32[]{:S(2)}, u32[]{:S(2)}) %collective-permute-start.6) | collective-permute-done | bytes 294944 | tf_op jit(solution)/shard_map/ppermute | solution.py:299
  17.2 1.3 %middle.1 = (bf16[256,256]{1,0:T(8,128)(2,1)S(1)}, bf16[256,256]{1,0:T(8,128)(2,1)S(1)}, bf16[256,256]{1,0:T(8,128)(2,1)S(1)}, bf16[144,256]{1,0:T(8,128)(2,1)S(...) custom-call(f32[12,256]{1,0:T(8,128)S(1)} %get-tuple-element.57.choi, ...), custom_call_target="tpu_custom_call" | custom-call | flops 377487360 | bytes 6291456 | tf_op jit(solution)/shard_map/middle/pallas_call | solution.py:473
  18.5 2.0 %collective-permute-start.9 = (bf16[256,256]{1,0:T(8,128)(2,1)S(1)}, bf16[256,256]{1,0:T(8,128)(2,1)S(1)}, u32[]{:S(2)}, u32[]{:S(2)}) collective-permute-start(bf16[256,256]{1,0:T(8,128)(2,1)S(1)} %get-tuple-element.56), channel_id=1, source_target_pairs={{0,6},{1,7},{2,4},{3,5},{4,2},{5,3},{6,0},{7,1},{8,14},{9,15},{10,... | collective-permute-start | bytes 393224 | tf_op jit(solution)/shard_map/ppermute | solution.py:299
  20.5 3.2 %collective-permute-start.8 = (bf16[128,256]{1,0:T(8,128)(2,1)S(1)}, bf16[128,256]{1,0:T(8,128)(2,1)S(1)}, u32[]{:S(2)}, u32[]{:S(2)}) collective-permute-start(bf16[128,256]{1,0:T(8,128)(2,1)S(1)} %get-tuple-element.54), channel_id=1, source_target_pairs={{0,24},{8,16},{16,8},{24,0},{1,25},{9,17},{17,9},{25,1},{2,26},{10... | collective-permute-start | bytes 196616 | tf_op jit(solution)/shard_map/ppermute | solution.py:299
  23.7 0.5 %collective-permute-start.12 = (bf16[256,256]{1,0:T(8,128)(2,1)S(1)}, bf16[256,256]{1,0:T(8,128)(2,1)S(1)}, u32[]{:S(2)}, u32[]{:S(2)}) collective-permute-start(bf16[256,256]{1,0:T(8,128)(2,1)S(1)} %get-tuple-element.65), channel_id=1, source_target_pairs={{0,4},{1,5},{2,6},{3,7},{4,0},{5,1},{6,2},{7,3},{8,12},{9,13},{10,... | collective-permute-start | bytes 393224 | tf_op jit(solution)/shard_map/ppermute | solution.py:299
  24.2 0.5 %collective-permute-start.13 = (bf16[256,256]{1,0:T(8,128)(2,1)S(1)}, bf16[256,256]{1,0:T(8,128)(2,1)S(1)}, u32[]{:S(2)}, u32[]{:S(2)}) collective-permute-start(bf16[256,256]{1,0:T(8,128)(2,1)S(1)} %get-tuple-element.66), channel_id=1, source_target_pairs={{0,2},{1,3},{2,0},{3,1},{4,6},{5,7},{6,4},{7,5},{8,10},{9,11},{10,... | collective-permute-start | bytes 393224 | tf_op jit(solution)/shard_map/ppermute | solution.py:299
  24.7 0.0 collective-permute-start.11
  24.7 0.3 %collective-permute-done.9.rest_1_.rest_3_ = bf16[256,256]{1,0:T(8,128)(2,1)S(1)} collective-permute-done((bf16[256,256]{1,0:T(8,128)(2,1)S(1)}, bf16[256,256]{1,0:T(8,128)(2,1)S(1)}, u32[]{:S(2)}, u32[]{:S(2)}) %collective-permute-start.9) | collective-permute-done | bytes 131104 | tf_op jit(solution)/shard_map/ppermute | solution.py:299
  25.0 1.4 %collective-permute-start.10 = (bf16[144,256]{1,0:T(8,128)(2,1)S(1)}, bf16[144,256]{1,0:T(8,128)(2,1)S(1)}, u32[]{:S(2)}, u32[]{:S(2)}) collective-permute-start(bf16[144,256]{1,0:T(8,128)(2,1)S(1)} %get-tuple-element.63), channel_id=1, source_target_pairs={{0,8},{8,0},{16,24},{24,16},{1,9},{9,1},{17,25},{25,17},{2,10},{10... | collective-permute-start | bytes 221192 | tf_op jit(solution)/shard_map/ppermute | solution.py:299
  26.5 0.4 %collective-permute-done.8.rest_2_ = bf16[128,256]{1,0:T(8,128)(2,1)S(1)} collective-permute-done((bf16[128,256]{1,0:T(8,128)(2,1)S(1)}, bf16[128,256]{1,0:T(8,128)(2,1)S(1)}, u32[]{:S(2)}, u32[]{:S(2)}) %collective-permute-start.8) | collective-permute-done | bytes 65568 | tf_op jit(solution)/shard_map/ppermute | solution.py:299
  26.9 0.0 collective-permute-start.14
  26.9 0.3 %own.1 = (f32[384,256]{1,0:T(8,128)S(1)}, f32[12,256]{1,0:T(8,128)S(1)}) custom-call(bf16[272,256]{1,0:T(8,128)(2,1)S(1)} %collective-permute-done.near.rest_0_, bf16[272,256]{1,0:T(8,128)(2,1)S(1)} %collective-permute-done.1.message.far.rest_1_, bf16[272,256]{1,0:T(8,128)(2,1)S(1)} %collective-permute-done.2.rest_1_.rest_2_, ...), custom_call_target="tpu_custom_call" | custom-call | flops 1000000000 | bytes 2097152 | tf_op jit(solution)/shard_map/own/pallas_call | solution.py:500
  27.2 1.5 %collective-permute-done.12.rest_4_.rest_1_ = bf16[256,256]{1,0:T(8,128)(2,1)S(1)} collective-permute-done((bf16[256,256]{1,0:T(8,128)(2,1)S(1)}, bf16[256,256]{1,0:T(8,128)(2,1)S(1)}, u32[]{:S(2)}, u32[]{:S(2)}) %collective-permute-start.12) | collective-permute-done | bytes 131104 | tf_op jit(solution)/shard_map/ppermute | solution.py:299
  28.7 0.5 %collective-permute-done.13.rest_5_.rest_0_ = bf16[256,256]{1,0:T(8,128)(2,1)S(1)} collective-permute-done((bf16[256,256]{1,0:T(8,128)(2,1)S(1)}, bf16[256,256]{1,0:T(8,128)(2,1)S(1)}, u32[]{:S(2)}, u32[]{:S(2)}) %collective-permute-start.13) | collective-permute-done | bytes 131104 | tf_op jit(solution)/shard_map/ppermute | solution.py:299
  29.2 0.1 collective-permute-start.15
  29.3 0.9 %collective-permute-done.11.rest_1_ = bf16[128,256]{1,0:T(8,128)(2,1)S(1)} collective-permute-done((bf16[128,256]{1,0:T(8,128)(2,1)S(1)}, bf16[128,256]{1,0:T(8,128)(2,1)S(1)}, u32[]{:S(2)}, u32[]{:S(2)}) %collective-permute-start.11) | collective-permute-done | bytes 65568 | tf_op jit(solution)/shard_map/ppermute | solution.py:299
  30.1 0.0 collective-permute-done.10.rest_0_
  30.1 0.2 add.1.total
  30.3 0.0 collective-permute-done.14.rest_0_
  30.4 0.2 collective-permute-done.15.rest_1_
  30.6 0.8 %final.1 = bf16[384,256]{1,0:T(8,128)(2,1)} custom-call(f32[12,256]{1,0:T(8,128)S(1)} %get-tuple-element.61.owner, f32[384,256]{1,0:T(8,128)S(1)} %add.1.total, bf16[256,256]{1,0:T(8,128)(2,1)S(1)} %collective-permute-done.14.rest_0_, bf16[256,256]{1,0:T(8,128)(2,1)S(1)} %collective-permute-done.15.rest_1_), custom_call_target="tpu_custom_call" | custom-call | flops 393216 | bytes 1048576 | tf_op jit(solution)/shard_map/final/pallas_call | solution.py:530
  (3 shorter events, 0.0 us)
Async XLA Ops:
  0.9 10.9 %collective-permute-start.1 = (bf16[272,256]{1,0:T(8,128)(2,1)S(1)}, bf16[272,256]{1,0:T(8,128)(2,1)S(1)}, u32[]{:S(2)}, u32[]{:S(2)}) collective-permute-start(bf16[272,256]{1,0:T(8,128)(2,1)S(1)} %get-tuple-element.37.rest_0_), channel_id=1, source_target_pairs={{0,16},{8,24},{16,0},{24,8},{1,17},{9,25},{17,1},{25,9},{2,18},{10... | collective-permute-start | bytes 417800 | tf_op jit(solution)/shard_map/ppermute | solution.py:299
  5.0 7.0 %collective-permute-start = (bf16[272,256]{1,0:T(8,128)(2,1)S(1)}, bf16[272,256]{1,0:T(8,128)(2,1)S(1)}, u32[]{:S(2)}, u32[]{:S(2)}) collective-permute-start(bf16[272,256]{1,0:T(8,128)(2,1)S(1)} %get-tuple-element.37.rest_0_), channel_id=1, source_target_pairs={{0,8},{8,0},{16,24},{24,16},{1,9},{9,1},{17,25},{25,17},{2,10},{10... | collective-permute-start | bytes 417800 | tf_op jit(solution)/shard_map/ppermute | solution.py:299
  6.6 8.2 %collective-permute-start.4 = (bf16[272,256]{1,0:T(8,128)(2,1)S(1)}, bf16[272,256]{1,0:T(8,128)(2,1)S(1)}, u32[]{:S(2)}, u32[]{:S(2)}) collective-permute-start(bf16[272,256]{1,0:T(8,128)(2,1)S(1)} %get-tuple-element.37.rest_0_), channel_id=1, source_target_pairs={{0,6},{1,7},{2,4},{3,5},{4,2},{5,3},{6,0},{7,1},{8,14},{9,15},{10,... | collective-permute-start | bytes 417800 | tf_op jit(solution)/shard_map/ppermute | solution.py:299
  9.0 6.3 %collective-permute-start.3 = (bf16[272,256]{1,0:T(8,128)(2,1)S(1)}, bf16[272,256]{1,0:T(8,128)(2,1)S(1)}, u32[]{:S(2)}, u32[]{:S(2)}) collective-permute-start(bf16[272,256]{1,0:T(8,128)(2,1)S(1)} %get-tuple-element.37.rest_0_), channel_id=1, source_target_pairs={{0,4},{1,5},{2,6},{3,7},{4,0},{5,1},{6,2},{7,3},{8,12},{9,13},{10,... | collective-permute-start | bytes 417800 | tf_op jit(solution)/shard_map/ppermute | solution.py:299
  9.5 5.8 %collective-permute-start.2 = (bf16[272,256]{1,0:T(8,128)(2,1)S(1)}, bf16[272,256]{1,0:T(8,128)(2,1)S(1)}, u32[]{:S(2)}, u32[]{:S(2)}) collective-permute-start(bf16[272,256]{1,0:T(8,128)(2,1)S(1)} %get-tuple-element.37.rest_0_), channel_id=1, source_target_pairs={{0,2},{1,3},{2,0},{3,1},{4,6},{5,7},{6,4},{7,5},{8,10},{9,11},{10,... | collective-permute-start | bytes 417800 | tf_op jit(solution)/shard_map/ppermute | solution.py:299
  12.1 4.3 %collective-permute-start.7 = (bf16[128,256]{1,0:T(8,128)(2,1)S(1)}, bf16[128,256]{1,0:T(8,128)(2,1)S(1)}, u32[]{:S(2)}, u32[]{:S(2)}) collective-permute-start(bf16[128,256]{1,0:T(8,128)(2,1)S(1)} %relay.1), channel_id=1, source_target_pairs={{0,8},{8,0},{16,24},{24,16},{1,9},{9,1},{17,25},{25,17},{2,10},{10... | collective-permute-start | bytes 196616 | tf_op jit(solution)/shard_map/ppermute | solution.py:299
  13.6 1.2 %collective-permute-start.5 = (bf16[16,256]{1,0:T(8,128)(2,1)S(1)}, bf16[16,256]{1,0:T(8,128)(2,1)S(1)}, u32[]{:S(2)}, u32[]{:S(2)}) collective-permute-start(bf16[16,256]{1,0:T(8,128)(2,1)S(1)} %get-tuple-element.39), channel_id=1, source_target_pairs={{0,1},{1,0},{2,3},{3,2},{4,5},{5,4},{6,7},{7,6},{8,9},{9,8},{10,11... | collective-permute-start | bytes 24584 | tf_op jit(solution)/shard_map/ppermute | solution.py:299
  15.5 1.6 %collective-permute-start.6 = (bf16[576,256]{1,0:T(8,128)(2,1)S(1)}, bf16[576,256]{1,0:T(8,128)(2,1)S(1)}, u32[]{:S(2)}, u32[]{:S(2)}) collective-permute-start(bf16[576,256]{1,0:T(8,128)(2,1)S(1)} %trade.1), channel_id=1, source_target_pairs={{0,1},{1,0},{2,3},{3,2},{4,5},{5,4},{6,7},{7,6},{8,9},{9,8},{10,11... | collective-permute-start | bytes 884744 | tf_op jit(solution)/shard_map/ppermute | solution.py:299
  18.5 6.5 %collective-permute-start.9 = (bf16[256,256]{1,0:T(8,128)(2,1)S(1)}, bf16[256,256]{1,0:T(8,128)(2,1)S(1)}, u32[]{:S(2)}, u32[]{:S(2)}) collective-permute-start(bf16[256,256]{1,0:T(8,128)(2,1)S(1)} %get-tuple-element.56), channel_id=1, source_target_pairs={{0,6},{1,7},{2,4},{3,5},{4,2},{5,3},{6,0},{7,1},{8,14},{9,15},{10,... | collective-permute-start | bytes 393224 | tf_op jit(solution)/shard_map/ppermute | solution.py:299
  20.5 6.4 %collective-permute-start.8 = (bf16[128,256]{1,0:T(8,128)(2,1)S(1)}, bf16[128,256]{1,0:T(8,128)(2,1)S(1)}, u32[]{:S(2)}, u32[]{:S(2)}) collective-permute-start(bf16[128,256]{1,0:T(8,128)(2,1)S(1)} %get-tuple-element.54), channel_id=1, source_target_pairs={{0,24},{8,16},{16,8},{24,0},{1,25},{9,17},{17,9},{25,1},{2,26},{10... | collective-permute-start | bytes 196616 | tf_op jit(solution)/shard_map/ppermute | solution.py:299
  23.7 5.0 %collective-permute-start.12 = (bf16[256,256]{1,0:T(8,128)(2,1)S(1)}, bf16[256,256]{1,0:T(8,128)(2,1)S(1)}, u32[]{:S(2)}, u32[]{:S(2)}) collective-permute-start(bf16[256,256]{1,0:T(8,128)(2,1)S(1)} %get-tuple-element.65), channel_id=1, source_target_pairs={{0,4},{1,5},{2,6},{3,7},{4,0},{5,1},{6,2},{7,3},{8,12},{9,13},{10,... | collective-permute-start | bytes 393224 | tf_op jit(solution)/shard_map/ppermute | solution.py:299
  24.2 5.0 %collective-permute-start.13 = (bf16[256,256]{1,0:T(8,128)(2,1)S(1)}, bf16[256,256]{1,0:T(8,128)(2,1)S(1)}, u32[]{:S(2)}, u32[]{:S(2)}) collective-permute-start(bf16[256,256]{1,0:T(8,128)(2,1)S(1)} %get-tuple-element.66), channel_id=1, source_target_pairs={{0,2},{1,3},{2,0},{3,1},{4,6},{5,7},{6,4},{7,5},{8,10},{9,11},{10,... | collective-permute-start | bytes 393224 | tf_op jit(solution)/shard_map/ppermute | solution.py:299
  24.7 5.4 %collective-permute-start.11 = (bf16[128,256]{1,0:T(8,128)(2,1)S(1)}, bf16[128,256]{1,0:T(8,128)(2,1)S(1)}, u32[]{:S(2)}, u32[]{:S(2)}) collective-permute-start(bf16[128,256]{1,0:T(8,128)(2,1)S(1)} %get-tuple-element.64), channel_id=1, source_target_pairs={{0,16},{8,24},{16,0},{24,8},{1,17},{9,25},{17,1},{25,9},{2,18},{10... | collective-permute-start | bytes 196616 | tf_op jit(solution)/shard_map/ppermute | solution.py:299
  25.0 5.1 %collective-permute-start.10 = (bf16[144,256]{1,0:T(8,128)(2,1)S(1)}, bf16[144,256]{1,0:T(8,128)(2,1)S(1)}, u32[]{:S(2)}, u32[]{:S(2)}) collective-permute-start(bf16[144,256]{1,0:T(8,128)(2,1)S(1)} %get-tuple-element.63), channel_id=1, source_target_pairs={{0,8},{8,0},{16,24},{24,16},{1,9},{9,1},{17,25},{25,17},{2,10},{10... | collective-permute-start | bytes 221192 | tf_op jit(solution)/shard_map/ppermute | solution.py:299
  26.9 3.5 %collective-permute-start.14 = (bf16[256,256]{1,0:T(8,128)(2,1)S(1)}, bf16[256,256]{1,0:T(8,128)(2,1)S(1)}, u32[]{:S(2)}, u32[]{:S(2)}) collective-permute-start(bf16[256,256]{1,0:T(8,128)(2,1)S(1)} %early.1), channel_id=1, source_target_pairs={{0,1},{1,0},{2,3},{3,2},{4,5},{5,4},{6,7},{7,6},{8,9},{9,8},{10,11... | collective-permute-start | bytes 393224 | tf_op jit(solution)/shard_map/ppermute | solution.py:299
  29.2 1.4 %collective-permute-start.15 = (bf16[256,256]{1,0:T(8,128)(2,1)S(1)}, bf16[256,256]{1,0:T(8,128)(2,1)S(1)}, u32[]{:S(2)}, u32[]{:S(2)}) collective-permute-start(bf16[256,256]{1,0:T(8,128)(2,1)S(1)} %turn.1), channel_id=1, source_target_pairs={{0,1},{1,0},{2,3},{3,2},{4,5},{5,4},{6,7},{7,6},{8,9},{9,8},{10,11... | collective-permute-start | bytes 393224 | tf_op jit(solution)/shard_map/ppermute | solution.py:299

commit v15 on v14

--- a/solution.py
+++ b/solution.py
@@ -215,20 +215,20 @@
     grad = (grad_out[...].astype(F32) * gelu_slope(pre)).astype(BF)
     grad_pre[...] = grad
     spread[...] = (dot_right_transposed(grad, w_neigh[...]) * inv).astype(BF)
-    partial = dot(dense_t[own * size :, :], spread[...]).astype(BF)
-
-    def of(slot, count=1):
-        return partial[slot * size : (slot + count) * size, :]
+
+    def partial(slot, count=1):
+        rows = slice((own + slot) * size, (own + slot + count) * size)
+        return dot(dense_t[rows, :], spread[...]).astype(BF)
 
     for i, target in enumerate(pairs):
-        target[...] = of(2 * (i + 1), 2)
+        target[...] = partial(2 * (i + 1), 2)
     for i, target in enumerate(along):
-        target[0:size, :] = of(sub_count + 1 + i)
+        target[0:size, :] = partial(sub_count + 1 + i)
     for i, value in enumerate(rows):
         along[0][size + i * EXTRA : size + (i + 1) * EXTRA, :] = value[...]
-    sibling[...] = of(1)
-    kept[0] = of(0)
-    kept[1] = of(sub_count)
+    sibling[...] = partial(1)
+    kept[0] = partial(0)
+    kept[1] = partial(sub_count)
 
 
 def split(total, value, second, size):
@@ -255,21 +255,16 @@
         owner[slot : slot + 1, :] = jnp.broadcast_to(index, (1, width))
 
 
-def add_kernel(own, sub_count, parts, rows, owner, before, *rest):
+def add_kernel(own, parts, owner, before, *rest):
     received, total = rest[:-1], rest[-1]
     size = total.shape[0] // own
     total[...] = before[...]
     for slot, at, row in parts:
         value = received[at][row : row + size, :].astype(F32)
-        index = owner[slot : slot + 1, :]
-        if slot in rows:
-            where, first = rows[slot]
-            indices = received[where][first : first + EXTRA, :].astype(F32)[0:1, :]
-            index = lane_of(indices, sub_count + lax.axis_index("cluster"))
-        split(total, value, index > 0.5, size)
-
-
-def final_kernel(own, parts, owner, total, *rest):
+        split(total, value, owner[slot : slot + 1, :] > 0.5, size)
+
+
+def final_kernel(own, sub_count, parts, rows, owner, total, *rest):
     received, (out, done, sems) = rest[:-3], rest[-3:]
     size = total.shape[0] // own
     copies = []
@@ -284,10 +279,17 @@
         copies[-1].start()
 
     leave(2 * size, own * size, total[2 * size :, :])
+    indices = []
+    for slot, at, row in parts:
+        index = owner[slot : slot + 1, :]
+        if slot in rows:
+            where, first = rows[slot]
+            row_of = received[where][first : first + EXTRA, :].astype(F32)[0:1, :]
+            index = lane_of(row_of, sub_count + lax.axis_index("cluster"))
+        indices.append(index)
     for block in range(2):
         value = total[block * size : (block + 1) * size, :]
-        for slot, at, row in parts:
-            index = owner[slot : slot + 1, :]
+        for index, (slot, at, row) in zip(indices, parts):
             mine = index > 0.5 if block else index <= 0.5
             value = value + jnp.where(mine, received[at][row : row + size, :].astype(F32), 0.0)
         leave(block * size, (block + 1) * size, value)
@@ -516,27 +518,30 @@
         *[after(value, total) for _, value in rest],
     )
     turned = across(turned, 1)
-    more = [*far, *near[::-1]]
+    more = [*[pair for pair in far if pair[0] - sub_count in direct], *near[::-1]]
     parts = [(slot, i, 0) for i, (slot, _) in enumerate(more)]
-    places = {slot: (0, size + i * EXTRA) for i, slot in enumerate(sub_count + d for d in relayed)}
     total = call(
-        functools.partial(
-            add_kernel, own, sub_count, parts, places
-        ),
-        wide, "add", 10**10, owner, total, *[value for _, value in more],
-    )
-    parts = [(1, 0, 0), *[(d + 1, 0, size) for d, _ in soon]]
-    parts += [(d + 1, 1, i * size) for i, (d, _) in enumerate(rest)]
+        functools.partial(add_kernel, own, parts), wide, "add", 10**10,
+        owner, total, *[value for _, value in more],
+    )
+    last = [pair for pair in far if pair[0] - sub_count not in direct]
+    parts = [(slot, i, 0) for i, (slot, _) in enumerate(last)]
+    parts += [(1, len(last), 0), *[(d + 1, len(last), size) for d, _ in soon]]
+    parts += [(d + 1, len(last) + 1, i * size) for i, (d, _) in enumerate(rest)]
+    beside = [i for i, (slot, _) in enumerate(last) if slot == sub_count + 1]
+    places = {
+        sub_count + d: (beside[0], size + i * EXTRA) for i, d in enumerate(relayed)
+    }
     return pl.pallas_call(
-        functools.partial(final_kernel, own, parts),
+        functools.partial(final_kernel, own, sub_count, parts, places),
         out_shape=narrow,
-        in_specs=[VMEM] * 4,
+        in_specs=[VMEM] * (4 + len(last)),
         out_specs=HBM,
         scratch_shapes=[pltpu.VMEM((rows, width), BF), pltpu.SemaphoreType.DMA((3,))],
         compiler_params=PARAMS,
         cost_estimate=cost(rows * width * 4, 1024 * 1024),
         name="final",
-    )(owner, total, early, turned)
+    )(owner, total, *[value for _, value in last], early, turned)
 
 
 def solution(mesh):

time: 31.6 us -> 31.6 us (level)
  no operation moved by 1% of the time
where the time goes in v15:
time: 31.6 us; the launch traced here: 31.4 us
  starting transfers between devices  18.5 us (59%)
  Pallas kernels  6.78 us (21%)
  waiting for transfers between devices  6.04 us (19%)
    ppermute x16, starting transfers between devices, swap(): return lax.ppermute(value, axis, [(i, i ^ d) for i in range(count)])  18.5 us
    ppermute x16, waiting for transfers between devices, swap(): return lax.ppermute(value, axis, [(i, i ^ d) for i in range(count)])  6.04 us
    pallas_call x1, Pallas kernels, shards(): pl.pallas_call(functools.partial(prepare_kernel, *counts), out_shape=[jax...  1.63 us
    pallas_call x1, Pallas kernels, shards(): pl.pallas_call(functools.partial(middle_kernel, *counts, late_halos, len(...  1.25 us
    pallas_call x3, Pallas kernels, sum_call(): pl.pallas_call(functools.partial(kernel, own, halos), out_shape=out_shape...  0.99 us
    pallas_call x1, Pallas kernels, shards(): pl.pallas_call(edge_kernel, out_shape=[jax.ShapeDtypeStruct((BOUNDARY * s...  0.89 us
    pallas_call x1, Pallas kernels, shards(): pl.pallas_call(functools.partial(final_kernel, own, sub_count, parts, pla...  0.87 us
    pallas_call x7, Pallas kernels, call(): pl.pallas_call(kernel, out_shape=out_shape, in_specs=[VMEM] * len(operand...  0.84 us
  transfers between devices with their start and end apart: 16, of which 12 were waited for; matrix products, arithmetic and copies ran while one was open for 0% of the time, Pallas kernels for 12%

profile of v15, /device:TPU:0, one launch (start us, length us, event | category | flops | bytes accessed | tf_op | source)
XLA Modules:
  0.0 31.4 jit_solution(18149571391648044029)
XLA Ops:
  0.0 0.9 %edge.1 = (bf16[272,256]{1,0:T(8,128)(2,1)S(1)}, bf16[16,256]{1,0:T(8,128)(2,1)S(1)}) custom-call(s32[1,8]{1,0:T(1,128)} %recv_sub_hbm.1, s32[1,4]{1,0:T(1,128)} %recv_cluster_hbm.1, bf16[384,256]{1,0:T(8,128)(2,1)} %features_hbm.1), custom_call_target="tpu_custom_call" | custom-call | flops 1024 | bytes 262144 | tf_op jit(solution)/shard_map/edge/pallas_call | solution.py:334
  0.9 4.1 %collective-permute-start.1 = (bf16[272,256]{1,0:T(8,128)(2,1)S(1)}, bf16[272,256]{1,0:T(8,128)(2,1)S(1)}, u32[]{:S(2)}, u32[]{:S(2)}) collective-permute-start(bf16[272,256]{1,0:T(8,128)(2,1)S(1)} %get-tuple-element.37.rest_0_), channel_id=1, source_target_pairs={{0,16},{8,24},{16,0},{24,8},{1,17},{9,25},{17,1},{25,9},{2,18},{10... | collective-permute-start | bytes 417800 | tf_op jit(solution)/shard_map/ppermute | solution.py:301
  5.0 1.6 %collective-permute-start = (bf16[272,256]{1,0:T(8,128)(2,1)S(1)}, bf16[272,256]{1,0:T(8,128)(2,1)S(1)}, u32[]{:S(2)}, u32[]{:S(2)}) collective-permute-start(bf16[272,256]{1,0:T(8,128)(2,1)S(1)} %get-tuple-element.37.rest_0_), channel_id=1, source_target_pairs={{0,8},{8,0},{16,24},{24,16},{1,9},{9,1},{17,25},{25,17},{2,10},{10... | collective-permute-start | bytes 417800 | tf_op jit(solution)/shard_map/ppermute | solution.py:301
  6.6 2.4 %collective-permute-start.4 = (bf16[272,256]{1,0:T(8,128)(2,1)S(1)}, bf16[272,256]{1,0:T(8,128)(2,1)S(1)}, u32[]{:S(2)}, u32[]{:S(2)}) collective-permute-start(bf16[272,256]{1,0:T(8,128)(2,1)S(1)} %get-tuple-element.37.rest_0_), channel_id=1, source_target_pairs={{0,6},{1,7},{2,4},{3,5},{4,2},{5,3},{6,0},{7,1},{8,14},{9,15},{10,... | collective-permute-start | bytes 417800 | tf_op jit(solution)/shard_map/ppermute | solution.py:301
  9.0 0.5 %collective-permute-start.3 = (bf16[272,256]{1,0:T(8,128)(2,1)S(1)}, bf16[272,256]{1,0:T(8,128)(2,1)S(1)}, u32[]{:S(2)}, u32[]{:S(2)}) collective-permute-start(bf16[272,256]{1,0:T(8,128)(2,1)S(1)} %get-tuple-element.37.rest_0_), channel_id=1, source_target_pairs={{0,4},{1,5},{2,6},{3,7},{4,0},{5,1},{6,2},{7,3},{8,12},{9,13},{10,... | collective-permute-start | bytes 417800 | tf_op jit(solution)/shard_map/ppermute | solution.py:301
  9.5 0.5 %collective-permute-start.2 = (bf16[272,256]{1,0:T(8,128)(2,1)S(1)}, bf16[272,256]{1,0:T(8,128)(2,1)S(1)}, u32[]{:S(2)}, u32[]{:S(2)}) collective-permute-start(bf16[272,256]{1,0:T(8,128)(2,1)S(1)} %get-tuple-element.37.rest_0_), channel_id=1, source_target_pairs={{0,2},{1,3},{2,0},{3,1},{4,6},{5,7},{6,4},{7,5},{8,10},{9,11},{10,... | collective-permute-start | bytes 417800 | tf_op jit(solution)/shard_map/ppermute | solution.py:301
  10.1 1.6 %prepare.1 = (bf16[384,1920]{1,0:T(8,128)(2,1)S(1)}, f32[12,256]{1,0:T(8,128)S(1)}, bf16[384,256]{1,0:T(8,128)(2,1)S(1)}, bf16[256,256]{1,0:T(8,128)(2,1)S(1)}, ...) custom-call(s32[24]{0:T(128)} %tile_dst_hbm.1, s32[24]{0:T(128)} %tile_src_hbm.1, ...), custom_call_target="tpu_custom_call" | custom-call | flops 100000000 | bytes 6291456 | tf_op jit(solution)/shard_map/prepare/pallas_call | solution.py:368
  11.7 0.1 collective-permute-done.1.message.far.rest_1_
  11.8 0.2 collective-permute-done.near.rest_0_
  12.0 0.1 relay.1
  12.1 1.5 %collective-permute-start.7 = (bf16[128,256]{1,0:T(8,128)(2,1)S(1)}, bf16[128,256]{1,0:T(8,128)(2,1)S(1)}, u32[]{:S(2)}, u32[]{:S(2)}) collective-permute-start(bf16[128,256]{1,0:T(8,128)(2,1)S(1)} %relay.1), channel_id=1, source_target_pairs={{0,8},{8,0},{16,24},{24,16},{1,9},{9,1},{17,25},{25,17},{2,10},{10... | collective-permute-start | bytes 196616 | tf_op jit(solution)/shard_map/ppermute | solution.py:301
  13.6 0.0 collective-permute-start.5
  13.6 0.5 %first.1 = (f32[384,256]{1,0:T(8,128)S(1)}, f32[384,256]{1,0:T(8,128)S(1)}, f32[384,128]{1,0:T(8,128)S(1)}) custom-call(f32[12,256]{1,0:T(8,128)S(1)} %get-tuple-element.57.choice.rest_6_, bf16[384,1920]{1,0:T(8,128)(2,1)S(1)} %get-tuple-element.50.dense, bf16[384,256]{1,0:T(8,128)(2,1)S(1)} %get-tuple-element.46.features, ...), custom_call_target="tpu_custom_call" | custom-call | flops 1000000000 | bytes 3145728 | tf_op jit(solution)/shard_map/first/pallas_call | solution.py:420
  14.1 0.7 %collective-permute-done.5.rest_4_ = bf16[16,256]{1,0:T(8,128)(2,1)S(1)} collective-permute-done((bf16[16,256]{1,0:T(8,128)(2,1)S(1)}, bf16[16,256]{1,0:T(8,128)(2,1)S(1)}, u32[]{:S(2)}, u32[]{:S(2)}) %collective-permute-start.5) | collective-permute-done | bytes 8224 | tf_op jit(solution)/shard_map/ppermute | solution.py:301
  14.8 0.0 collective-permute-done.4.rest_3_.rest_4_
  14.8 0.5 %collective-permute-done.3.rest_2_.rest_3_ = bf16[272,256]{1,0:T(8,128)(2,1)S(1)} collective-permute-done((bf16[272,256]{1,0:T(8,128)(2,1)S(1)}, bf16[272,256]{1,0:T(8,128)(2,1)S(1)}, u32[]{:S(2)}, u32[]{:S(2)}) %collective-permute-start.3) | collective-permute-done | bytes 139296 | tf_op jit(solution)/shard_map/ppermute | solution.py:301
  15.3 0.1 collective-permute-done.2.rest_1_.rest_2_
  15.4 0.2 trade.1
  15.5 0.1 collective-permute-start.6
  15.6 0.3 near.1.before
  15.9 0.4 %flip.1.dense_t.rest_8_ = bf16[1920,384]{1,0:T(8,128)(2,1)S(1)} custom-call(bf16[384,1920]{1,0:T(8,128)(2,1)S(1)} %get-tuple-element.50.dense), custom_call_target="tpu_custom_call" | custom-call | flops 10000000 | bytes 1048576 | tf_op jit(solution)/shard_map/flip/pallas_call | solution.py:398
  16.4 0.0 collective-permute-done.7.rest_0_
  16.4 0.2 late.1.before
  16.6 0.6 %collective-permute-done.6.rest_0_.rest_5_ = bf16[576,256]{1,0:T(8,128)(2,1)S(1)} collective-permute-done((bf16[576,256]{1,0:T(8,128)(2,1)S(1)}, bf16[576,256]{1,0:T(8,128)(2,1)S(1)}, u32[]{:S(2)}, u32[]{:S(2)}) %collective-permute-start.6) | collective-permute-done | bytes 294944 | tf_op jit(solution)/shard_map/ppermute | solution.py:301
  17.2 1.2 %middle.1 = (bf16[256,256]{1,0:T(8,128)(2,1)S(1)}, bf16[256,256]{1,0:T(8,128)(2,1)S(1)}, bf16[256,256]{1,0:T(8,128)(2,1)S(1)}, bf16[144,256]{1,0:T(8,128)(2,1)S(...) custom-call(f32[12,256]{1,0:T(8,128)S(1)} %get-tuple-element.57.choi, ...), custom_call_target="tpu_custom_call" | custom-call | flops 377487360 | bytes 6291456 | tf_op jit(solution)/shard_map/middle/pallas_call | solution.py:475
  18.4 2.0 %collective-permute-start.9 = (bf16[256,256]{1,0:T(8,128)(2,1)S(1)}, bf16[256,256]{1,0:T(8,128)(2,1)S(1)}, u32[]{:S(2)}, u32[]{:S(2)}) collective-permute-start(bf16[256,256]{1,0:T(8,128)(2,1)S(1)} %get-tuple-element.56), channel_id=1, source_target_pairs={{0,6},{1,7},{2,4},{3,5},{4,2},{5,3},{6,0},{7,1},{8,14},{9,15},{10,... | collective-permute-start | bytes 393224 | tf_op jit(solution)/shard_map/ppermute | solution.py:301
  20.4 3.2 %collective-permute-start.8 = (bf16[128,256]{1,0:T(8,128)(2,1)S(1)}, bf16[128,256]{1,0:T(8,128)(2,1)S(1)}, u32[]{:S(2)}, u32[]{:S(2)}) collective-permute-start(bf16[128,256]{1,0:T(8,128)(2,1)S(1)} %get-tuple-element.54), channel_id=1, source_target_pairs={{0,24},{8,16},{16,8},{24,0},{1,25},{9,17},{17,9},{25,1},{2,26},{10... | collective-permute-start | bytes 196616 | tf_op jit(solution)/shard_map/ppermute | solution.py:301
  23.6 0.5 %collective-permute-start.11 = (bf16[256,256]{1,0:T(8,128)(2,1)S(1)}, bf16[256,256]{1,0:T(8,128)(2,1)S(1)}, u32[]{:S(2)}, u32[]{:S(2)}) collective-permute-start(bf16[256,256]{1,0:T(8,128)(2,1)S(1)} %get-tuple-element.64), channel_id=1, source_target_pairs={{0,4},{1,5},{2,6},{3,7},{4,0},{5,1},{6,2},{7,3},{8,12},{9,13},{10,... | collective-permute-start | bytes 393224 | tf_op jit(solution)/shard_map/ppermute | solution.py:301
  24.1 0.5 %collective-permute-start.12 = (bf16[256,256]{1,0:T(8,128)(2,1)S(1)}, bf16[256,256]{1,0:T(8,128)(2,1)S(1)}, u32[]{:S(2)}, u32[]{:S(2)}) collective-permute-start(bf16[256,256]{1,0:T(8,128)(2,1)S(1)} %get-tuple-element.65), channel_id=1, source_target_pairs={{0,2},{1,3},{2,0},{3,1},{4,6},{5,7},{6,4},{7,5},{8,10},{9,11},{10,... | collective-permute-start | bytes 393224 | tf_op jit(solution)/shard_map/ppermute | solution.py:301
  24.7 0.0 collective-permute-start.10
  24.7 0.3 %collective-permute-done.9.rest_1_ = bf16[256,256]{1,0:T(8,128)(2,1)S(1)} collective-permute-done((bf16[256,256]{1,0:T(8,128)(2,1)S(1)}, bf16[256,256]{1,0:T(8,128)(2,1)S(1)}, u32[]{:S(2)}, u32[]{:S(2)}) %collective-permute-start.9) | collective-permute-done | bytes 131104 | tf_op jit(solution)/shard_map/ppermute | solution.py:301
  25.0 1.4 %collective-permute-start.13 = (bf16[144,256]{1,0:T(8,128)(2,1)S(1)}, bf16[144,256]{1,0:T(8,128)(2,1)S(1)}, u32[]{:S(2)}, u32[]{:S(2)}) collective-permute-start(bf16[144,256]{1,0:T(8,128)(2,1)S(1)} %get-tuple-element.66), channel_id=1, source_target_pairs={{0,8},{8,0},{16,24},{24,16},{1,9},{9,1},{17,25},{25,17},{2,10},{10... | collective-permute-start | bytes 221192 | tf_op jit(solution)/shard_map/ppermute | solution.py:301
  26.4 0.4 %collective-permute-done.8.rest_1_ = bf16[128,256]{1,0:T(8,128)(2,1)S(1)} collective-permute-done((bf16[128,256]{1,0:T(8,128)(2,1)S(1)}, bf16[128,256]{1,0:T(8,128)(2,1)S(1)}, u32[]{:S(2)}, u32[]{:S(2)}) %collective-permute-start.8) | collective-permute-done | bytes 65568 | tf_op jit(solution)/shard_map/ppermute | solution.py:301
  26.8 0.0 collective-permute-start.14
  26.8 0.3 %own.1 = (f32[384,256]{1,0:T(8,128)S(1)}, f32[12,256]{1,0:T(8,128)S(1)}) custom-call(bf16[272,256]{1,0:T(8,128)(2,1)S(1)} %collective-permute-done.near.rest_0_, bf16[272,256]{1,0:T(8,128)(2,1)S(1)} %collective-permute-done.1.message.far.rest_1_, bf16[272,256]{1,0:T(8,128)(2,1)S(1)} %collective-permute-done.2.rest_1_.rest_2_, ...), custom_call_target="tpu_custom_call" | custom-call | flops 1000000000 | bytes 2097152 | tf_op jit(solution)/shard_map/own/pallas_call | solution.py:502
  27.1 1.5 %collective-permute-done.11.rest_2_.rest_1_ = bf16[256,256]{1,0:T(8,128)(2,1)S(1)} collective-permute-done((bf16[256,256]{1,0:T(8,128)(2,1)S(1)}, bf16[256,256]{1,0:T(8,128)(2,1)S(1)}, u32[]{:S(2)}, u32[]{:S(2)}) %collective-permute-start.11) | collective-permute-done | bytes 131104 | tf_op jit(solution)/shard_map/ppermute | solution.py:301
  28.6 0.5 %collective-permute-done.12.rest_3_.rest_0_ = bf16[256,256]{1,0:T(8,128)(2,1)S(1)} collective-permute-done((bf16[256,256]{1,0:T(8,128)(2,1)S(1)}, bf16[256,256]{1,0:T(8,128)(2,1)S(1)}, u32[]{:S(2)}, u32[]{:S(2)}) %collective-permute-start.12) | collective-permute-done | bytes 131104 | tf_op jit(solution)/shard_map/ppermute | solution.py:301
  29.1 0.1 collective-permute-start.15
  29.2 0.9 %collective-permute-done.10.rest_0_ = bf16[128,256]{1,0:T(8,128)(2,1)S(1)} collective-permute-done((bf16[128,256]{1,0:T(8,128)(2,1)S(1)}, bf16[128,256]{1,0:T(8,128)(2,1)S(1)}, u32[]{:S(2)}, u32[]{:S(2)}) %collective-permute-start.10) | collective-permute-done | bytes 65568 | tf_op jit(solution)/shard_map/ppermute | solution.py:301
  30.1 0.1 add.1.total
  30.2 0.0 collective-permute-done.13.rest_0_
  30.2 0.0 collective-permute-done.14.rest_2_
  30.2 0.3 collective-permute-done.15.rest_3_
  30.5 0.9 %final.1 = bf16[384,256]{1,0:T(8,128)(2,1)} custom-call(f32[12,256]{1,0:T(8,128)S(1)} %get-tuple-element.61.owner, f32[384,256]{1,0:T(8,128)S(1)} %add.1.total, bf16[144,256]{1,0:T(8,128)(2,1)S(1)} %collective-permute-done.13.rest_0_, bf16[128,256]{1,0:T(8,128)(2,1)S(1)} %collective-permute-done.8.rest_1_, ...), custom_call_target="tpu_custom_call" | custom-call | flops 393216 | bytes 1048576 | tf_op jit(solution)/shard_map/final/pallas_call | solution.py:535
  (3 shorter events, 0.0 us)
Async XLA Ops:
  0.9 10.9 %collective-permute-start.1 = (bf16[272,256]{1,0:T(8,128)(2,1)S(1)}, bf16[272,256]{1,0:T(8,128)(2,1)S(1)}, u32[]{:S(2)}, u32[]{:S(2)}) collective-permute-start(bf16[272,256]{1,0:T(8,128)(2,1)S(1)} %get-tuple-element.37.rest_0_), channel_id=1, source_target_pairs={{0,16},{8,24},{16,0},{24,8},{1,17},{9,25},{17,1},{25,9},{2,18},{10... | collective-permute-start | bytes 417800 | tf_op jit(solution)/shard_map/ppermute | solution.py:301
  5.0 7.0 %collective-permute-start = (bf16[272,256]{1,0:T(8,128)(2,1)S(1)}, bf16[272,256]{1,0:T(8,128)(2,1)S(1)}, u32[]{:S(2)}, u32[]{:S(2)}) collective-permute-start(bf16[272,256]{1,0:T(8,128)(2,1)S(1)} %get-tuple-element.37.rest_0_), channel_id=1, source_target_pairs={{0,8},{8,0},{16,24},{24,16},{1,9},{9,1},{17,25},{25,17},{2,10},{10... | collective-permute-start | bytes 417800 | tf_op jit(solution)/shard_map/ppermute | solution.py:301
  6.6 8.2 %collective-permute-start.4 = (bf16[272,256]{1,0:T(8,128)(2,1)S(1)}, bf16[272,256]{1,0:T(8,128)(2,1)S(1)}, u32[]{:S(2)}, u32[]{:S(2)}) collective-permute-start(bf16[272,256]{1,0:T(8,128)(2,1)S(1)} %get-tuple-element.37.rest_0_), channel_id=1, source_target_pairs={{0,6},{1,7},{2,4},{3,5},{4,2},{5,3},{6,0},{7,1},{8,14},{9,15},{10,... | collective-permute-start | bytes 417800 | tf_op jit(solution)/shard_map/ppermute | solution.py:301
  9.0 6.3 %collective-permute-start.3 = (bf16[272,256]{1,0:T(8,128)(2,1)S(1)}, bf16[272,256]{1,0:T(8,128)(2,1)S(1)}, u32[]{:S(2)}, u32[]{:S(2)}) collective-permute-start(bf16[272,256]{1,0:T(8,128)(2,1)S(1)} %get-tuple-element.37.rest_0_), channel_id=1, source_target_pairs={{0,4},{1,5},{2,6},{3,7},{4,0},{5,1},{6,2},{7,3},{8,12},{9,13},{10,... | collective-permute-start | bytes 417800 | tf_op jit(solution)/shard_map/ppermute | solution.py:301
  9.5 5.8 %collective-permute-start.2 = (bf16[272,256]{1,0:T(8,128)(2,1)S(1)}, bf16[272,256]{1,0:T(8,128)(2,1)S(1)}, u32[]{:S(2)}, u32[]{:S(2)}) collective-permute-start(bf16[272,256]{1,0:T(8,128)(2,1)S(1)} %get-tuple-element.37.rest_0_), channel_id=1, source_target_pairs={{0,2},{1,3},{2,0},{3,1},{4,6},{5,7},{6,4},{7,5},{8,10},{9,11},{10,... | collective-permute-start | bytes 417800 | tf_op jit(solution)/shard_map/ppermute | solution.py:301
  12.1 4.3 %collective-permute-start.7 = (bf16[128,256]{1,0:T(8,128)(2,1)S(1)}, bf16[128,256]{1,0:T(8,128)(2,1)S(1)}, u32[]{:S(2)}, u32[]{:S(2)}) collective-permute-start(bf16[128,256]{1,0:T(8,128)(2,1)S(1)} %relay.1), channel_id=1, source_target_pairs={{0,8},{8,0},{16,24},{24,16},{1,9},{9,1},{17,25},{25,17},{2,10},{10... | collective-permute-start | bytes 196616 | tf_op jit(solution)/shard_map/ppermute | solution.py:301
  13.6 1.2 %collective-permute-start.5 = (bf16[16,256]{1,0:T(8,128)(2,1)S(1)}, bf16[16,256]{1,0:T(8,128)(2,1)S(1)}, u32[]{:S(2)}, u32[]{:S(2)}) collective-permute-start(bf16[16,256]{1,0:T(8,128)(2,1)S(1)} %get-tuple-element.39), channel_id=1, source_target_pairs={{0,1},{1,0},{2,3},{3,2},{4,5},{5,4},{6,7},{7,6},{8,9},{9,8},{10,11... | collective-permute-start | bytes 24584 | tf_op jit(solution)/shard_map/ppermute | solution.py:301
  15.5 1.6 %collective-permute-start.6 = (bf16[576,256]{1,0:T(8,128)(2,1)S(1)}, bf16[576,256]{1,0:T(8,128)(2,1)S(1)}, u32[]{:S(2)}, u32[]{:S(2)}) collective-permute-start(bf16[576,256]{1,0:T(8,128)(2,1)S(1)} %trade.1), channel_id=1, source_target_pairs={{0,1},{1,0},{2,3},{3,2},{4,5},{5,4},{6,7},{7,6},{8,9},{9,8},{10,11... | collective-permute-start | bytes 884744 | tf_op jit(solution)/shard_map/ppermute | solution.py:301
  18.4 6.6 %collective-permute-start.9 = (bf16[256,256]{1,0:T(8,128)(2,1)S(1)}, bf16[256,256]{1,0:T(8,128)(2,1)S(1)}, u32[]{:S(2)}, u32[]{:S(2)}) collective-permute-start(bf16[256,256]{1,0:T(8,128)(2,1)S(1)} %get-tuple-element.56), channel_id=1, source_target_pairs={{0,6},{1,7},{2,4},{3,5},{4,2},{5,3},{6,0},{7,1},{8,14},{9,15},{10,... | collective-permute-start | bytes 393224 | tf_op jit(solution)/shard_map/ppermute | solution.py:301
  20.4 6.3 %collective-permute-start.8 = (bf16[128,256]{1,0:T(8,128)(2,1)S(1)}, bf16[128,256]{1,0:T(8,128)(2,1)S(1)}, u32[]{:S(2)}, u32[]{:S(2)}) collective-permute-start(bf16[128,256]{1,0:T(8,128)(2,1)S(1)} %get-tuple-element.54), channel_id=1, source_target_pairs={{0,24},{8,16},{16,8},{24,0},{1,25},{9,17},{17,9},{25,1},{2,26},{10... | collective-permute-start | bytes 196616 | tf_op jit(solution)/shard_map/ppermute | solution.py:301
  23.6 5.0 %collective-permute-start.11 = (bf16[256,256]{1,0:T(8,128)(2,1)S(1)}, bf16[256,256]{1,0:T(8,128)(2,1)S(1)}, u32[]{:S(2)}, u32[]{:S(2)}) collective-permute-start(bf16[256,256]{1,0:T(8,128)(2,1)S(1)} %get-tuple-element.64), channel_id=1, source_target_pairs={{0,4},{1,5},{2,6},{3,7},{4,0},{5,1},{6,2},{7,3},{8,12},{9,13},{10,... | collective-permute-start | bytes 393224 | tf_op jit(solution)/shard_map/ppermute | solution.py:301
  24.1 5.0 %collective-permute-start.12 = (bf16[256,256]{1,0:T(8,128)(2,1)S(1)}, bf16[256,256]{1,0:T(8,128)(2,1)S(1)}, u32[]{:S(2)}, u32[]{:S(2)}) collective-permute-start(bf16[256,256]{1,0:T(8,128)(2,1)S(1)} %get-tuple-element.65), channel_id=1, source_target_pairs={{0,2},{1,3},{2,0},{3,1},{4,6},{5,7},{6,4},{7,5},{8,10},{9,11},{10,... | collective-permute-start | bytes 393224 | tf_op jit(solution)/shard_map/ppermute | solution.py:301
  24.7 5.4 %collective-permute-start.10 = (bf16[128,256]{1,0:T(8,128)(2,1)S(1)}, bf16[128,256]{1,0:T(8,128)(2,1)S(1)}, u32[]{:S(2)}, u32[]{:S(2)}) collective-permute-start(bf16[128,256]{1,0:T(8,128)(2,1)S(1)} %get-tuple-element.63), channel_id=1, source_target_pairs={{0,16},{8,24},{16,0},{24,8},{1,17},{9,25},{17,1},{25,9},{2,18},{10... | collective-permute-start | bytes 196616 | tf_op jit(solution)/shard_map/ppermute | solution.py:301
  25.0 5.2 %collective-permute-start.13 = (bf16[144,256]{1,0:T(8,128)(2,1)S(1)}, bf16[144,256]{1,0:T(8,128)(2,1)S(1)}, u32[]{:S(2)}, u32[]{:S(2)}) collective-permute-start(bf16[144,256]{1,0:T(8,128)(2,1)S(1)} %get-tuple-element.66), channel_id=1, source_target_pairs={{0,8},{8,0},{16,24},{24,16},{1,9},{9,1},{17,25},{25,17},{2,10},{10... | collective-permute-start | bytes 221192 | tf_op jit(solution)/shard_map/ppermute | solution.py:301
  26.8 3.4 %collective-permute-start.14 = (bf16[256,256]{1,0:T(8,128)(2,1)S(1)}, bf16[256,256]{1,0:T(8,128)(2,1)S(1)}, u32[]{:S(2)}, u32[]{:S(2)}) collective-permute-start(bf16[256,256]{1,0:T(8,128)(2,1)S(1)} %early.1), channel_id=1, source_target_pairs={{0,1},{1,0},{2,3},{3,2},{4,5},{5,4},{6,7},{7,6},{8,9},{9,8},{10,11... | collective-permute-start | bytes 393224 | tf_op jit(solution)/shard_map/ppermute | solution.py:301
  29.1 1.4 %collective-permute-start.15 = (bf16[256,256]{1,0:T(8,128)(2,1)S(1)}, bf16[256,256]{1,0:T(8,128)(2,1)S(1)}, u32[]{:S(2)}, u32[]{:S(2)}) collective-permute-start(bf16[256,256]{1,0:T(8,128)(2,1)S(1)} %turn.1), channel_id=1, source_target_pairs={{0,1},{1,0},{2,3},{3,2},{4,5},{5,4},{6,7},{7,6},{8,9},{9,8},{10,11... | collective-permute-start | bytes 393224 | tf_op jit(solution)/shard_map/ppermute | solution.py:301

commit v16 on v12

--- a/solution.py
+++ b/solution.py
@@ -151,17 +151,27 @@
         out[i * size : (i + 1) * size, :] = message[last - size : last, :]
 
 
-def halo_sum(choice, dense, own, halos, refs, halo):
-    size = dense.shape[0] // own
-    columns = []
+def halo_blocks(choice, size, halos, refs, halo):
+    first = halos[0]
+    if all(
+        (at, row, picked) == (first[1], first[2] + i * size, True)
+        for i, (_, at, row, picked) in enumerate(halos)
+    ):
+        return refs[first[1]][first[2] : first[2] + len(halos) * size, :]
     for i, (slot, at, row, picked) in enumerate(halos):
         if picked:
             block = refs[at][row : row + size, :]
         else:
             block = pick(refs[at], choice[slot : slot + 1, :], size)
         halo[i * size : (i + 1) * size, :] = block
-        columns.append(dense[:, (own + slot) * size : (own + slot + 1) * size])
-    return dot(jnp.concatenate(columns, axis=1), halo[...])
+    return halo[...]
+
+
+def halo_sum(choice, dense, own, halos, refs, halo):
+    size = dense.shape[0] // own
+    blocks = halo_blocks(choice, size, halos, refs, halo)
+    columns = [dense[:, (own + slot) * size : (own + slot + 1) * size] for slot, *_ in halos]
+    return dot(jnp.concatenate(columns, axis=1), blocks)
 
 
 def flip_kernel(size, dense, dense_t):
@@ -412,7 +422,7 @@
             out_specs=jax.tree.map(lambda _: VMEM, out_shape),
             scratch_shapes=[pltpu.VMEM((len(slots) * size, width), BF)],
             compiler_params=PARAMS,
-            cost_estimate=cost(dict(first=10**9, near=10**9, late=10**10)[name], 3 * 1024 * 1024),
+            cost_estimate=cost(dict(first=10**9, near=10**10)[name], 3 * 1024 * 1024),
             name=name,
         )(*operands, *arrays)
 
@@ -451,13 +461,8 @@
         functools.partial(flip_kernel, size), jax.ShapeDtypeStruct((slots * size, rows), BF), "flip", 10**7,
         after(dense, near_sum),
     )
-    if relayed:
-        slots_late = [sub_count + d for d in relayed]
-        near_sum = sum_call(
-            near_kernel, wide, "late", slots_late, after(choice, dense_t), dense, near_sum
-        )
-
-    late = [1, *(d + 1 for d in even)]
+
+    late = [*(sub_count + d for d in relayed), 1, *(d + 1 for d in even)]
     late_arrays, late_at = unique(late)
     late_halos = [(slot, late_at[slot], got[slot][1], got[slot][2]) for slot in late]
     outs = pl.pallas_call(

time: 31.5 us -> 31.5 us (level)
    pallas_call x3 -> x2, Pallas kernels: 0.99 us -> 0.8 us  [sum_call(): pl.pallas_call(functools.partial(kernel, own, halos), out_shape=out_shape...]
  transfers between devices with their start and end apart: 16 -> 16, of which waited for: 12 -> 11; matrix products, arithmetic and copies ran while one was open for 0% -> 0% of each run, Pallas kernels for 12% -> 12%
where the time goes in v16:
time: 31.5 us; the launch traced here: 31.3 us
  starting transfers between devices  18.3 us (58%)
  Pallas kernels  6.75 us (21%)
  waiting for transfers between devices  6.14 us (19%)
    ppermute x16, starting transfers between devices, swap(): return lax.ppermute(value, axis, [(i, i ^ d) for i in range(count)])  18.3 us
    ppermute x16, waiting for transfers between devices, swap(): return lax.ppermute(value, axis, [(i, i ^ d) for i in range(count)])  6.14 us
    pallas_call x1, Pallas kernels, shards(): pl.pallas_call(functools.partial(prepare_kernel, *counts), out_shape=[jax...  1.63 us
    pallas_call x1, Pallas kernels, shards(): pl.pallas_call(functools.partial(middle_kernel, *counts, late_halos, len(...  1.42 us
    pallas_call x7, Pallas kernels, call(): pl.pallas_call(kernel, out_shape=out_shape, in_specs=[VMEM] * len(operand...  0.92 us
    pallas_call x1, Pallas kernels, shards(): pl.pallas_call(edge_kernel, out_shape=[jax.ShapeDtypeStruct((BOUNDARY * s...  0.89 us
    pallas_call x2, Pallas kernels, sum_call(): pl.pallas_call(functools.partial(kernel, own, halos), out_shape=out_shape...  0.8 us
    pallas_call x1, Pallas kernels, shards(): pl.pallas_call(functools.partial(final_kernel, own, parts), out_shape=nar...  0.78 us
  transfers between devices with their start and end apart: 16, of which 11 were waited for; matrix products, arithmetic and copies ran while one was open for 0% of the time, Pallas kernels for 12%

profile of v16, /device:TPU:0, one launch (start us, length us, event | category | flops | bytes accessed | tf_op | source)
XLA Modules:
  0.0 31.3 jit_solution(14664601941384235689)
XLA Ops:
  0.0 0.9 %edge.1 = (bf16[272,256]{1,0:T(8,128)(2,1)S(1)}, bf16[16,256]{1,0:T(8,128)(2,1)S(1)}) custom-call(s32[1,8]{1,0:T(1,128)} %recv_sub_hbm.1, s32[1,4]{1,0:T(1,128)} %recv_cluster_hbm.1, bf16[384,256]{1,0:T(8,128)(2,1)} %features_hbm.1), custom_call_target="tpu_custom_call" | custom-call | flops 1024 | bytes 262144 | tf_op jit(solution)/shard_map/edge/pallas_call | solution.py:332
  0.9 4.1 %collective-permute-start.1 = (bf16[272,256]{1,0:T(8,128)(2,1)S(1)}, bf16[272,256]{1,0:T(8,128)(2,1)S(1)}, u32[]{:S(2)}, u32[]{:S(2)}) collective-permute-start(bf16[272,256]{1,0:T(8,128)(2,1)S(1)} %get-tuple-element.36.rest_0_), channel_id=1, source_target_pairs={{0,16},{8,24},{16,0},{24,8},{1,17},{9,25},{17,1},{25,9},{2,18},{10... | collective-permute-start | bytes 417800 | tf_op jit(solution)/shard_map/ppermute | solution.py:299
  5.0 1.6 %collective-permute-start = (bf16[272,256]{1,0:T(8,128)(2,1)S(1)}, bf16[272,256]{1,0:T(8,128)(2,1)S(1)}, u32[]{:S(2)}, u32[]{:S(2)}) collective-permute-start(bf16[272,256]{1,0:T(8,128)(2,1)S(1)} %get-tuple-element.36.rest_0_), channel_id=1, source_target_pairs={{0,8},{8,0},{16,24},{24,16},{1,9},{9,1},{17,25},{25,17},{2,10},{10... | collective-permute-start | bytes 417800 | tf_op jit(solution)/shard_map/ppermute | solution.py:299
  6.6 2.4 %collective-permute-start.4 = (bf16[272,256]{1,0:T(8,128)(2,1)S(1)}, bf16[272,256]{1,0:T(8,128)(2,1)S(1)}, u32[]{:S(2)}, u32[]{:S(2)}) collective-permute-start(bf16[272,256]{1,0:T(8,128)(2,1)S(1)} %get-tuple-element.36.rest_0_), channel_id=1, source_target_pairs={{0,6},{1,7},{2,4},{3,5},{4,2},{5,3},{6,0},{7,1},{8,14},{9,15},{10,... | collective-permute-start | bytes 417800 | tf_op jit(solution)/shard_map/ppermute | solution.py:299
  9.0 0.5 %collective-permute-start.3 = (bf16[272,256]{1,0:T(8,128)(2,1)S(1)}, bf16[272,256]{1,0:T(8,128)(2,1)S(1)}, u32[]{:S(2)}, u32[]{:S(2)}) collective-permute-start(bf16[272,256]{1,0:T(8,128)(2,1)S(1)} %get-tuple-element.36.rest_0_), channel_id=1, source_target_pairs={{0,4},{1,5},{2,6},{3,7},{4,0},{5,1},{6,2},{7,3},{8,12},{9,13},{10,... | collective-permute-start | bytes 417800 | tf_op jit(solution)/shard_map/ppermute | solution.py:299
  9.5 0.5 %collective-permute-start.2 = (bf16[272,256]{1,0:T(8,128)(2,1)S(1)}, bf16[272,256]{1,0:T(8,128)(2,1)S(1)}, u32[]{:S(2)}, u32[]{:S(2)}) collective-permute-start(bf16[272,256]{1,0:T(8,128)(2,1)S(1)} %get-tuple-element.36.rest_0_), channel_id=1, source_target_pairs={{0,2},{1,3},{2,0},{3,1},{4,6},{5,7},{6,4},{7,5},{8,10},{9,11},{10,... | collective-permute-start | bytes 417800 | tf_op jit(solution)/shard_map/ppermute | solution.py:299
  10.1 1.6 %prepare.1 = (bf16[384,1920]{1,0:T(8,128)(2,1)S(1)}, f32[12,256]{1,0:T(8,128)S(1)}, bf16[384,256]{1,0:T(8,128)(2,1)S(1)}, bf16[256,256]{1,0:T(8,128)(2,1)S(1)}, ...) custom-call(s32[24]{0:T(128)} %tile_dst_hbm.1, s32[24]{0:T(128)} %tile_src_hbm.1, ...), custom_call_target="tpu_custom_call" | custom-call | flops 100000000 | bytes 6291456 | tf_op jit(solution)/shard_map/prepare/pallas_call | solution.py:366
  11.7 0.1 collective-permute-done.1.message.far.rest_1_
  11.8 0.2 collective-permute-done.near.rest_0_
  12.0 0.1 relay.1
  12.1 1.5 %collective-permute-start.7 = (bf16[128,256]{1,0:T(8,128)(2,1)S(1)}, bf16[128,256]{1,0:T(8,128)(2,1)S(1)}, u32[]{:S(2)}, u32[]{:S(2)}) collective-permute-start(bf16[128,256]{1,0:T(8,128)(2,1)S(1)} %relay.1), channel_id=1, source_target_pairs={{0,8},{8,0},{16,24},{24,16},{1,9},{9,1},{17,25},{25,17},{2,10},{10... | collective-permute-start | bytes 196616 | tf_op jit(solution)/shard_map/ppermute | solution.py:299
  13.6 0.0 collective-permute-start.5
  13.6 0.5 %first.1 = (f32[384,256]{1,0:T(8,128)S(1)}, f32[384,256]{1,0:T(8,128)S(1)}, f32[384,128]{1,0:T(8,128)S(1)}) custom-call(f32[12,256]{1,0:T(8,128)S(1)} %get-tuple-element.55.choice.rest_6_, bf16[384,1920]{1,0:T(8,128)(2,1)S(1)} %get-tuple-element.49.dense, bf16[384,256]{1,0:T(8,128)(2,1)S(1)} %get-tuple-element.45.features, ...), custom_call_target="tpu_custom_call" | custom-call | flops 1000000000 | bytes 3145728 | tf_op jit(solution)/shard_map/first/pallas_call | solution.py:418
  14.1 0.7 %collective-permute-done.5.rest_4_ = bf16[16,256]{1,0:T(8,128)(2,1)S(1)} collective-permute-done((bf16[16,256]{1,0:T(8,128)(2,1)S(1)}, bf16[16,256]{1,0:T(8,128)(2,1)S(1)}, u32[]{:S(2)}, u32[]{:S(2)}) %collective-permute-start.5) | collective-permute-done | bytes 8224 | tf_op jit(solution)/shard_map/ppermute | solution.py:299
  14.8 0.0 collective-permute-done.4.rest_3_.rest_4_
  14.8 0.5 %collective-permute-done.3.rest_2_.rest_3_ = bf16[272,256]{1,0:T(8,128)(2,1)S(1)} collective-permute-done((bf16[272,256]{1,0:T(8,128)(2,1)S(1)}, bf16[272,256]{1,0:T(8,128)(2,1)S(1)}, u32[]{:S(2)}, u32[]{:S(2)}) %collective-permute-start.3) | collective-permute-done | bytes 139296 | tf_op jit(solution)/shard_map/ppermute | solution.py:299
  15.3 0.1 collective-permute-done.2.rest_1_.rest_2_
  15.4 0.2 trade.1
  15.5 0.1 collective-permute-start.6
  15.6 0.3 near.1.before
  15.9 0.4 %flip.1.dense_t.rest_8_ = bf16[1920,384]{1,0:T(8,128)(2,1)S(1)} custom-call(bf16[384,1920]{1,0:T(8,128)(2,1)S(1)} %get-tuple-element.49.dense), custom_call_target="tpu_custom_call" | custom-call | flops 10000000 | bytes 1048576 | tf_op jit(solution)/shard_map/flip/pallas_call | solution.py:396
  16.4 0.0 collective-permute-done.7.rest_0_
  16.4 0.8 %collective-permute-done.6.rest_1_.rest_5_ = bf16[576,256]{1,0:T(8,128)(2,1)S(1)} collective-permute-done((bf16[576,256]{1,0:T(8,128)(2,1)S(1)}, bf16[576,256]{1,0:T(8,128)(2,1)S(1)}, u32[]{:S(2)}, u32[]{:S(2)}) %collective-permute-start.6) | collective-permute-done | bytes 294944 | tf_op jit(solution)/shard_map/ppermute | solution.py:299
  17.2 1.4 %middle.1 = (bf16[256,256]{1,0:T(8,128)(2,1)S(1)}, bf16[256,256]{1,0:T(8,128)(2,1)S(1)}, bf16[256,256]{1,0:T(8,128)(2,1)S(1)}, bf16[144,256]{1,0:T(8,128)(2,1)S(...) custom-call(f32[12,256]{1,0:T(8,128)S(1)} %get-tuple-element.55.choi, ...), custom_call_target="tpu_custom_call" | custom-call | flops 377487360 | bytes 6291456 | tf_op jit(solution)/shard_map/middle/pallas_call | solution.py:468
  18.6 1.9 %collective-permute-start.9 = (bf16[256,256]{1,0:T(8,128)(2,1)S(1)}, bf16[256,256]{1,0:T(8,128)(2,1)S(1)}, u32[]{:S(2)}, u32[]{:S(2)}) collective-permute-start(bf16[256,256]{1,0:T(8,128)(2,1)S(1)} %get-tuple-element.54), channel_id=1, source_target_pairs={{0,6},{1,7},{2,4},{3,5},{4,2},{5,3},{6,0},{7,1},{8,14},{9,15},{10,... | collective-permute-start | bytes 393224 | tf_op jit(solution)/shard_map/ppermute | solution.py:299
  20.5 3.0 %collective-permute-start.8 = (bf16[128,256]{1,0:T(8,128)(2,1)S(1)}, bf16[128,256]{1,0:T(8,128)(2,1)S(1)}, u32[]{:S(2)}, u32[]{:S(2)}) collective-permute-start(bf16[128,256]{1,0:T(8,128)(2,1)S(1)} %get-tuple-element.52), channel_id=1, source_target_pairs={{0,24},{8,16},{16,8},{24,0},{1,25},{9,17},{17,9},{25,1},{2,26},{10... | collective-permute-start | bytes 196616 | tf_op jit(solution)/shard_map/ppermute | solution.py:299
  23.6 0.5 %collective-permute-start.12 = (bf16[256,256]{1,0:T(8,128)(2,1)S(1)}, bf16[256,256]{1,0:T(8,128)(2,1)S(1)}, u32[]{:S(2)}, u32[]{:S(2)}) collective-permute-start(bf16[256,256]{1,0:T(8,128)(2,1)S(1)} %get-tuple-element.63), channel_id=1, source_target_pairs={{0,4},{1,5},{2,6},{3,7},{4,0},{5,1},{6,2},{7,3},{8,12},{9,13},{10,... | collective-permute-start | bytes 393224 | tf_op jit(solution)/shard_map/ppermute | solution.py:299
  24.1 0.5 %collective-permute-start.13 = (bf16[256,256]{1,0:T(8,128)(2,1)S(1)}, bf16[256,256]{1,0:T(8,128)(2,1)S(1)}, u32[]{:S(2)}, u32[]{:S(2)}) collective-permute-start(bf16[256,256]{1,0:T(8,128)(2,1)S(1)} %get-tuple-element.64), channel_id=1, source_target_pairs={{0,2},{1,3},{2,0},{3,1},{4,6},{5,7},{6,4},{7,5},{8,10},{9,11},{10,... | collective-permute-start | bytes 393224 | tf_op jit(solution)/shard_map/ppermute | solution.py:299
  24.6 0.0 collective-permute-start.11
  24.6 0.5 %collective-permute-done.9.rest_1_.rest_3_ = bf16[256,256]{1,0:T(8,128)(2,1)S(1)} collective-permute-done((bf16[256,256]{1,0:T(8,128)(2,1)S(1)}, bf16[256,256]{1,0:T(8,128)(2,1)S(1)}, u32[]{:S(2)}, u32[]{:S(2)}) %collective-permute-start.9) | collective-permute-done | bytes 131104 | tf_op jit(solution)/shard_map/ppermute | solution.py:299
  25.1 1.4 %collective-permute-start.10 = (bf16[144,256]{1,0:T(8,128)(2,1)S(1)}, bf16[144,256]{1,0:T(8,128)(2,1)S(1)}, u32[]{:S(2)}, u32[]{:S(2)}) collective-permute-start(bf16[144,256]{1,0:T(8,128)(2,1)S(1)} %get-tuple-element.61), channel_id=1, source_target_pairs={{0,8},{8,0},{16,24},{24,16},{1,9},{9,1},{17,25},{25,17},{2,10},{10... | collective-permute-start | bytes 221192 | tf_op jit(solution)/shard_map/ppermute | solution.py:299
  26.6 0.3 collective-permute-done.8.rest_2_
  26.8 0.0 collective-permute-start.14
  26.8 0.3 %own.1 = (f32[384,256]{1,0:T(8,128)S(1)}, f32[12,256]{1,0:T(8,128)S(1)}) custom-call(bf16[272,256]{1,0:T(8,128)(2,1)S(1)} %collective-permute-done.near.rest_0_, bf16[272,256]{1,0:T(8,128)(2,1)S(1)} %collective-permute-done.1.message.far.rest_1_, bf16[272,256]{1,0:T(8,128)(2,1)S(1)} %collective-permute-done.2.rest_1_.rest_2_, ...), custom_call_target="tpu_custom_call" | custom-call | flops 1000000000 | bytes 2097152 | tf_op jit(solution)/shard_map/own/pallas_call | solution.py:495
  27.1 1.4 %collective-permute-done.12.rest_4_.rest_1_ = bf16[256,256]{1,0:T(8,128)(2,1)S(1)} collective-permute-done((bf16[256,256]{1,0:T(8,128)(2,1)S(1)}, bf16[256,256]{1,0:T(8,128)(2,1)S(1)}, u32[]{:S(2)}, u32[]{:S(2)}) %collective-permute-start.12) | collective-permute-done | bytes 131104 | tf_op jit(solution)/shard_map/ppermute | solution.py:299
  28.5 0.5 %collective-permute-done.13.rest_5_.rest_0_ = bf16[256,256]{1,0:T(8,128)(2,1)S(1)} collective-permute-done((bf16[256,256]{1,0:T(8,128)(2,1)S(1)}, bf16[256,256]{1,0:T(8,128)(2,1)S(1)}, u32[]{:S(2)}, u32[]{:S(2)}) %collective-permute-start.13) | collective-permute-done | bytes 131104 | tf_op jit(solution)/shard_map/ppermute | solution.py:299
  29.1 0.1 collective-permute-start.15
  29.1 1.1 %collective-permute-done.11.rest_1_ = bf16[128,256]{1,0:T(8,128)(2,1)S(1)} collective-permute-done((bf16[128,256]{1,0:T(8,128)(2,1)S(1)}, bf16[128,256]{1,0:T(8,128)(2,1)S(1)}, u32[]{:S(2)}, u32[]{:S(2)}) %collective-permute-start.11) | collective-permute-done | bytes 65568 | tf_op jit(solution)/shard_map/ppermute | solution.py:299
  30.2 0.0 collective-permute-done.10.rest_0_
  30.2 0.2 add.1.total
  30.4 0.0 collective-permute-done.14.rest_0_
  30.4 0.0 collective-permute-done.15.rest_1_
  30.5 0.8 %final.1 = bf16[384,256]{1,0:T(8,128)(2,1)} custom-call(f32[12,256]{1,0:T(8,128)S(1)} %get-tuple-element.59.owner, f32[384,256]{1,0:T(8,128)S(1)} %add.1.total, bf16[256,256]{1,0:T(8,128)(2,1)S(1)} %collective-permute-done.14.rest_0_, bf16[256,256]{1,0:T(8,128)(2,1)S(1)} %collective-permute-done.15.rest_1_), custom_call_target="tpu_custom_call" | custom-call | flops 393216 | bytes 1048576 | tf_op jit(solution)/shard_map/final/pallas_call | solution.py:525
  (3 shorter events, 0.0 us)
Async XLA Ops:
  0.9 10.9 %collective-permute-start.1 = (bf16[272,256]{1,0:T(8,128)(2,1)S(1)}, bf16[272,256]{1,0:T(8,128)(2,1)S(1)}, u32[]{:S(2)}, u32[]{:S(2)}) collective-permute-start(bf16[272,256]{1,0:T(8,128)(2,1)S(1)} %get-tuple-element.36.rest_0_), channel_id=1, source_target_pairs={{0,16},{8,24},{16,0},{24,8},{1,17},{9,25},{17,1},{25,9},{2,18},{10... | collective-permute-start | bytes 417800 | tf_op jit(solution)/shard_map/ppermute | solution.py:299
  5.0 7.0 %collective-permute-start = (bf16[272,256]{1,0:T(8,128)(2,1)S(1)}, bf16[272,256]{1,0:T(8,128)(2,1)S(1)}, u32[]{:S(2)}, u32[]{:S(2)}) collective-permute-start(bf16[272,256]{1,0:T(8,128)(2,1)S(1)} %get-tuple-element.36.rest_0_), channel_id=1, source_target_pairs={{0,8},{8,0},{16,24},{24,16},{1,9},{9,1},{17,25},{25,17},{2,10},{10... | collective-permute-start | bytes 417800 | tf_op jit(solution)/shard_map/ppermute | solution.py:299
  6.6 8.2 %collective-permute-start.4 = (bf16[272,256]{1,0:T(8,128)(2,1)S(1)}, bf16[272,256]{1,0:T(8,128)(2,1)S(1)}, u32[]{:S(2)}, u32[]{:S(2)}) collective-permute-start(bf16[272,256]{1,0:T(8,128)(2,1)S(1)} %get-tuple-element.36.rest_0_), channel_id=1, source_target_pairs={{0,6},{1,7},{2,4},{3,5},{4,2},{5,3},{6,0},{7,1},{8,14},{9,15},{10,... | collective-permute-start | bytes 417800 | tf_op jit(solution)/shard_map/ppermute | solution.py:299
  9.0 6.3 %collective-permute-start.3 = (bf16[272,256]{1,0:T(8,128)(2,1)S(1)}, bf16[272,256]{1,0:T(8,128)(2,1)S(1)}, u32[]{:S(2)}, u32[]{:S(2)}) collective-permute-start(bf16[272,256]{1,0:T(8,128)(2,1)S(1)} %get-tuple-element.36.rest_0_), channel_id=1, source_target_pairs={{0,4},{1,5},{2,6},{3,7},{4,0},{5,1},{6,2},{7,3},{8,12},{9,13},{10,... | collective-permute-start | bytes 417800 | tf_op jit(solution)/shard_map/ppermute | solution.py:299
  9.5 5.8 %collective-permute-start.2 = (bf16[272,256]{1,0:T(8,128)(2,1)S(1)}, bf16[272,256]{1,0:T(8,128)(2,1)S(1)}, u32[]{:S(2)}, u32[]{:S(2)}) collective-permute-start(bf16[272,256]{1,0:T(8,128)(2,1)S(1)} %get-tuple-element.36.rest_0_), channel_id=1, source_target_pairs={{0,2},{1,3},{2,0},{3,1},{4,6},{5,7},{6,4},{7,5},{8,10},{9,11},{10,... | collective-permute-start | bytes 417800 | tf_op jit(solution)/shard_map/ppermute | solution.py:299
  12.1 4.3 %collective-permute-start.7 = (bf16[128,256]{1,0:T(8,128)(2,1)S(1)}, bf16[128,256]{1,0:T(8,128)(2,1)S(1)}, u32[]{:S(2)}, u32[]{:S(2)}) collective-permute-start(bf16[128,256]{1,0:T(8,128)(2,1)S(1)} %relay.1), channel_id=1, source_target_pairs={{0,8},{8,0},{16,24},{24,16},{1,9},{9,1},{17,25},{25,17},{2,10},{10... | collective-permute-start | bytes 196616 | tf_op jit(solution)/shard_map/ppermute | solution.py:299
  13.6 1.2 %collective-permute-start.5 = (bf16[16,256]{1,0:T(8,128)(2,1)S(1)}, bf16[16,256]{1,0:T(8,128)(2,1)S(1)}, u32[]{:S(2)}, u32[]{:S(2)}) collective-permute-start(bf16[16,256]{1,0:T(8,128)(2,1)S(1)} %get-tuple-element.38), channel_id=1, source_target_pairs={{0,1},{1,0},{2,3},{3,2},{4,5},{5,4},{6,7},{7,6},{8,9},{9,8},{10,11... | collective-permute-start | bytes 24584 | tf_op jit(solution)/shard_map/ppermute | solution.py:299
  15.5 1.6 %collective-permute-start.6 = (bf16[576,256]{1,0:T(8,128)(2,1)S(1)}, bf16[576,256]{1,0:T(8,128)(2,1)S(1)}, u32[]{:S(2)}, u32[]{:S(2)}) collective-permute-start(bf16[576,256]{1,0:T(8,128)(2,1)S(1)} %trade.1), channel_id=1, source_target_pairs={{0,1},{1,0},{2,3},{3,2},{4,5},{5,4},{6,7},{7,6},{8,9},{9,8},{10,11... | collective-permute-start | bytes 884744 | tf_op jit(solution)/shard_map/ppermute | solution.py:299
  18.6 6.5 %collective-permute-start.9 = (bf16[256,256]{1,0:T(8,128)(2,1)S(1)}, bf16[256,256]{1,0:T(8,128)(2,1)S(1)}, u32[]{:S(2)}, u32[]{:S(2)}) collective-permute-start(bf16[256,256]{1,0:T(8,128)(2,1)S(1)} %get-tuple-element.54), channel_id=1, source_target_pairs={{0,6},{1,7},{2,4},{3,5},{4,2},{5,3},{6,0},{7,1},{8,14},{9,15},{10,... | collective-permute-start | bytes 393224 | tf_op jit(solution)/shard_map/ppermute | solution.py:299
  20.5 6.3 %collective-permute-start.8 = (bf16[128,256]{1,0:T(8,128)(2,1)S(1)}, bf16[128,256]{1,0:T(8,128)(2,1)S(1)}, u32[]{:S(2)}, u32[]{:S(2)}) collective-permute-start(bf16[128,256]{1,0:T(8,128)(2,1)S(1)} %get-tuple-element.52), channel_id=1, source_target_pairs={{0,24},{8,16},{16,8},{24,0},{1,25},{9,17},{17,9},{25,1},{2,26},{10... | collective-permute-start | bytes 196616 | tf_op jit(solution)/shard_map/ppermute | solution.py:299
  23.6 5.0 %collective-permute-start.12 = (bf16[256,256]{1,0:T(8,128)(2,1)S(1)}, bf16[256,256]{1,0:T(8,128)(2,1)S(1)}, u32[]{:S(2)}, u32[]{:S(2)}) collective-permute-start(bf16[256,256]{1,0:T(8,128)(2,1)S(1)} %get-tuple-element.63), channel_id=1, source_target_pairs={{0,4},{1,5},{2,6},{3,7},{4,0},{5,1},{6,2},{7,3},{8,12},{9,13},{10,... | collective-permute-start | bytes 393224 | tf_op jit(solution)/shard_map/ppermute | solution.py:299
  24.1 5.0 %collective-permute-start.13 = (bf16[256,256]{1,0:T(8,128)(2,1)S(1)}, bf16[256,256]{1,0:T(8,128)(2,1)S(1)}, u32[]{:S(2)}, u32[]{:S(2)}) collective-permute-start(bf16[256,256]{1,0:T(8,128)(2,1)S(1)} %get-tuple-element.64), channel_id=1, source_target_pairs={{0,2},{1,3},{2,0},{3,1},{4,6},{5,7},{6,4},{7,5},{8,10},{9,11},{10,... | collective-permute-start | bytes 393224 | tf_op jit(solution)/shard_map/ppermute | solution.py:299
  24.6 5.6 %collective-permute-start.11 = (bf16[128,256]{1,0:T(8,128)(2,1)S(1)}, bf16[128,256]{1,0:T(8,128)(2,1)S(1)}, u32[]{:S(2)}, u32[]{:S(2)}) collective-permute-start(bf16[128,256]{1,0:T(8,128)(2,1)S(1)} %get-tuple-element.62), channel_id=1, source_target_pairs={{0,16},{8,24},{16,0},{24,8},{1,17},{9,25},{17,1},{25,9},{2,18},{10... | collective-permute-start | bytes 196616 | tf_op jit(solution)/shard_map/ppermute | solution.py:299
  25.1 5.1 %collective-permute-start.10 = (bf16[144,256]{1,0:T(8,128)(2,1)S(1)}, bf16[144,256]{1,0:T(8,128)(2,1)S(1)}, u32[]{:S(2)}, u32[]{:S(2)}) collective-permute-start(bf16[144,256]{1,0:T(8,128)(2,1)S(1)} %get-tuple-element.61), channel_id=1, source_target_pairs={{0,8},{8,0},{16,24},{24,16},{1,9},{9,1},{17,25},{25,17},{2,10},{10... | collective-permute-start | bytes 221192 | tf_op jit(solution)/shard_map/ppermute | solution.py:299
  26.8 3.6 %collective-permute-start.14 = (bf16[256,256]{1,0:T(8,128)(2,1)S(1)}, bf16[256,256]{1,0:T(8,128)(2,1)S(1)}, u32[]{:S(2)}, u32[]{:S(2)}) collective-permute-start(bf16[256,256]{1,0:T(8,128)(2,1)S(1)} %early.1), channel_id=1, source_target_pairs={{0,1},{1,0},{2,3},{3,2},{4,5},{5,4},{6,7},{7,6},{8,9},{9,8},{10,11... | collective-permute-start | bytes 393224 | tf_op jit(solution)/shard_map/ppermute | solution.py:299
  29.1 1.4 %collective-permute-start.15 = (bf16[256,256]{1,0:T(8,128)(2,1)S(1)}, bf16[256,256]{1,0:T(8,128)(2,1)S(1)}, u32[]{:S(2)}, u32[]{:S(2)}) collective-permute-start(bf16[256,256]{1,0:T(8,128)(2,1)S(1)} %turn.1), channel_id=1, source_target_pairs={{0,1},{1,0},{2,3},{3,2},{4,5},{5,4},{6,7},{7,6},{8,9},{9,8},{10,11... | collective-permute-start | bytes 393224 | tf_op jit(solution)/shard_map/ppermute | solution.py:299

commit v17 on v12

--- a/solution.py
+++ b/solution.py
@@ -428,22 +428,23 @@
             "relay", 10**6, far, far_rows, got[sub_count + 1][0],
         )
         carried.append(far_rows)
+        relay_value = value
         got[sub_count + d] = (along(value, 1), 0, True, None)
     first_sum, own_pre, inverse = sum_call(
         first_kernel, [wide, wide, jax.ShapeDtypeStruct((rows, size), F32)], "first", [0, sub_count, *(sub_count + d for d in direct)],
         choice, dense, features, w_self, bias,
     )
-    traded = [0, *even]
-    sibling_rows = across(after(rows_only, value), 1)
-    value = call(
-        functools.partial(trade_kernel, traded),
-        jax.ShapeDtypeStruct((len(traded) * (size + EXTRA), width), BF),
-        "trade", 10**6, *[got[d][0] for d in traded], after(sibling_rows, (choice, value)),
-    )
-    trade_value = value
-    value = across(value, 1)
-    for i, d in enumerate(traded):
-        got[d + 1] = (value, i * size, True, len(traded) * size + i * EXTRA)
+    sibling_rows = across(after(rows_only, relay_value), 1)
+    trade_value = relay_value
+    for name, traded in (("trade", [0, *even[-1:]]), ("trade2", even[:-1])):
+        trade_value = call(
+            functools.partial(trade_kernel, traded),
+            jax.ShapeDtypeStruct((len(traded) * (size + EXTRA), width), BF),
+            name, 10**6, *[got[d][0] for d in traded], after(sibling_rows, (choice, trade_value)),
+        )
+        value = across(trade_value, 1)
+        for i, d in enumerate(traded):
+            got[d + 1] = (value, i * size, True, len(traded) * size + i * EXTRA)
     near_sum = sum_call(
         near_kernel, wide, "near", [sub_count + 1, *even], after(choice, trade_value), dense, first_sum
     )
@@ -457,7 +458,7 @@
             near_kernel, wide, "late", slots_late, after(choice, dense_t), dense, near_sum
         )
 
-    late = [1, *(d + 1 for d in even)]
+    late = [1, even[-1] + 1, *(d + 1 for d in even[:-1])]
     late_arrays, late_at = unique(late)
     late_halos = [(slot, late_at[slot], got[slot][1], got[slot][2]) for slot in late]
     outs = pl.pallas_call(

time: 31.5 us -> 31.5 us (level)
  waiting for transfers between devices: 5.97 us -> 5.49 us
  starting transfers between devices: 18.5 us -> 18.9 us
    ppermute x16 -> x17, waiting for transfers between devices: 5.97 us -> 5.49 us  [swap(): return lax.ppermute(value, axis, [(i, i ^ d) for i in range(count)])]
    ppermute x16 -> x17, starting transfers between devices: 18.5 us -> 18.9 us  [swap(): return lax.ppermute(value, axis, [(i, i ^ d) for i in range(count)])]
    pallas_call x7 -> x8, Pallas kernels: 0.92 us -> 1.01 us  [call(): pl.pallas_call(kernel, out_shape=out_shape, in_specs=[VMEM] * len(operand...]
  transfers between devices with their start and end apart: 16 -> 17, of which waited for: 12 -> 12; matrix products, arithmetic and copies ran while one was open for 0% -> 0% of each run, Pallas kernels for 12% -> 13%
where the time goes in v17:
time: 31.5 us; the launch traced here: 31.3 us
  starting transfers between devices  18.9 us (60%)
  Pallas kernels  6.86 us (22%)
  waiting for transfers between devices  5.49 us (17%)
    ppermute x17, starting transfers between devices, swap(): return lax.ppermute(value, axis, [(i, i ^ d) for i in range(count)])  18.9 us
    ppermute x17, waiting for transfers between devices, swap(): return lax.ppermute(value, axis, [(i, i ^ d) for i in range(count)])  5.49 us
    pallas_call x1, Pallas kernels, shards(): pl.pallas_call(functools.partial(prepare_kernel, *counts), out_shape=[jax...  1.63 us
    pallas_call x1, Pallas kernels, shards(): pl.pallas_call(functools.partial(middle_kernel, *counts, late_halos, len(...  1.27 us
    pallas_call x8, Pallas kernels, call(): pl.pallas_call(kernel, out_shape=out_shape, in_specs=[VMEM] * len(operand...  1.01 us
    pallas_call x3, Pallas kernels, sum_call(): pl.pallas_call(functools.partial(kernel, own, halos), out_shape=out_shape...  0.98 us
    pallas_call x1, Pallas kernels, shards(): pl.pallas_call(edge_kernel, out_shape=[jax.ShapeDtypeStruct((BOUNDARY * s...  0.89 us
    pallas_call x1, Pallas kernels, shards(): pl.pallas_call(functools.partial(final_kernel, own, parts), out_shape=nar...  0.78 us
  transfers between devices with their start and end apart: 17, of which 12 were waited for; matrix products, arithmetic and copies ran while one was open for 0% of the time, Pallas kernels for 13%

profile of v17, /device:TPU:0, one launch (start us, length us, event | category | flops | bytes accessed | tf_op | source)
XLA Modules:
  0.0 31.3 jit_solution(3588963127997274594)
XLA Ops:
  0.0 0.9 %edge.1 = (bf16[272,256]{1,0:T(8,128)(2,1)S(1)}, bf16[16,256]{1,0:T(8,128)(2,1)S(1)}) custom-call(s32[1,8]{1,0:T(1,128)} %recv_sub_hbm.1, s32[1,4]{1,0:T(1,128)} %recv_cluster_hbm.1, bf16[384,256]{1,0:T(8,128)(2,1)} %features_hbm.1), custom_call_target="tpu_custom_call" | custom-call | flops 1024 | bytes 262144 | tf_op jit(solution)/shard_map/edge/pallas_call | solution.py:322
  0.9 4.1 %collective-permute-start.1 = (bf16[272,256]{1,0:T(8,128)(2,1)S(1)}, bf16[272,256]{1,0:T(8,128)(2,1)S(1)}, u32[]{:S(2)}, u32[]{:S(2)}) collective-permute-start(bf16[272,256]{1,0:T(8,128)(2,1)S(1)} %get-tuple-element.38.rest_0_), channel_id=1, source_target_pairs={{0,16},{8,24},{16,0},{24,8},{1,17},{9,25},{17,1},{25,9},{2,18},{10... | collective-permute-start | bytes 417800 | tf_op jit(solution)/shard_map/ppermute | solution.py:289
  5.0 1.6 %collective-permute-start = (bf16[272,256]{1,0:T(8,128)(2,1)S(1)}, bf16[272,256]{1,0:T(8,128)(2,1)S(1)}, u32[]{:S(2)}, u32[]{:S(2)}) collective-permute-start(bf16[272,256]{1,0:T(8,128)(2,1)S(1)} %get-tuple-element.38.rest_0_), channel_id=1, source_target_pairs={{0,8},{8,0},{16,24},{24,16},{1,9},{9,1},{17,25},{25,17},{2,10},{10... | collective-permute-start | bytes 417800 | tf_op jit(solution)/shard_map/ppermute | solution.py:289
  6.6 2.4 %collective-permute-start.4 = (bf16[272,256]{1,0:T(8,128)(2,1)S(1)}, bf16[272,256]{1,0:T(8,128)(2,1)S(1)}, u32[]{:S(2)}, u32[]{:S(2)}) collective-permute-start(bf16[272,256]{1,0:T(8,128)(2,1)S(1)} %get-tuple-element.38.rest_0_), channel_id=1, source_target_pairs={{0,6},{1,7},{2,4},{3,5},{4,2},{5,3},{6,0},{7,1},{8,14},{9,15},{10,... | collective-permute-start | bytes 417800 | tf_op jit(solution)/shard_map/ppermute | solution.py:289
  9.0 0.5 %collective-permute-start.3 = (bf16[272,256]{1,0:T(8,128)(2,1)S(1)}, bf16[272,256]{1,0:T(8,128)(2,1)S(1)}, u32[]{:S(2)}, u32[]{:S(2)}) collective-permute-start(bf16[272,256]{1,0:T(8,128)(2,1)S(1)} %get-tuple-element.38.rest_0_), channel_id=1, source_target_pairs={{0,4},{1,5},{2,6},{3,7},{4,0},{5,1},{6,2},{7,3},{8,12},{9,13},{10,... | collective-permute-start | bytes 417800 | tf_op jit(solution)/shard_map/ppermute | solution.py:289
  9.5 0.5 %collective-permute-start.2 = (bf16[272,256]{1,0:T(8,128)(2,1)S(1)}, bf16[272,256]{1,0:T(8,128)(2,1)S(1)}, u32[]{:S(2)}, u32[]{:S(2)}) collective-permute-start(bf16[272,256]{1,0:T(8,128)(2,1)S(1)} %get-tuple-element.38.rest_0_), channel_id=1, source_target_pairs={{0,2},{1,3},{2,0},{3,1},{4,6},{5,7},{6,4},{7,5},{8,10},{9,11},{10,... | collective-permute-start | bytes 417800 | tf_op jit(solution)/shard_map/ppermute | solution.py:289
  10.1 1.6 %prepare.1 = (bf16[384,1920]{1,0:T(8,128)(2,1)S(1)}, f32[12,256]{1,0:T(8,128)S(1)}, bf16[384,256]{1,0:T(8,128)(2,1)S(1)}, bf16[256,256]{1,0:T(8,128)(2,1)S(1)}, ...) custom-call(s32[24]{0:T(128)} %tile_dst_hbm.1, s32[24]{0:T(128)} %tile_src_hbm.1, ...), custom_call_target="tpu_custom_call" | custom-call | flops 100000000 | bytes 6291456 | tf_op jit(solution)/shard_map/prepare/pallas_call | solution.py:356
  11.7 0.1 collective-permute-done.1.message.far.rest_1_
  11.8 0.2 collective-permute-done.near.rest_0_
  12.0 0.1 relay.1
  12.1 1.5 %collective-permute-start.8 = (bf16[128,256]{1,0:T(8,128)(2,1)S(1)}, bf16[128,256]{1,0:T(8,128)(2,1)S(1)}, u32[]{:S(2)}, u32[]{:S(2)}) collective-permute-start(bf16[128,256]{1,0:T(8,128)(2,1)S(1)} %relay.1), channel_id=1, source_target_pairs={{0,8},{8,0},{16,24},{24,16},{1,9},{9,1},{17,25},{25,17},{2,10},{10... | collective-permute-start | bytes 196616 | tf_op jit(solution)/shard_map/ppermute | solution.py:289
  13.6 0.0 collective-permute-start.5
  13.6 0.5 %first.1 = (f32[384,256]{1,0:T(8,128)S(1)}, f32[384,256]{1,0:T(8,128)S(1)}, f32[384,128]{1,0:T(8,128)S(1)}) custom-call(f32[12,256]{1,0:T(8,128)S(1)} %get-tuple-element.59.choice.rest_7_, bf16[384,1920]{1,0:T(8,128)(2,1)S(1)} %get-tuple-element.52.dense, bf16[384,256]{1,0:T(8,128)(2,1)S(1)} %get-tuple-element.48.features, ...), custom_call_target="tpu_custom_call" | custom-call | flops 1000000000 | bytes 3145728 | tf_op jit(solution)/shard_map/first/pallas_call | solution.py:408
  14.1 0.7 %collective-permute-done.5.rest_2_ = bf16[16,256]{1,0:T(8,128)(2,1)S(1)} collective-permute-done((bf16[16,256]{1,0:T(8,128)(2,1)S(1)}, bf16[16,256]{1,0:T(8,128)(2,1)S(1)}, u32[]{:S(2)}, u32[]{:S(2)}) %collective-permute-start.5) | collective-permute-done | bytes 8224 | tf_op jit(solution)/shard_map/ppermute | solution.py:289
  14.8 0.0 collective-permute-done.4.rest_1_.rest_3_.rest_4_
  14.8 0.1 trade.1
  14.9 0.4 %collective-permute-done.3.rest_1_.rest_2_.rest_3_ = bf16[272,256]{1,0:T(8,128)(2,1)S(1)} collective-permute-done((bf16[272,256]{1,0:T(8,128)(2,1)S(1)}, bf16[272,256]{1,0:T(8,128)(2,1)S(1)}, u32[]{:S(2)}, u32[]{:S(2)}) %collective-permute-start.3) | collective-permute-done | bytes 139296 | tf_op jit(solution)/shard_map/ppermute | solution.py:289
  15.3 0.1 collective-permute-done.2.rest_0_.rest_1_.rest_2_
  15.4 0.1 trade2.1
  15.5 0.1 collective-permute-start.6
  15.6 0.5 %collective-permute-start.7 = (bf16[288,256]{1,0:T(8,128)(2,1)S(1)}, bf16[288,256]{1,0:T(8,128)(2,1)S(1)}, u32[]{:S(2)}, u32[]{:S(2)}) collective-permute-start(bf16[288,256]{1,0:T(8,128)(2,1)S(1)} %trade.1), channel_id=1, source_target_pairs={{0,1},{1,0},{2,3},{3,2},{4,5},{5,4},{6,7},{7,6},{8,9},{9,8},{10,11... | collective-permute-start | bytes 442376 | tf_op jit(solution)/shard_map/ppermute | solution.py:289
  16.1 0.3 near.1.before
  16.4 0.4 %flip.1.dense_t.rest_9_ = bf16[1920,384]{1,0:T(8,128)(2,1)S(1)} custom-call(bf16[384,1920]{1,0:T(8,128)(2,1)S(1)} %get-tuple-element.52.dense), custom_call_target="tpu_custom_call" | custom-call | flops 10000000 | bytes 1048576 | tf_op jit(solution)/shard_map/flip/pallas_call | solution.py:386
  16.8 0.0 collective-permute-done.8.rest_0_
  16.8 0.2 late.1.before
  17.0 0.0 collective-permute-done.6.rest_1_.rest_5_
  17.0 0.1 collective-permute-done.7.rest_0_.rest_6_
  17.1 1.3 %middle.1 = (bf16[256,256]{1,0:T(8,128)(2,1)S(1)}, bf16[256,256]{1,0:T(8,128)(2,1)S(1)}, bf16[256,256]{1,0:T(8,128)(2,1)S(1)}, bf16[144,256]{1,0:T(8,128)(2,1)S(...) custom-call(f32[12,256]{1,0:T(8,128)S(1)} %get-tuple-element.59.choi, ...), custom_call_target="tpu_custom_call" | custom-call | flops 377487360 | bytes 6291456 | tf_op jit(solution)/shard_map/middle/pallas_call | solution.py:464
  18.4 2.1 %collective-permute-start.10 = (bf16[256,256]{1,0:T(8,128)(2,1)S(1)}, bf16[256,256]{1,0:T(8,128)(2,1)S(1)}, u32[]{:S(2)}, u32[]{:S(2)}) collective-permute-start(bf16[256,256]{1,0:T(8,128)(2,1)S(1)} %get-tuple-element.58), channel_id=1, source_target_pairs={{0,6},{1,7},{2,4},{3,5},{4,2},{5,3},{6,0},{7,1},{8,14},{9,15},{10,... | collective-permute-start | bytes 393224 | tf_op jit(solution)/shard_map/ppermute | solution.py:289
  20.5 3.2 %collective-permute-start.9 = (bf16[128,256]{1,0:T(8,128)(2,1)S(1)}, bf16[128,256]{1,0:T(8,128)(2,1)S(1)}, u32[]{:S(2)}, u32[]{:S(2)}) collective-permute-start(bf16[128,256]{1,0:T(8,128)(2,1)S(1)} %get-tuple-element.56), channel_id=1, source_target_pairs={{0,24},{8,16},{16,8},{24,0},{1,25},{9,17},{17,9},{25,1},{2,26},{10... | collective-permute-start | bytes 196616 | tf_op jit(solution)/shard_map/ppermute | solution.py:289
  23.6 0.5 %collective-permute-start.13 = (bf16[256,256]{1,0:T(8,128)(2,1)S(1)}, bf16[256,256]{1,0:T(8,128)(2,1)S(1)}, u32[]{:S(2)}, u32[]{:S(2)}) collective-permute-start(bf16[256,256]{1,0:T(8,128)(2,1)S(1)} %get-tuple-element.67), channel_id=1, source_target_pairs={{0,4},{1,5},{2,6},{3,7},{4,0},{5,1},{6,2},{7,3},{8,12},{9,13},{10,... | collective-permute-start | bytes 393224 | tf_op jit(solution)/shard_map/ppermute | solution.py:289
  24.2 0.5 %collective-permute-start.14 = (bf16[256,256]{1,0:T(8,128)(2,1)S(1)}, bf16[256,256]{1,0:T(8,128)(2,1)S(1)}, u32[]{:S(2)}, u32[]{:S(2)}) collective-permute-start(bf16[256,256]{1,0:T(8,128)(2,1)S(1)} %get-tuple-element.68), channel_id=1, source_target_pairs={{0,2},{1,3},{2,0},{3,1},{4,6},{5,7},{6,4},{7,5},{8,10},{9,11},{10,... | collective-permute-start | bytes 393224 | tf_op jit(solution)/shard_map/ppermute | solution.py:289
  24.7 0.0 collective-permute-start.12
  24.7 0.4 %collective-permute-done.10.rest_1_.rest_3_ = bf16[256,256]{1,0:T(8,128)(2,1)S(1)} collective-permute-done((bf16[256,256]{1,0:T(8,128)(2,1)S(1)}, bf16[256,256]{1,0:T(8,128)(2,1)S(1)}, u32[]{:S(2)}, u32[]{:S(2)}) %collective-permute-start.10) | collective-permute-done | bytes 131104 | tf_op jit(solution)/shard_map/ppermute | solution.py:289
  25.1 1.2 %collective-permute-start.11 = (bf16[144,256]{1,0:T(8,128)(2,1)S(1)}, bf16[144,256]{1,0:T(8,128)(2,1)S(1)}, u32[]{:S(2)}, u32[]{:S(2)}) collective-permute-start(bf16[144,256]{1,0:T(8,128)(2,1)S(1)} %get-tuple-element.65), channel_id=1, source_target_pairs={{0,8},{8,0},{16,24},{24,16},{1,9},{9,1},{17,25},{25,17},{2,10},{10... | collective-permute-start | bytes 221192 | tf_op jit(solution)/shard_map/ppermute | solution.py:289
  26.4 0.2 collective-permute-done.9.rest_2_
  26.6 0.0 collective-permute-start.15
  26.6 0.3 %own.1 = (f32[384,256]{1,0:T(8,128)S(1)}, f32[12,256]{1,0:T(8,128)S(1)}) custom-call(bf16[272,256]{1,0:T(8,128)(2,1)S(1)} %collective-permute-done.near.rest_0_, bf16[272,256]{1,0:T(8,128)(2,1)S(1)} %collective-permute-done.1.message.far.rest_1_, bf16[272,256]{1,0:T(8,128)(2,1)S(1)} %collective-permute-done.2.rest_0_.rest_1_.rest_2_, ...), custom_call_target="tpu_custom_call" | custom-call | flops 1000000000 | bytes 2097152 | tf_op jit(solution)/shard_map/own/pallas_call | solution.py:491
  26.9 1.7 %collective-permute-done.13.rest_4_.rest_1_ = bf16[256,256]{1,0:T(8,128)(2,1)S(1)} collective-permute-done((bf16[256,256]{1,0:T(8,128)(2,1)S(1)}, bf16[256,256]{1,0:T(8,128)(2,1)S(1)}, u32[]{:S(2)}, u32[]{:S(2)}) %collective-permute-start.13) | collective-permute-done | bytes 131104 | tf_op jit(solution)/shard_map/ppermute | solution.py:289
  28.6 0.5 %collective-permute-done.14.rest_5_.rest_0_ = bf16[256,256]{1,0:T(8,128)(2,1)S(1)} collective-permute-done((bf16[256,256]{1,0:T(8,128)(2,1)S(1)}, bf16[256,256]{1,0:T(8,128)(2,1)S(1)}, u32[]{:S(2)}, u32[]{:S(2)}) %collective-permute-start.14) | collective-permute-done | bytes 131104 | tf_op jit(solution)/shard_map/ppermute | solution.py:289
  29.1 0.1 collective-permute-start.16
  29.2 0.9 %collective-permute-done.12.rest_1_ = bf16[128,256]{1,0:T(8,128)(2,1)S(1)} collective-permute-done((bf16[128,256]{1,0:T(8,128)(2,1)S(1)}, bf16[128,256]{1,0:T(8,128)(2,1)S(1)}, u32[]{:S(2)}, u32[]{:S(2)}) %collective-permute-start.12) | collective-permute-done | bytes 65568 | tf_op jit(solution)/shard_map/ppermute | solution.py:289
  30.2 0.0 collective-permute-done.11.rest_0_
  30.2 0.2 add.1.total
  30.4 0.0 collective-permute-done.15.rest_0_
  30.4 0.1 collective-permute-done.16.rest_1_
  30.6 0.8 %final.1 = bf16[384,256]{1,0:T(8,128)(2,1)} custom-call(f32[12,256]{1,0:T(8,128)S(1)} %get-tuple-element.63.owner, f32[384,256]{1,0:T(8,128)S(1)} %add.1.total, bf16[256,256]{1,0:T(8,128)(2,1)S(1)} %collective-permute-done.15.rest_0_, bf16[256,256]{1,0:T(8,128)(2,1)S(1)} %collective-permute-done.16.rest_1_), custom_call_target="tpu_custom_call" | custom-call | flops 393216 | bytes 1048576 | tf_op jit(solution)/shard_map/final/pallas_call | solution.py:521
  (3 shorter events, 0.0 us)
Async XLA Ops:
  0.9 10.9 %collective-permute-start.1 = (bf16[272,256]{1,0:T(8,128)(2,1)S(1)}, bf16[272,256]{1,0:T(8,128)(2,1)S(1)}, u32[]{:S(2)}, u32[]{:S(2)}) collective-permute-start(bf16[272,256]{1,0:T(8,128)(2,1)S(1)} %get-tuple-element.38.rest_0_), channel_id=1, source_target_pairs={{0,16},{8,24},{16,0},{24,8},{1,17},{9,25},{17,1},{25,9},{2,18},{10... | collective-permute-start | bytes 417800 | tf_op jit(solution)/shard_map/ppermute | solution.py:289
  5.0 7.0 %collective-permute-start = (bf16[272,256]{1,0:T(8,128)(2,1)S(1)}, bf16[272,256]{1,0:T(8,128)(2,1)S(1)}, u32[]{:S(2)}, u32[]{:S(2)}) collective-permute-start(bf16[272,256]{1,0:T(8,128)(2,1)S(1)} %get-tuple-element.38.rest_0_), channel_id=1, source_target_pairs={{0,8},{8,0},{16,24},{24,16},{1,9},{9,1},{17,25},{25,17},{2,10},{10... | collective-permute-start | bytes 417800 | tf_op jit(solution)/shard_map/ppermute | solution.py:289
  6.6 8.2 %collective-permute-start.4 = (bf16[272,256]{1,0:T(8,128)(2,1)S(1)}, bf16[272,256]{1,0:T(8,128)(2,1)S(1)}, u32[]{:S(2)}, u32[]{:S(2)}) collective-permute-start(bf16[272,256]{1,0:T(8,128)(2,1)S(1)} %get-tuple-element.38.rest_0_), channel_id=1, source_target_pairs={{0,6},{1,7},{2,4},{3,5},{4,2},{5,3},{6,0},{7,1},{8,14},{9,15},{10,... | collective-permute-start | bytes 417800 | tf_op jit(solution)/shard_map/ppermute | solution.py:289
  9.0 6.3 %collective-permute-start.3 = (bf16[272,256]{1,0:T(8,128)(2,1)S(1)}, bf16[272,256]{1,0:T(8,128)(2,1)S(1)}, u32[]{:S(2)}, u32[]{:S(2)}) collective-permute-start(bf16[272,256]{1,0:T(8,128)(2,1)S(1)} %get-tuple-element.38.rest_0_), channel_id=1, source_target_pairs={{0,4},{1,5},{2,6},{3,7},{4,0},{5,1},{6,2},{7,3},{8,12},{9,13},{10,... | collective-permute-start | bytes 417800 | tf_op jit(solution)/shard_map/ppermute | solution.py:289
  9.5 5.8 %collective-permute-start.2 = (bf16[272,256]{1,0:T(8,128)(2,1)S(1)}, bf16[272,256]{1,0:T(8,128)(2,1)S(1)}, u32[]{:S(2)}, u32[]{:S(2)}) collective-permute-start(bf16[272,256]{1,0:T(8,128)(2,1)S(1)} %get-tuple-element.38.rest_0_), channel_id=1, source_target_pairs={{0,2},{1,3},{2,0},{3,1},{4,6},{5,7},{6,4},{7,5},{8,10},{9,11},{10,... | collective-permute-start | bytes 417800 | tf_op jit(solution)/shard_map/ppermute | solution.py:289
  12.1 4.8 %collective-permute-start.8 = (bf16[128,256]{1,0:T(8,128)(2,1)S(1)}, bf16[128,256]{1,0:T(8,128)(2,1)S(1)}, u32[]{:S(2)}, u32[]{:S(2)}) collective-permute-start(bf16[128,256]{1,0:T(8,128)(2,1)S(1)} %relay.1), channel_id=1, source_target_pairs={{0,8},{8,0},{16,24},{24,16},{1,9},{9,1},{17,25},{25,17},{2,10},{10... | collective-permute-start | bytes 196616 | tf_op jit(solution)/shard_map/ppermute | solution.py:289
  13.6 1.2 %collective-permute-start.5 = (bf16[16,256]{1,0:T(8,128)(2,1)S(1)}, bf16[16,256]{1,0:T(8,128)(2,1)S(1)}, u32[]{:S(2)}, u32[]{:S(2)}) collective-permute-start(bf16[16,256]{1,0:T(8,128)(2,1)S(1)} %get-tuple-element.40), channel_id=1, source_target_pairs={{0,1},{1,0},{2,3},{3,2},{4,5},{5,4},{6,7},{7,6},{8,9},{9,8},{10,11... | collective-permute-start | bytes 24584 | tf_op jit(solution)/shard_map/ppermute | solution.py:289
  15.5 1.5 %collective-permute-start.6 = (bf16[288,256]{1,0:T(8,128)(2,1)S(1)}, bf16[288,256]{1,0:T(8,128)(2,1)S(1)}, u32[]{:S(2)}, u32[]{:S(2)}) collective-permute-start(bf16[288,256]{1,0:T(8,128)(2,1)S(1)} %trade2.1), channel_id=1, source_target_pairs={{0,1},{1,0},{2,3},{3,2},{4,5},{5,4},{6,7},{7,6},{8,9},{9,8},{10,11... | collective-permute-start | bytes 442376 | tf_op jit(solution)/shard_map/ppermute | solution.py:289
  15.6 1.6 %collective-permute-start.7 = (bf16[288,256]{1,0:T(8,128)(2,1)S(1)}, bf16[288,256]{1,0:T(8,128)(2,1)S(1)}, u32[]{:S(2)}, u32[]{:S(2)}) collective-permute-start(bf16[288,256]{1,0:T(8,128)(2,1)S(1)} %trade.1), channel_id=1, source_target_pairs={{0,1},{1,0},{2,3},{3,2},{4,5},{5,4},{6,7},{7,6},{8,9},{9,8},{10,11... | collective-permute-start | bytes 442376 | tf_op jit(solution)/shard_map/ppermute | solution.py:289
  18.4 6.7 %collective-permute-start.10 = (bf16[256,256]{1,0:T(8,128)(2,1)S(1)}, bf16[256,256]{1,0:T(8,128)(2,1)S(1)}, u32[]{:S(2)}, u32[]{:S(2)}) collective-permute-start(bf16[256,256]{1,0:T(8,128)(2,1)S(1)} %get-tuple-element.58), channel_id=1, source_target_pairs={{0,6},{1,7},{2,4},{3,5},{4,2},{5,3},{6,0},{7,1},{8,14},{9,15},{10,... | collective-permute-start | bytes 393224 | tf_op jit(solution)/shard_map/ppermute | solution.py:289
  20.5 6.1 %collective-permute-start.9 = (bf16[128,256]{1,0:T(8,128)(2,1)S(1)}, bf16[128,256]{1,0:T(8,128)(2,1)S(1)}, u32[]{:S(2)}, u32[]{:S(2)}) collective-permute-start(bf16[128,256]{1,0:T(8,128)(2,1)S(1)} %get-tuple-element.56), channel_id=1, source_target_pairs={{0,24},{8,16},{16,8},{24,0},{1,25},{9,17},{17,9},{25,1},{2,26},{10... | collective-permute-start | bytes 196616 | tf_op jit(solution)/shard_map/ppermute | solution.py:289
  23.6 5.0 %collective-permute-start.13 = (bf16[256,256]{1,0:T(8,128)(2,1)S(1)}, bf16[256,256]{1,0:T(8,128)(2,1)S(1)}, u32[]{:S(2)}, u32[]{:S(2)}) collective-permute-start(bf16[256,256]{1,0:T(8,128)(2,1)S(1)} %get-tuple-element.67), channel_id=1, source_target_pairs={{0,4},{1,5},{2,6},{3,7},{4,0},{5,1},{6,2},{7,3},{8,12},{9,13},{10,... | collective-permute-start | bytes 393224 | tf_op jit(solution)/shard_map/ppermute | solution.py:289
  24.2 5.0 %collective-permute-start.14 = (bf16[256,256]{1,0:T(8,128)(2,1)S(1)}, bf16[256,256]{1,0:T(8,128)(2,1)S(1)}, u32[]{:S(2)}, u32[]{:S(2)}) collective-permute-start(bf16[256,256]{1,0:T(8,128)(2,1)S(1)} %get-tuple-element.68), channel_id=1, source_target_pairs={{0,2},{1,3},{2,0},{3,1},{4,6},{5,7},{6,4},{7,5},{8,10},{9,11},{10,... | collective-permute-start | bytes 393224 | tf_op jit(solution)/shard_map/ppermute | solution.py:289
  24.7 5.5 %collective-permute-start.12 = (bf16[128,256]{1,0:T(8,128)(2,1)S(1)}, bf16[128,256]{1,0:T(8,128)(2,1)S(1)}, u32[]{:S(2)}, u32[]{:S(2)}) collective-permute-start(bf16[128,256]{1,0:T(8,128)(2,1)S(1)} %get-tuple-element.66), channel_id=1, source_target_pairs={{0,16},{8,24},{16,0},{24,8},{1,17},{9,25},{17,1},{25,9},{2,18},{10... | collective-permute-start | bytes 196616 | tf_op jit(solution)/shard_map/ppermute | solution.py:289
  25.1 5.1 %collective-permute-start.11 = (bf16[144,256]{1,0:T(8,128)(2,1)S(1)}, bf16[144,256]{1,0:T(8,128)(2,1)S(1)}, u32[]{:S(2)}, u32[]{:S(2)}) collective-permute-start(bf16[144,256]{1,0:T(8,128)(2,1)S(1)} %get-tuple-element.65), channel_id=1, source_target_pairs={{0,8},{8,0},{16,24},{24,16},{1,9},{9,1},{17,25},{25,17},{2,10},{10... | collective-permute-start | bytes 221192 | tf_op jit(solution)/shard_map/ppermute | solution.py:289
  26.6 3.8 %collective-permute-start.15 = (bf16[256,256]{1,0:T(8,128)(2,1)S(1)}, bf16[256,256]{1,0:T(8,128)(2,1)S(1)}, u32[]{:S(2)}, u32[]{:S(2)}) collective-permute-start(bf16[256,256]{1,0:T(8,128)(2,1)S(1)} %early.1), channel_id=1, source_target_pairs={{0,1},{1,0},{2,3},{3,2},{4,5},{5,4},{6,7},{7,6},{8,9},{9,8},{10,11... | collective-permute-start | bytes 393224 | tf_op jit(solution)/shard_map/ppermute | solution.py:289
  29.1 1.4 %collective-permute-start.16 = (bf16[256,256]{1,0:T(8,128)(2,1)S(1)}, bf16[256,256]{1,0:T(8,128)(2,1)S(1)}, u32[]{:S(2)}, u32[]{:S(2)}) collective-permute-start(bf16[256,256]{1,0:T(8,128)(2,1)S(1)} %turn.1), channel_id=1, source_target_pairs={{0,1},{1,0},{2,3},{3,2},{4,5},{5,4},{6,7},{7,6},{8,9},{9,8},{10,11... | collective-permute-start | bytes 393224 | tf_op jit(solution)/shard_map/ppermute | solution.py:289

commit v18 on v17

--- a/solution.py
+++ b/solution.py
@@ -416,6 +416,10 @@
             name=name,
         )(*operands, *arrays)
 
+    dense_t = call(
+        functools.partial(flip_kernel, size), jax.ShapeDtypeStruct((slots * size, rows), BF), "flip", 10**7,
+        after(dense, choice),
+    )
     carried = []
     for d in relayed:
         far = got[sub_count + d - 1][0]
@@ -425,7 +429,7 @@
         value = call(
             functools.partial(relay_kernel, sub_count, d - 1),
             block,
-            "relay", 10**6, far, far_rows, got[sub_count + 1][0],
+            "relay", 10**6, far, far_rows, after(got[sub_count + 1][0], dense_t),
         )
         carried.append(far_rows)
         relay_value = value
@@ -440,7 +444,7 @@
         trade_value = call(
             functools.partial(trade_kernel, traded),
             jax.ShapeDtypeStruct((len(traded) * (size + EXTRA), width), BF),
-            name, 10**6, *[got[d][0] for d in traded], after(sibling_rows, (choice, trade_value)),
+            name, 10**6 if name == 'trade' else 10**10, *[got[d][0] for d in traded], after(sibling_rows, (choice, trade_value)),
         )
         value = across(trade_value, 1)
         for i, d in enumerate(traded):
@@ -448,17 +452,13 @@
     near_sum = sum_call(
         near_kernel, wide, "near", [sub_count + 1, *even], after(choice, trade_value), dense, first_sum
     )
-    dense_t = call(
-        functools.partial(flip_kernel, size), jax.ShapeDtypeStruct((slots * size, rows), BF), "flip", 10**7,
-        after(dense, near_sum),
-    )
     if relayed:
-        slots_late = [sub_count + d for d in relayed]
+        slots_late = [*(sub_count + d for d in relayed), 1, even[-1] + 1]
         near_sum = sum_call(
-            near_kernel, wide, "late", slots_late, after(choice, dense_t), dense, near_sum
+            near_kernel, wide, "late", slots_late, choice, dense, near_sum
         )
 
-    late = [1, even[-1] + 1, *(d + 1 for d in even[:-1])]
+    late = [d + 1 for d in even[:-1]]
     late_arrays, late_at = unique(late)
     late_halos = [(slot, late_at[slot], got[slot][1], got[slot][2]) for slot in late]
     outs = pl.pallas_call(

time: 31.5 us -> 31.5 us (level)
  transfers between devices with their start and end apart: 17 -> 17, of which waited for: 12 -> 9; matrix products, arithmetic and copies ran while one was open for 0% -> 0% of each run, Pallas kernels for 13% -> 13%
where the time goes in v18:
time: 31.5 us; the launch traced here: 31.3 us
  starting transfers between devices  18.9 us (60%)
  Pallas kernels  6.88 us (22%)
  waiting for transfers between devices  5.43 us (17%)
    ppermute x17, starting transfers between devices, swap(): return lax.ppermute(value, axis, [(i, i ^ d) for i in range(count)])  18.9 us
    ppermute x17, waiting for transfers between devices, swap(): return lax.ppermute(value, axis, [(i, i ^ d) for i in range(count)])  5.43 us
    pallas_call x1, Pallas kernels, shards(): pl.pallas_call(functools.partial(prepare_kernel, *counts), out_shape=[jax...  1.63 us
    pallas_call x1, Pallas kernels, shards(): pl.pallas_call(functools.partial(middle_kernel, *counts, late_halos, len(...  1.21 us
    pallas_call x3, Pallas kernels, sum_call(): pl.pallas_call(functools.partial(kernel, own, halos), out_shape=out_shape...  1.04 us
    pallas_call x8, Pallas kernels, call(): pl.pallas_call(kernel, out_shape=out_shape, in_specs=[VMEM] * len(operand...  1.02 us
    pallas_call x1, Pallas kernels, shards(): pl.pallas_call(edge_kernel, out_shape=[jax.ShapeDtypeStruct((BOUNDARY * s...  0.89 us
    pallas_call x1, Pallas kernels, shards(): pl.pallas_call(functools.partial(final_kernel, own, parts), out_shape=nar...  0.78 us
  transfers between devices with their start and end apart: 17, of which 9 were waited for; matrix products, arithmetic and copies ran while one was open for 0% of the time, Pallas kernels for 13%

profile of v18, /device:TPU:0, one launch (start us, length us, event | category | flops | bytes accessed | tf_op | source)
XLA Modules:
  0.0 31.3 jit_solution(784339100970959836)
XLA Ops:
  0.0 0.9 %edge.1 = (bf16[272,256]{1,0:T(8,128)(2,1)S(1)}, bf16[16,256]{1,0:T(8,128)(2,1)S(1)}) custom-call(s32[1,8]{1,0:T(1,128)} %recv_sub_hbm.1, s32[1,4]{1,0:T(1,128)} %recv_cluster_hbm.1, bf16[384,256]{1,0:T(8,128)(2,1)} %features_hbm.1), custom_call_target="tpu_custom_call" | custom-call | flops 1024 | bytes 262144 | tf_op jit(solution)/shard_map/edge/pallas_call | solution.py:322
  0.9 4.1 %collective-permute-start.1 = (bf16[272,256]{1,0:T(8,128)(2,1)S(1)}, bf16[272,256]{1,0:T(8,128)(2,1)S(1)}, u32[]{:S(2)}, u32[]{:S(2)}) collective-permute-start(bf16[272,256]{1,0:T(8,128)(2,1)S(1)} %get-tuple-element.38.rest_0_), channel_id=1, source_target_pairs={{0,16},{8,24},{16,0},{24,8},{1,17},{9,25},{17,1},{25,9},{2,18},{10... | collective-permute-start | bytes 417800 | tf_op jit(solution)/shard_map/ppermute | solution.py:289
  5.0 1.6 %collective-permute-start = (bf16[272,256]{1,0:T(8,128)(2,1)S(1)}, bf16[272,256]{1,0:T(8,128)(2,1)S(1)}, u32[]{:S(2)}, u32[]{:S(2)}) collective-permute-start(bf16[272,256]{1,0:T(8,128)(2,1)S(1)} %get-tuple-element.38.rest_0_), channel_id=1, source_target_pairs={{0,8},{8,0},{16,24},{24,16},{1,9},{9,1},{17,25},{25,17},{2,10},{10... | collective-permute-start | bytes 417800 | tf_op jit(solution)/shard_map/ppermute | solution.py:289
  6.6 2.4 %collective-permute-start.4 = (bf16[272,256]{1,0:T(8,128)(2,1)S(1)}, bf16[272,256]{1,0:T(8,128)(2,1)S(1)}, u32[]{:S(2)}, u32[]{:S(2)}) collective-permute-start(bf16[272,256]{1,0:T(8,128)(2,1)S(1)} %get-tuple-element.38.rest_0_), channel_id=1, source_target_pairs={{0,6},{1,7},{2,4},{3,5},{4,2},{5,3},{6,0},{7,1},{8,14},{9,15},{10,... | collective-permute-start | bytes 417800 | tf_op jit(solution)/shard_map/ppermute | solution.py:289
  9.0 0.5 %collective-permute-start.3 = (bf16[272,256]{1,0:T(8,128)(2,1)S(1)}, bf16[272,256]{1,0:T(8,128)(2,1)S(1)}, u32[]{:S(2)}, u32[]{:S(2)}) collective-permute-start(bf16[272,256]{1,0:T(8,128)(2,1)S(1)} %get-tuple-element.38.rest_0_), channel_id=1, source_target_pairs={{0,4},{1,5},{2,6},{3,7},{4,0},{5,1},{6,2},{7,3},{8,12},{9,13},{10,... | collective-permute-start | bytes 417800 | tf_op jit(solution)/shard_map/ppermute | solution.py:289
  9.5 0.5 %collective-permute-start.2 = (bf16[272,256]{1,0:T(8,128)(2,1)S(1)}, bf16[272,256]{1,0:T(8,128)(2,1)S(1)}, u32[]{:S(2)}, u32[]{:S(2)}) collective-permute-start(bf16[272,256]{1,0:T(8,128)(2,1)S(1)} %get-tuple-element.38.rest_0_), channel_id=1, source_target_pairs={{0,2},{1,3},{2,0},{3,1},{4,6},{5,7},{6,4},{7,5},{8,10},{9,11},{10,... | collective-permute-start | bytes 417800 | tf_op jit(solution)/shard_map/ppermute | solution.py:289
  10.1 1.6 %prepare.1 = (bf16[384,1920]{1,0:T(8,128)(2,1)S(1)}, f32[12,256]{1,0:T(8,128)S(1)}, bf16[384,256]{1,0:T(8,128)(2,1)S(1)}, bf16[256,256]{1,0:T(8,128)(2,1)S(1)}, ...) custom-call(s32[24]{0:T(128)} %tile_dst_hbm.1, s32[24]{0:T(128)} %tile_src_hbm.1, ...), custom_call_target="tpu_custom_call" | custom-call | flops 100000000 | bytes 6291456 | tf_op jit(solution)/shard_map/prepare/pallas_call | solution.py:356
  11.7 0.4 %flip.1.dense_t.rest_9_ = bf16[1920,384]{1,0:T(8,128)(2,1)S(1)} custom-call(bf16[384,1920]{1,0:T(8,128)(2,1)S(1)} %get-tuple-element.42.dense), custom_call_target="tpu_custom_call" | custom-call | flops 10000000 | bytes 1048576 | tf_op jit(solution)/shard_map/flip/pallas_call | solution.py:386
  12.1 0.0 collective-permute-done.1.message.far.rest_1_
  12.2 0.0 collective-permute-done.near.rest_0_
  12.2 0.1 relay.1
  12.3 1.3 %collective-permute-start.8 = (bf16[128,256]{1,0:T(8,128)(2,1)S(1)}, bf16[128,256]{1,0:T(8,128)(2,1)S(1)}, u32[]{:S(2)}, u32[]{:S(2)}) collective-permute-start(bf16[128,256]{1,0:T(8,128)(2,1)S(1)} %relay.1), channel_id=1, source_target_pairs={{0,8},{8,0},{16,24},{24,16},{1,9},{9,1},{17,25},{25,17},{2,10},{10... | collective-permute-start | bytes 196616 | tf_op jit(solution)/shard_map/ppermute | solution.py:289
  13.6 0.0 collective-permute-start.5
  13.6 0.5 %first.1 = (f32[384,256]{1,0:T(8,128)S(1)}, f32[384,256]{1,0:T(8,128)S(1)}, f32[384,128]{1,0:T(8,128)S(1)}) custom-call(f32[12,256]{1,0:T(8,128)S(1)} %get-tuple-element.59.choice.rest_7_, bf16[384,1920]{1,0:T(8,128)(2,1)S(1)} %get-tuple-element.42.dense, bf16[384,256]{1,0:T(8,128)(2,1)S(1)} %get-tuple-element.50.features, ...), custom_call_target="tpu_custom_call" | custom-call | flops 1000000000 | bytes 3145728 | tf_op jit(solution)/shard_map/first/pallas_call | solution.py:408
  14.1 0.7 %collective-permute-done.5.rest_2_ = bf16[16,256]{1,0:T(8,128)(2,1)S(1)} collective-permute-done((bf16[16,256]{1,0:T(8,128)(2,1)S(1)}, bf16[16,256]{1,0:T(8,128)(2,1)S(1)}, u32[]{:S(2)}, u32[]{:S(2)}) %collective-permute-start.5) | collective-permute-done | bytes 8224 | tf_op jit(solution)/shard_map/ppermute | solution.py:289
  14.8 0.0 collective-permute-done.4.rest_1_.rest_3_.rest_4_
  14.8 0.1 trade.1
  14.9 0.2 collective-permute-start.7
  15.1 0.2 collective-permute-done.3.rest_1_.rest_2_.rest_3_
  15.3 0.1 collective-permute-done.2.rest_0_.rest_1_.rest_2_
  15.4 0.1 trade2.1
  15.5 0.2 collective-permute-start.6
  15.7 0.3 near.1.before
  16.0 0.6 %collective-permute-done.8.rest_0_ = bf16[128,256]{1,0:T(8,128)(2,1)S(1)} collective-permute-done((bf16[128,256]{1,0:T(8,128)(2,1)S(1)}, bf16[128,256]{1,0:T(8,128)(2,1)S(1)}, u32[]{:S(2)}, u32[]{:S(2)}) %collective-permute-start.8) | collective-permute-done | bytes 65568 | tf_op jit(solution)/shard_map/ppermute | solution.py:289
  16.6 0.0 collective-permute-done.7.rest_1_.rest_6_
  16.6 0.3 late.1.before
  16.9 0.0 collective-permute-done.6.rest_0_.rest_5_
  16.9 1.2 %middle.1 = (bf16[256,256]{1,0:T(8,128)(2,1)S(1)}, bf16[256,256]{1,0:T(8,128)(2,1)S(1)}, bf16[256,256]{1,0:T(8,128)(2,1)S(1)}, bf16[144,256]{1,0:T(8,128)(2,1)S(...) custom-call(f32[12,256]{1,0:T(8,128)S(1)} %get-tuple-element.59.choi, ...), custom_call_target="tpu_custom_call" | custom-call | flops 377487360 | bytes 6291456 | tf_op jit(solution)/shard_map/middle/pallas_call | solution.py:464
  18.2 2.5 %collective-permute-start.10 = (bf16[256,256]{1,0:T(8,128)(2,1)S(1)}, bf16[256,256]{1,0:T(8,128)(2,1)S(1)}, u32[]{:S(2)}, u32[]{:S(2)}) collective-permute-start(bf16[256,256]{1,0:T(8,128)(2,1)S(1)} %get-tuple-element.58), channel_id=1, source_target_pairs={{0,6},{1,7},{2,4},{3,5},{4,2},{5,3},{6,0},{7,1},{8,14},{9,15},{10,... | collective-permute-start | bytes 393224 | tf_op jit(solution)/shard_map/ppermute | solution.py:289
  20.6 3.0 %collective-permute-start.9 = (bf16[128,256]{1,0:T(8,128)(2,1)S(1)}, bf16[128,256]{1,0:T(8,128)(2,1)S(1)}, u32[]{:S(2)}, u32[]{:S(2)}) collective-permute-start(bf16[128,256]{1,0:T(8,128)(2,1)S(1)} %get-tuple-element.56), channel_id=1, source_target_pairs={{0,24},{8,16},{16,8},{24,0},{1,25},{9,17},{17,9},{25,1},{2,26},{10... | collective-permute-start | bytes 196616 | tf_op jit(solution)/shard_map/ppermute | solution.py:289
  23.6 0.5 %collective-permute-start.13 = (bf16[256,256]{1,0:T(8,128)(2,1)S(1)}, bf16[256,256]{1,0:T(8,128)(2,1)S(1)}, u32[]{:S(2)}, u32[]{:S(2)}) collective-permute-start(bf16[256,256]{1,0:T(8,128)(2,1)S(1)} %get-tuple-element.67), channel_id=1, source_target_pairs={{0,4},{1,5},{2,6},{3,7},{4,0},{5,1},{6,2},{7,3},{8,12},{9,13},{10,... | collective-permute-start | bytes 393224 | tf_op jit(solution)/shard_map/ppermute | solution.py:289
  24.2 0.5 %collective-permute-start.14 = (bf16[256,256]{1,0:T(8,128)(2,1)S(1)}, bf16[256,256]{1,0:T(8,128)(2,1)S(1)}, u32[]{:S(2)}, u32[]{:S(2)}) collective-permute-start(bf16[256,256]{1,0:T(8,128)(2,1)S(1)} %get-tuple-element.68), channel_id=1, source_target_pairs={{0,2},{1,3},{2,0},{3,1},{4,6},{5,7},{6,4},{7,5},{8,10},{9,11},{10,... | collective-permute-start | bytes 393224 | tf_op jit(solution)/shard_map/ppermute | solution.py:289
  24.7 0.0 collective-permute-start.12
  24.7 0.0 collective-permute-done.10.rest_1_.rest_3_
  24.7 1.4 %collective-permute-start.11 = (bf16[144,256]{1,0:T(8,128)(2,1)S(1)}, bf16[144,256]{1,0:T(8,128)(2,1)S(1)}, u32[]{:S(2)}, u32[]{:S(2)}) collective-permute-start(bf16[144,256]{1,0:T(8,128)(2,1)S(1)} %get-tuple-element.65), channel_id=1, source_target_pairs={{0,8},{8,0},{16,24},{24,16},{1,9},{9,1},{17,25},{25,17},{2,10},{10... | collective-permute-start | bytes 221192 | tf_op jit(solution)/shard_map/ppermute | solution.py:289
  26.1 0.8 %collective-permute-done.9.rest_2_ = bf16[128,256]{1,0:T(8,128)(2,1)S(1)} collective-permute-done((bf16[128,256]{1,0:T(8,128)(2,1)S(1)}, bf16[128,256]{1,0:T(8,128)(2,1)S(1)}, u32[]{:S(2)}, u32[]{:S(2)}) %collective-permute-start.9) | collective-permute-done | bytes 65568 | tf_op jit(solution)/shard_map/ppermute | solution.py:289
  27.0 0.0 collective-permute-start.15
  27.0 0.3 own.1
  27.3 1.3 %collective-permute-done.13.rest_4_.rest_1_ = bf16[256,256]{1,0:T(8,128)(2,1)S(1)} collective-permute-done((bf16[256,256]{1,0:T(8,128)(2,1)S(1)}, bf16[256,256]{1,0:T(8,128)(2,1)S(1)}, u32[]{:S(2)}, u32[]{:S(2)}) %collective-permute-start.13) | collective-permute-done | bytes 131104 | tf_op jit(solution)/shard_map/ppermute | solution.py:289
  28.6 0.5 %collective-permute-done.14.rest_5_.rest_0_ = bf16[256,256]{1,0:T(8,128)(2,1)S(1)} collective-permute-done((bf16[256,256]{1,0:T(8,128)(2,1)S(1)}, bf16[256,256]{1,0:T(8,128)(2,1)S(1)}, u32[]{:S(2)}, u32[]{:S(2)}) %collective-permute-start.14) | collective-permute-done | bytes 131104 | tf_op jit(solution)/shard_map/ppermute | solution.py:289
  29.1 0.1 collective-permute-start.16
  29.2 0.8 %collective-permute-done.12.rest_1_ = bf16[128,256]{1,0:T(8,128)(2,1)S(1)} collective-permute-done((bf16[128,256]{1,0:T(8,128)(2,1)S(1)}, bf16[128,256]{1,0:T(8,128)(2,1)S(1)}, u32[]{:S(2)}, u32[]{:S(2)}) %collective-permute-start.12) | collective-permute-done | bytes 65568 | tf_op jit(solution)/shard_map/ppermute | solution.py:289
  30.0 0.0 collective-permute-done.11.rest_0_
  30.0 0.2 add.1.total
  30.2 0.0 collective-permute-done.15.rest_0_
  30.2 0.3 %collective-permute-done.16.rest_1_ = bf16[256,256]{1,0:T(8,128)(2,1)S(1)} collective-permute-done((bf16[256,256]{1,0:T(8,128)(2,1)S(1)}, bf16[256,256]{1,0:T(8,128)(2,1)S(1)}, u32[]{:S(2)}, u32[]{:S(2)}) %collective-permute-start.16) | collective-permute-done | bytes 131104 | tf_op jit(solution)/shard_map/ppermute | solution.py:289
  30.6 0.8 %final.1 = bf16[384,256]{1,0:T(8,128)(2,1)} custom-call(f32[12,256]{1,0:T(8,128)S(1)} %get-tuple-element.63.owner, f32[384,256]{1,0:T(8,128)S(1)} %add.1.total, bf16[256,256]{1,0:T(8,128)(2,1)S(1)} %collective-permute-done.15.rest_0_, bf16[256,256]{1,0:T(8,128)(2,1)S(1)} %collective-permute-done.16.rest_1_), custom_call_target="tpu_custom_call" | custom-call | flops 393216 | bytes 1048576 | tf_op jit(solution)/shard_map/final/pallas_call | solution.py:521
  (3 shorter events, 0.0 us)
Async XLA Ops:
  0.9 11.2 %collective-permute-start.1 = (bf16[272,256]{1,0:T(8,128)(2,1)S(1)}, bf16[272,256]{1,0:T(8,128)(2,1)S(1)}, u32[]{:S(2)}, u32[]{:S(2)}) collective-permute-start(bf16[272,256]{1,0:T(8,128)(2,1)S(1)} %get-tuple-element.38.rest_0_), channel_id=1, source_target_pairs={{0,16},{8,24},{16,0},{24,8},{1,17},{9,25},{17,1},{25,9},{2,18},{10... | collective-permute-start | bytes 417800 | tf_op jit(solution)/shard_map/ppermute | solution.py:289
  5.0 7.2 %collective-permute-start = (bf16[272,256]{1,0:T(8,128)(2,1)S(1)}, bf16[272,256]{1,0:T(8,128)(2,1)S(1)}, u32[]{:S(2)}, u32[]{:S(2)}) collective-permute-start(bf16[272,256]{1,0:T(8,128)(2,1)S(1)} %get-tuple-element.38.rest_0_), channel_id=1, source_target_pairs={{0,8},{8,0},{16,24},{24,16},{1,9},{9,1},{17,25},{25,17},{2,10},{10... | collective-permute-start | bytes 417800 | tf_op jit(solution)/shard_map/ppermute | solution.py:289
  6.6 8.2 %collective-permute-start.4 = (bf16[272,256]{1,0:T(8,128)(2,1)S(1)}, bf16[272,256]{1,0:T(8,128)(2,1)S(1)}, u32[]{:S(2)}, u32[]{:S(2)}) collective-permute-start(bf16[272,256]{1,0:T(8,128)(2,1)S(1)} %get-tuple-element.38.rest_0_), channel_id=1, source_target_pairs={{0,6},{1,7},{2,4},{3,5},{4,2},{5,3},{6,0},{7,1},{8,14},{9,15},{10,... | collective-permute-start | bytes 417800 | tf_op jit(solution)/shard_map/ppermute | solution.py:289
  9.0 6.3 %collective-permute-start.3 = (bf16[272,256]{1,0:T(8,128)(2,1)S(1)}, bf16[272,256]{1,0:T(8,128)(2,1)S(1)}, u32[]{:S(2)}, u32[]{:S(2)}) collective-permute-start(bf16[272,256]{1,0:T(8,128)(2,1)S(1)} %get-tuple-element.38.rest_0_), channel_id=1, source_target_pairs={{0,4},{1,5},{2,6},{3,7},{4,0},{5,1},{6,2},{7,3},{8,12},{9,13},{10,... | collective-permute-start | bytes 417800 | tf_op jit(solution)/shard_map/ppermute | solution.py:289
  9.5 5.8 %collective-permute-start.2 = (bf16[272,256]{1,0:T(8,128)(2,1)S(1)}, bf16[272,256]{1,0:T(8,128)(2,1)S(1)}, u32[]{:S(2)}, u32[]{:S(2)}) collective-permute-start(bf16[272,256]{1,0:T(8,128)(2,1)S(1)} %get-tuple-element.38.rest_0_), channel_id=1, source_target_pairs={{0,2},{1,3},{2,0},{3,1},{4,6},{5,7},{6,4},{7,5},{8,10},{9,11},{10,... | collective-permute-start | bytes 417800 | tf_op jit(solution)/shard_map/ppermute | solution.py:289
  12.3 4.3 %collective-permute-start.8 = (bf16[128,256]{1,0:T(8,128)(2,1)S(1)}, bf16[128,256]{1,0:T(8,128)(2,1)S(1)}, u32[]{:S(2)}, u32[]{:S(2)}) collective-permute-start(bf16[128,256]{1,0:T(8,128)(2,1)S(1)} %relay.1), channel_id=1, source_target_pairs={{0,8},{8,0},{16,24},{24,16},{1,9},{9,1},{17,25},{25,17},{2,10},{10... | collective-permute-start | bytes 196616 | tf_op jit(solution)/shard_map/ppermute | solution.py:289
  13.6 1.2 %collective-permute-start.5 = (bf16[16,256]{1,0:T(8,128)(2,1)S(1)}, bf16[16,256]{1,0:T(8,128)(2,1)S(1)}, u32[]{:S(2)}, u32[]{:S(2)}) collective-permute-start(bf16[16,256]{1,0:T(8,128)(2,1)S(1)} %get-tuple-element.44), channel_id=1, source_target_pairs={{0,1},{1,0},{2,3},{3,2},{4,5},{5,4},{6,7},{7,6},{8,9},{9,8},{10,11... | collective-permute-start | bytes 24584 | tf_op jit(solution)/shard_map/ppermute | solution.py:289
  14.9 1.7 %collective-permute-start.7 = (bf16[288,256]{1,0:T(8,128)(2,1)S(1)}, bf16[288,256]{1,0:T(8,128)(2,1)S(1)}, u32[]{:S(2)}, u32[]{:S(2)}) collective-permute-start(bf16[288,256]{1,0:T(8,128)(2,1)S(1)} %trade.1), channel_id=1, source_target_pairs={{0,1},{1,0},{2,3},{3,2},{4,5},{5,4},{6,7},{7,6},{8,9},{9,8},{10,11... | collective-permute-start | bytes 442376 | tf_op jit(solution)/shard_map/ppermute | solution.py:289
  15.5 1.4 %collective-permute-start.6 = (bf16[288,256]{1,0:T(8,128)(2,1)S(1)}, bf16[288,256]{1,0:T(8,128)(2,1)S(1)}, u32[]{:S(2)}, u32[]{:S(2)}) collective-permute-start(bf16[288,256]{1,0:T(8,128)(2,1)S(1)} %trade2.1), channel_id=1, source_target_pairs={{0,1},{1,0},{2,3},{3,2},{4,5},{5,4},{6,7},{7,6},{8,9},{9,8},{10,11... | collective-permute-start | bytes 442376 | tf_op jit(solution)/shard_map/ppermute | solution.py:289
  18.2 6.6 %collective-permute-start.10 = (bf16[256,256]{1,0:T(8,128)(2,1)S(1)}, bf16[256,256]{1,0:T(8,128)(2,1)S(1)}, u32[]{:S(2)}, u32[]{:S(2)}) collective-permute-start(bf16[256,256]{1,0:T(8,128)(2,1)S(1)} %get-tuple-element.58), channel_id=1, source_target_pairs={{0,6},{1,7},{2,4},{3,5},{4,2},{5,3},{6,0},{7,1},{8,14},{9,15},{10,... | collective-permute-start | bytes 393224 | tf_op jit(solution)/shard_map/ppermute | solution.py:289
  20.6 6.3 %collective-permute-start.9 = (bf16[128,256]{1,0:T(8,128)(2,1)S(1)}, bf16[128,256]{1,0:T(8,128)(2,1)S(1)}, u32[]{:S(2)}, u32[]{:S(2)}) collective-permute-start(bf16[128,256]{1,0:T(8,128)(2,1)S(1)} %get-tuple-element.56), channel_id=1, source_target_pairs={{0,24},{8,16},{16,8},{24,0},{1,25},{9,17},{17,9},{25,1},{2,26},{10... | collective-permute-start | bytes 196616 | tf_op jit(solution)/shard_map/ppermute | solution.py:289
  23.6 5.0 %collective-permute-start.13 = (bf16[256,256]{1,0:T(8,128)(2,1)S(1)}, bf16[256,256]{1,0:T(8,128)(2,1)S(1)}, u32[]{:S(2)}, u32[]{:S(2)}) collective-permute-start(bf16[256,256]{1,0:T(8,128)(2,1)S(1)} %get-tuple-element.67), channel_id=1, source_target_pairs={{0,4},{1,5},{2,6},{3,7},{4,0},{5,1},{6,2},{7,3},{8,12},{9,13},{10,... | collective-permute-start | bytes 393224 | tf_op jit(solution)/shard_map/ppermute | solution.py:289
  24.2 5.0 %collective-permute-start.14 = (bf16[256,256]{1,0:T(8,128)(2,1)S(1)}, bf16[256,256]{1,0:T(8,128)(2,1)S(1)}, u32[]{:S(2)}, u32[]{:S(2)}) collective-permute-start(bf16[256,256]{1,0:T(8,128)(2,1)S(1)} %get-tuple-element.68), channel_id=1, source_target_pairs={{0,2},{1,3},{2,0},{3,1},{4,6},{5,7},{6,4},{7,5},{8,10},{9,11},{10,... | collective-permute-start | bytes 393224 | tf_op jit(solution)/shard_map/ppermute | solution.py:289
  24.7 5.3 %collective-permute-start.12 = (bf16[128,256]{1,0:T(8,128)(2,1)S(1)}, bf16[128,256]{1,0:T(8,128)(2,1)S(1)}, u32[]{:S(2)}, u32[]{:S(2)}) collective-permute-start(bf16[128,256]{1,0:T(8,128)(2,1)S(1)} %get-tuple-element.66), channel_id=1, source_target_pairs={{0,16},{8,24},{16,0},{24,8},{1,17},{9,25},{17,1},{25,9},{2,18},{10... | collective-permute-start | bytes 196616 | tf_op jit(solution)/shard_map/ppermute | solution.py:289
  24.7 5.3 %collective-permute-start.11 = (bf16[144,256]{1,0:T(8,128)(2,1)S(1)}, bf16[144,256]{1,0:T(8,128)(2,1)S(1)}, u32[]{:S(2)}, u32[]{:S(2)}) collective-permute-start(bf16[144,256]{1,0:T(8,128)(2,1)S(1)} %get-tuple-element.65), channel_id=1, source_target_pairs={{0,8},{8,0},{16,24},{24,16},{1,9},{9,1},{17,25},{25,17},{2,10},{10... | collective-permute-start | bytes 221192 | tf_op jit(solution)/shard_map/ppermute | solution.py:289
  27.0 3.3 %collective-permute-start.15 = (bf16[256,256]{1,0:T(8,128)(2,1)S(1)}, bf16[256,256]{1,0:T(8,128)(2,1)S(1)}, u32[]{:S(2)}, u32[]{:S(2)}) collective-permute-start(bf16[256,256]{1,0:T(8,128)(2,1)S(1)} %early.1), channel_id=1, source_target_pairs={{0,1},{1,0},{2,3},{3,2},{4,5},{5,4},{6,7},{7,6},{8,9},{9,8},{10,11... | collective-permute-start | bytes 393224 | tf_op jit(solution)/shard_map/ppermute | solution.py:289
  29.1 1.4 %collective-permute-start.16 = (bf16[256,256]{1,0:T(8,128)(2,1)S(1)}, bf16[256,256]{1,0:T(8,128)(2,1)S(1)}, u32[]{:S(2)}, u32[]{:S(2)}) collective-permute-start(bf16[256,256]{1,0:T(8,128)(2,1)S(1)} %turn.1), channel_id=1, source_target_pairs={{0,1},{1,0},{2,3},{3,2},{4,5},{5,4},{6,7},{7,6},{8,9},{9,8},{10,11... | collective-permute-start | bytes 393224 | tf_op jit(solution)/shard_map/ppermute | solution.py:289

commit v19 on v12

--- a/solution.py
+++ b/solution.py
@@ -416,6 +416,10 @@
             name=name,
         )(*operands, *arrays)
 
+    dense_t = call(
+        functools.partial(flip_kernel, size), jax.ShapeDtypeStruct((slots * size, rows), BF), "flip", 10**7,
+        after(dense, choice),
+    )
     carried = []
     for d in relayed:
         far = got[sub_count + d - 1][0]
@@ -425,7 +429,7 @@
         value = call(
             functools.partial(relay_kernel, sub_count, d - 1),
             block,
-            "relay", 10**6, far, far_rows, got[sub_count + 1][0],
+            "relay", 10**6, far, far_rows, after(got[sub_count + 1][0], dense_t),
         )
         carried.append(far_rows)
         got[sub_count + d] = (along(value, 1), 0, True, None)
@@ -447,14 +451,10 @@
     near_sum = sum_call(
         near_kernel, wide, "near", [sub_count + 1, *even], after(choice, trade_value), dense, first_sum
     )
-    dense_t = call(
-        functools.partial(flip_kernel, size), jax.ShapeDtypeStruct((slots * size, rows), BF), "flip", 10**7,
-        after(dense, near_sum),
-    )
     if relayed:
         slots_late = [sub_count + d for d in relayed]
         near_sum = sum_call(
-            near_kernel, wide, "late", slots_late, after(choice, dense_t), dense, near_sum
+            near_kernel, wide, "late", slots_late, choice, dense, near_sum
         )
 
     late = [1, *(d + 1 for d in even)]
@@ -483,7 +483,7 @@
     soon, rest = near[-1:], near[:-1]
     early = call(
         turn_kernel, jax.ShapeDtypeStruct((2 * size, width), BF), "early", 10**8,
-        sibling, *[value for _, value in soon],
+        after(sibling, far[0][1]), *[value for _, value in soon],
     )
     order = [sub_count + 1, *(sub_count + d for d in direct), *even, *(d + 1 for d in even), 1]
     arrays, at = unique(order)

time: 31.5 us -> 32.3 us (1.025)
  starting transfers between devices: 18.5 us -> 19.7 us
  waiting for transfers between devices: 5.97 us -> 5.45 us
    ppermute x16, starting transfers between devices: 18.5 us -> 19.7 us  [swap(): return lax.ppermute(value, axis, [(i, i ^ d) for i in range(count)])]
    ppermute x16, waiting for transfers between devices: 5.97 us -> 5.45 us  [swap(): return lax.ppermute(value, axis, [(i, i ^ d) for i in range(count)])]
  transfers between devices with their start and end apart: 16 -> 16, of which waited for: 12 -> 9; matrix products, arithmetic and copies ran while one was open for 0% -> 0% of each run, Pallas kernels for 12% -> 12%
where the time goes in v19:
time: 32.3 us; the launch traced here: 32.1 us
  starting transfers between devices  19.7 us (61%)
  Pallas kernels  6.77 us (21%)
  waiting for transfers between devices  5.45 us (17%)
    ppermute x16, starting transfers between devices, swap(): return lax.ppermute(value, axis, [(i, i ^ d) for i in range(count)])  19.7 us
    ppermute x16, waiting for transfers between devices, swap(): return lax.ppermute(value, axis, [(i, i ^ d) for i in range(count)])  5.45 us
    pallas_call x1, Pallas kernels, shards(): pl.pallas_call(functools.partial(prepare_kernel, *counts), out_shape=[jax...  1.63 us
    pallas_call x1, Pallas kernels, shards(): pl.pallas_call(functools.partial(middle_kernel, *counts, late_halos, len(...  1.25 us
    pallas_call x3, Pallas kernels, sum_call(): pl.pallas_call(functools.partial(kernel, own, halos), out_shape=out_shape...  0.99 us
    pallas_call x7, Pallas kernels, call(): pl.pallas_call(kernel, out_shape=out_shape, in_specs=[VMEM] * len(operand...  0.93 us
    pallas_call x1, Pallas kernels, shards(): pl.pallas_call(edge_kernel, out_shape=[jax.ShapeDtypeStruct((BOUNDARY * s...  0.89 us
    pallas_call x1, Pallas kernels, shards(): pl.pallas_call(functools.partial(final_kernel, own, parts), out_shape=nar...  0.78 us
  transfers between devices with their start and end apart: 16, of which 9 were waited for; matrix products, arithmetic and copies ran while one was open for 0% of the time, Pallas kernels for 12%

profile of v19, /device:TPU:0, one launch (start us, length us, event | category | flops | bytes accessed | tf_op | source)
XLA Modules:
  0.0 32.1 jit_solution(10902512210045781219)
XLA Ops:
  0.0 0.9 %edge.1 = (bf16[272,256]{1,0:T(8,128)(2,1)S(1)}, bf16[16,256]{1,0:T(8,128)(2,1)S(1)}) custom-call(s32[1,8]{1,0:T(1,128)} %recv_sub_hbm.1, s32[1,4]{1,0:T(1,128)} %recv_cluster_hbm.1, bf16[384,256]{1,0:T(8,128)(2,1)} %features_hbm.1), custom_call_target="tpu_custom_call" | custom-call | flops 1024 | bytes 262144 | tf_op jit(solution)/shard_map/edge/pallas_call | solution.py:322
  0.9 4.1 %collective-permute-start.1 = (bf16[272,256]{1,0:T(8,128)(2,1)S(1)}, bf16[272,256]{1,0:T(8,128)(2,1)S(1)}, u32[]{:S(2)}, u32[]{:S(2)}) collective-permute-start(bf16[272,256]{1,0:T(8,128)(2,1)S(1)} %get-tuple-element.38.rest_0_), channel_id=1, source_target_pairs={{0,16},{8,24},{16,0},{24,8},{1,17},{9,25},{17,1},{25,9},{2,18},{10... | collective-permute-start | bytes 417800 | tf_op jit(solution)/shard_map/ppermute | solution.py:289
  5.0 1.6 %collective-permute-start = (bf16[272,256]{1,0:T(8,128)(2,1)S(1)}, bf16[272,256]{1,0:T(8,128)(2,1)S(1)}, u32[]{:S(2)}, u32[]{:S(2)}) collective-permute-start(bf16[272,256]{1,0:T(8,128)(2,1)S(1)} %get-tuple-element.38.rest_0_), channel_id=1, source_target_pairs={{0,8},{8,0},{16,24},{24,16},{1,9},{9,1},{17,25},{25,17},{2,10},{10... | collective-permute-start | bytes 417800 | tf_op jit(solution)/shard_map/ppermute | solution.py:289
  6.6 2.4 %collective-permute-start.4 = (bf16[272,256]{1,0:T(8,128)(2,1)S(1)}, bf16[272,256]{1,0:T(8,128)(2,1)S(1)}, u32[]{:S(2)}, u32[]{:S(2)}) collective-permute-start(bf16[272,256]{1,0:T(8,128)(2,1)S(1)} %get-tuple-element.38.rest_0_), channel_id=1, source_target_pairs={{0,6},{1,7},{2,4},{3,5},{4,2},{5,3},{6,0},{7,1},{8,14},{9,15},{10,... | collective-permute-start | bytes 417800 | tf_op jit(solution)/shard_map/ppermute | solution.py:289
  9.0 0.5 %collective-permute-start.3 = (bf16[272,256]{1,0:T(8,128)(2,1)S(1)}, bf16[272,256]{1,0:T(8,128)(2,1)S(1)}, u32[]{:S(2)}, u32[]{:S(2)}) collective-permute-start(bf16[272,256]{1,0:T(8,128)(2,1)S(1)} %get-tuple-element.38.rest_0_), channel_id=1, source_target_pairs={{0,4},{1,5},{2,6},{3,7},{4,0},{5,1},{6,2},{7,3},{8,12},{9,13},{10,... | collective-permute-start | bytes 417800 | tf_op jit(solution)/shard_map/ppermute | solution.py:289
  9.5 0.5 %collective-permute-start.2 = (bf16[272,256]{1,0:T(8,128)(2,1)S(1)}, bf16[272,256]{1,0:T(8,128)(2,1)S(1)}, u32[]{:S(2)}, u32[]{:S(2)}) collective-permute-start(bf16[272,256]{1,0:T(8,128)(2,1)S(1)} %get-tuple-element.38.rest_0_), channel_id=1, source_target_pairs={{0,2},{1,3},{2,0},{3,1},{4,6},{5,7},{6,4},{7,5},{8,10},{9,11},{10,... | collective-permute-start | bytes 417800 | tf_op jit(solution)/shard_map/ppermute | solution.py:289
  10.1 1.6 %prepare.1 = (bf16[384,1920]{1,0:T(8,128)(2,1)S(1)}, f32[12,256]{1,0:T(8,128)S(1)}, bf16[384,256]{1,0:T(8,128)(2,1)S(1)}, bf16[256,256]{1,0:T(8,128)(2,1)S(1)}, ...) custom-call(s32[24]{0:T(128)} %tile_dst_hbm.1, s32[24]{0:T(128)} %tile_src_hbm.1, ...), custom_call_target="tpu_custom_call" | custom-call | flops 100000000 | bytes 6291456 | tf_op jit(solution)/shard_map/prepare/pallas_call | solution.py:356
  11.7 0.4 %flip.1.dense_t.rest_8_ = bf16[1920,384]{1,0:T(8,128)(2,1)S(1)} custom-call(bf16[384,1920]{1,0:T(8,128)(2,1)S(1)} %get-tuple-element.42.dense), custom_call_target="tpu_custom_call" | custom-call | flops 10000000 | bytes 1048576 | tf_op jit(solution)/shard_map/flip/pallas_call | solution.py:386
  12.1 0.0 collective-permute-done.1.message.far.rest_1_
  12.2 0.0 collective-permute-done.near.rest_0_
  12.2 0.1 relay.1
  12.3 1.3 %collective-permute-start.7 = (bf16[128,256]{1,0:T(8,128)(2,1)S(1)}, bf16[128,256]{1,0:T(8,128)(2,1)S(1)}, u32[]{:S(2)}, u32[]{:S(2)}) collective-permute-start(bf16[128,256]{1,0:T(8,128)(2,1)S(1)} %relay.1), channel_id=1, source_target_pairs={{0,8},{8,0},{16,24},{24,16},{1,9},{9,1},{17,25},{25,17},{2,10},{10... | collective-permute-start | bytes 196616 | tf_op jit(solution)/shard_map/ppermute | solution.py:289
  13.6 0.0 collective-permute-start.5
  13.6 0.5 %first.1 = (f32[384,256]{1,0:T(8,128)S(1)}, f32[384,256]{1,0:T(8,128)S(1)}, f32[384,128]{1,0:T(8,128)S(1)}) custom-call(f32[12,256]{1,0:T(8,128)S(1)} %get-tuple-element.60.choice.rest_6_, bf16[384,1920]{1,0:T(8,128)(2,1)S(1)} %get-tuple-element.42.dense, bf16[384,256]{1,0:T(8,128)(2,1)S(1)} %get-tuple-element.49.features, ...), custom_call_target="tpu_custom_call" | custom-call | flops 1000000000 | bytes 3145728 | tf_op jit(solution)/shard_map/first/pallas_call | solution.py:408
  14.1 0.7 %collective-permute-done.5.rest_4_ = bf16[16,256]{1,0:T(8,128)(2,1)S(1)} collective-permute-done((bf16[16,256]{1,0:T(8,128)(2,1)S(1)}, bf16[16,256]{1,0:T(8,128)(2,1)S(1)}, u32[]{:S(2)}, u32[]{:S(2)}) %collective-permute-start.5) | collective-permute-done | bytes 8224 | tf_op jit(solution)/shard_map/ppermute | solution.py:289
  14.8 0.0 collective-permute-done.4.rest_3_.rest_4_
  14.8 0.5 %collective-permute-done.3.rest_2_.rest_3_ = bf16[272,256]{1,0:T(8,128)(2,1)S(1)} collective-permute-done((bf16[272,256]{1,0:T(8,128)(2,1)S(1)}, bf16[272,256]{1,0:T(8,128)(2,1)S(1)}, u32[]{:S(2)}, u32[]{:S(2)}) %collective-permute-start.3) | collective-permute-done | bytes 139296 | tf_op jit(solution)/shard_map/ppermute | solution.py:289
  15.3 0.1 collective-permute-done.2.rest_1_.rest_2_
  15.4 0.2 trade.1
  15.5 0.1 collective-permute-start.6
  15.6 0.3 near.1.before
  15.9 0.7 %collective-permute-done.7.rest_0_ = bf16[128,256]{1,0:T(8,128)(2,1)S(1)} collective-permute-done((bf16[128,256]{1,0:T(8,128)(2,1)S(1)}, bf16[128,256]{1,0:T(8,128)(2,1)S(1)}, u32[]{:S(2)}, u32[]{:S(2)}) %collective-permute-start.7) | collective-permute-done | bytes 65568 | tf_op jit(solution)/shard_map/ppermute | solution.py:289
  16.6 0.2 late.1.before
  16.8 0.4 %collective-permute-done.6.rest_0_.rest_5_ = bf16[576,256]{1,0:T(8,128)(2,1)S(1)} collective-permute-done((bf16[576,256]{1,0:T(8,128)(2,1)S(1)}, bf16[576,256]{1,0:T(8,128)(2,1)S(1)}, u32[]{:S(2)}, u32[]{:S(2)}) %collective-permute-start.6) | collective-permute-done | bytes 294944 | tf_op jit(solution)/shard_map/ppermute | solution.py:289
  17.2 1.2 %middle.1 = (bf16[256,256]{1,0:T(8,128)(2,1)S(1)}, bf16[256,256]{1,0:T(8,128)(2,1)S(1)}, bf16[256,256]{1,0:T(8,128)(2,1)S(1)}, bf16[144,256]{1,0:T(8,128)(2,1)S(...) custom-call(f32[12,256]{1,0:T(8,128)S(1)} %get-tuple-element.60.choi, ...), custom_call_target="tpu_custom_call" | custom-call | flops 377487360 | bytes 6291456 | tf_op jit(solution)/shard_map/middle/pallas_call | solution.py:463
  18.4 2.2 %collective-permute-start.10 = (bf16[256,256]{1,0:T(8,128)(2,1)S(1)}, bf16[256,256]{1,0:T(8,128)(2,1)S(1)}, u32[]{:S(2)}, u32[]{:S(2)}) collective-permute-start(bf16[256,256]{1,0:T(8,128)(2,1)S(1)} %get-tuple-element.59), channel_id=1, source_target_pairs={{0,6},{1,7},{2,4},{3,5},{4,2},{5,3},{6,0},{7,1},{8,14},{9,15},{10,... | collective-permute-start | bytes 393224 | tf_op jit(solution)/shard_map/ppermute | solution.py:289
  20.6 1.2 %collective-permute-start.9 = (bf16[144,256]{1,0:T(8,128)(2,1)S(1)}, bf16[144,256]{1,0:T(8,128)(2,1)S(1)}, u32[]{:S(2)}, u32[]{:S(2)}) collective-permute-start(bf16[144,256]{1,0:T(8,128)(2,1)S(1)} %get-tuple-element.57), channel_id=1, source_target_pairs={{0,8},{8,0},{16,24},{24,16},{1,9},{9,1},{17,25},{25,17},{2,10},{10... | collective-permute-start | bytes 221192 | tf_op jit(solution)/shard_map/ppermute | solution.py:289
  21.8 2.3 %collective-permute-start.8 = (bf16[128,256]{1,0:T(8,128)(2,1)S(1)}, bf16[128,256]{1,0:T(8,128)(2,1)S(1)}, u32[]{:S(2)}, u32[]{:S(2)}) collective-permute-start(bf16[128,256]{1,0:T(8,128)(2,1)S(1)} %get-tuple-element.55), channel_id=1, source_target_pairs={{0,24},{8,16},{16,8},{24,0},{1,25},{9,17},{17,9},{25,1},{2,26},{10... | collective-permute-start | bytes 196616 | tf_op jit(solution)/shard_map/ppermute | solution.py:289
  24.2 0.5 %collective-permute-start.12 = (bf16[256,256]{1,0:T(8,128)(2,1)S(1)}, bf16[256,256]{1,0:T(8,128)(2,1)S(1)}, u32[]{:S(2)}, u32[]{:S(2)}) collective-permute-start(bf16[256,256]{1,0:T(8,128)(2,1)S(1)} %get-tuple-element.67), channel_id=1, source_target_pairs={{0,4},{1,5},{2,6},{3,7},{4,0},{5,1},{6,2},{7,3},{8,12},{9,13},{10,... | collective-permute-start | bytes 393224 | tf_op jit(solution)/shard_map/ppermute | solution.py:289
  24.7 0.5 %collective-permute-start.13 = (bf16[256,256]{1,0:T(8,128)(2,1)S(1)}, bf16[256,256]{1,0:T(8,128)(2,1)S(1)}, u32[]{:S(2)}, u32[]{:S(2)}) collective-permute-start(bf16[256,256]{1,0:T(8,128)(2,1)S(1)} %get-tuple-element.68), channel_id=1, source_target_pairs={{0,2},{1,3},{2,0},{3,1},{4,6},{5,7},{6,4},{7,5},{8,10},{9,11},{10,... | collective-permute-start | bytes 393224 | tf_op jit(solution)/shard_map/ppermute | solution.py:289
  25.2 0.0 collective-permute-done.9.rest_0_
  25.2 2.3 %collective-permute-start.11 = (bf16[128,256]{1,0:T(8,128)(2,1)S(1)}, bf16[128,256]{1,0:T(8,128)(2,1)S(1)}, u32[]{:S(2)}, u32[]{:S(2)}) collective-permute-start(bf16[128,256]{1,0:T(8,128)(2,1)S(1)} %get-tuple-element.66), channel_id=1, source_target_pairs={{0,16},{8,24},{16,0},{24,8},{1,17},{9,25},{17,1},{25,9},{2,18},{10... | collective-permute-start | bytes 196616 | tf_op jit(solution)/shard_map/ppermute | solution.py:289
  27.5 0.0 collective-permute-done.10.rest_1_.rest_3_
  27.5 0.1 collective-permute-start.14
  27.6 0.9 %collective-permute-done.8.rest_2_ = bf16[128,256]{1,0:T(8,128)(2,1)S(1)} collective-permute-done((bf16[128,256]{1,0:T(8,128)(2,1)S(1)}, bf16[128,256]{1,0:T(8,128)(2,1)S(1)}, u32[]{:S(2)}, u32[]{:S(2)}) %collective-permute-start.8) | collective-permute-done | bytes 65568 | tf_op jit(solution)/shard_map/ppermute | solution.py:289
  28.5 0.3 own.1
  28.8 0.4 %collective-permute-done.12.rest_4_.rest_1_ = bf16[256,256]{1,0:T(8,128)(2,1)S(1)} collective-permute-done((bf16[256,256]{1,0:T(8,128)(2,1)S(1)}, bf16[256,256]{1,0:T(8,128)(2,1)S(1)}, u32[]{:S(2)}, u32[]{:S(2)}) %collective-permute-start.12) | collective-permute-done | bytes 131104 | tf_op jit(solution)/shard_map/ppermute | solution.py:289
  29.1 0.5 %collective-permute-done.13.rest_5_.rest_0_ = bf16[256,256]{1,0:T(8,128)(2,1)S(1)} collective-permute-done((bf16[256,256]{1,0:T(8,128)(2,1)S(1)}, bf16[256,256]{1,0:T(8,128)(2,1)S(1)}, u32[]{:S(2)}, u32[]{:S(2)}) %collective-permute-start.13) | collective-permute-done | bytes 131104 | tf_op jit(solution)/shard_map/ppermute | solution.py:289
  29.7 0.1 collective-permute-start.15
  29.7 1.3 %collective-permute-done.11.rest_1_ = bf16[128,256]{1,0:T(8,128)(2,1)S(1)} collective-permute-done((bf16[128,256]{1,0:T(8,128)(2,1)S(1)}, bf16[128,256]{1,0:T(8,128)(2,1)S(1)}, u32[]{:S(2)}, u32[]{:S(2)}) %collective-permute-start.11) | collective-permute-done | bytes 65568 | tf_op jit(solution)/shard_map/ppermute | solution.py:289
  31.1 0.2 add.1.total
  31.3 0.0 collective-permute-done.14.rest_0_
  31.3 0.0 collective-permute-done.15.rest_1_
  31.3 0.8 %final.1 = bf16[384,256]{1,0:T(8,128)(2,1)} custom-call(f32[12,256]{1,0:T(8,128)S(1)} %get-tuple-element.64.owner, f32[384,256]{1,0:T(8,128)S(1)} %add.1.total, bf16[256,256]{1,0:T(8,128)(2,1)S(1)} %collective-permute-done.14.rest_0_, bf16[256,256]{1,0:T(8,128)(2,1)S(1)} %collective-permute-done.15.rest_1_), custom_call_target="tpu_custom_call" | custom-call | flops 393216 | bytes 1048576 | tf_op jit(solution)/shard_map/final/pallas_call | solution.py:520
  (3 shorter events, 0.0 us)
Async XLA Ops:
  0.9 11.2 %collective-permute-start.1 = (bf16[272,256]{1,0:T(8,128)(2,1)S(1)}, bf16[272,256]{1,0:T(8,128)(2,1)S(1)}, u32[]{:S(2)}, u32[]{:S(2)}) collective-permute-start(bf16[272,256]{1,0:T(8,128)(2,1)S(1)} %get-tuple-element.38.rest_0_), channel_id=1, source_target_pairs={{0,16},{8,24},{16,0},{24,8},{1,17},{9,25},{17,1},{25,9},{2,18},{10... | collective-permute-start | bytes 417800 | tf_op jit(solution)/shard_map/ppermute | solution.py:289
  5.0 7.2 %collective-permute-start = (bf16[272,256]{1,0:T(8,128)(2,1)S(1)}, bf16[272,256]{1,0:T(8,128)(2,1)S(1)}, u32[]{:S(2)}, u32[]{:S(2)}) collective-permute-start(bf16[272,256]{1,0:T(8,128)(2,1)S(1)} %get-tuple-element.38.rest_0_), channel_id=1, source_target_pairs={{0,8},{8,0},{16,24},{24,16},{1,9},{9,1},{17,25},{25,17},{2,10},{10... | collective-permute-start | bytes 417800 | tf_op jit(solution)/shard_map/ppermute | solution.py:289
  6.6 8.2 %collective-permute-start.4 = (bf16[272,256]{1,0:T(8,128)(2,1)S(1)}, bf16[272,256]{1,0:T(8,128)(2,1)S(1)}, u32[]{:S(2)}, u32[]{:S(2)}) collective-permute-start(bf16[272,256]{1,0:T(8,128)(2,1)S(1)} %get-tuple-element.38.rest_0_), channel_id=1, source_target_pairs={{0,6},{1,7},{2,4},{3,5},{4,2},{5,3},{6,0},{7,1},{8,14},{9,15},{10,... | collective-permute-start | bytes 417800 | tf_op jit(solution)/shard_map/ppermute | solution.py:289
  9.0 6.3 %collective-permute-start.3 = (bf16[272,256]{1,0:T(8,128)(2,1)S(1)}, bf16[272,256]{1,0:T(8,128)(2,1)S(1)}, u32[]{:S(2)}, u32[]{:S(2)}) collective-permute-start(bf16[272,256]{1,0:T(8,128)(2,1)S(1)} %get-tuple-element.38.rest_0_), channel_id=1, source_target_pairs={{0,4},{1,5},{2,6},{3,7},{4,0},{5,1},{6,2},{7,3},{8,12},{9,13},{10,... | collective-permute-start | bytes 417800 | tf_op jit(solution)/shard_map/ppermute | solution.py:289
  9.5 5.8 %collective-permute-start.2 = (bf16[272,256]{1,0:T(8,128)(2,1)S(1)}, bf16[272,256]{1,0:T(8,128)(2,1)S(1)}, u32[]{:S(2)}, u32[]{:S(2)}) collective-permute-start(bf16[272,256]{1,0:T(8,128)(2,1)S(1)} %get-tuple-element.38.rest_0_), channel_id=1, source_target_pairs={{0,2},{1,3},{2,0},{3,1},{4,6},{5,7},{6,4},{7,5},{8,10},{9,11},{10,... | collective-permute-start | bytes 417800 | tf_op jit(solution)/shard_map/ppermute | solution.py:289
  12.3 4.3 %collective-permute-start.7 = (bf16[128,256]{1,0:T(8,128)(2,1)S(1)}, bf16[128,256]{1,0:T(8,128)(2,1)S(1)}, u32[]{:S(2)}, u32[]{:S(2)}) collective-permute-start(bf16[128,256]{1,0:T(8,128)(2,1)S(1)} %relay.1), channel_id=1, source_target_pairs={{0,8},{8,0},{16,24},{24,16},{1,9},{9,1},{17,25},{25,17},{2,10},{10... | collective-permute-start | bytes 196616 | tf_op jit(solution)/shard_map/ppermute | solution.py:289
  13.6 1.2 %collective-permute-start.5 = (bf16[16,256]{1,0:T(8,128)(2,1)S(1)}, bf16[16,256]{1,0:T(8,128)(2,1)S(1)}, u32[]{:S(2)}, u32[]{:S(2)}) collective-permute-start(bf16[16,256]{1,0:T(8,128)(2,1)S(1)} %get-tuple-element.44), channel_id=1, source_target_pairs={{0,1},{1,0},{2,3},{3,2},{4,5},{5,4},{6,7},{7,6},{8,9},{9,8},{10,11... | collective-permute-start | bytes 24584 | tf_op jit(solution)/shard_map/ppermute | solution.py:289
  15.5 1.6 %collective-permute-start.6 = (bf16[576,256]{1,0:T(8,128)(2,1)S(1)}, bf16[576,256]{1,0:T(8,128)(2,1)S(1)}, u32[]{:S(2)}, u32[]{:S(2)}) collective-permute-start(bf16[576,256]{1,0:T(8,128)(2,1)S(1)} %trade.1), channel_id=1, source_target_pairs={{0,1},{1,0},{2,3},{3,2},{4,5},{5,4},{6,7},{7,6},{8,9},{9,8},{10,11... | collective-permute-start | bytes 884744 | tf_op jit(solution)/shard_map/ppermute | solution.py:289
  18.4 9.0 %collective-permute-start.10 = (bf16[256,256]{1,0:T(8,128)(2,1)S(1)}, bf16[256,256]{1,0:T(8,128)(2,1)S(1)}, u32[]{:S(2)}, u32[]{:S(2)}) collective-permute-start(bf16[256,256]{1,0:T(8,128)(2,1)S(1)} %get-tuple-element.59), channel_id=1, source_target_pairs={{0,6},{1,7},{2,4},{3,5},{4,2},{5,3},{6,0},{7,1},{8,14},{9,15},{10,... | collective-permute-start | bytes 393224 | tf_op jit(solution)/shard_map/ppermute | solution.py:289
  20.6 4.6 %collective-permute-start.9 = (bf16[144,256]{1,0:T(8,128)(2,1)S(1)}, bf16[144,256]{1,0:T(8,128)(2,1)S(1)}, u32[]{:S(2)}, u32[]{:S(2)}) collective-permute-start(bf16[144,256]{1,0:T(8,128)(2,1)S(1)} %get-tuple-element.57), channel_id=1, source_target_pairs={{0,8},{8,0},{16,24},{24,16},{1,9},{9,1},{17,25},{25,17},{2,10},{10... | collective-permute-start | bytes 221192 | tf_op jit(solution)/shard_map/ppermute | solution.py:289
  21.8 6.6 %collective-permute-start.8 = (bf16[128,256]{1,0:T(8,128)(2,1)S(1)}, bf16[128,256]{1,0:T(8,128)(2,1)S(1)}, u32[]{:S(2)}, u32[]{:S(2)}) collective-permute-start(bf16[128,256]{1,0:T(8,128)(2,1)S(1)} %get-tuple-element.55), channel_id=1, source_target_pairs={{0,24},{8,16},{16,8},{24,0},{1,25},{9,17},{17,9},{25,1},{2,26},{10... | collective-permute-start | bytes 196616 | tf_op jit(solution)/shard_map/ppermute | solution.py:289
  24.2 5.0 %collective-permute-start.12 = (bf16[256,256]{1,0:T(8,128)(2,1)S(1)}, bf16[256,256]{1,0:T(8,128)(2,1)S(1)}, u32[]{:S(2)}, u32[]{:S(2)}) collective-permute-start(bf16[256,256]{1,0:T(8,128)(2,1)S(1)} %get-tuple-element.67), channel_id=1, source_target_pairs={{0,4},{1,5},{2,6},{3,7},{4,0},{5,1},{6,2},{7,3},{8,12},{9,13},{10,... | collective-permute-start | bytes 393224 | tf_op jit(solution)/shard_map/ppermute | solution.py:289
  24.7 5.0 %collective-permute-start.13 = (bf16[256,256]{1,0:T(8,128)(2,1)S(1)}, bf16[256,256]{1,0:T(8,128)(2,1)S(1)}, u32[]{:S(2)}, u32[]{:S(2)}) collective-permute-start(bf16[256,256]{1,0:T(8,128)(2,1)S(1)} %get-tuple-element.68), channel_id=1, source_target_pairs={{0,2},{1,3},{2,0},{3,1},{4,6},{5,7},{6,4},{7,5},{8,10},{9,11},{10,... | collective-permute-start | bytes 393224 | tf_op jit(solution)/shard_map/ppermute | solution.py:289
  25.2 5.9 %collective-permute-start.11 = (bf16[128,256]{1,0:T(8,128)(2,1)S(1)}, bf16[128,256]{1,0:T(8,128)(2,1)S(1)}, u32[]{:S(2)}, u32[]{:S(2)}) collective-permute-start(bf16[128,256]{1,0:T(8,128)(2,1)S(1)} %get-tuple-element.66), channel_id=1, source_target_pairs={{0,16},{8,24},{16,0},{24,8},{1,17},{9,25},{17,1},{25,9},{2,18},{10... | collective-permute-start | bytes 196616 | tf_op jit(solution)/shard_map/ppermute | solution.py:289
  27.5 3.8 %collective-permute-start.14 = (bf16[256,256]{1,0:T(8,128)(2,1)S(1)}, bf16[256,256]{1,0:T(8,128)(2,1)S(1)}, u32[]{:S(2)}, u32[]{:S(2)}) collective-permute-start(bf16[256,256]{1,0:T(8,128)(2,1)S(1)} %early.1), channel_id=1, source_target_pairs={{0,1},{1,0},{2,3},{3,2},{4,5},{5,4},{6,7},{7,6},{8,9},{9,8},{10,11... | collective-permute-start | bytes 393224 | tf_op jit(solution)/shard_map/ppermute | solution.py:289
  29.7 1.6 %collective-permute-start.15 = (bf16[256,256]{1,0:T(8,128)(2,1)S(1)}, bf16[256,256]{1,0:T(8,128)(2,1)S(1)}, u32[]{:S(2)}, u32[]{:S(2)}) collective-permute-start(bf16[256,256]{1,0:T(8,128)(2,1)S(1)} %turn.1), channel_id=1, source_target_pairs={{0,1},{1,0},{2,3},{3,2},{4,5},{5,4},{6,7},{7,6},{8,9},{9,8},{10,11... | collective-permute-start | bytes 393224 | tf_op jit(solution)/shard_map/ppermute | solution.py:289

commit v20 on v12

--- a/solution.py
+++ b/solution.py
@@ -498,12 +498,12 @@
         compiler_params=PARAMS,
         cost_estimate=cost(10**9, 2 * 1024 * 1024),
         name="own",
-    )(*arrays, after(choice, (far[-1][1], early)), w_self, dense_t, kept, spread, grad_pre)
+    )(*arrays, after(choice, early), w_self, dense_t, kept, spread, grad_pre)
 
     early = across(early, 1)
     turned = call(
         turn_kernel, jax.ShapeDtypeStruct((len(rest) * size, width), BF), "turn", 10**6,
-        *[after(value, total) for _, value in rest],
+        *[after(value, (total, far[-1][1])) for _, value in rest],
     )
     turned = across(turned, 1)
     more = [*far, *near[::-1]]

time: 31.5 us -> 32.5 us (1.032)
  waiting for transfers between devices: 5.97 us -> 6.82 us
    ppermute x16, waiting for transfers between devices: 5.97 us -> 6.82 us  [swap(): return lax.ppermute(value, axis, [(i, i ^ d) for i in range(count)])]
  transfers between devices with their start and end apart: 16 -> 16, of which waited for: 12 -> 11; matrix products, arithmetic and copies ran while one was open for 0% -> 0% of each run, Pallas kernels for 12% -> 12%
where the time goes in v20:
time: 32.5 us; the launch traced here: 32.3 us
  starting transfers between devices  18.6 us (57%)
  waiting for transfers between devices  6.82 us (21%)
  Pallas kernels  6.77 us (21%)
    ppermute x16, starting transfers between devices, swap(): return lax.ppermute(value, axis, [(i, i ^ d) for i in range(count)])  18.6 us
    ppermute x16, waiting for transfers between devices, swap(): return lax.ppermute(value, axis, [(i, i ^ d) for i in range(count)])  6.82 us
    pallas_call x1, Pallas kernels, shards(): pl.pallas_call(functools.partial(prepare_kernel, *counts), out_shape=[jax...  1.63 us
    pallas_call x1, Pallas kernels, shards(): pl.pallas_call(functools.partial(middle_kernel, *counts, late_halos, len(...  1.25 us
    pallas_call x3, Pallas kernels, sum_call(): pl.pallas_call(functools.partial(kernel, own, halos), out_shape=out_shape...  0.99 us
    pallas_call x7, Pallas kernels, call(): pl.pallas_call(kernel, out_shape=out_shape, in_specs=[VMEM] * len(operand...  0.92 us
    pallas_call x1, Pallas kernels, shards(): pl.pallas_call(edge_kernel, out_shape=[jax.ShapeDtypeStruct((BOUNDARY * s...  0.89 us
    pallas_call x1, Pallas kernels, shards(): pl.pallas_call(functools.partial(final_kernel, own, parts), out_shape=nar...  0.78 us
  transfers between devices with their start and end apart: 16, of which 11 were waited for; matrix products, arithmetic and copies ran while one was open for 0% of the time, Pallas kernels for 12%

profile of v20, /device:TPU:0, one launch (start us, length us, event | category | flops | bytes accessed | tf_op | source)
XLA Modules:
  0.0 32.3 jit_solution(2633684517962980532)
XLA Ops:
  0.0 0.9 %edge.1 = (bf16[272,256]{1,0:T(8,128)(2,1)S(1)}, bf16[16,256]{1,0:T(8,128)(2,1)S(1)}) custom-call(s32[1,8]{1,0:T(1,128)} %recv_sub_hbm.1, s32[1,4]{1,0:T(1,128)} %recv_cluster_hbm.1, bf16[384,256]{1,0:T(8,128)(2,1)} %features_hbm.1), custom_call_target="tpu_custom_call" | custom-call | flops 1024 | bytes 262144 | tf_op jit(solution)/shard_map/edge/pallas_call | solution.py:322
  0.9 4.1 %collective-permute-start.1 = (bf16[272,256]{1,0:T(8,128)(2,1)S(1)}, bf16[272,256]{1,0:T(8,128)(2,1)S(1)}, u32[]{:S(2)}, u32[]{:S(2)}) collective-permute-start(bf16[272,256]{1,0:T(8,128)(2,1)S(1)} %get-tuple-element.37.rest_0_), channel_id=1, source_target_pairs={{0,16},{8,24},{16,0},{24,8},{1,17},{9,25},{17,1},{25,9},{2,18},{10... | collective-permute-start | bytes 417800 | tf_op jit(solution)/shard_map/ppermute | solution.py:289
  5.0 1.6 %collective-permute-start = (bf16[272,256]{1,0:T(8,128)(2,1)S(1)}, bf16[272,256]{1,0:T(8,128)(2,1)S(1)}, u32[]{:S(2)}, u32[]{:S(2)}) collective-permute-start(bf16[272,256]{1,0:T(8,128)(2,1)S(1)} %get-tuple-element.37.rest_0_), channel_id=1, source_target_pairs={{0,8},{8,0},{16,24},{24,16},{1,9},{9,1},{17,25},{25,17},{2,10},{10... | collective-permute-start | bytes 417800 | tf_op jit(solution)/shard_map/ppermute | solution.py:289
  6.6 2.4 %collective-permute-start.4 = (bf16[272,256]{1,0:T(8,128)(2,1)S(1)}, bf16[272,256]{1,0:T(8,128)(2,1)S(1)}, u32[]{:S(2)}, u32[]{:S(2)}) collective-permute-start(bf16[272,256]{1,0:T(8,128)(2,1)S(1)} %get-tuple-element.37.rest_0_), channel_id=1, source_target_pairs={{0,6},{1,7},{2,4},{3,5},{4,2},{5,3},{6,0},{7,1},{8,14},{9,15},{10,... | collective-permute-start | bytes 417800 | tf_op jit(solution)/shard_map/ppermute | solution.py:289
  9.0 0.5 %collective-permute-start.3 = (bf16[272,256]{1,0:T(8,128)(2,1)S(1)}, bf16[272,256]{1,0:T(8,128)(2,1)S(1)}, u32[]{:S(2)}, u32[]{:S(2)}) collective-permute-start(bf16[272,256]{1,0:T(8,128)(2,1)S(1)} %get-tuple-element.37.rest_0_), channel_id=1, source_target_pairs={{0,4},{1,5},{2,6},{3,7},{4,0},{5,1},{6,2},{7,3},{8,12},{9,13},{10,... | collective-permute-start | bytes 417800 | tf_op jit(solution)/shard_map/ppermute | solution.py:289
  9.5 0.5 %collective-permute-start.2 = (bf16[272,256]{1,0:T(8,128)(2,1)S(1)}, bf16[272,256]{1,0:T(8,128)(2,1)S(1)}, u32[]{:S(2)}, u32[]{:S(2)}) collective-permute-start(bf16[272,256]{1,0:T(8,128)(2,1)S(1)} %get-tuple-element.37.rest_0_), channel_id=1, source_target_pairs={{0,2},{1,3},{2,0},{3,1},{4,6},{5,7},{6,4},{7,5},{8,10},{9,11},{10,... | collective-permute-start | bytes 417800 | tf_op jit(solution)/shard_map/ppermute | solution.py:289
  10.1 1.6 %prepare.1 = (bf16[384,1920]{1,0:T(8,128)(2,1)S(1)}, f32[12,256]{1,0:T(8,128)S(1)}, bf16[384,256]{1,0:T(8,128)(2,1)S(1)}, bf16[256,256]{1,0:T(8,128)(2,1)S(1)}, ...) custom-call(s32[24]{0:T(128)} %tile_dst_hbm.1, s32[24]{0:T(128)} %tile_src_hbm.1, ...), custom_call_target="tpu_custom_call" | custom-call | flops 100000000 | bytes 6291456 | tf_op jit(solution)/shard_map/prepare/pallas_call | solution.py:356
  11.7 0.1 collective-permute-done.1.message.far.rest_1_
  11.8 0.2 collective-permute-done.near.rest_0_
  12.0 0.1 relay.1
  12.1 1.5 %collective-permute-start.7 = (bf16[128,256]{1,0:T(8,128)(2,1)S(1)}, bf16[128,256]{1,0:T(8,128)(2,1)S(1)}, u32[]{:S(2)}, u32[]{:S(2)}) collective-permute-start(bf16[128,256]{1,0:T(8,128)(2,1)S(1)} %relay.1), channel_id=1, source_target_pairs={{0,8},{8,0},{16,24},{24,16},{1,9},{9,1},{17,25},{25,17},{2,10},{10... | collective-permute-start | bytes 196616 | tf_op jit(solution)/shard_map/ppermute | solution.py:289
  13.6 0.0 collective-permute-start.5
  13.6 0.5 %first.1 = (f32[384,256]{1,0:T(8,128)S(1)}, f32[384,256]{1,0:T(8,128)S(1)}, f32[384,128]{1,0:T(8,128)S(1)}) custom-call(f32[12,256]{1,0:T(8,128)S(1)} %get-tuple-element.56.choice.rest_6_, bf16[384,1920]{1,0:T(8,128)(2,1)S(1)} %get-tuple-element.50.dense, bf16[384,256]{1,0:T(8,128)(2,1)S(1)} %get-tuple-element.46.features, ...), custom_call_target="tpu_custom_call" | custom-call | flops 1000000000 | bytes 3145728 | tf_op jit(solution)/shard_map/first/pallas_call | solution.py:408
  14.1 0.7 %collective-permute-done.5.rest_4_ = bf16[16,256]{1,0:T(8,128)(2,1)S(1)} collective-permute-done((bf16[16,256]{1,0:T(8,128)(2,1)S(1)}, bf16[16,256]{1,0:T(8,128)(2,1)S(1)}, u32[]{:S(2)}, u32[]{:S(2)}) %collective-permute-start.5) | collective-permute-done | bytes 8224 | tf_op jit(solution)/shard_map/ppermute | solution.py:289
  14.8 0.0 collective-permute-done.4.rest_3_.rest_4_
  14.8 0.5 %collective-permute-done.3.rest_2_.rest_3_ = bf16[272,256]{1,0:T(8,128)(2,1)S(1)} collective-permute-done((bf16[272,256]{1,0:T(8,128)(2,1)S(1)}, bf16[272,256]{1,0:T(8,128)(2,1)S(1)}, u32[]{:S(2)}, u32[]{:S(2)}) %collective-permute-start.3) | collective-permute-done | bytes 139296 | tf_op jit(solution)/shard_map/ppermute | solution.py:289
  15.3 0.1 collective-permute-done.2.rest_1_.rest_2_
  15.4 0.2 trade.1
  15.5 0.1 collective-permute-start.6
  15.6 0.3 near.1.before
  15.9 0.4 %flip.1.dense_t.rest_8_ = bf16[1920,384]{1,0:T(8,128)(2,1)S(1)} custom-call(bf16[384,1920]{1,0:T(8,128)(2,1)S(1)} %get-tuple-element.50.dense), custom_call_target="tpu_custom_call" | custom-call | flops 10000000 | bytes 1048576 | tf_op jit(solution)/shard_map/flip/pallas_call | solution.py:386
  16.4 0.0 collective-permute-done.7.rest_0_
  16.4 0.2 late.1.before
  16.6 0.6 %collective-permute-done.6.rest_0_.rest_5_ = bf16[576,256]{1,0:T(8,128)(2,1)S(1)} collective-permute-done((bf16[576,256]{1,0:T(8,128)(2,1)S(1)}, bf16[576,256]{1,0:T(8,128)(2,1)S(1)}, u32[]{:S(2)}, u32[]{:S(2)}) %collective-permute-start.6) | collective-permute-done | bytes 294944 | tf_op jit(solution)/shard_map/ppermute | solution.py:289
  17.2 1.2 %middle.1 = (bf16[256,256]{1,0:T(8,128)(2,1)S(1)}, bf16[256,256]{1,0:T(8,128)(2,1)S(1)}, bf16[256,256]{1,0:T(8,128)(2,1)S(1)}, bf16[144,256]{1,0:T(8,128)(2,1)S(...) custom-call(f32[12,256]{1,0:T(8,128)S(1)} %get-tuple-element.56.choi, ...), custom_call_target="tpu_custom_call" | custom-call | flops 377487360 | bytes 6291456 | tf_op jit(solution)/shard_map/middle/pallas_call | solution.py:463
  18.4 2.0 %collective-permute-start.8 = (bf16[256,256]{1,0:T(8,128)(2,1)S(1)}, bf16[256,256]{1,0:T(8,128)(2,1)S(1)}, u32[]{:S(2)}, u32[]{:S(2)}) collective-permute-start(bf16[256,256]{1,0:T(8,128)(2,1)S(1)} %get-tuple-element.55), channel_id=1, source_target_pairs={{0,6},{1,7},{2,4},{3,5},{4,2},{5,3},{6,0},{7,1},{8,14},{9,15},{10,... | collective-permute-start | bytes 393224 | tf_op jit(solution)/shard_map/ppermute | solution.py:289
  20.4 1.1 %collective-permute-start.12 = (bf16[256,256]{1,0:T(8,128)(2,1)S(1)}, bf16[256,256]{1,0:T(8,128)(2,1)S(1)}, u32[]{:S(2)}, u32[]{:S(2)}) collective-permute-start(bf16[256,256]{1,0:T(8,128)(2,1)S(1)} %get-tuple-element.65), channel_id=1, source_target_pairs={{0,4},{1,5},{2,6},{3,7},{4,0},{5,1},{6,2},{7,3},{8,12},{9,13},{10,... | collective-permute-start | bytes 393224 | tf_op jit(solution)/shard_map/ppermute | solution.py:289
  21.5 0.5 %collective-permute-start.13 = (bf16[256,256]{1,0:T(8,128)(2,1)S(1)}, bf16[256,256]{1,0:T(8,128)(2,1)S(1)}, u32[]{:S(2)}, u32[]{:S(2)}) collective-permute-start(bf16[256,256]{1,0:T(8,128)(2,1)S(1)} %get-tuple-element.66), channel_id=1, source_target_pairs={{0,2},{1,3},{2,0},{3,1},{4,6},{5,7},{6,4},{7,5},{8,10},{9,11},{10,... | collective-permute-start | bytes 393224 | tf_op jit(solution)/shard_map/ppermute | solution.py:289
  22.0 1.8 %collective-permute-start.10 = (bf16[128,256]{1,0:T(8,128)(2,1)S(1)}, bf16[128,256]{1,0:T(8,128)(2,1)S(1)}, u32[]{:S(2)}, u32[]{:S(2)}) collective-permute-start(bf16[128,256]{1,0:T(8,128)(2,1)S(1)} %get-tuple-element.63), channel_id=1, source_target_pairs={{0,16},{8,24},{16,0},{24,8},{1,17},{9,25},{17,1},{25,9},{2,18},{10... | collective-permute-start | bytes 196616 | tf_op jit(solution)/shard_map/ppermute | solution.py:289
  23.7 1.5 %collective-permute-start.11 = (bf16[128,256]{1,0:T(8,128)(2,1)S(1)}, bf16[128,256]{1,0:T(8,128)(2,1)S(1)}, u32[]{:S(2)}, u32[]{:S(2)}) collective-permute-start(bf16[128,256]{1,0:T(8,128)(2,1)S(1)} %get-tuple-element.64), channel_id=1, source_target_pairs={{0,24},{8,16},{16,8},{24,0},{1,25},{9,17},{17,9},{25,1},{2,26},{10... | collective-permute-start | bytes 196616 | tf_op jit(solution)/shard_map/ppermute | solution.py:289
  25.3 0.5 %collective-permute-done.8.rest_1_.rest_3_ = bf16[256,256]{1,0:T(8,128)(2,1)S(1)} collective-permute-done((bf16[256,256]{1,0:T(8,128)(2,1)S(1)}, bf16[256,256]{1,0:T(8,128)(2,1)S(1)}, u32[]{:S(2)}, u32[]{:S(2)}) %collective-permute-start.8) | collective-permute-done | bytes 131104 | tf_op jit(solution)/shard_map/ppermute | solution.py:289
  25.7 0.5 %collective-permute-start.9 = (bf16[144,256]{1,0:T(8,128)(2,1)S(1)}, bf16[144,256]{1,0:T(8,128)(2,1)S(1)}, u32[]{:S(2)}, u32[]{:S(2)}) collective-permute-start(bf16[144,256]{1,0:T(8,128)(2,1)S(1)} %get-tuple-element.62), channel_id=1, source_target_pairs={{0,8},{8,0},{16,24},{24,16},{1,9},{9,1},{17,25},{25,17},{2,10},{10... | collective-permute-start | bytes 221192 | tf_op jit(solution)/shard_map/ppermute | solution.py:289
  26.2 0.3 own.1
  26.5 3.4 %collective-permute-done.11.rest_2_ = bf16[128,256]{1,0:T(8,128)(2,1)S(1)} collective-permute-done((bf16[128,256]{1,0:T(8,128)(2,1)S(1)}, bf16[128,256]{1,0:T(8,128)(2,1)S(1)}, u32[]{:S(2)}, u32[]{:S(2)}) %collective-permute-start.11) | collective-permute-done | bytes 65568 | tf_op jit(solution)/shard_map/ppermute | solution.py:289
  30.0 0.0 collective-permute-start.14
  30.0 0.0 collective-permute-done.12.rest_4_.rest_1_
  30.0 0.0 collective-permute-done.13.rest_5_.rest_0_
  30.0 0.6 %collective-permute-start.15 = (bf16[256,256]{1,0:T(8,128)(2,1)S(1)}, bf16[256,256]{1,0:T(8,128)(2,1)S(1)}, u32[]{:S(2)}, u32[]{:S(2)}) collective-permute-start(bf16[256,256]{1,0:T(8,128)(2,1)S(1)} %turn.1), channel_id=1, source_target_pairs={{0,1},{1,0},{2,3},{3,2},{4,5},{5,4},{6,7},{7,6},{8,9},{9,8},{10,11... | collective-permute-start | bytes 393224 | tf_op jit(solution)/shard_map/ppermute | solution.py:289
  30.6 0.0 collective-permute-done.10.rest_1_
  30.6 0.1 collective-permute-done.9.rest_0_
  30.7 0.2 add.1.total
  30.9 0.4 %collective-permute-done.14.rest_0_ = bf16[256,256]{1,0:T(8,128)(2,1)S(1)} collective-permute-done((bf16[256,256]{1,0:T(8,128)(2,1)S(1)}, bf16[256,256]{1,0:T(8,128)(2,1)S(1)}, u32[]{:S(2)}, u32[]{:S(2)}) %collective-permute-start.14) | collective-permute-done | bytes 131104 | tf_op jit(solution)/shard_map/ppermute | solution.py:289
  31.3 0.2 collective-permute-done.15.rest_1_
  31.6 0.8 %final.1 = bf16[384,256]{1,0:T(8,128)(2,1)} custom-call(f32[12,256]{1,0:T(8,128)S(1)} %get-tuple-element.60.owner, f32[384,256]{1,0:T(8,128)S(1)} %add.1.total, bf16[256,256]{1,0:T(8,128)(2,1)S(1)} %collective-permute-done.14.rest_0_, bf16[256,256]{1,0:T(8,128)(2,1)S(1)} %collective-permute-done.15.rest_1_), custom_call_target="tpu_custom_call" | custom-call | flops 393216 | bytes 1048576 | tf_op jit(solution)/shard_map/final/pallas_call | solution.py:520
  (3 shorter events, 0.0 us)
Async XLA Ops:
  0.9 10.9 %collective-permute-start.1 = (bf16[272,256]{1,0:T(8,128)(2,1)S(1)}, bf16[272,256]{1,0:T(8,128)(2,1)S(1)}, u32[]{:S(2)}, u32[]{:S(2)}) collective-permute-start(bf16[272,256]{1,0:T(8,128)(2,1)S(1)} %get-tuple-element.37.rest_0_), channel_id=1, source_target_pairs={{0,16},{8,24},{16,0},{24,8},{1,17},{9,25},{17,1},{25,9},{2,18},{10... | collective-permute-start | bytes 417800 | tf_op jit(solution)/shard_map/ppermute | solution.py:289
  5.0 7.0 %collective-permute-start = (bf16[272,256]{1,0:T(8,128)(2,1)S(1)}, bf16[272,256]{1,0:T(8,128)(2,1)S(1)}, u32[]{:S(2)}, u32[]{:S(2)}) collective-permute-start(bf16[272,256]{1,0:T(8,128)(2,1)S(1)} %get-tuple-element.37.rest_0_), channel_id=1, source_target_pairs={{0,8},{8,0},{16,24},{24,16},{1,9},{9,1},{17,25},{25,17},{2,10},{10... | collective-permute-start | bytes 417800 | tf_op jit(solution)/shard_map/ppermute | solution.py:289
  6.6 8.2 %collective-permute-start.4 = (bf16[272,256]{1,0:T(8,128)(2,1)S(1)}, bf16[272,256]{1,0:T(8,128)(2,1)S(1)}, u32[]{:S(2)}, u32[]{:S(2)}) collective-permute-start(bf16[272,256]{1,0:T(8,128)(2,1)S(1)} %get-tuple-element.37.rest_0_), channel_id=1, source_target_pairs={{0,6},{1,7},{2,4},{3,5},{4,2},{5,3},{6,0},{7,1},{8,14},{9,15},{10,... | collective-permute-start | bytes 417800 | tf_op jit(solution)/shard_map/ppermute | solution.py:289
  9.0 6.3 %collective-permute-start.3 = (bf16[272,256]{1,0:T(8,128)(2,1)S(1)}, bf16[272,256]{1,0:T(8,128)(2,1)S(1)}, u32[]{:S(2)}, u32[]{:S(2)}) collective-permute-start(bf16[272,256]{1,0:T(8,128)(2,1)S(1)} %get-tuple-element.37.rest_0_), channel_id=1, source_target_pairs={{0,4},{1,5},{2,6},{3,7},{4,0},{5,1},{6,2},{7,3},{8,12},{9,13},{10,... | collective-permute-start | bytes 417800 | tf_op jit(solution)/shard_map/ppermute | solution.py:289
  9.5 5.8 %collective-permute-start.2 = (bf16[272,256]{1,0:T(8,128)(2,1)S(1)}, bf16[272,256]{1,0:T(8,128)(2,1)S(1)}, u32[]{:S(2)}, u32[]{:S(2)}) collective-permute-start(bf16[272,256]{1,0:T(8,128)(2,1)S(1)} %get-tuple-element.37.rest_0_), channel_id=1, source_target_pairs={{0,2},{1,3},{2,0},{3,1},{4,6},{5,7},{6,4},{7,5},{8,10},{9,11},{10,... | collective-permute-start | bytes 417800 | tf_op jit(solution)/shard_map/ppermute | solution.py:289
  12.1 4.3 %collective-permute-start.7 = (bf16[128,256]{1,0:T(8,128)(2,1)S(1)}, bf16[128,256]{1,0:T(8,128)(2,1)S(1)}, u32[]{:S(2)}, u32[]{:S(2)}) collective-permute-start(bf16[128,256]{1,0:T(8,128)(2,1)S(1)} %relay.1), channel_id=1, source_target_pairs={{0,8},{8,0},{16,24},{24,16},{1,9},{9,1},{17,25},{25,17},{2,10},{10... | collective-permute-start | bytes 196616 | tf_op jit(solution)/shard_map/ppermute | solution.py:289
  13.6 1.2 %collective-permute-start.5 = (bf16[16,256]{1,0:T(8,128)(2,1)S(1)}, bf16[16,256]{1,0:T(8,128)(2,1)S(1)}, u32[]{:S(2)}, u32[]{:S(2)}) collective-permute-start(bf16[16,256]{1,0:T(8,128)(2,1)S(1)} %get-tuple-element.39), channel_id=1, source_target_pairs={{0,1},{1,0},{2,3},{3,2},{4,5},{5,4},{6,7},{7,6},{8,9},{9,8},{10,11... | collective-permute-start | bytes 24584 | tf_op jit(solution)/shard_map/ppermute | solution.py:289
  15.5 1.6 %collective-permute-start.6 = (bf16[576,256]{1,0:T(8,128)(2,1)S(1)}, bf16[576,256]{1,0:T(8,128)(2,1)S(1)}, u32[]{:S(2)}, u32[]{:S(2)}) collective-permute-start(bf16[576,256]{1,0:T(8,128)(2,1)S(1)} %trade.1), channel_id=1, source_target_pairs={{0,1},{1,0},{2,3},{3,2},{4,5},{5,4},{6,7},{7,6},{8,9},{9,8},{10,11... | collective-permute-start | bytes 884744 | tf_op jit(solution)/shard_map/ppermute | solution.py:289
  18.4 7.3 %collective-permute-start.8 = (bf16[256,256]{1,0:T(8,128)(2,1)S(1)}, bf16[256,256]{1,0:T(8,128)(2,1)S(1)}, u32[]{:S(2)}, u32[]{:S(2)}) collective-permute-start(bf16[256,256]{1,0:T(8,128)(2,1)S(1)} %get-tuple-element.55), channel_id=1, source_target_pairs={{0,6},{1,7},{2,4},{3,5},{4,2},{5,3},{6,0},{7,1},{8,14},{9,15},{10,... | collective-permute-start | bytes 393224 | tf_op jit(solution)/shard_map/ppermute | solution.py:289
  20.4 9.5 %collective-permute-start.12 = (bf16[256,256]{1,0:T(8,128)(2,1)S(1)}, bf16[256,256]{1,0:T(8,128)(2,1)S(1)}, u32[]{:S(2)}, u32[]{:S(2)}) collective-permute-start(bf16[256,256]{1,0:T(8,128)(2,1)S(1)} %get-tuple-element.65), channel_id=1, source_target_pairs={{0,4},{1,5},{2,6},{3,7},{4,0},{5,1},{6,2},{7,3},{8,12},{9,13},{10,... | collective-permute-start | bytes 393224 | tf_op jit(solution)/shard_map/ppermute | solution.py:289
  21.5 8.5 %collective-permute-start.13 = (bf16[256,256]{1,0:T(8,128)(2,1)S(1)}, bf16[256,256]{1,0:T(8,128)(2,1)S(1)}, u32[]{:S(2)}, u32[]{:S(2)}) collective-permute-start(bf16[256,256]{1,0:T(8,128)(2,1)S(1)} %get-tuple-element.66), channel_id=1, source_target_pairs={{0,2},{1,3},{2,0},{3,1},{4,6},{5,7},{6,4},{7,5},{8,10},{9,11},{10,... | collective-permute-start | bytes 393224 | tf_op jit(solution)/shard_map/ppermute | solution.py:289
  22.0 8.6 %collective-permute-start.10 = (bf16[128,256]{1,0:T(8,128)(2,1)S(1)}, bf16[128,256]{1,0:T(8,128)(2,1)S(1)}, u32[]{:S(2)}, u32[]{:S(2)}) collective-permute-start(bf16[128,256]{1,0:T(8,128)(2,1)S(1)} %get-tuple-element.63), channel_id=1, source_target_pairs={{0,16},{8,24},{16,0},{24,8},{1,17},{9,25},{17,1},{25,9},{2,18},{10... | collective-permute-start | bytes 196616 | tf_op jit(solution)/shard_map/ppermute | solution.py:289
  23.7 6.2 %collective-permute-start.11 = (bf16[128,256]{1,0:T(8,128)(2,1)S(1)}, bf16[128,256]{1,0:T(8,128)(2,1)S(1)}, u32[]{:S(2)}, u32[]{:S(2)}) collective-permute-start(bf16[128,256]{1,0:T(8,128)(2,1)S(1)} %get-tuple-element.64), channel_id=1, source_target_pairs={{0,24},{8,16},{16,8},{24,0},{1,25},{9,17},{17,9},{25,1},{2,26},{10... | collective-permute-start | bytes 196616 | tf_op jit(solution)/shard_map/ppermute | solution.py:289
  25.7 5.0 %collective-permute-start.9 = (bf16[144,256]{1,0:T(8,128)(2,1)S(1)}, bf16[144,256]{1,0:T(8,128)(2,1)S(1)}, u32[]{:S(2)}, u32[]{:S(2)}) collective-permute-start(bf16[144,256]{1,0:T(8,128)(2,1)S(1)} %get-tuple-element.62), channel_id=1, source_target_pairs={{0,8},{8,0},{16,24},{24,16},{1,9},{9,1},{17,25},{25,17},{2,10},{10... | collective-permute-start | bytes 221192 | tf_op jit(solution)/shard_map/ppermute | solution.py:289
  30.0 1.3 %collective-permute-start.14 = (bf16[256,256]{1,0:T(8,128)(2,1)S(1)}, bf16[256,256]{1,0:T(8,128)(2,1)S(1)}, u32[]{:S(2)}, u32[]{:S(2)}) collective-permute-start(bf16[256,256]{1,0:T(8,128)(2,1)S(1)} %early.1), channel_id=1, source_target_pairs={{0,1},{1,0},{2,3},{3,2},{4,5},{5,4},{6,7},{7,6},{8,9},{9,8},{10,11... | collective-permute-start | bytes 393224 | tf_op jit(solution)/shard_map/ppermute | solution.py:289
  30.0 1.6 %collective-permute-start.15 = (bf16[256,256]{1,0:T(8,128)(2,1)S(1)}, bf16[256,256]{1,0:T(8,128)(2,1)S(1)}, u32[]{:S(2)}, u32[]{:S(2)}) collective-permute-start(bf16[256,256]{1,0:T(8,128)(2,1)S(1)} %turn.1), channel_id=1, source_target_pairs={{0,1},{1,0},{2,3},{3,2},{4,5},{5,4},{6,7},{7,6},{8,9},{9,8},{10,11... | collective-permute-start | bytes 393224 | tf_op jit(solution)/shard_map/ppermute | solution.py:289

commit v21 on v19

--- a/solution.py
+++ b/solution.py
@@ -483,7 +483,7 @@
     soon, rest = near[-1:], near[:-1]
     early = call(
         turn_kernel, jax.ShapeDtypeStruct((2 * size, width), BF), "early", 10**8,
-        after(sibling, far[0][1]), *[value for _, value in soon],
+        sibling, *[value for _, value in soon],
     )
     order = [sub_count + 1, *(sub_count + d for d in direct), *even, *(d + 1 for d in even), 1]
     arrays, at = unique(order)

time: 32.3 us -> 31.5 us (0.975)
  starting transfers between devices: 19.7 us -> 18.2 us
  waiting for transfers between devices: 5.45 us -> 6.17 us
    ppermute x16, starting transfers between devices: 19.7 us -> 18.2 us  [swap(): return lax.ppermute(value, axis, [(i, i ^ d) for i in range(count)])]
    ppermute x16, waiting for transfers between devices: 5.45 us -> 6.17 us  [swap(): return lax.ppermute(value, axis, [(i, i ^ d) for i in range(count)])]
  transfers between devices with their start and end apart: 16 -> 16, of which waited for: 9 -> 11; matrix products, arithmetic and copies ran while one was open for 0% -> 0% of each run, Pallas kernels for 12% -> 12%
where the time goes in v21:
time: 31.5 us; the launch traced here: 31.3 us
  starting transfers between devices  18.2 us (58%)
  Pallas kernels  6.77 us (21%)
  waiting for transfers between devices  6.17 us (20%)
    ppermute x16, starting transfers between devices, swap(): return lax.ppermute(value, axis, [(i, i ^ d) for i in range(count)])  18.2 us
    ppermute x16, waiting for transfers between devices, swap(): return lax.ppermute(value, axis, [(i, i ^ d) for i in range(count)])  6.17 us
    pallas_call x1, Pallas kernels, shards(): pl.pallas_call(functools.partial(prepare_kernel, *counts), out_shape=[jax...  1.63 us
    pallas_call x1, Pallas kernels, shards(): pl.pallas_call(functools.partial(middle_kernel, *counts, late_halos, len(...  1.25 us
    pallas_call x3, Pallas kernels, sum_call(): pl.pallas_call(functools.partial(kernel, own, halos), out_shape=out_shape...  0.99 us
    pallas_call x7, Pallas kernels, call(): pl.pallas_call(kernel, out_shape=out_shape, in_specs=[VMEM] * len(operand...  0.93 us
    pallas_call x1, Pallas kernels, shards(): pl.pallas_call(edge_kernel, out_shape=[jax.ShapeDtypeStruct((BOUNDARY * s...  0.89 us
    pallas_call x1, Pallas kernels, shards(): pl.pallas_call(functools.partial(final_kernel, own, parts), out_shape=nar...  0.78 us
  transfers between devices with their start and end apart: 16, of which 11 were waited for; matrix products, arithmetic and copies ran while one was open for 0% of the time, Pallas kernels for 12%

profile of v21, /device:TPU:0, one launch (start us, length us, event | category | flops | bytes accessed | tf_op | source)
XLA Modules:
  0.0 31.3 jit_solution(2918158664311762537)
XLA Ops:
  0.0 0.9 %edge.1 = (bf16[272,256]{1,0:T(8,128)(2,1)S(1)}, bf16[16,256]{1,0:T(8,128)(2,1)S(1)}) custom-call(s32[1,8]{1,0:T(1,128)} %recv_sub_hbm.1, s32[1,4]{1,0:T(1,128)} %recv_cluster_hbm.1, bf16[384,256]{1,0:T(8,128)(2,1)} %features_hbm.1), custom_call_target="tpu_custom_call" | custom-call | flops 1024 | bytes 262144 | tf_op jit(solution)/shard_map/edge/pallas_call | solution.py:322
  0.9 4.1 %collective-permute-start.1 = (bf16[272,256]{1,0:T(8,128)(2,1)S(1)}, bf16[272,256]{1,0:T(8,128)(2,1)S(1)}, u32[]{:S(2)}, u32[]{:S(2)}) collective-permute-start(bf16[272,256]{1,0:T(8,128)(2,1)S(1)} %get-tuple-element.37.rest_0_), channel_id=1, source_target_pairs={{0,16},{8,24},{16,0},{24,8},{1,17},{9,25},{17,1},{25,9},{2,18},{10... | collective-permute-start | bytes 417800 | tf_op jit(solution)/shard_map/ppermute | solution.py:289
  5.0 1.6 %collective-permute-start = (bf16[272,256]{1,0:T(8,128)(2,1)S(1)}, bf16[272,256]{1,0:T(8,128)(2,1)S(1)}, u32[]{:S(2)}, u32[]{:S(2)}) collective-permute-start(bf16[272,256]{1,0:T(8,128)(2,1)S(1)} %get-tuple-element.37.rest_0_), channel_id=1, source_target_pairs={{0,8},{8,0},{16,24},{24,16},{1,9},{9,1},{17,25},{25,17},{2,10},{10... | collective-permute-start | bytes 417800 | tf_op jit(solution)/shard_map/ppermute | solution.py:289
  6.6 2.4 %collective-permute-start.4 = (bf16[272,256]{1,0:T(8,128)(2,1)S(1)}, bf16[272,256]{1,0:T(8,128)(2,1)S(1)}, u32[]{:S(2)}, u32[]{:S(2)}) collective-permute-start(bf16[272,256]{1,0:T(8,128)(2,1)S(1)} %get-tuple-element.37.rest_0_), channel_id=1, source_target_pairs={{0,6},{1,7},{2,4},{3,5},{4,2},{5,3},{6,0},{7,1},{8,14},{9,15},{10,... | collective-permute-start | bytes 417800 | tf_op jit(solution)/shard_map/ppermute | solution.py:289
  9.0 0.5 %collective-permute-start.3 = (bf16[272,256]{1,0:T(8,128)(2,1)S(1)}, bf16[272,256]{1,0:T(8,128)(2,1)S(1)}, u32[]{:S(2)}, u32[]{:S(2)}) collective-permute-start(bf16[272,256]{1,0:T(8,128)(2,1)S(1)} %get-tuple-element.37.rest_0_), channel_id=1, source_target_pairs={{0,4},{1,5},{2,6},{3,7},{4,0},{5,1},{6,2},{7,3},{8,12},{9,13},{10,... | collective-permute-start | bytes 417800 | tf_op jit(solution)/shard_map/ppermute | solution.py:289
  9.5 0.5 %collective-permute-start.2 = (bf16[272,256]{1,0:T(8,128)(2,1)S(1)}, bf16[272,256]{1,0:T(8,128)(2,1)S(1)}, u32[]{:S(2)}, u32[]{:S(2)}) collective-permute-start(bf16[272,256]{1,0:T(8,128)(2,1)S(1)} %get-tuple-element.37.rest_0_), channel_id=1, source_target_pairs={{0,2},{1,3},{2,0},{3,1},{4,6},{5,7},{6,4},{7,5},{8,10},{9,11},{10,... | collective-permute-start | bytes 417800 | tf_op jit(solution)/shard_map/ppermute | solution.py:289
  10.1 1.6 %prepare.1 = (bf16[384,1920]{1,0:T(8,128)(2,1)S(1)}, f32[12,256]{1,0:T(8,128)S(1)}, bf16[384,256]{1,0:T(8,128)(2,1)S(1)}, bf16[256,256]{1,0:T(8,128)(2,1)S(1)}, ...) custom-call(s32[24]{0:T(128)} %tile_dst_hbm.1, s32[24]{0:T(128)} %tile_src_hbm.1, ...), custom_call_target="tpu_custom_call" | custom-call | flops 100000000 | bytes 6291456 | tf_op jit(solution)/shard_map/prepare/pallas_call | solution.py:356
  11.7 0.4 %flip.1.dense_t.rest_8_ = bf16[1920,384]{1,0:T(8,128)(2,1)S(1)} custom-call(bf16[384,1920]{1,0:T(8,128)(2,1)S(1)} %get-tuple-element.41.dense), custom_call_target="tpu_custom_call" | custom-call | flops 10000000 | bytes 1048576 | tf_op jit(solution)/shard_map/flip/pallas_call | solution.py:386
  12.1 0.0 collective-permute-done.1.message.far.rest_1_
  12.2 0.0 collective-permute-done.near.rest_0_
  12.2 0.1 relay.1
  12.3 1.3 %collective-permute-start.7 = (bf16[128,256]{1,0:T(8,128)(2,1)S(1)}, bf16[128,256]{1,0:T(8,128)(2,1)S(1)}, u32[]{:S(2)}, u32[]{:S(2)}) collective-permute-start(bf16[128,256]{1,0:T(8,128)(2,1)S(1)} %relay.1), channel_id=1, source_target_pairs={{0,8},{8,0},{16,24},{24,16},{1,9},{9,1},{17,25},{25,17},{2,10},{10... | collective-permute-start | bytes 196616 | tf_op jit(solution)/shard_map/ppermute | solution.py:289
  13.6 0.0 collective-permute-start.5
  13.6 0.5 %first.1 = (f32[384,256]{1,0:T(8,128)S(1)}, f32[384,256]{1,0:T(8,128)S(1)}, f32[384,128]{1,0:T(8,128)S(1)}) custom-call(f32[12,256]{1,0:T(8,128)S(1)} %get-tuple-element.57.choice.rest_6_, bf16[384,1920]{1,0:T(8,128)(2,1)S(1)} %get-tuple-element.41.dense, bf16[384,256]{1,0:T(8,128)(2,1)S(1)} %get-tuple-element.48.features, ...), custom_call_target="tpu_custom_call" | custom-call | flops 1000000000 | bytes 3145728 | tf_op jit(solution)/shard_map/first/pallas_call | solution.py:408
  14.1 0.7 %collective-permute-done.5.rest_4_ = bf16[16,256]{1,0:T(8,128)(2,1)S(1)} collective-permute-done((bf16[16,256]{1,0:T(8,128)(2,1)S(1)}, bf16[16,256]{1,0:T(8,128)(2,1)S(1)}, u32[]{:S(2)}, u32[]{:S(2)}) %collective-permute-start.5) | collective-permute-done | bytes 8224 | tf_op jit(solution)/shard_map/ppermute | solution.py:289
  14.8 0.0 collective-permute-done.4.rest_3_.rest_4_
  14.8 0.5 %collective-permute-done.3.rest_2_.rest_3_ = bf16[272,256]{1,0:T(8,128)(2,1)S(1)} collective-permute-done((bf16[272,256]{1,0:T(8,128)(2,1)S(1)}, bf16[272,256]{1,0:T(8,128)(2,1)S(1)}, u32[]{:S(2)}, u32[]{:S(2)}) %collective-permute-start.3) | collective-permute-done | bytes 139296 | tf_op jit(solution)/shard_map/ppermute | solution.py:289
  15.3 0.1 collective-permute-done.2.rest_1_.rest_2_
  15.4 0.2 trade.1
  15.5 0.1 collective-permute-start.6
  15.6 0.3 near.1.before
  15.9 0.7 %collective-permute-done.7.rest_0_ = bf16[128,256]{1,0:T(8,128)(2,1)S(1)} collective-permute-done((bf16[128,256]{1,0:T(8,128)(2,1)S(1)}, bf16[128,256]{1,0:T(8,128)(2,1)S(1)}, u32[]{:S(2)}, u32[]{:S(2)}) %collective-permute-start.7) | collective-permute-done | bytes 65568 | tf_op jit(solution)/shard_map/ppermute | solution.py:289
  16.6 0.2 late.1.before
  16.8 0.4 %collective-permute-done.6.rest_0_.rest_5_ = bf16[576,256]{1,0:T(8,128)(2,1)S(1)} collective-permute-done((bf16[576,256]{1,0:T(8,128)(2,1)S(1)}, bf16[576,256]{1,0:T(8,128)(2,1)S(1)}, u32[]{:S(2)}, u32[]{:S(2)}) %collective-permute-start.6) | collective-permute-done | bytes 294944 | tf_op jit(solution)/shard_map/ppermute | solution.py:289
  17.2 1.2 %middle.1 = (bf16[256,256]{1,0:T(8,128)(2,1)S(1)}, bf16[256,256]{1,0:T(8,128)(2,1)S(1)}, bf16[256,256]{1,0:T(8,128)(2,1)S(1)}, bf16[144,256]{1,0:T(8,128)(2,1)S(...) custom-call(f32[12,256]{1,0:T(8,128)S(1)} %get-tuple-element.57.choi, ...), custom_call_target="tpu_custom_call" | custom-call | flops 377487360 | bytes 6291456 | tf_op jit(solution)/shard_map/middle/pallas_call | solution.py:463
  18.4 2.2 %collective-permute-start.9 = (bf16[256,256]{1,0:T(8,128)(2,1)S(1)}, bf16[256,256]{1,0:T(8,128)(2,1)S(1)}, u32[]{:S(2)}, u32[]{:S(2)}) collective-permute-start(bf16[256,256]{1,0:T(8,128)(2,1)S(1)} %get-tuple-element.56), channel_id=1, source_target_pairs={{0,6},{1,7},{2,4},{3,5},{4,2},{5,3},{6,0},{7,1},{8,14},{9,15},{10,... | collective-permute-start | bytes 393224 | tf_op jit(solution)/shard_map/ppermute | solution.py:289
  20.6 3.0 %collective-permute-start.8 = (bf16[128,256]{1,0:T(8,128)(2,1)S(1)}, bf16[128,256]{1,0:T(8,128)(2,1)S(1)}, u32[]{:S(2)}, u32[]{:S(2)}) collective-permute-start(bf16[128,256]{1,0:T(8,128)(2,1)S(1)} %get-tuple-element.54), channel_id=1, source_target_pairs={{0,24},{8,16},{16,8},{24,0},{1,25},{9,17},{17,9},{25,1},{2,26},{10... | collective-permute-start | bytes 196616 | tf_op jit(solution)/shard_map/ppermute | solution.py:289
  23.6 0.5 %collective-permute-start.12 = (bf16[256,256]{1,0:T(8,128)(2,1)S(1)}, bf16[256,256]{1,0:T(8,128)(2,1)S(1)}, u32[]{:S(2)}, u32[]{:S(2)}) collective-permute-start(bf16[256,256]{1,0:T(8,128)(2,1)S(1)} %get-tuple-element.65), channel_id=1, source_target_pairs={{0,4},{1,5},{2,6},{3,7},{4,0},{5,1},{6,2},{7,3},{8,12},{9,13},{10,... | collective-permute-start | bytes 393224 | tf_op jit(solution)/shard_map/ppermute | solution.py:289
  24.1 0.5 %collective-permute-start.13 = (bf16[256,256]{1,0:T(8,128)(2,1)S(1)}, bf16[256,256]{1,0:T(8,128)(2,1)S(1)}, u32[]{:S(2)}, u32[]{:S(2)}) collective-permute-start(bf16[256,256]{1,0:T(8,128)(2,1)S(1)} %get-tuple-element.66), channel_id=1, source_target_pairs={{0,2},{1,3},{2,0},{3,1},{4,6},{5,7},{6,4},{7,5},{8,10},{9,11},{10,... | collective-permute-start | bytes 393224 | tf_op jit(solution)/shard_map/ppermute | solution.py:289
  24.7 0.0 collective-permute-start.11
  24.7 0.3 %collective-permute-done.9.rest_1_.rest_3_ = bf16[256,256]{1,0:T(8,128)(2,1)S(1)} collective-permute-done((bf16[256,256]{1,0:T(8,128)(2,1)S(1)}, bf16[256,256]{1,0:T(8,128)(2,1)S(1)}, u32[]{:S(2)}, u32[]{:S(2)}) %collective-permute-start.9) | collective-permute-done | bytes 131104 | tf_op jit(solution)/shard_map/ppermute | solution.py:289
  25.0 1.4 %collective-permute-start.10 = (bf16[144,256]{1,0:T(8,128)(2,1)S(1)}, bf16[144,256]{1,0:T(8,128)(2,1)S(1)}, u32[]{:S(2)}, u32[]{:S(2)}) collective-permute-start(bf16[144,256]{1,0:T(8,128)(2,1)S(1)} %get-tuple-element.63), channel_id=1, source_target_pairs={{0,8},{8,0},{16,24},{24,16},{1,9},{9,1},{17,25},{25,17},{2,10},{10... | collective-permute-start | bytes 221192 | tf_op jit(solution)/shard_map/ppermute | solution.py:289
  26.4 0.8 %collective-permute-done.8.rest_2_ = bf16[128,256]{1,0:T(8,128)(2,1)S(1)} collective-permute-done((bf16[128,256]{1,0:T(8,128)(2,1)S(1)}, bf16[128,256]{1,0:T(8,128)(2,1)S(1)}, u32[]{:S(2)}, u32[]{:S(2)}) %collective-permute-start.8) | collective-permute-done | bytes 65568 | tf_op jit(solution)/shard_map/ppermute | solution.py:289
  27.2 0.0 collective-permute-start.14
  27.2 0.3 %own.1 = (f32[384,256]{1,0:T(8,128)S(1)}, f32[12,256]{1,0:T(8,128)S(1)}) custom-call(bf16[272,256]{1,0:T(8,128)(2,1)S(1)} %collective-permute-done.near.rest_0_, bf16[272,256]{1,0:T(8,128)(2,1)S(1)} %collective-permute-done.1.message.far.rest_1_, bf16[272,256]{1,0:T(8,128)(2,1)S(1)} %collective-permute-done.2.rest_1_.rest_2_, ...), custom_call_target="tpu_custom_call" | custom-call | flops 1000000000 | bytes 2097152 | tf_op jit(solution)/shard_map/own/pallas_call | solution.py:490
  27.5 1.1 %collective-permute-done.12.rest_4_.rest_1_ = bf16[256,256]{1,0:T(8,128)(2,1)S(1)} collective-permute-done((bf16[256,256]{1,0:T(8,128)(2,1)S(1)}, bf16[256,256]{1,0:T(8,128)(2,1)S(1)}, u32[]{:S(2)}, u32[]{:S(2)}) %collective-permute-start.12) | collective-permute-done | bytes 131104 | tf_op jit(solution)/shard_map/ppermute | solution.py:289
  28.6 0.5 %collective-permute-done.13.rest_5_.rest_0_ = bf16[256,256]{1,0:T(8,128)(2,1)S(1)} collective-permute-done((bf16[256,256]{1,0:T(8,128)(2,1)S(1)}, bf16[256,256]{1,0:T(8,128)(2,1)S(1)}, u32[]{:S(2)}, u32[]{:S(2)}) %collective-permute-start.13) | collective-permute-done | bytes 131104 | tf_op jit(solution)/shard_map/ppermute | solution.py:289
  29.1 0.1 collective-permute-start.15
  29.2 0.9 %collective-permute-done.11.rest_1_ = bf16[128,256]{1,0:T(8,128)(2,1)S(1)} collective-permute-done((bf16[128,256]{1,0:T(8,128)(2,1)S(1)}, bf16[128,256]{1,0:T(8,128)(2,1)S(1)}, u32[]{:S(2)}, u32[]{:S(2)}) %collective-permute-start.11) | collective-permute-done | bytes 65568 | tf_op jit(solution)/shard_map/ppermute | solution.py:289
  30.1 0.0 collective-permute-done.10.rest_0_
  30.1 0.2 add.1.total
  30.3 0.0 collective-permute-done.14.rest_0_
  30.3 0.2 collective-permute-done.15.rest_1_
  30.5 0.8 %final.1 = bf16[384,256]{1,0:T(8,128)(2,1)} custom-call(f32[12,256]{1,0:T(8,128)S(1)} %get-tuple-element.61.owner, f32[384,256]{1,0:T(8,128)S(1)} %add.1.total, bf16[256,256]{1,0:T(8,128)(2,1)S(1)} %collective-permute-done.14.rest_0_, bf16[256,256]{1,0:T(8,128)(2,1)S(1)} %collective-permute-done.15.rest_1_), custom_call_target="tpu_custom_call" | custom-call | flops 393216 | bytes 1048576 | tf_op jit(solution)/shard_map/final/pallas_call | solution.py:520
  (3 shorter events, 0.0 us)
Async XLA Ops:
  0.9 11.2 %collective-permute-start.1 = (bf16[272,256]{1,0:T(8,128)(2,1)S(1)}, bf16[272,256]{1,0:T(8,128)(2,1)S(1)}, u32[]{:S(2)}, u32[]{:S(2)}) collective-permute-start(bf16[272,256]{1,0:T(8,128)(2,1)S(1)} %get-tuple-element.37.rest_0_), channel_id=1, source_target_pairs={{0,16},{8,24},{16,0},{24,8},{1,17},{9,25},{17,1},{25,9},{2,18},{10... | collective-permute-start | bytes 417800 | tf_op jit(solution)/shard_map/ppermute | solution.py:289
  5.0 7.2 %collective-permute-start = (bf16[272,256]{1,0:T(8,128)(2,1)S(1)}, bf16[272,256]{1,0:T(8,128)(2,1)S(1)}, u32[]{:S(2)}, u32[]{:S(2)}) collective-permute-start(bf16[272,256]{1,0:T(8,128)(2,1)S(1)} %get-tuple-element.37.rest_0_), channel_id=1, source_target_pairs={{0,8},{8,0},{16,24},{24,16},{1,9},{9,1},{17,25},{25,17},{2,10},{10... | collective-permute-start | bytes 417800 | tf_op jit(solution)/shard_map/ppermute | solution.py:289
  6.6 8.2 %collective-permute-start.4 = (bf16[272,256]{1,0:T(8,128)(2,1)S(1)}, bf16[272,256]{1,0:T(8,128)(2,1)S(1)}, u32[]{:S(2)}, u32[]{:S(2)}) collective-permute-start(bf16[272,256]{1,0:T(8,128)(2,1)S(1)} %get-tuple-element.37.rest_0_), channel_id=1, source_target_pairs={{0,6},{1,7},{2,4},{3,5},{4,2},{5,3},{6,0},{7,1},{8,14},{9,15},{10,... | collective-permute-start | bytes 417800 | tf_op jit(solution)/shard_map/ppermute | solution.py:289
  9.0 6.3 %collective-permute-start.3 = (bf16[272,256]{1,0:T(8,128)(2,1)S(1)}, bf16[272,256]{1,0:T(8,128)(2,1)S(1)}, u32[]{:S(2)}, u32[]{:S(2)}) collective-permute-start(bf16[272,256]{1,0:T(8,128)(2,1)S(1)} %get-tuple-element.37.rest_0_), channel_id=1, source_target_pairs={{0,4},{1,5},{2,6},{3,7},{4,0},{5,1},{6,2},{7,3},{8,12},{9,13},{10,... | collective-permute-start | bytes 417800 | tf_op jit(solution)/shard_map/ppermute | solution.py:289
  9.5 5.8 %collective-permute-start.2 = (bf16[272,256]{1,0:T(8,128)(2,1)S(1)}, bf16[272,256]{1,0:T(8,128)(2,1)S(1)}, u32[]{:S(2)}, u32[]{:S(2)}) collective-permute-start(bf16[272,256]{1,0:T(8,128)(2,1)S(1)} %get-tuple-element.37.rest_0_), channel_id=1, source_target_pairs={{0,2},{1,3},{2,0},{3,1},{4,6},{5,7},{6,4},{7,5},{8,10},{9,11},{10,... | collective-permute-start | bytes 417800 | tf_op jit(solution)/shard_map/ppermute | solution.py:289
  12.3 4.3 %collective-permute-start.7 = (bf16[128,256]{1,0:T(8,128)(2,1)S(1)}, bf16[128,256]{1,0:T(8,128)(2,1)S(1)}, u32[]{:S(2)}, u32[]{:S(2)}) collective-permute-start(bf16[128,256]{1,0:T(8,128)(2,1)S(1)} %relay.1), channel_id=1, source_target_pairs={{0,8},{8,0},{16,24},{24,16},{1,9},{9,1},{17,25},{25,17},{2,10},{10... | collective-permute-start | bytes 196616 | tf_op jit(solution)/shard_map/ppermute | solution.py:289
  13.6 1.2 %collective-permute-start.5 = (bf16[16,256]{1,0:T(8,128)(2,1)S(1)}, bf16[16,256]{1,0:T(8,128)(2,1)S(1)}, u32[]{:S(2)}, u32[]{:S(2)}) collective-permute-start(bf16[16,256]{1,0:T(8,128)(2,1)S(1)} %get-tuple-element.43), channel_id=1, source_target_pairs={{0,1},{1,0},{2,3},{3,2},{4,5},{5,4},{6,7},{7,6},{8,9},{9,8},{10,11... | collective-permute-start | bytes 24584 | tf_op jit(solution)/shard_map/ppermute | solution.py:289
  15.5 1.6 %collective-permute-start.6 = (bf16[576,256]{1,0:T(8,128)(2,1)S(1)}, bf16[576,256]{1,0:T(8,128)(2,1)S(1)}, u32[]{:S(2)}, u32[]{:S(2)}) collective-permute-start(bf16[576,256]{1,0:T(8,128)(2,1)S(1)} %trade.1), channel_id=1, source_target_pairs={{0,1},{1,0},{2,3},{3,2},{4,5},{5,4},{6,7},{7,6},{8,9},{9,8},{10,11... | collective-permute-start | bytes 884744 | tf_op jit(solution)/shard_map/ppermute | solution.py:289
  18.4 6.6 %collective-permute-start.9 = (bf16[256,256]{1,0:T(8,128)(2,1)S(1)}, bf16[256,256]{1,0:T(8,128)(2,1)S(1)}, u32[]{:S(2)}, u32[]{:S(2)}) collective-permute-start(bf16[256,256]{1,0:T(8,128)(2,1)S(1)} %get-tuple-element.56), channel_id=1, source_target_pairs={{0,6},{1,7},{2,4},{3,5},{4,2},{5,3},{6,0},{7,1},{8,14},{9,15},{10,... | collective-permute-start | bytes 393224 | tf_op jit(solution)/shard_map/ppermute | solution.py:289
  20.6 6.5 %collective-permute-start.8 = (bf16[128,256]{1,0:T(8,128)(2,1)S(1)}, bf16[128,256]{1,0:T(8,128)(2,1)S(1)}, u32[]{:S(2)}, u32[]{:S(2)}) collective-permute-start(bf16[128,256]{1,0:T(8,128)(2,1)S(1)} %get-tuple-element.54), channel_id=1, source_target_pairs={{0,24},{8,16},{16,8},{24,0},{1,25},{9,17},{17,9},{25,1},{2,26},{10... | collective-permute-start | bytes 196616 | tf_op jit(solution)/shard_map/ppermute | solution.py:289
  23.6 5.0 %collective-permute-start.12 = (bf16[256,256]{1,0:T(8,128)(2,1)S(1)}, bf16[256,256]{1,0:T(8,128)(2,1)S(1)}, u32[]{:S(2)}, u32[]{:S(2)}) collective-permute-start(bf16[256,256]{1,0:T(8,128)(2,1)S(1)} %get-tuple-element.65), channel_id=1, source_target_pairs={{0,4},{1,5},{2,6},{3,7},{4,0},{5,1},{6,2},{7,3},{8,12},{9,13},{10,... | collective-permute-start | bytes 393224 | tf_op jit(solution)/shard_map/ppermute | solution.py:289
  24.1 5.0 %collective-permute-start.13 = (bf16[256,256]{1,0:T(8,128)(2,1)S(1)}, bf16[256,256]{1,0:T(8,128)(2,1)S(1)}, u32[]{:S(2)}, u32[]{:S(2)}) collective-permute-start(bf16[256,256]{1,0:T(8,128)(2,1)S(1)} %get-tuple-element.66), channel_id=1, source_target_pairs={{0,2},{1,3},{2,0},{3,1},{4,6},{5,7},{6,4},{7,5},{8,10},{9,11},{10,... | collective-permute-start | bytes 393224 | tf_op jit(solution)/shard_map/ppermute | solution.py:289
  24.7 5.4 %collective-permute-start.11 = (bf16[128,256]{1,0:T(8,128)(2,1)S(1)}, bf16[128,256]{1,0:T(8,128)(2,1)S(1)}, u32[]{:S(2)}, u32[]{:S(2)}) collective-permute-start(bf16[128,256]{1,0:T(8,128)(2,1)S(1)} %get-tuple-element.64), channel_id=1, source_target_pairs={{0,16},{8,24},{16,0},{24,8},{1,17},{9,25},{17,1},{25,9},{2,18},{10... | collective-permute-start | bytes 196616 | tf_op jit(solution)/shard_map/ppermute | solution.py:289
  25.0 5.1 %collective-permute-start.10 = (bf16[144,256]{1,0:T(8,128)(2,1)S(1)}, bf16[144,256]{1,0:T(8,128)(2,1)S(1)}, u32[]{:S(2)}, u32[]{:S(2)}) collective-permute-start(bf16[144,256]{1,0:T(8,128)(2,1)S(1)} %get-tuple-element.63), channel_id=1, source_target_pairs={{0,8},{8,0},{16,24},{24,16},{1,9},{9,1},{17,25},{25,17},{2,10},{10... | collective-permute-start | bytes 221192 | tf_op jit(solution)/shard_map/ppermute | solution.py:289
  27.2 3.1 %collective-permute-start.14 = (bf16[256,256]{1,0:T(8,128)(2,1)S(1)}, bf16[256,256]{1,0:T(8,128)(2,1)S(1)}, u32[]{:S(2)}, u32[]{:S(2)}) collective-permute-start(bf16[256,256]{1,0:T(8,128)(2,1)S(1)} %early.1), channel_id=1, source_target_pairs={{0,1},{1,0},{2,3},{3,2},{4,5},{5,4},{6,7},{7,6},{8,9},{9,8},{10,11... | collective-permute-start | bytes 393224 | tf_op jit(solution)/shard_map/ppermute | solution.py:289
  29.1 1.4 %collective-permute-start.15 = (bf16[256,256]{1,0:T(8,128)(2,1)S(1)}, bf16[256,256]{1,0:T(8,128)(2,1)S(1)}, u32[]{:S(2)}, u32[]{:S(2)}) collective-permute-start(bf16[256,256]{1,0:T(8,128)(2,1)S(1)} %turn.1), channel_id=1, source_target_pairs={{0,1},{1,0},{2,3},{3,2},{4,5},{5,4},{6,7},{7,6},{8,9},{9,8},{10,11... | collective-permute-start | bytes 393224 | tf_op jit(solution)/shard_map/ppermute | solution.py:289
